TPU v7x, 32 devices: a whole 2x2x4 slice. The times are simulated.
32 devices in a mesh: groups: 2 (over y), ctx: 4 (over x, core), chan: 4 (over z).
Axes of the slice: x: 2, y: 2, z: 4, core: 2. Of those that a mesh axis runs over, the one named last changes fastest.
Arguments:
- stream: bfloat16 [1536, 4096], P(('groups', 'ctx'), 'chan'), parts along dimension 0, may hold values from -30 to 30
- in_weights: bfloat16 [2, 4096, 3, 2048], P(None, 'ctx', None, 'chan'), may hold values from -0.09375 to 0.09375
- out_weights: bfloat16 [2, 4096, 2048], P(None, 'ctx', 'chan'), may hold values from -0.125 to 0.125
- short_taps: bfloat16 [7, 2048], P(None, 'chan'), may hold values from -2.390625 to 2.390625
- medium_taps: bfloat16 [128, 128], P(None, 'chan'), may hold values from -0.5390625 to 0.5390625
- plan: int32 [4], replicated, may hold values from 0 to 1
Outputs:
- result: bfloat16 [1536, 4096], P(('groups', 'ctx'), 'chan'), parts along dimension 0
There are 2 independent parts, one for each index of `groups`. A program takes and returns all parts, laid end to end along the dimension named above; an argument that names none is the same for every part. Nothing has to cross between parts.
All inputs are finite; a program needn't handle non-finite values.
Results may differ from a plain program's by a relative error of at most 0.03.
Values may be sent and summed in bfloat16 or wider, within the bound.
No kernel may reach another device: no remote copies, remote signals or barrier semaphores. Data moves between devices by JAX's collectives and lax.ppermute only.
A program may use at most 128 MiB of HBM per device.

v0:
```python
from functools import partial

import jax
import jax.numpy as jnp
from jax import lax
from jax.experimental import pallas as pl
from jax.experimental.pallas import tpu as pltpu
from jax.sharding import PartitionSpec as P

STEPS = 4
MIB = 1024 * 1024


def passed_along(value, axis, steps):
    count = lax.axis_size(axis)
    leading, last = (max(0, -steps), min(count, count - steps))
    return lax.ppermute(value, axis, [(source, source + steps) for source in range(leading, last)])


def section_taps(section, short_taps, medium_taps):
    reach = medium_taps.shape[0]
    channels = short_taps.shape[1]
    padding = jnp.zeros((reach - short_taps.shape[0], channels), short_taps.dtype)
    short_full = jnp.concatenate([short_taps, padding], 0)
    group_size = channels // medium_taps.shape[1]
    medium_full = jnp.broadcast_to(
        medium_taps[:, :, None], (reach, medium_taps.shape[1], group_size)
    ).reshape(reach, channels)
    return jnp.where(section == 0, short_full, medium_full)


def causal_filter(extended, filter_taps):
    filtered = lax.conv_general_dilated(
        extended[None],
        filter_taps[::-1][:, None, :],
        (1,),
        "VALID",
        dimension_numbers=("NWC", "WIO", "NWC"),
        feature_group_count=filter_taps.shape[1],
        preferred_element_type=jnp.float32,
    )
    return filtered[0]


def filter_gate(projected, section, short_taps, medium_taps):
    query_bf = projected[:, 0].astype(jnp.bfloat16)
    mixed_bf = (projected[:, 1] * projected[:, 2]).astype(jnp.bfloat16)
    reach = medium_taps.shape[0]
    earlier = passed_along(mixed_bf[-reach:], "ctx", 1)
    extended = jnp.concatenate([earlier[1:], mixed_bf], 0)
    filtered = causal_filter(extended, section_taps(section, short_taps, medium_taps))
    return (query_bf.astype(jnp.float32) * filtered).astype(jnp.bfloat16)


def general_shards(stream, in_weights, out_weights, short_taps, medium_taps, plan):
    hidden = stream
    weights_in = lax.all_gather(in_weights, "ctx", axis=1, tiled=True)
    weights_out = lax.all_gather(out_weights, "ctx", axis=1, tiled=True)
    for step in range(STEPS):
        section = plan[step]
        full_rows = lax.all_gather(hidden, "chan", axis=1, tiled=True)
        widened = full_rows.astype(jnp.float32)
        row_scale = lax.rsqrt(jnp.mean(widened * widened, axis=1, keepdims=True) + 1e-05)
        chosen = lax.dynamic_index_in_dim(weights_in, section, 0, keepdims=False)
        projected = jnp.dot(
            full_rows, chosen.reshape(chosen.shape[0], -1), preferred_element_type=jnp.float32
        )
        projected = projected.reshape(full_rows.shape[0], 3, -1) * row_scale[:, :, None]
        gated = filter_gate(projected, section, short_taps, medium_taps)
        chosen = lax.dynamic_index_in_dim(weights_out, section, 0, keepdims=False)
        product = lax.dot_general(
            gated, chosen, (((1,), (1,)), ((), ())), preferred_element_type=jnp.float32
        )
        update = lax.psum_scatter(
            product.astype(jnp.bfloat16), "chan", scatter_dimension=1, tiled=True
        ).astype(jnp.float32)
        hidden = (hidden.astype(jnp.float32) + update).astype(jnp.bfloat16)
    return hidden


SECOND, GROUP, SAME, ROW_OWN, ROW_CORE, ROW_CHIP, ROW_BOTH, HELD = range(8)


def ctx_pairs(change):
    return [(i, i ^ change) for i in range(4)]


def flat(i, j, g=None):
    return (i * 4 + j) if g is None else (g * 16 + i * 4 + j)


def in_kernel(sections, meta, section_ref, *refs):
    count = 1 if sections == 1 else 4
    pieces, refs = refs[:count], refs[count:]
    own_in, core_in = refs[:2]
    weights = [refs[2 + 6 * s : 8 + 6 * s] for s in range(sections)]
    query_ref, mixed_ref, hidden, held, total, held_sem = refs[2 + 6 * sections :]
    width = hidden.shape[2]
    part = width // 2
    group = meta[GROUP]
    section = section_ref[0]
    rows = (ROW_OWN, ROW_CORE, ROW_CHIP, ROW_BOTH)

    def span(q):
        return pl.ds(pl.multiple_of(q * part, part), part)

    def start(p, r, source, at, q):
        pltpu.make_async_copy(source, held.at[p, r, at], held_sem.at[p, r, q]).start()

    def start_section(chip, chip_y, both, both_y, chip_q, both_q):
        for p in (1, 2, 0):
            for q in range(2):
                start(p, 0, own_in.at[section, p, span(q)], span(q), q)
                start(p, 1, core_in.at[section, p, span(q)], span(q), q)
                if p == 0:
                    start(p, 2, chip_q.at[span(q)], span(q), q)
                    start(p, 3, both_q.at[span(q)], span(q), q)
            if p > 0:
                start(p, 2, chip.at[p - 1], span(group), 0)
                start(p, 2, chip_y.at[p - 1], span(1 - group), 1)
                start(p, 3, both.at[p - 1], span(group), 0)
                start(p, 3, both_y.at[p - 1], span(1 - group), 1)

    if sections == 1:
        start_section(*weights[0])
    else:
        for s in range(sections):
            pl.when(meta[SECOND] == s)(partial(start_section, *weights[s]))

    square = jnp.zeros((hidden.shape[1], 1), jnp.float32)
    for k in range(4):
        piece = pieces[k][...] if count > 1 else pieces[0][:, k * width : (k + 1) * width]
        hidden[meta[HELD + k] if count > 1 else k] = piece
        wide = piece.astype(jnp.float32)
        square = square + jnp.sum(wide * wide, axis=1, keepdims=True)
    scale = lax.rsqrt(square / (4 * width) + 1e-05)

    for p in (1, 2, 0):
        for r in range(4):
            for q in range(2):
                pltpu.make_async_copy(
                    own_in.at[0, 0, pl.ds(0, part)], held.at[p, r, pl.ds(0, part)], held_sem.at[p, r, q]
                ).wait()
            product = jnp.dot(
                hidden[meta[rows[r]]], held[p, r], preferred_element_type=jnp.float32
            )
            if r == 0:
                total[p] = product
            else:
                total[p] += product
    query_ref[...] = (total[0] * scale).astype(query_ref.dtype)
    mixed_ref[...] = ((total[1] * scale) * (total[2] * scale)).astype(mixed_ref.dtype)


def project_in(meta, section, pieces, own_in, core_in, weights):
    width, channels = own_in.shape[2:]
    tokens = pieces[0].shape[0]
    sections = len(weights)
    far = pl.BlockSpec(memory_space=pl.ANY)
    vmem = pl.BlockSpec(memory_space=pltpu.VMEM)
    smem = pl.BlockSpec(memory_space=pltpu.SMEM)
    out = jax.ShapeDtypeStruct((tokens, channels), jnp.bfloat16)
    return pl.pallas_call(
        partial(in_kernel, sections),
        out_shape=(out, out),
        in_specs=[smem] * 2 + [vmem] * len(pieces) + [far] * (2 + sum(len(w) for w in weights)),
        out_specs=(vmem, vmem),
        scratch_shapes=[
            pltpu.VMEM((4, tokens, width), jnp.bfloat16),
            pltpu.VMEM((3, 4, width, channels), jnp.bfloat16),
            pltpu.VMEM((3, tokens, channels), jnp.float32),
            pltpu.SemaphoreType.DMA((3, 4, 2)),
        ],
        compiler_params=pltpu.CompilerParams(vmem_limit_bytes=24 * MIB),
        cost_estimate=pl.CostEstimate(
            flops=24 * tokens * width * channels,
            bytes_accessed=24 * width * channels,
            transcendentals=0,
        ),
        name="project_in",
    )(meta, section, *pieces, own_in, core_in, *[w for ws in weights for w in ws])


BLOCK = 64


def filter_kernel(meta, halo, mixed, query, bands, short, gated, extended):
    reach, tokens = halo.shape[0], mixed.shape[0]
    channels = mixed.shape[1]
    group_size = channels // (bands.shape[0] // BLOCK)

    @pl.when(meta[0] == 0)
    def _():
        extended[:reach] = halo[...].astype(jnp.float32)
        extended[reach:] = mixed[...].astype(jnp.float32)
        taps = short[...].astype(jnp.float32)
        total = jnp.zeros((tokens, channels), jnp.float32)
        for t in range(taps.shape[0]):
            total = total + taps[t : t + 1] * extended[reach - t : reach - t + tokens]
        gated[...] = (query[...].astype(jnp.float32) * total).astype(gated.dtype)

    @pl.when(meta[0] != 0)
    def _():
        lanes = 128
        per_tile = lanes // group_size
        lane_group = lax.broadcasted_iota(jnp.int32, (BLOCK, lanes), 1) // group_size
        for tile in range(channels // lanes):
            at = slice(tile * lanes, (tile + 1) * lanes)
            column = jnp.concatenate([halo[:, at], mixed[:, at]], 0)
            band = bands[tile * per_tile * BLOCK : (tile + 1) * per_tile * BLOCK]
            for b in range(tokens // BLOCK):
                window = column[b * BLOCK : b * BLOCK + reach + BLOCK]
                product = jnp.dot(band, window, preferred_element_type=jnp.float32)
                total = product[:BLOCK]
                for m in range(1, per_tile):
                    total = jnp.where(
                        lane_group == m, product[m * BLOCK : (m + 1) * BLOCK], total
                    )
                rows = slice(b * BLOCK, (b + 1) * BLOCK)
                gated[rows, at] = (query[rows, at].astype(jnp.float32) * total).astype(gated.dtype)


def filter_and_gate(section, halo, mixed, query, bands, short):
    tokens, channels = mixed.shape
    vmem = pl.BlockSpec(memory_space=pltpu.VMEM)
    return pl.pallas_call(
        filter_kernel,
        out_shape=jax.ShapeDtypeStruct(mixed.shape, jnp.bfloat16),
        in_specs=[pl.BlockSpec(memory_space=pltpu.SMEM)] + [vmem] * 5,
        out_specs=vmem,
        scratch_shapes=[pltpu.VMEM((halo.shape[0] + tokens, channels), jnp.float32)],
        compiler_params=pltpu.CompilerParams(vmem_limit_bytes=8 * MIB),
        cost_estimate=pl.CostEstimate(
            flops=2 * tokens * channels * 1024, bytes_accessed=8 * tokens * channels, transcendentals=0
        ),
        name="filter_and_gate",
    )(section, halo, mixed, query, bands, short)


def tap_bands(medium_taps):
    reach, groups = medium_taps.shape
    length = 2 * reach
    zero = jnp.zeros((groups, 1), medium_taps.dtype)
    tail = jnp.zeros((groups, reach - 1), medium_taps.dtype)
    cycle = jnp.concatenate([zero, medium_taps[::-1].T, tail], 1)
    skewed = jnp.broadcast_to(cycle[:, None], (groups, BLOCK, length)).reshape(groups, -1)
    skewed = skewed[:, : BLOCK * (length - 1)].reshape(groups, BLOCK, length - 1)
    return skewed[:, :, : reach + BLOCK].reshape(groups * BLOCK, reach + BLOCK)


def out_kernel(sections, meta, section_ref, *refs):
    own_gated, core_gated, own_hidden, core_hidden, near = refs[:5]
    weights = [refs[5 + 4 * s : 9 + 4 * s] for s in range(sections)]
    own_out, core_out, held, held_sem = refs[5 + 4 * sections :]
    tokens, width = own_hidden.shape
    part = width // 2
    group = meta[GROUP]
    section = section_ref[0]
    mine = pl.ds(pl.multiple_of(group * part, part), part)
    other = pl.ds(pl.multiple_of((1 - group) * part, part), part)

    def start(k, first, second):
        pltpu.make_async_copy(first, held.at[k, mine], held_sem.at[k, 0]).start()
        pltpu.make_async_copy(second, held.at[k, other], held_sem.at[k, 1]).start()

    def start_same(came, came_y, sent, sent_y):
        start(0, near.at[section, mine], near.at[section, other])
        for k in range(1, 4):
            start(k, came.at[k - 1], came_y.at[k - 1])

    def start_cross(came, came_y, sent, sent_y):
        for k in range(4):
            start(k, sent.at[k], sent_y.at[k])

    for s in range(sections):
        for same in range(2):
            here = meta[SAME] == same
            if sections > 1:
                here = jnp.logical_and(here, meta[SECOND] == s)
            pl.when(here)(partial(start_same if same else start_cross, *weights[s]))

    total = None
    for k in range(4):
        for n, at in enumerate((mine, other)):
            pltpu.make_async_copy(weights[0][0].at[0], held.at[k, at], held_sem.at[k, n]).wait()
        both = jnp.concatenate([own_gated[k], core_gated[k]], 0)
        product = lax.dot_general(
            both, held[k], (((1,), (1,)), ((), ())), preferred_element_type=jnp.float32
        )
        total = product if total is None else total + product
    own_out[...] = (own_hidden[...].astype(jnp.float32) + total[:tokens]).astype(own_out.dtype)
    core_out[...] = (core_hidden[...].astype(jnp.float32) + total[tokens:]).astype(core_out.dtype)


def project_out(meta, section, own_gated, core_gated, own_hidden, core_hidden, near, weights):
    tokens, width = own_hidden.shape
    channels = own_gated.shape[2]
    sections = len(weights)
    far = pl.BlockSpec(memory_space=pl.ANY)
    vmem = pl.BlockSpec(memory_space=pltpu.VMEM)
    smem = pl.BlockSpec(memory_space=pltpu.SMEM)
    out = jax.ShapeDtypeStruct((tokens, width), jnp.bfloat16)
    return pl.pallas_call(
        partial(out_kernel, sections),
        out_shape=(out, out),
        in_specs=[smem] * 2 + [vmem] * 4 + [far] * (1 + 4 * sections),
        out_specs=(vmem, vmem),
        scratch_shapes=[
            pltpu.VMEM((4, width, channels), jnp.bfloat16),
            pltpu.SemaphoreType.DMA((4, 2)),
        ],
        compiler_params=pltpu.CompilerParams(vmem_limit_bytes=16 * MIB),
        cost_estimate=pl.CostEstimate(
            flops=16 * tokens * width * channels,
            bytes_accessed=8 * width * channels,
            transcendentals=0,
        ),
        name="project_out",
    )(
        meta,
        section,
        own_gated,
        core_gated,
        own_hidden,
        core_hidden,
        near,
        *[w for ws in weights for w in ws],
    )


def taken_kernel(at, in_ref, out_ref, out_half, kv_half, query, sem):
    section = at[0]
    part = out_half.shape[0]
    mine = pl.ds(pl.multiple_of(at[1] * part, part), part)
    copies = [
        pltpu.make_async_copy(in_ref.at[section, 1, mine], kv_half.at[0], sem.at[0]),
        pltpu.make_async_copy(in_ref.at[section, 2, mine], kv_half.at[1], sem.at[1]),
        pltpu.make_async_copy(out_ref.at[section, mine], out_half, sem.at[2]),
        pltpu.make_async_copy(in_ref.at[section, 0], query, sem.at[3]),
    ]
    for copy in copies:
        copy.start()
    for copy in copies:
        copy.wait()


def taken(section, g, in_weights, out_weights):
    width, channels = out_weights.shape[1:]
    part = width // 2
    far = pl.BlockSpec(memory_space=pl.ANY)
    near = pl.BlockSpec(memory_space=pltpu.VMEM)
    shapes = [(part, channels), (2, part, channels), (width, channels)]
    return pl.pallas_call(
        taken_kernel,
        out_shape=tuple(jax.ShapeDtypeStruct(shape, jnp.bfloat16) for shape in shapes),
        in_specs=[pl.BlockSpec(memory_space=pltpu.SMEM), far, far],
        out_specs=(near,) * len(shapes),
        scratch_shapes=[pltpu.SemaphoreType.DMA((4,))],
        compiler_params=pltpu.CompilerParams(vmem_limit_bytes=8 * MIB),
        name="taken",
    )(jnp.stack([section, g]).astype(jnp.int32), in_weights, out_weights)


def after(value, *others):
    return lax.optimization_barrier((value,) + others)[0]


EVERY = ("groups", "ctx", "chan")
PLANE = ("ctx", "chan")


class Rounds:
    def __init__(self):
        self.before, self.now = [], []

    def __call__(self, value, axes, pairs):
        return self.join(after(value, *self.before) if self.before else value, axes, pairs)

    def join(self, value, axes, pairs):
        self.now.append(lax.ppermute(value, axes, pairs))
        return self.now[-1]

    def turn(self):
        self.before, self.now = self.now, []


def along(k):
    return [
        (flat(2 * x + (j % 2), (j - k) % 4), flat(3 * x, j)) for x in range(2) for j in range(4)
    ]


def over_chips(source):
    return [(flat(source(x, j), j), flat(2 - x, j)) for x in range(2) for j in range(4)]


def over_groups(core):
    return [
        (flat(core(x), j, q), flat(core(x), j, 1 - q))
        for x in range(2)
        for j in range(4)
        for q in range(2)
    ]


CORES = ctx_pairs(1)
CHIPS = ctx_pairs(2)
GROUPS = [(0, 1), (1, 0)]
FROM_HOLDER = over_chips(lambda x, j: 2 * x + j % 2)
FROM_SAME = over_chips(lambda x, j: 3 * x)
SWAP_SAME = over_groups(lambda x: 3 * x)
SWAP_CROSS = over_groups(lambda x: 2 - x)
BESIDE = [(s, s ^ 1) for s in range(4)]
HALO = [(0, 1), (1, 2), (2, 3)]


def around(k):
    return [(s, (s + k) % 4) for s in range(4)]


def shards(stream, in_weights, out_weights, short_taps, medium_taps, plan):
    g, i, j = lax.axis_index("groups"), lax.axis_index("ctx"), lax.axis_index("chan")
    x, c, h = i // 2, i % 2, j % 2
    first = plan[0]
    reach = medium_taps.shape[0]
    width = stream.shape[1]
    part = width // 2
    in_weights = in_weights.transpose(0, 2, 1, 3)
    near = (j // 2) == c
    send = Rounds()
    bands = tap_bands(medium_taps)

    whole = lax.all_gather(stream, "chan", axis=1, tiled=True)
    send.now.append(whole)
    out_a, kv_a, q_a = taken(first, g, in_weights, out_weights)
    x_kv = send(kv_a, "ctx", CHIPS)
    x_q = send(q_a, "ctx", CHIPS)
    core_in = send(after(in_weights, q_a), "ctx", CORES)
    near_out = send(after(out_weights, q_a), PLANE, along(0))
    out_b, kv_b, q_b = taken(after(1 - first, q_a), g, in_weights, out_weights)
    send.now += [out_b, bands]

    def near_half(section):
        return lax.dynamic_slice(near_out, (section, g * part, 0), (1, part, near_out.shape[2]))

    send.turn()
    c_kv = send(x_kv, "ctx", CORES)
    c_q = send(x_q, "ctx", CORES)
    y_kv = send(x_kv, "groups", GROUPS)
    x_kv_b = send(kv_b, "ctx", CHIPS)
    z_a = {k: send(out_a, PLANE, along(k)) for k in (2, 1, 3)}

    send.turn()
    cy_kv = send(y_kv, "ctx", CORES)
    rest_a = jnp.stack([z_a[1], z_a[2], z_a[3]])
    sent_a = send(jnp.concatenate([near_half(first), rest_a]), PLANE, FROM_SAME)
    rest_y = send(rest_a, EVERY, SWAP_SAME)
    z_b = {k: send(out_b, PLANE, along(k)) for k in (2, 1, 3)}
    rest_b = jnp.stack([z_b[1], z_b[2], z_b[3]])

    send.turn()
    sent_y = send(sent_a, EVERY, SWAP_CROSS)
    x_q_b = send(q_b, "ctx", CHIPS)
    weights_in = [[x_kv, y_kv, c_kv, cy_kv, x_q, c_q]]
    weights_out = [[rest_a, rest_y, sent_a, sent_y]]

    own_hidden = lax.dynamic_slice_in_dim(whole, (2 * c + h) * width, width, 1)
    to_core = lax.dynamic_slice_in_dim(whole, (2 * (1 - c) + h) * width, width, 1)
    core_hidden = lax.ppermute(to_core, "ctx", CORES)
    pieces, slices = [whole], []

    for step in range(STEPS):
        count = 1 if step == 0 else 2
        section = plan[step]
        second = (section != first).astype(jnp.int32)
        section = section.reshape(1)
        scalars = [second, g, (x == c).astype(jnp.int32), i, i ^ 1, i ^ 2, i ^ 3] + slices
        meta = jnp.stack([jnp.asarray(s, jnp.int32) for s in scalars])
        query, mixed = project_in(meta, section, pieces, in_weights, core_in, weights_in[:count])
        halo = lax.ppermute(mixed[-reach:], "ctx", HALO)
        gated = filter_and_gate(section, halo, mixed, query, bands, short_taps)
        g_2, g_3, g_1 = (send.join(gated, "chan", around(k)) for k in (2, 3, 1))
        if step == 0:
            send.turn()
            y_kv_b = send(x_kv_b, "groups", GROUPS)
            sent_b = send(jnp.concatenate([near_half(1 - first), rest_b]), PLANE, FROM_SAME)
        own_gated = jnp.stack([gated, g_1, g_2, g_3])
        core_gated = lax.ppermute(own_gated, "ctx", CORES)
        own_hidden, core_hidden = project_out(
            meta,
            section,
            own_gated,
            core_gated,
            own_hidden,
            core_hidden,
            near_out,
            weights_out[:count],
        )
        swapped = lax.ppermute(core_hidden, "ctx", CORES)
        if step == STEPS - 1:
            return jnp.where(near, own_hidden, swapped)
        beside = send.join(own_hidden, "chan", BESIDE)
        beside_core = send.join(swapped, "chan", BESIDE)
        pieces = [own_hidden, swapped, beside, beside_core]
        slices = [2 * c + h, 2 * (1 - c) + h, 2 * c + 1 - h, 2 * (1 - c) + 1 - h]
        if step == 0:
            send.turn()
            c_q_b = send(x_q_b, "ctx", CORES)
            cy_kv_b = send(y_kv_b, "ctx", CORES)
            c_kv_b = send(x_kv_b, "ctx", CORES)
            rest_b_y = send(rest_b, EVERY, SWAP_SAME)
            sent_b_y = send(sent_b, EVERY, SWAP_CROSS)
            weights_in.append([x_kv_b, y_kv_b, c_kv_b, cy_kv_b, x_q_b, c_q_b])
            weights_out.append([rest_b, rest_b_y, sent_b, sent_b_y])


def solution(mesh):
    special = dict(mesh.shape) == {"groups": 2, "ctx": 4, "chan": 4}
    return jax.shard_map(
        shards if special else general_shards,
        mesh=mesh,
        in_specs=(
            P(("groups", "ctx"), "chan"),
            P(None, "ctx", None, "chan"),
            P(None, "ctx", "chan"),
            P(None, "chan"),
            P(None, "chan"),
            P(),
        ),
        out_specs=P(("groups", "ctx"), "chan"),
        check_vma=False,
    )
```

profile of v0, /device:TPU:0, one launch (start us, length us, event | category | flops | bytes accessed | tf_op | source)
XLA Modules:
  0.0 409.0 jit_solution(10340426884111179602)
XLA Ops:
  8.6 1.6 copy-done.15
  10.2 2.1 taken.2
  14.8 2.3 collective-permute-start.3
  17.1 2.9 collective-permute-start.1
  20.3 1.5 copy.7
  21.9 4.3 %reshape.11 = bf16[32,64,255]{2,1,0:T(8,128)(2,1)S(1)} reshape(bf16[32,16320]{1,0:T(8,128)(2,1)} %bitcast.57) | data formatting | bytes 2088960 | tf_op jit(solution)/shard_map/reshape | solution.py:247
  26.8 1.6 copy-done.16
  28.4 3.1 taken.3
  33.3 11.0 %collective-permute-done.1.refs_3_.refs_6_ = bf16[2,512,512]{2,1,0:T(8,128)(2,1)} collective-permute-done((bf16[2,512,512]{2,1,0:T(8,128)(2,1)}, bf16[2,512,512]{2,1,0:T(8,128)(2,1)}, u32[]{:S(2)}, u32[]{:S(2)}) %collective-permute-start.1) | collective-permute-done | bytes 1048608 | tf_op jit(solution)/shard_map/ppermute | solution.py:380
  44.3 21.0 %collective-permute-done.2.refs_7_.refs_10_ = bf16[1024,512]{1,0:T(8,128)(2,1)} collective-permute-done((bf16[1024,512]{1,0:T(8,128)(2,1)}, bf16[1024,512]{1,0:T(8,128)(2,1)}, u32[]{:S(2)}, u32[]{:S(2)}) %collective-permute-start.2) | collective-permute-done | bytes 1048608 | tf_op jit(solution)/shard_map/ppermute | solution.py:380
  67.9 6.4 %collective-permute-start.5 = (bf16[2,512,512]{2,1,0:T(8,128)(2,1)}, bf16[2,512,512]{2,1,0:T(8,128)(2,1)}, u32[]{:S(2)}, u32[]{:S(2)}) collective-permute-start(bf16[2,512,512]{2,1,0:T(8,128)(2,1)} %collective-permute-done.1.refs_3_.refs_6_), channel_id=1, source_target_pairs={{0,4},{4,0},{8,12},{12,8},{1,5},{5,1},{9,13},{13,9},{2,6},{6,2},{1... | collective-permute-start | bytes 3145736 | tf_op jit(solution)/shard_map/ppermute | solution.py:380
  76.7 7.6 %collective-permute-done.9 = bf16[512,512]{1,0:T(8,128)(2,1)} collective-permute-done((bf16[512,512]{1,0:T(8,128)(2,1)}, bf16[512,512]{1,0:T(8,128)(2,1)}, u32[]{:S(2)}, u32[]{:S(2)}) %collective-permute-start.9) | collective-permute-done | bytes 524320 | tf_op jit(solution)/shard_map/ppermute | solution.py:380
  84.3 3.8 collective-permute-start.8
  91.3 11.0 %collective-permute-done.8 = bf16[512,512]{1,0:T(8,128)(2,1)} collective-permute-done((bf16[512,512]{1,0:T(8,128)(2,1)}, bf16[512,512]{1,0:T(8,128)(2,1)}, u32[]{:S(2)}, u32[]{:S(2)}) %collective-permute-start.8) | collective-permute-done | bytes 524320 | tf_op jit(solution)/shard_map/ppermute | solution.py:380
  102.2 1.6 pad_maximum_fusion
  103.9 2.7 collective-permute-start.19
  108.2 3.4 collective-permute-start.18
  114.1 5.4 %collective-permute-start.11 = (bf16[2,512,512]{2,1,0:T(8,128)(2,1)}, bf16[2,512,512]{2,1,0:T(8,128)(2,1)S(1)}, u32[]{:S(2)}, u32[]{:S(2)}) collective-permute-start(bf16[2,512,512]{2,1,0:T(8,128)(2,1)} %collective-permute-done.4.refs_4_.refs_7_), channel_id=1, source_target_pairs={{0,4},{4,0},{8,12},{12,8},{1,5},{5,1},{9,13},{13,9},{2,6},{6,2},{1... | collective-permute-start | bytes 3145736 | tf_op jit(solution)/shard_map/ppermute | solution.py:380
  120.8 3.1 collective-permute-done.22
  123.9 5.0 %collective-permute-start.20 = (bf16[512,512]{1,0:T(8,128)(2,1)S(1)}, bf16[512,512]{1,0:T(8,128)(2,1)S(1)}, u32[]{:S(2)}, u32[]{:S(2)}) collective-permute-start(bf16[512,512]{1,0:T(8,128)(2,1)S(1)} %copy-done.36), channel_id=1, source_target_pairs={{2,0},{7,1},{0,2},{5,3},{10,12},{15,13},{8,14},{13,15},{18,16},{23... | collective-permute-start | bytes 1572872 | tf_op jit(solution)/shard_map/ppermute | solution.py:380
  128.9 6.4 %collective-permute-done.21 = bf16[512,512]{1,0:T(8,128)(2,1)S(1)} collective-permute-done((bf16[512,512]{1,0:T(8,128)(2,1)S(1)}, bf16[512,512]{1,0:T(8,128)(2,1)S(1)}, u32[]{:S(2)}, u32[]{:S(2)}) %collective-permute-start.21) | collective-permute-done | bytes 524320 | tf_op jit(solution)/shard_map/ppermute | solution.py:380
  135.3 8.2 %collective-permute-done.20 = bf16[512,512]{1,0:T(8,128)(2,1)S(1)} collective-permute-done((bf16[512,512]{1,0:T(8,128)(2,1)S(1)}, bf16[512,512]{1,0:T(8,128)(2,1)S(1)}, u32[]{:S(2)}, u32[]{:S(2)}) %collective-permute-start.20) | collective-permute-done | bytes 524320 | tf_op jit(solution)/shard_map/ppermute | solution.py:380
  145.9 2.0 collective-permute-start.23
  150.6 6.5 %project_in.4 = (bf16[192,512]{1,0:T(8,128)(2,1)S(1)}, bf16[192,512]{1,0:T(8,128)(2,1)S(1)}) custom-call(s32[7]{0:T(128)S(1)} %stack.205.meta, s32[1]{0:T(128)} %get-tuple-element.94.section_ref.meta, bf16[192,4096]{1,0:T(8,128)(2,1)S(1)} %copy-done.17, bf16[2,3,1024,512]{3,2,1,0:T(8,128)(2,1)} %bitcast.17.in_ref.refs_1_.refs_4_, ...), custom_call_target="tpu_custom_call" | custom-call | flops 2415919104 | bytes 12582912 | tf_op jit(solution)/shard_map/project_in/pallas_call | solution.py:163
  160.7 2.7 collective-permute-start.15
  164.1 1.6 pad_maximum_fusion.1
  166.6 8.7 %collective-permute-done.14 = bf16[192,512]{1,0:T(8,128)(2,1)S(1)} collective-permute-done((bf16[192,512]{1,0:T(8,128)(2,1)S(1)}, bf16[192,512]{1,0:T(8,128)(2,1)S(1)}, u32[]{:S(2)}, u32[]{:S(2)}) %collective-permute-start.14) | collective-permute-done | bytes 196640 | tf_op jit(solution)/shard_map/ppermute | solution.py:380
  175.3 13.9 %collective-permute-start.29 = (bf16[4,512,512]{2,1,0:T(8,128)(2,1)}, bf16[4,512,512]{2,1,0:T(8,128)(2,1)}, u32[]{:S(2)}, u32[]{:S(2)}) collective-permute-start(bf16[4,512,512]{2,1,0:T(8,128)(2,1)} %pad_maximum_fusion.1), channel_id=1, source_target_pairs={{0,8},{1,9},{2,10},{3,11},{12,4},{13,5},{14,6},{15,7},{16,24},{17,... | collective-permute-start | bytes 6291464 | tf_op jit(solution)/shard_map/ppermute | solution.py:380
  194.9 4.7 %project_out.4 = (bf16[192,1024]{1,0:T(8,128)(2,1)S(1)}, bf16[192,1024]{1,0:T(8,128)(2,1)S(1)}) custom-call(s32[7]{0:T(128)S(1)} %stack.205.meta, s32[1]{0:T(128)} %get-tuple-element.94.section_ref.meta, bf16[4,192,512]{2,1,0:T(8,128)(2,1)} %pad_maximum_fusion.4.refs_0_, bf16[4,192,512]{2,1,0:T(8,128)(2,1)} %collective-permute-done.16.refs_1_, ...), custom_call_target="tpu_custom_call" | custom-call | flops 1610612736 | bytes 4194304 | tf_op jit(solution)/shard_map/project_out/pallas_call | solution.py:303
  204.5 9.2 %collective-permute-done.25.refs_2_ = bf16[192,1024]{1,0:T(8,128)(2,1)S(1)} collective-permute-done((bf16[192,1024]{1,0:T(8,128)(2,1)S(1)}, bf16[192,1024]{1,0:T(8,128)(2,1)S(1)}, u32[]{:S(2)}, u32[]{:S(2)}) %collective-permute-start.25) | collective-permute-done | bytes 393248 | tf_op jit(solution)/shard_map/ppermute | solution.py:380
  214.5 6.7 %collective-permute-done.26.refs_3_ = bf16[192,1024]{1,0:T(8,128)(2,1)S(1)} collective-permute-done((bf16[192,1024]{1,0:T(8,128)(2,1)S(1)}, bf16[192,1024]{1,0:T(8,128)(2,1)S(1)}, u32[]{:S(2)}, u32[]{:S(2)}) %collective-permute-start.26) | collective-permute-done | bytes 393248 | tf_op jit(solution)/shard_map/ppermute | solution.py:380
  222.5 2.0 collective-permute-start.39
  225.9 2.4 collective-permute-start.38
  233.8 6.5 %project_in.5 = (bf16[192,512]{1,0:T(8,128)(2,1)S(1)}, bf16[192,512]{1,0:T(8,128)(2,1)S(1)}) custom-call(s32[11]{0:T(128)S(1)} %stack.204.meta, s32[1]{0:T(128)} %get-tuple-element.93.section_ref.meta, bf16[192,1024]{1,0:T(8,128)(2,1)S(1)} %get-tuple-element.66.refs_0_.refs_2_, bf16[192,1024]{1,0:T(8,128)(2,1)S(1)} %copy-done.26, ...), custom_call_target="tpu_custom_call" | custom-call | flops 2415919104 | bytes 12582912 | tf_op jit(solution)/shard_map/project_in/pallas_call | solution.py:163
  240.4 2.2 collective-permute-start.33
  244.8 1.9 collective-permute-start.36
  247.0 1.9 collective-permute-start.34
  248.9 3.8 collective-permute-done.36
  252.8 12.2 %collective-permute-done.35 = bf16[192,512]{1,0:T(8,128)(2,1)S(1)} collective-permute-done((bf16[192,512]{1,0:T(8,128)(2,1)S(1)}, bf16[192,512]{1,0:T(8,128)(2,1)S(1)}, u32[]{:S(2)}, u32[]{:S(2)}) %collective-permute-start.35) | collective-permute-done | bytes 196640 | tf_op jit(solution)/shard_map/ppermute | solution.py:380
  265.4 2.1 collective-permute-done.37.refs_1_
  267.5 4.3 %project_out.5 = (bf16[192,1024]{1,0:T(8,128)(2,1)}, bf16[192,1024]{1,0:T(8,128)(2,1)S(1)}) custom-call(s32[11]{0:T(128)S(1)} %stack.204.meta, s32[1]{0:T(128)} %get-tuple-element.93.section_ref.meta, bf16[4,192,512]{2,1,0:T(8,128)(2,1)S(1)} %pad_maximum_fusion.5.refs_0_, bf16[4,192,512]{2,1,0:T(8,128)(2,1)S(1)} %collective-permute-done.37.refs_1_, ...), custom_call_target="tpu_custom_call" | custom-call | flops 1610612736 | bytes 4194304 | tf_op jit(solution)/shard_map/project_out/pallas_call | solution.py:303
  277.2 9.0 %collective-permute-done.41.refs_2_ = bf16[192,1024]{1,0:T(8,128)(2,1)} collective-permute-done((bf16[192,1024]{1,0:T(8,128)(2,1)}, bf16[192,1024]{1,0:T(8,128)(2,1)}, u32[]{:S(2)}, u32[]{:S(2)}) %collective-permute-start.41) | collective-permute-done | bytes 393248 | tf_op jit(solution)/shard_map/ppermute | solution.py:380
  286.2 7.5 %collective-permute-done.42.refs_3_ = bf16[192,1024]{1,0:T(8,128)(2,1)} collective-permute-done((bf16[192,1024]{1,0:T(8,128)(2,1)S(1)}, bf16[192,1024]{1,0:T(8,128)(2,1)}, u32[]{:S(2)}, u32[]{:S(2)}) %collective-permute-start.42) | collective-permute-done | bytes 393248 | tf_op jit(solution)/shard_map/ppermute | solution.py:380
  294.9 7.2 %project_in.6 = (bf16[192,512]{1,0:T(8,128)(2,1)S(1)}, bf16[192,512]{1,0:T(8,128)(2,1)S(1)}) custom-call(s32[11]{0:T(128)S(1)} %stack.201.meta, s32[1]{0:T(128)} %get-tuple-element.96.section_ref.meta, bf16[192,1024]{1,0:T(8,128)(2,1)} %get-tuple-element.79.refs_0_.refs_2_, bf16[192,1024]{1,0:T(8,128)(2,1)S(1)} %collective-permute-done.40.refs_1_, ...), custom_call_target="tpu_custom_call" | custom-call | flops 2415919104 | bytes 12582912 | tf_op jit(solution)/shard_map/project_in/pallas_call | solution.py:163
  302.2 1.6 collective-permute-start.43
  306.2 3.0 collective-permute-start.46
  309.3 1.9 collective-permute-start.44
  311.2 3.3 collective-permute-done.46
  314.5 13.0 %collective-permute-done.45 = bf16[192,512]{1,0:T(8,128)(2,1)S(1)} collective-permute-done((bf16[192,512]{1,0:T(8,128)(2,1)S(1)}, bf16[192,512]{1,0:T(8,128)(2,1)S(1)}, u32[]{:S(2)}, u32[]{:S(2)}) %collective-permute-start.45) | collective-permute-done | bytes 196640 | tf_op jit(solution)/shard_map/ppermute | solution.py:380
  327.8 2.2 collective-permute-done.47.refs_1_
  330.0 4.1 %project_out.6 = (bf16[192,1024]{1,0:T(8,128)(2,1)S(1)}, bf16[192,1024]{1,0:T(8,128)(2,1)S(1)}) custom-call(s32[11]{0:T(128)S(1)} %stack.201.meta, s32[1]{0:T(128)} %get-tuple-element.96.section_ref.meta, bf16[4,192,512]{2,1,0:T(8,128)(2,1)S(1)} %pad_maximum_fusion.6.refs_0_, bf16[4,192,512]{2,1,0:T(8,128)(2,1)S(1)} %collective-permute-done.47.refs_1_, ...), custom_call_target="tpu_custom_call" | custom-call | flops 1610612736 | bytes 4194304 | tf_op jit(solution)/shard_map/project_out/pallas_call | solution.py:303
  339.5 8.8 %collective-permute-done.49.refs_2_ = bf16[192,1024]{1,0:T(8,128)(2,1)} collective-permute-done((bf16[192,1024]{1,0:T(8,128)(2,1)S(1)}, bf16[192,1024]{1,0:T(8,128)(2,1)}, u32[]{:S(2)}, u32[]{:S(2)}) %collective-permute-start.49) | collective-permute-done | bytes 393248 | tf_op jit(solution)/shard_map/ppermute | solution.py:380
  348.3 7.5 %collective-permute-done.50.refs_3_ = bf16[192,1024]{1,0:T(8,128)(2,1)} collective-permute-done((bf16[192,1024]{1,0:T(8,128)(2,1)}, bf16[192,1024]{1,0:T(8,128)(2,1)}, u32[]{:S(2)}, u32[]{:S(2)}) %collective-permute-start.50) | collective-permute-done | bytes 393248 | tf_op jit(solution)/shard_map/ppermute | solution.py:380
  357.0 7.5 %project_in.7 = (bf16[192,512]{1,0:T(8,128)(2,1)S(1)}, bf16[192,512]{1,0:T(8,128)(2,1)S(1)}) custom-call(s32[11]{0:T(128)S(1)} %stack.198.meta, s32[1]{0:T(128)} %get-tuple-element.95.section_ref.meta, bf16[192,1024]{1,0:T(8,128)(2,1)S(1)} %get-tuple-element.83.refs_0_.refs_2_, bf16[192,1024]{1,0:T(8,128)(2,1)} %collective-permute-done.48.refs_1_, ...), custom_call_target="tpu_custom_call" | custom-call | flops 2415919104 | bytes 12582912 | tf_op jit(solution)/shard_map/project_in/pallas_call | solution.py:163
  364.6 1.6 collective-permute-start.51
  367.1 1.6 filter_and_gate.7
  368.7 2.7 collective-permute-start.54
  371.6 1.9 collective-permute-start.52
  373.6 3.2 collective-permute-done.54
  376.8 13.1 %collective-permute-done.53 = bf16[192,512]{1,0:T(8,128)(2,1)S(1)} collective-permute-done((bf16[192,512]{1,0:T(8,128)(2,1)S(1)}, bf16[192,512]{1,0:T(8,128)(2,1)S(1)}, u32[]{:S(2)}, u32[]{:S(2)}) %collective-permute-start.53) | collective-permute-done | bytes 196640 | tf_op jit(solution)/shard_map/ppermute | solution.py:380
  390.1 2.2 collective-permute-done.55.refs_1_
  392.3 5.3 %project_out.7 = (bf16[192,1024]{1,0:T(8,128)(2,1)S(1)}, bf16[192,1024]{1,0:T(8,128)(2,1)}) custom-call(s32[11]{0:T(128)S(1)} %stack.198.meta, s32[1]{0:T(128)} %get-tuple-element.95.section_ref.meta, bf16[4,192,512]{2,1,0:T(8,128)(2,1)S(1)} %pad_maximum_fusion.7.refs_0_, bf16[4,192,512]{2,1,0:T(8,128)(2,1)S(1)} %collective-permute-done.55.refs_1_, ...), custom_call_target="tpu_custom_call" | custom-call | flops 1610612736 | bytes 4194304 | tf_op jit(solution)/shard_map/project_out/pallas_call | solution.py:303
  398.8 1.6 collective-permute-done.56
  400.3 1.8 broadcast_select_fusion
  (195 shorter events, 65.9 us)
Async XLA Ops:
  6.5 58.8 %all-gather.2.cloned.1.call-start = ((), (), s32[]{:S(2)}) async-start(), calls=%async_computation | async-start | bytes 1966080 | tf_op jit(solution)/shard_map/all_gather | solution.py:433
  14.3 51.0 %collective-permute-start = (bf16[2,3,1024,512]{3,2,1,0:T(8,128)(2,1)}, bf16[2,3,1024,512]{3,2,1,0:T(8,128)(2,1)}, u32[]{:S(2)}, u32[]{:S(2)}) collective-permute-start(bf16[2,3,1024,512]{3,2,1,0:T(8,128)(2,1)} %bitcast.17.in_ref.refs_1_.refs_4_), channel_id=1, source_target_pairs={{0,4},{4,0},{8,12},{12,8},{1,5},{5,1},{9,13},{13,9},{2,6},{6,2},{1... | collective-permute-start | bytes 18874376 | tf_op jit(solution)/shard_map/ppermute | solution.py:380
  14.8 50.5 %collective-permute-start.3 = (bf16[2,1024,512]{2,1,0:T(8,128)(2,1)}, bf16[2,1024,512]{2,1,0:T(8,128)(2,1)S(1)}, u32[]{:S(2)}, u32[]{:S(2)}) collective-permute-start(bf16[2,1024,512]{2,1,0:T(8,128)(2,1)} %out_ref.3), channel_id=1, source_target_pairs={{0,0},{5,1},{2,2},{7,3},{8,12},{13,13},{10,14},{15,15},{16,16},{21... | collective-permute-start | bytes 6291464 | tf_op jit(solution)/shard_map/ppermute | solution.py:380
  17.1 27.2 %collective-permute-start.1 = (bf16[2,512,512]{2,1,0:T(8,128)(2,1)}, bf16[2,512,512]{2,1,0:T(8,128)(2,1)}, u32[]{:S(2)}, u32[]{:S(2)}) collective-permute-start(bf16[2,512,512]{2,1,0:T(8,128)(2,1)} %copy-done.34), channel_id=1, source_target_pairs={{0,8},{4,12},{8,0},{12,4},{1,9},{5,13},{9,1},{13,5},{2,10},{6,14},... | collective-permute-start | bytes 3145736 | tf_op jit(solution)/shard_map/ppermute | solution.py:380
  19.9 45.4 %collective-permute-start.2 = (bf16[1024,512]{1,0:T(8,128)(2,1)}, bf16[1024,512]{1,0:T(8,128)(2,1)}, u32[]{:S(2)}, u32[]{:S(2)}) collective-permute-start(bf16[1024,512]{1,0:T(8,128)(2,1)} %copy-done.33), channel_id=1, source_target_pairs={{0,8},{4,12},{8,0},{12,4},{1,9},{5,13},{9,1},{13,5},{2,10},{6,14},... | collective-permute-start | bytes 3145736 | tf_op jit(solution)/shard_map/ppermute | solution.py:380
  65.3 11.4 %collective-permute-start.10 = (bf16[512,512]{1,0:T(8,128)(2,1)}, bf16[512,512]{1,0:T(8,128)(2,1)}, u32[]{:S(2)}, u32[]{:S(2)}) collective-permute-start(bf16[512,512]{1,0:T(8,128)(2,1)} %copy-done.37), channel_id=1, source_target_pairs={{1,0},{6,1},{3,2},{4,3},{9,12},{14,13},{11,14},{12,15},{17,16},{22... | collective-permute-start | bytes 1572872 | tf_op jit(solution)/shard_map/ppermute | solution.py:380
  66.6 17.7 %collective-permute-start.9 = (bf16[512,512]{1,0:T(8,128)(2,1)}, bf16[512,512]{1,0:T(8,128)(2,1)}, u32[]{:S(2)}, u32[]{:S(2)}) collective-permute-start(bf16[512,512]{1,0:T(8,128)(2,1)} %copy-done.37), channel_id=1, source_target_pairs={{3,0},{4,1},{1,2},{6,3},{11,12},{12,13},{9,14},{14,15},{19,16},{20... | collective-permute-start | bytes 1572872 | tf_op jit(solution)/shard_map/ppermute | solution.py:380
  67.9 36.0 %collective-permute-start.5 = (bf16[2,512,512]{2,1,0:T(8,128)(2,1)}, bf16[2,512,512]{2,1,0:T(8,128)(2,1)}, u32[]{:S(2)}, u32[]{:S(2)}) collective-permute-start(bf16[2,512,512]{2,1,0:T(8,128)(2,1)} %collective-permute-done.1.refs_3_.refs_6_), channel_id=1, source_target_pairs={{0,4},{4,0},{8,12},{12,8},{1,5},{5,1},{9,13},{13,9},{2,6},{6,2},{1... | collective-permute-start | bytes 3145736 | tf_op jit(solution)/shard_map/ppermute | solution.py:380
  74.3 29.6 %collective-permute-start.4 = (bf16[2,512,512]{2,1,0:T(8,128)(2,1)}, bf16[2,512,512]{2,1,0:T(8,128)(2,1)}, u32[]{:S(2)}, u32[]{:S(2)}) collective-permute-start(bf16[2,512,512]{2,1,0:T(8,128)(2,1)} %collective-permute-done.1.refs_3_.refs_6_), channel_id=1, source_target_pairs={{0,16},{16,0},{1,17},{17,1},{2,18},{18,2},{3,19},{19,3},{4,20},{20... | collective-permute-start | bytes 3145736 | tf_op jit(solution)/shard_map/ppermute | solution.py:380
  75.8 28.1 %collective-permute-start.6 = (bf16[1024,512]{1,0:T(8,128)(2,1)}, bf16[1024,512]{1,0:T(8,128)(2,1)}, u32[]{:S(2)}, u32[]{:S(2)}) collective-permute-start(bf16[1024,512]{1,0:T(8,128)(2,1)} %collective-permute-done.2.refs_7_.refs_10_), channel_id=1, source_target_pairs={{0,4},{4,0},{8,12},{12,8},{1,5},{5,1},{9,13},{13,9},{2,6},{6,2},{1... | collective-permute-start | bytes 3145736 | tf_op jit(solution)/shard_map/ppermute | solution.py:380
  76.7 27.2 %collective-permute-start.7 = (bf16[2,512,512]{2,1,0:T(8,128)(2,1)}, bf16[2,512,512]{2,1,0:T(8,128)(2,1)}, u32[]{:S(2)}, u32[]{:S(2)}) collective-permute-start(bf16[2,512,512]{2,1,0:T(8,128)(2,1)} %copy-done.32), channel_id=1, source_target_pairs={{0,8},{4,12},{8,0},{12,4},{1,9},{5,13},{9,1},{13,5},{2,10},{6,14},... | collective-permute-start | bytes 3145736 | tf_op jit(solution)/shard_map/ppermute | solution.py:380
  84.3 17.9 %collective-permute-start.8 = (bf16[512,512]{1,0:T(8,128)(2,1)}, bf16[512,512]{1,0:T(8,128)(2,1)}, u32[]{:S(2)}, u32[]{:S(2)}) collective-permute-start(bf16[512,512]{1,0:T(8,128)(2,1)} %copy-done.37), channel_id=1, source_target_pairs={{2,0},{7,1},{0,2},{5,3},{10,12},{15,13},{8,14},{13,15},{18,16},{23... | collective-permute-start | bytes 1572872 | tf_op jit(solution)/shard_map/ppermute | solution.py:380
  103.9 42.0 %collective-permute-start.19 = (bf16[4,512,512]{2,1,0:T(8,128)(2,1)S(1)}, bf16[4,512,512]{2,1,0:T(8,128)(2,1)}, u32[]{:S(2)}, u32[]{:S(2)}) collective-permute-start(bf16[4,512,512]{2,1,0:T(8,128)(2,1)S(1)} %pad_maximum_fusion), channel_id=1, source_target_pairs={{0,8},{1,9},{2,10},{3,11},{12,4},{13,5},{14,6},{15,7},{16,24},{17,... | collective-permute-start | bytes 6291464 | tf_op jit(solution)/shard_map/ppermute | solution.py:380
  108.2 36.5 %collective-permute-start.18 = (bf16[3,512,512]{2,1,0:T(8,128)(2,1)S(1)}, bf16[3,512,512]{2,1,0:T(8,128)(2,1)S(1)}, u32[]{:S(2)}, u32[]{:S(2)}) collective-permute-start(bf16[3,512,512]{2,1,0:T(8,128)(2,1)S(1)} %pad_maximum_fusion.2.refs_5_), channel_id=1, source_target_pairs={{0,16},{16,0},{1,17},{17,1},{2,18},{18,2},{3,19},{19,3},{12,28},{2... | collective-permute-start | bytes 4718600 | tf_op jit(solution)/shard_map/ppermute | solution.py:380
  112.8 11.1 %collective-permute-start.22 = (bf16[512,512]{1,0:T(8,128)(2,1)S(1)}, bf16[512,512]{1,0:T(8,128)(2,1)S(1)}, u32[]{:S(2)}, u32[]{:S(2)}) collective-permute-start(bf16[512,512]{1,0:T(8,128)(2,1)S(1)} %copy-done.36), channel_id=1, source_target_pairs={{1,0},{6,1},{3,2},{4,3},{9,12},{14,13},{11,14},{12,15},{17,16},{22... | collective-permute-start | bytes 1572872 | tf_op jit(solution)/shard_map/ppermute | solution.py:380
  114.1 29.5 %collective-permute-start.11 = (bf16[2,512,512]{2,1,0:T(8,128)(2,1)}, bf16[2,512,512]{2,1,0:T(8,128)(2,1)S(1)}, u32[]{:S(2)}, u32[]{:S(2)}) collective-permute-start(bf16[2,512,512]{2,1,0:T(8,128)(2,1)} %collective-permute-done.4.refs_4_.refs_7_), channel_id=1, source_target_pairs={{0,4},{4,0},{8,12},{12,8},{1,5},{5,1},{9,13},{13,9},{2,6},{6,2},{1... | collective-permute-start | bytes 3145736 | tf_op jit(solution)/shard_map/ppermute | solution.py:380
  119.5 15.9 %collective-permute-start.21 = (bf16[512,512]{1,0:T(8,128)(2,1)S(1)}, bf16[512,512]{1,0:T(8,128)(2,1)S(1)}, u32[]{:S(2)}, u32[]{:S(2)}) collective-permute-start(bf16[512,512]{1,0:T(8,128)(2,1)S(1)} %copy-done.36), channel_id=1, source_target_pairs={{3,0},{4,1},{1,2},{6,3},{11,12},{12,13},{9,14},{14,15},{19,16},{20... | collective-permute-start | bytes 1572872 | tf_op jit(solution)/shard_map/ppermute | solution.py:380
  123.9 19.7 %collective-permute-start.20 = (bf16[512,512]{1,0:T(8,128)(2,1)S(1)}, bf16[512,512]{1,0:T(8,128)(2,1)S(1)}, u32[]{:S(2)}, u32[]{:S(2)}) collective-permute-start(bf16[512,512]{1,0:T(8,128)(2,1)S(1)} %copy-done.36), channel_id=1, source_target_pairs={{2,0},{7,1},{0,2},{5,3},{10,12},{15,13},{8,14},{13,15},{18,16},{23... | collective-permute-start | bytes 1572872 | tf_op jit(solution)/shard_map/ppermute | solution.py:380
  145.9 29.4 %collective-permute-start.23 = (bf16[4,512,512]{2,1,0:T(8,128)(2,1)}, bf16[4,512,512]{2,1,0:T(8,128)(2,1)}, u32[]{:S(2)}, u32[]{:S(2)}) collective-permute-start(bf16[4,512,512]{2,1,0:T(8,128)(2,1)} %collective-permute-done.19.refs_7_), channel_id=1, source_target_pairs={{8,24},{24,8},{9,25},{25,9},{10,26},{26,10},{11,27},{27,11},{4,20}... | collective-permute-start | bytes 6291464 | tf_op jit(solution)/shard_map/ppermute | solution.py:380
  147.9 27.5 %collective-permute-start.27 = (bf16[1024,512]{1,0:T(8,128)(2,1)}, bf16[1024,512]{1,0:T(8,128)(2,1)}, u32[]{:S(2)}, u32[]{:S(2)}) collective-permute-start(bf16[1024,512]{1,0:T(8,128)(2,1)} %get-tuple-element.69), channel_id=1, source_target_pairs={{0,8},{4,12},{8,0},{12,4},{1,9},{5,13},{9,1},{13,5},{2,10},{6,14},... | collective-permute-start | bytes 3145736 | tf_op jit(solution)/shard_map/ppermute | solution.py:380
  157.2 2.4 collective-permute-start.12
  160.7 5.9 %collective-permute-start.15 = (bf16[192,512]{1,0:T(8,128)(2,1)S(1)}, bf16[192,512]{1,0:T(8,128)(2,1)S(1)}, u32[]{:S(2)}, u32[]{:S(2)}) collective-permute-start(bf16[192,512]{1,0:T(8,128)(2,1)S(1)} %filter_and_gate.4), channel_id=1, source_target_pairs={{0,3},{1,0},{2,1},{3,2},{4,7},{5,4},{6,5},{7,6},{8,11},{9,8},{10,9... | collective-permute-start | bytes 589832 | tf_op jit(solution)/shard_map/ppermute | solution.py:380
  163.4 11.9 %collective-permute-start.14 = (bf16[192,512]{1,0:T(8,128)(2,1)S(1)}, bf16[192,512]{1,0:T(8,128)(2,1)S(1)}, u32[]{:S(2)}, u32[]{:S(2)}) collective-permute-start(bf16[192,512]{1,0:T(8,128)(2,1)S(1)} %filter_and_gate.4), channel_id=1, source_target_pairs={{0,2},{1,3},{2,0},{3,1},{4,6},{5,7},{6,4},{7,5},{8,10},{9,11},{10,... | collective-permute-start | bytes 589832 | tf_op jit(solution)/shard_map/ppermute | solution.py:380
  163.4 11.9 %collective-permute-start.13 = (bf16[192,512]{1,0:T(8,128)(2,1)S(1)}, bf16[192,512]{1,0:T(8,128)(2,1)S(1)}, u32[]{:S(2)}, u32[]{:S(2)}) collective-permute-start(bf16[192,512]{1,0:T(8,128)(2,1)S(1)} %filter_and_gate.4), channel_id=1, source_target_pairs={{0,1},{1,2},{2,3},{3,0},{4,5},{5,6},{6,7},{7,4},{8,9},{9,10},{10,1... | collective-permute-start | bytes 589832 | tf_op jit(solution)/shard_map/ppermute | solution.py:380
  175.3 46.6 %collective-permute-start.29 = (bf16[4,512,512]{2,1,0:T(8,128)(2,1)}, bf16[4,512,512]{2,1,0:T(8,128)(2,1)}, u32[]{:S(2)}, u32[]{:S(2)}) collective-permute-start(bf16[4,512,512]{2,1,0:T(8,128)(2,1)} %pad_maximum_fusion.1), channel_id=1, source_target_pairs={{0,8},{1,9},{2,10},{3,11},{12,4},{13,5},{14,6},{15,7},{16,24},{17,... | collective-permute-start | bytes 6291464 | tf_op jit(solution)/shard_map/ppermute | solution.py:380
  190.2 3.2 collective-permute-start.16
  191.5 1.9 collective-permute-start.17
  192.1 29.8 %collective-permute-start.28 = (bf16[2,512,512]{2,1,0:T(8,128)(2,1)}, bf16[2,512,512]{2,1,0:T(8,128)(2,1)}, u32[]{:S(2)}, u32[]{:S(2)}) collective-permute-start(bf16[2,512,512]{2,1,0:T(8,128)(2,1)} %collective-permute-done.7.refs_12_), channel_id=1, source_target_pairs={{0,16},{16,0},{1,17},{17,1},{2,18},{18,2},{3,19},{19,3},{4,20},{20... | collective-permute-start | bytes 3145736 | tf_op jit(solution)/shard_map/ppermute | solution.py:380
  194.9 29.6 %copy-start.40 = (bf16[512,512]{1,0:T(8,128)(2,1)S(1)}, bf16[512,512]{1,0:T(8,128)(2,1)}, u32[]{:S(2)}) copy-start(bf16[512,512]{1,0:T(8,128)(2,1)} %copy-done.38) | copy-start | bytes 1572868
  194.9 29.6 %copy-start.43 = (bf16[512,512]{1,0:T(8,128)(2,1)S(1)}, bf16[512,512]{1,0:T(8,128)(2,1)}, u32[]{:S(2)}) copy-start(bf16[512,512]{1,0:T(8,128)(2,1)} %copy-done.41) | copy-start | bytes 1572868
  194.9 29.6 %copy-start.46 = (bf16[512,512]{1,0:T(8,128)(2,1)S(1)}, bf16[512,512]{1,0:T(8,128)(2,1)}, u32[]{:S(2)}) copy-start(bf16[512,512]{1,0:T(8,128)(2,1)} %copy-done.44) | copy-start | bytes 1572868
  199.6 2.7 collective-permute-start.24
  201.7 12.0 %collective-permute-start.25 = (bf16[192,1024]{1,0:T(8,128)(2,1)S(1)}, bf16[192,1024]{1,0:T(8,128)(2,1)S(1)}, u32[]{:S(2)}, u32[]{:S(2)}) collective-permute-start(bf16[192,1024]{1,0:T(8,128)(2,1)S(1)} %get-tuple-element.66.refs_0_.refs_2_), channel_id=1, source_target_pairs={{0,1},{1,0},{2,3},{3,2},{4,5},{5,4},{6,7},{7,6},{8,9},{9,8},{10,11... | collective-permute-start | bytes 1179656 | tf_op jit(solution)/shard_map/ppermute | solution.py:380
  202.3 18.9 %collective-permute-start.26 = (bf16[192,1024]{1,0:T(8,128)(2,1)S(1)}, bf16[192,1024]{1,0:T(8,128)(2,1)S(1)}, u32[]{:S(2)}, u32[]{:S(2)}) collective-permute-start(bf16[192,1024]{1,0:T(8,128)(2,1)S(1)} %collective-permute-done.24.refs_1_), channel_id=1, source_target_pairs={{0,1},{1,0},{2,3},{3,2},{4,5},{5,4},{6,7},{7,6},{8,9},{9,8},{10,11... | collective-permute-start | bytes 1179656 | tf_op jit(solution)/shard_map/ppermute | solution.py:380
  221.9 7.6 %collective-permute-start.30 = (bf16[2,512,512]{2,1,0:T(8,128)(2,1)}, bf16[2,512,512]{2,1,0:T(8,128)(2,1)}, u32[]{:S(2)}, u32[]{:S(2)}) collective-permute-start(bf16[2,512,512]{2,1,0:T(8,128)(2,1)} %collective-permute-done.7.refs_12_), channel_id=1, source_target_pairs={{0,4},{4,0},{8,12},{12,8},{1,5},{5,1},{9,13},{13,9},{2,6},{6,2},{1... | collective-permute-start | bytes 3145736 | tf_op jit(solution)/shard_map/ppermute | solution.py:380
  221.9 7.6 %collective-permute-start.31 = (bf16[2,512,512]{2,1,0:T(8,128)(2,1)}, bf16[2,512,512]{2,1,0:T(8,128)(2,1)}, u32[]{:S(2)}, u32[]{:S(2)}) collective-permute-start(bf16[2,512,512]{2,1,0:T(8,128)(2,1)} %collective-permute-done.28.refs_13_), channel_id=1, source_target_pairs={{0,4},{4,0},{8,12},{12,8},{1,5},{5,1},{9,13},{13,9},{2,6},{6,2},{1... | collective-permute-start | bytes 3145736 | tf_op jit(solution)/shard_map/ppermute | solution.py:380
  222.4 7.1 %collective-permute-start.32 = (bf16[1024,512]{1,0:T(8,128)(2,1)}, bf16[1024,512]{1,0:T(8,128)(2,1)}, u32[]{:S(2)}, u32[]{:S(2)}) collective-permute-start(bf16[1024,512]{1,0:T(8,128)(2,1)} %collective-permute-done.27.refs_16_), channel_id=1, source_target_pairs={{0,4},{4,0},{8,12},{12,8},{1,5},{5,1},{9,13},{13,9},{2,6},{6,2},{1... | collective-permute-start | bytes 3145736 | tf_op jit(solution)/shard_map/ppermute | solution.py:380
  222.5 42.9 %collective-permute-start.39 = (bf16[4,512,512]{2,1,0:T(8,128)(2,1)}, bf16[4,512,512]{2,1,0:T(8,128)(2,1)}, u32[]{:S(2)}, u32[]{:S(2)}) collective-permute-start(bf16[4,512,512]{2,1,0:T(8,128)(2,1)} %collective-permute-done.29.refs_11_), channel_id=1, source_target_pairs={{8,24},{24,8},{9,25},{25,9},{10,26},{26,10},{11,27},{27,11},{4,20}... | collective-permute-start | bytes 6291464 | tf_op jit(solution)/shard_map/ppermute | solution.py:380
  225.9 39.5 %collective-permute-start.38 = (bf16[3,512,512]{2,1,0:T(8,128)(2,1)}, bf16[3,512,512]{2,1,0:T(8,128)(2,1)}, u32[]{:S(2)}, u32[]{:S(2)}) collective-permute-start(bf16[3,512,512]{2,1,0:T(8,128)(2,1)} %pad_maximum_fusion.3.refs_9_), channel_id=1, source_target_pairs={{0,16},{16,0},{1,17},{17,1},{2,18},{18,2},{3,19},{19,3},{12,28},{2... | collective-permute-start | bytes 4718600 | tf_op jit(solution)/shard_map/ppermute | solution.py:380
  240.4 3.2 collective-permute-start.33
  244.8 8.0 %collective-permute-start.36 = (bf16[192,512]{1,0:T(8,128)(2,1)S(1)}, bf16[192,512]{1,0:T(8,128)(2,1)S(1)}, u32[]{:S(2)}, u32[]{:S(2)}) collective-permute-start(bf16[192,512]{1,0:T(8,128)(2,1)S(1)} %filter_and_gate.5), channel_id=1, source_target_pairs={{0,3},{1,0},{2,1},{3,2},{4,7},{5,4},{6,5},{7,6},{8,11},{9,8},{10,9... | collective-permute-start | bytes 589832 | tf_op jit(solution)/shard_map/ppermute | solution.py:380
  246.6 18.4 %collective-permute-start.35 = (bf16[192,512]{1,0:T(8,128)(2,1)S(1)}, bf16[192,512]{1,0:T(8,128)(2,1)S(1)}, u32[]{:S(2)}, u32[]{:S(2)}) collective-permute-start(bf16[192,512]{1,0:T(8,128)(2,1)S(1)} %filter_and_gate.5), channel_id=1, source_target_pairs={{0,2},{1,3},{2,0},{3,1},{4,6},{5,7},{6,4},{7,5},{8,10},{9,11},{10,... | collective-permute-start | bytes 589832 | tf_op jit(solution)/shard_map/ppermute | solution.py:380
  247.0 18.0 %collective-permute-start.34 = (bf16[192,512]{1,0:T(8,128)(2,1)S(1)}, bf16[192,512]{1,0:T(8,128)(2,1)S(1)}, u32[]{:S(2)}, u32[]{:S(2)}) collective-permute-start(bf16[192,512]{1,0:T(8,128)(2,1)S(1)} %filter_and_gate.5), channel_id=1, source_target_pairs={{0,1},{1,2},{2,3},{3,0},{4,5},{5,6},{6,7},{7,4},{8,9},{9,10},{10,1... | collective-permute-start | bytes 589832 | tf_op jit(solution)/shard_map/ppermute | solution.py:380
  265.1 2.4 collective-permute-start.37
  271.8 3.1 collective-permute-start.40
  273.9 12.3 %collective-permute-start.41 = (bf16[192,1024]{1,0:T(8,128)(2,1)}, bf16[192,1024]{1,0:T(8,128)(2,1)}, u32[]{:S(2)}, u32[]{:S(2)}) collective-permute-start(bf16[192,1024]{1,0:T(8,128)(2,1)} %get-tuple-element.79.refs_0_.refs_2_), channel_id=1, source_target_pairs={{0,1},{1,0},{2,3},{3,2},{4,5},{5,4},{6,7},{7,6},{8,9},{9,8},{10,11... | collective-permute-start | bytes 1179656 | tf_op jit(solution)/shard_map/ppermute | solution.py:380
  275.0 18.7 %collective-permute-start.42 = (bf16[192,1024]{1,0:T(8,128)(2,1)S(1)}, bf16[192,1024]{1,0:T(8,128)(2,1)}, u32[]{:S(2)}, u32[]{:S(2)}) collective-permute-start(bf16[192,1024]{1,0:T(8,128)(2,1)S(1)} %collective-permute-done.40.refs_1_), channel_id=1, source_target_pairs={{0,1},{1,0},{2,3},{3,2},{4,5},{5,4},{6,7},{7,6},{8,9},{9,8},{10,11... | collective-permute-start | bytes 1179656 | tf_op jit(solution)/shard_map/ppermute | solution.py:380
  302.1 27.9 %copy-start.3 = (bf16[3,512,512]{2,1,0:T(8,128)(2,1)S(1)}, bf16[3,512,512]{2,1,0:T(8,128)(2,1)}, u32[]{:S(2)}) copy-start(bf16[3,512,512]{2,1,0:T(8,128)(2,1)} %copy-done) | copy-start | bytes 4718596
  302.1 27.9 %copy-start.8 = (bf16[3,512,512]{2,1,0:T(8,128)(2,1)S(1)}, bf16[3,512,512]{2,1,0:T(8,128)(2,1)}, u32[]{:S(2)}) copy-start(bf16[3,512,512]{2,1,0:T(8,128)(2,1)} %copy-done.5) | copy-start | bytes 4718596
  302.1 27.9 %copy-start.24 = (bf16[192,1024]{1,0:T(8,128)(2,1)S(1)}, bf16[192,1024]{1,0:T(8,128)(2,1)}, u32[]{:S(2)}) copy-start(bf16[192,1024]{1,0:T(8,128)(2,1)} %copy-done.23) | copy-start | bytes 1179652
  302.2 2.5 collective-permute-start.43
  306.2 8.3 %collective-permute-start.46 = (bf16[192,512]{1,0:T(8,128)(2,1)S(1)}, bf16[192,512]{1,0:T(8,128)(2,1)S(1)}, u32[]{:S(2)}, u32[]{:S(2)}) collective-permute-start(bf16[192,512]{1,0:T(8,128)(2,1)S(1)} %filter_and_gate.6), channel_id=1, source_target_pairs={{0,3},{1,0},{2,1},{3,2},{4,7},{5,4},{6,5},{7,6},{8,11},{9,8},{10,9... | collective-permute-start | bytes 589832 | tf_op jit(solution)/shard_map/ppermute | solution.py:380
  309.1 18.4 %collective-permute-start.45 = (bf16[192,512]{1,0:T(8,128)(2,1)S(1)}, bf16[192,512]{1,0:T(8,128)(2,1)S(1)}, u32[]{:S(2)}, u32[]{:S(2)}) collective-permute-start(bf16[192,512]{1,0:T(8,128)(2,1)S(1)} %filter_and_gate.6), channel_id=1, source_target_pairs={{0,2},{1,3},{2,0},{3,1},{4,6},{5,7},{6,4},{7,5},{8,10},{9,11},{10,... | collective-permute-start | bytes 589832 | tf_op jit(solution)/shard_map/ppermute | solution.py:380
  309.3 18.3 %collective-permute-start.44 = (bf16[192,512]{1,0:T(8,128)(2,1)S(1)}, bf16[192,512]{1,0:T(8,128)(2,1)S(1)}, u32[]{:S(2)}, u32[]{:S(2)}) collective-permute-start(bf16[192,512]{1,0:T(8,128)(2,1)S(1)} %filter_and_gate.6), channel_id=1, source_target_pairs={{0,1},{1,2},{2,3},{3,0},{4,5},{5,6},{6,7},{7,4},{8,9},{9,10},{10,1... | collective-permute-start | bytes 589832 | tf_op jit(solution)/shard_map/ppermute | solution.py:380
  327.6 2.4 collective-permute-start.47
  334.1 3.0 collective-permute-start.48
  336.2 12.1 %collective-permute-start.49 = (bf16[192,1024]{1,0:T(8,128)(2,1)S(1)}, bf16[192,1024]{1,0:T(8,128)(2,1)}, u32[]{:S(2)}, u32[]{:S(2)}) collective-permute-start(bf16[192,1024]{1,0:T(8,128)(2,1)S(1)} %get-tuple-element.83.refs_0_.refs_2_), channel_id=1, source_target_pairs={{0,1},{1,0},{2,3},{3,2},{4,5},{5,4},{6,7},{7,6},{8,9},{9,8},{10,11... | collective-permute-start | bytes 1179656 | tf_op jit(solution)/shard_map/ppermute | solution.py:380
  337.1 18.6 %collective-permute-start.50 = (bf16[192,1024]{1,0:T(8,128)(2,1)}, bf16[192,1024]{1,0:T(8,128)(2,1)}, u32[]{:S(2)}, u32[]{:S(2)}) collective-permute-start(bf16[192,1024]{1,0:T(8,128)(2,1)} %collective-permute-done.48.refs_1_), channel_id=1, source_target_pairs={{0,1},{1,0},{2,3},{3,2},{4,5},{5,4},{6,7},{7,6},{8,9},{9,8},{10,11... | collective-permute-start | bytes 1179656 | tf_op jit(solution)/shard_map/ppermute | solution.py:380
  364.6 2.5 collective-permute-start.51
  368.7 8.1 %collective-permute-start.54 = (bf16[192,512]{1,0:T(8,128)(2,1)S(1)}, bf16[192,512]{1,0:T(8,128)(2,1)S(1)}, u32[]{:S(2)}, u32[]{:S(2)}) collective-permute-start(bf16[192,512]{1,0:T(8,128)(2,1)S(1)} %filter_and_gate.7), channel_id=1, source_target_pairs={{0,3},{1,0},{2,1},{3,2},{4,7},{5,4},{6,5},{7,6},{8,11},{9,8},{10,9... | collective-permute-start | bytes 589832 | tf_op jit(solution)/shard_map/ppermute | solution.py:380
  371.4 18.5 %collective-permute-start.53 = (bf16[192,512]{1,0:T(8,128)(2,1)S(1)}, bf16[192,512]{1,0:T(8,128)(2,1)S(1)}, u32[]{:S(2)}, u32[]{:S(2)}) collective-permute-start(bf16[192,512]{1,0:T(8,128)(2,1)S(1)} %filter_and_gate.7), channel_id=1, source_target_pairs={{0,2},{1,3},{2,0},{3,1},{4,6},{5,7},{6,4},{7,5},{8,10},{9,11},{10,... | collective-permute-start | bytes 589832 | tf_op jit(solution)/shard_map/ppermute | solution.py:380
  371.6 18.2 %collective-permute-start.52 = (bf16[192,512]{1,0:T(8,128)(2,1)S(1)}, bf16[192,512]{1,0:T(8,128)(2,1)S(1)}, u32[]{:S(2)}, u32[]{:S(2)}) collective-permute-start(bf16[192,512]{1,0:T(8,128)(2,1)S(1)} %filter_and_gate.7), channel_id=1, source_target_pairs={{0,1},{1,2},{2,3},{3,0},{4,5},{5,6},{6,7},{7,4},{8,9},{9,10},{10,1... | collective-permute-start | bytes 589832 | tf_op jit(solution)/shard_map/ppermute | solution.py:380
  390.0 2.4 collective-permute-start.55
  398.4 1.9 collective-permute-start.56
  (43 other events, 303.0 us)
Sparse Core Ops, SparseCore 0:
  14.9 39.4 all-gather.1
where the time goes:
time: 411 us; the launch traced here: 409 us
  waiting for transfers between devices  189 us (46%)
  starting transfers between devices  95.6 us (23%)
  Pallas kernels  56.9 us (14%)
  local copies, waits for them, and re-layouts  36.6 us (9%)
  between operations  20.4 us (5%)
  other arithmetic  10 us (2%)
    ppermute x44, waiting for transfers between devices, join(): self.now.append(lax.ppermute(value, axes, pairs))  176 us
    ppermute x44, starting transfers between devices, join(): self.now.append(lax.ppermute(value, axes, pairs))  83.4 us
    unnamed x99, local copies, waits for them, and re-layouts  28 us
    pallas_call x4, Pallas kernels, project_in(): pl.pallas_call(partial(in_kernel, sections), out_shape=(out, out), in_spe...  27.7 us
    pallas_call x4, Pallas kernels, project_out(): pl.pallas_call(partial(out_kernel, sections), out_shape=(out, out), in_sp...  18.4 us
  transfers between devices with their start and end apart: 58, of which 33 were waited for; matrix products, arithmetic and copies ran while one was open for 4% of the time, Pallas kernels for 6%

commit v1 on v0

--- a/solution.py
+++ b/solution.py
@@ -78,7 +78,7 @@
     return hidden
 
 
-SECOND, GROUP, SAME, ROW_OWN, ROW_CORE, ROW_CHIP, ROW_BOTH, HELD = range(8)
+SECOND, GROUP, SAME, MATCH, ROW = range(5)
 
 
 def ctx_pairs(change):
@@ -89,96 +89,133 @@
     return (i * 4 + j) if g is None else (g * 16 + i * 4 + j)
 
 
-def in_kernel(sections, meta, section_ref, *refs):
-    count = 1 if sections == 1 else 4
+OWN, CORE, CHIP, BOTH = range(4)
+
+
+def in_kernel(mode, sections, meta, section_ref, *refs):
+    count = 1 if mode == "whole" else 2
     pieces, refs = refs[:count], refs[count:]
+    if mode == "last":
+        earlier, earlier_square, refs = refs[0], refs[1], refs[2:]
     own_in, core_in = refs[:2]
-    weights = [refs[2 + 6 * s : 8 + 6 * s] for s in range(sections)]
-    query_ref, mixed_ref, hidden, held, total, held_sem = refs[2 + 6 * sections :]
-    width = hidden.shape[2]
+    weights = [refs[2 + 5 * s : 7 + 5 * s] for s in range(sections)]
+    out_ref, out_ref2, hidden, held, total, held_sem = refs[2 + 5 * sections :]
+    tokens, width = hidden.shape[1:]
     part = width // 2
     group = meta[GROUP]
     section = section_ref[0]
-    rows = (ROW_OWN, ROW_CORE, ROW_CHIP, ROW_BOTH)
+    slots = held.shape[1]
 
     def span(q):
         return pl.ds(pl.multiple_of(q * part, part), part)
 
-    def start(p, r, source, at, q):
-        pltpu.make_async_copy(source, held.at[p, r, at], held_sem.at[p, r, q]).start()
-
-    def start_section(chip, chip_y, both, both_y, chip_q, both_q):
+    def start(kind, p, slot, sources):
+        chip, chip_y, chip_q, both = sources[:4]
+        if kind in (OWN, CORE):
+            source = own_in if kind == OWN else core_in
+            halves = [(source.at[section, p, span(q)], span(q)) for q in range(2)]
+        elif p == 0:
+            sources = chip_q if kind == CHIP else both
+            halves = [(sources.at[q], span(q)) for q in range(2)]
+        elif kind == CHIP:
+            halves = [(chip.at[p - 1], span(group)), (chip_y.at[p - 1], span(1 - group))]
+        else:
+            halves = [(sources[4].at[p - 1], span(group)), (both.at[p + 1], span(1 - group))]
+        for q in range(2):
+            pltpu.make_async_copy(
+                halves[q][0], held.at[p, slot, halves[q][1]], held_sem.at[p, slot, q]
+            ).start()
+
+    def start_kinds(kinds, sources):
         for p in (1, 2, 0):
-            for q in range(2):
-                start(p, 0, own_in.at[section, p, span(q)], span(q), q)
-                start(p, 1, core_in.at[section, p, span(q)], span(q), q)
-                if p == 0:
-                    start(p, 2, chip_q.at[span(q)], span(q), q)
-                    start(p, 3, both_q.at[span(q)], span(q), q)
-            if p > 0:
-                start(p, 2, chip.at[p - 1], span(group), 0)
-                start(p, 2, chip_y.at[p - 1], span(1 - group), 1)
-                start(p, 3, both.at[p - 1], span(group), 0)
-                start(p, 3, both_y.at[p - 1], span(1 - group), 1)
-
-    if sections == 1:
-        start_section(*weights[0])
+            for slot, kind in enumerate(kinds):
+                start(kind, p, slot, sources)
+
+    if mode == "whole":
+        start_kinds((OWN, CORE, CHIP, BOTH), weights[0])
     else:
-        for s in range(sections):
-            pl.when(meta[SECOND] == s)(partial(start_section, *weights[s]))
-
-    square = jnp.zeros((hidden.shape[1], 1), jnp.float32)
-    for k in range(4):
-        piece = pieces[k][...] if count > 1 else pieces[0][:, k * width : (k + 1) * width]
-        hidden[meta[HELD + k] if count > 1 else k] = piece
+        for match in range(2):
+            kinds = (OWN, CHIP) if match == (mode == "first") else (CORE, BOTH)
+            for s in range(sections):
+                here = jnp.logical_and(meta[MATCH] == match, meta[SECOND] == s)
+                pl.when(here)(partial(start_kinds, kinds, weights[s]))
+
+    square = jnp.zeros((tokens, 1), jnp.float32)
+    for k in range(slots):
+        if mode == "whole":
+            piece = pieces[0][:, k * width : (k + 1) * width]
+            hidden[k] = piece
+        else:
+            piece = pieces[k][...]
+            hidden[1 - meta[SAME] if k == 0 else meta[SAME]] = piece
         wide = piece.astype(jnp.float32)
         square = square + jnp.sum(wide * wide, axis=1, keepdims=True)
-    scale = lax.rsqrt(square / (4 * width) + 1e-05)
+    if mode == "last":
+        square = square + earlier_square[:, :1]
+    if mode == "first":
+        out_ref2[...] = jnp.broadcast_to(square, out_ref2.shape)
+    else:
+        scale = lax.rsqrt(square / (4 * width) + 1e-05)
 
     for p in (1, 2, 0):
-        for r in range(4):
+        for slot in range(slots):
             for q in range(2):
                 pltpu.make_async_copy(
-                    own_in.at[0, 0, pl.ds(0, part)], held.at[p, r, pl.ds(0, part)], held_sem.at[p, r, q]
+                    own_in.at[0, 0, pl.ds(0, part)],
+                    held.at[p, slot, pl.ds(0, part)],
+                    held_sem.at[p, slot, q],
                 ).wait()
-            product = jnp.dot(
-                hidden[meta[rows[r]]], held[p, r], preferred_element_type=jnp.float32
-            )
-            if r == 0:
+            at = meta[ROW + slot] if mode == "whole" else slot
+            product = jnp.dot(hidden[at], held[p, slot], preferred_element_type=jnp.float32)
+            if slot > 0:
+                total[p] += product
+            elif mode == "last":
+                total[p] = earlier[p] + product
+            else:
                 total[p] = product
-            else:
-                total[p] += product
-    query_ref[...] = (total[0] * scale).astype(query_ref.dtype)
-    mixed_ref[...] = ((total[1] * scale) * (total[2] * scale)).astype(mixed_ref.dtype)
-
-
-def project_in(meta, section, pieces, own_in, core_in, weights):
+    if mode == "first":
+        out_ref[...] = total[...]
+    else:
+        out_ref[...] = (total[0] * scale).astype(out_ref.dtype)
+        out_ref2[...] = ((total[1] * scale) * (total[2] * scale)).astype(out_ref2.dtype)
+
+
+def project_in(mode, meta, section, pieces, earlier, own_in, core_in, weights):
     width, channels = own_in.shape[2:]
     tokens = pieces[0].shape[0]
     sections = len(weights)
-    far = pl.BlockSpec(memory_space=pl.ANY)
+    slots = 4 if mode == "whole" else 2
+    anywhere = pl.BlockSpec(memory_space=pl.ANY)
     vmem = pl.BlockSpec(memory_space=pltpu.VMEM)
     smem = pl.BlockSpec(memory_space=pltpu.SMEM)
-    out = jax.ShapeDtypeStruct((tokens, channels), jnp.bfloat16)
+    if mode == "first":
+        out = (
+            jax.ShapeDtypeStruct((3, tokens, channels), jnp.float32),
+            jax.ShapeDtypeStruct((tokens, 128), jnp.float32),
+        )
+    else:
+        out = (jax.ShapeDtypeStruct((tokens, channels), jnp.bfloat16),) * 2
     return pl.pallas_call(
-        partial(in_kernel, sections),
-        out_shape=(out, out),
-        in_specs=[smem] * 2 + [vmem] * len(pieces) + [far] * (2 + sum(len(w) for w in weights)),
+        partial(in_kernel, mode, sections),
+        out_shape=out,
+        in_specs=[smem] * 2
+        + [vmem] * (len(pieces) + len(earlier))
+        + [anywhere] * (2 + sum(len(w) for w in weights)),
         out_specs=(vmem, vmem),
         scratch_shapes=[
-            pltpu.VMEM((4, tokens, width), jnp.bfloat16),
-            pltpu.VMEM((3, 4, width, channels), jnp.bfloat16),
+            pltpu.VMEM((slots, tokens, width), jnp.bfloat16),
+            pltpu.VMEM((3, slots, width, channels), jnp.bfloat16),
             pltpu.VMEM((3, tokens, channels), jnp.float32),
-            pltpu.SemaphoreType.DMA((3, 4, 2)),
+            pltpu.SemaphoreType.DMA((3, slots, 2)),
         ],
-        compiler_params=pltpu.CompilerParams(vmem_limit_bytes=24 * MIB),
+        compiler_params=pltpu.CompilerParams(vmem_limit_bytes=44 * MIB),
         cost_estimate=pl.CostEstimate(
-            flops=24 * tokens * width * channels,
-            bytes_accessed=24 * width * channels,
+            flops=6 * slots * tokens * width * channels,
+            bytes_accessed=6 * slots * width * channels,
             transcendentals=0,
         ),
-        name="project_in",
-    )(meta, section, *pieces, own_in, core_in, *[w for ws in weights for w in ws])
+        name="project_in_" + mode,
+    )(meta, section, *pieces, *earlier, own_in, core_in, *[w for ws in weights for w in ws])
 
 
 BLOCK = 64
@@ -248,36 +285,32 @@
     return skewed[:, :, : reach + BLOCK].reshape(groups * BLOCK, reach + BLOCK)
 
 
-def out_kernel(sections, meta, section_ref, *refs):
-    own_gated, core_gated, own_hidden, core_hidden, near = refs[:5]
-    weights = [refs[5 + 4 * s : 9 + 4 * s] for s in range(sections)]
-    own_out, core_out, held, held_sem = refs[5 + 4 * sections :]
+def out_kernel(sections, meta, *refs):
+    own_gated, core_gated, own_hidden, core_hidden = refs[:4]
+    weights = [refs[4 + 5 * s : 9 + 5 * s] for s in range(sections)]
+    own_out, core_out, held, held_sem = refs[4 + 5 * sections :]
     tokens, width = own_hidden.shape
     part = width // 2
     group = meta[GROUP]
-    section = section_ref[0]
     mine = pl.ds(pl.multiple_of(group * part, part), part)
     other = pl.ds(pl.multiple_of((1 - group) * part, part), part)
 
-    def start(k, first, second):
-        pltpu.make_async_copy(first, held.at[k, mine], held_sem.at[k, 0]).start()
-        pltpu.make_async_copy(second, held.at[k, other], held_sem.at[k, 1]).start()
-
-    def start_same(came, came_y, sent, sent_y):
-        start(0, near.at[section, mine], near.at[section, other])
-        for k in range(1, 4):
-            start(k, came.at[k - 1], came_y.at[k - 1])
-
-    def start_cross(came, came_y, sent, sent_y):
+    def start(first, second):
         for k in range(4):
-            start(k, sent.at[k], sent_y.at[k])
+            pltpu.make_async_copy(first.at[k], held.at[k, mine], held_sem.at[k, 0]).start()
+            pltpu.make_async_copy(second.at[k], held.at[k, other], held_sem.at[k, 1]).start()
 
     for s in range(sections):
-        for same in range(2):
-            here = meta[SAME] == same
+        shard, same_mine, same_other, cross_mine, cross_other = weights[s]
+        cases = (
+            (meta[SAME] == 0, cross_mine, cross_other),
+            (meta[SAME] + meta[MATCH] == 2, shard, same_other),
+            (meta[SAME] - meta[MATCH] == 1, same_mine, same_other),
+        )
+        for here, first, second in cases:
             if sections > 1:
                 here = jnp.logical_and(here, meta[SECOND] == s)
-            pl.when(here)(partial(start_same if same else start_cross, *weights[s]))
+            pl.when(here)(partial(start, first, second))
 
     total = None
     for k in range(4):
@@ -292,18 +325,18 @@
     core_out[...] = (core_hidden[...].astype(jnp.float32) + total[tokens:]).astype(core_out.dtype)
 
 
-def project_out(meta, section, own_gated, core_gated, own_hidden, core_hidden, near, weights):
+def project_out(meta, own_gated, core_gated, own_hidden, core_hidden, weights):
     tokens, width = own_hidden.shape
     channels = own_gated.shape[2]
     sections = len(weights)
-    far = pl.BlockSpec(memory_space=pl.ANY)
+    anywhere = pl.BlockSpec(memory_space=pl.ANY)
     vmem = pl.BlockSpec(memory_space=pltpu.VMEM)
     smem = pl.BlockSpec(memory_space=pltpu.SMEM)
     out = jax.ShapeDtypeStruct((tokens, width), jnp.bfloat16)
     return pl.pallas_call(
         partial(out_kernel, sections),
         out_shape=(out, out),
-        in_specs=[smem] * 2 + [vmem] * 4 + [far] * (1 + 4 * sections),
+        in_specs=[smem] + [vmem] * 4 + [anywhere] * (5 * sections),
         out_specs=(vmem, vmem),
         scratch_shapes=[
             pltpu.VMEM((4, width, channels), jnp.bfloat16),
@@ -316,16 +349,7 @@
             transcendentals=0,
         ),
         name="project_out",
-    )(
-        meta,
-        section,
-        own_gated,
-        core_gated,
-        own_hidden,
-        core_hidden,
-        near,
-        *[w for ws in weights for w in ws],
-    )
+    )(meta, own_gated, core_gated, own_hidden, core_hidden, *[w for ws in weights for w in ws])
 
 
 def taken_kernel(at, in_ref, out_ref, out_half, kv_half, query, sem):
@@ -336,7 +360,8 @@
         pltpu.make_async_copy(in_ref.at[section, 1, mine], kv_half.at[0], sem.at[0]),
         pltpu.make_async_copy(in_ref.at[section, 2, mine], kv_half.at[1], sem.at[1]),
         pltpu.make_async_copy(out_ref.at[section, mine], out_half, sem.at[2]),
-        pltpu.make_async_copy(in_ref.at[section, 0], query, sem.at[3]),
+        pltpu.make_async_copy(in_ref.at[section, 0, pl.ds(0, part)], query.at[0], sem.at[3]),
+        pltpu.make_async_copy(in_ref.at[section, 0, pl.ds(part, part)], query.at[1], sem.at[4]),
     ]
     for copy in copies:
         copy.start()
@@ -349,13 +374,13 @@
     part = width // 2
     far = pl.BlockSpec(memory_space=pl.ANY)
     near = pl.BlockSpec(memory_space=pltpu.VMEM)
-    shapes = [(part, channels), (2, part, channels), (width, channels)]
+    shapes = [(part, channels), (2, part, channels), (2, part, channels)]
     return pl.pallas_call(
         taken_kernel,
         out_shape=tuple(jax.ShapeDtypeStruct(shape, jnp.bfloat16) for shape in shapes),
         in_specs=[pl.BlockSpec(memory_space=pltpu.SMEM), far, far],
         out_specs=(near,) * len(shapes),
-        scratch_shapes=[pltpu.SemaphoreType.DMA((4,))],
+        scratch_shapes=[pltpu.SemaphoreType.DMA((5,))],
         compiler_params=pltpu.CompilerParams(vmem_limit_bytes=8 * MIB),
         name="taken",
     )(jnp.stack([section, g]).astype(jnp.int32), in_weights, out_weights)
@@ -384,19 +409,25 @@
         self.before, self.now = self.now, []
 
 
-def along(k):
+def holder(x, j):
+    return 2 * x + j % 2
+
+
+def keeper(x, j):
+    return 3 * x
+
+
+def other_keeper(x, j):
+    return 2 - x
+
+
+def plane_pairs(source, target):
+    return [(flat(source(x, j), j), flat(target(x, j), j)) for x in range(2) for j in range(4)]
+
+
+def group_pairs(source, target):
     return [
-        (flat(2 * x + (j % 2), (j - k) % 4), flat(3 * x, j)) for x in range(2) for j in range(4)
-    ]
-
-
-def over_chips(source):
-    return [(flat(source(x, j), j), flat(2 - x, j)) for x in range(2) for j in range(4)]
-
-
-def over_groups(core):
-    return [
-        (flat(core(x), j, q), flat(core(x), j, 1 - q))
+        (flat(source(x, j), j, q), flat(target(x, j), j, 1 - q))
         for x in range(2)
         for j in range(4)
         for q in range(2)
@@ -406,10 +437,14 @@
 CORES = ctx_pairs(1)
 CHIPS = ctx_pairs(2)
 GROUPS = [(0, 1), (1, 0)]
-FROM_HOLDER = over_chips(lambda x, j: 2 * x + j % 2)
-FROM_SAME = over_chips(lambda x, j: 3 * x)
-SWAP_SAME = over_groups(lambda x: 3 * x)
-SWAP_CROSS = over_groups(lambda x: 2 - x)
+ALONG = {
+    k: [(flat(holder(x, j), (j - k) % 4), flat(holder(x, j), j)) for x in range(2) for j in range(4)]
+    for k in (1, 2, 3)
+}
+TO_KEEPER = [pair for pair in plane_pairs(holder, keeper) if pair[0] != pair[1]]
+TO_OTHER_KEEPER = plane_pairs(holder, other_keeper)
+TO_KEEPER_OVER = group_pairs(holder, keeper)
+OTHER_KEEPERS_OVER = group_pairs(other_keeper, other_keeper)
 BESIDE = [(s, s ^ 1) for s in range(4)]
 HALO = [(0, 1), (1, 2), (2, 3)]
 
@@ -436,82 +471,76 @@
     x_kv = send(kv_a, "ctx", CHIPS)
     x_q = send(q_a, "ctx", CHIPS)
     core_in = send(after(in_weights, q_a), "ctx", CORES)
-    near_out = send(after(out_weights, q_a), PLANE, along(0))
     out_b, kv_b, q_b = taken(after(1 - first, q_a), g, in_weights, out_weights)
     send.now += [out_b, bands]
 
-    def near_half(section):
-        return lax.dynamic_slice(near_out, (section, g * part, 0), (1, part, near_out.shape[2]))
-
     send.turn()
-    c_kv = send(x_kv, "ctx", CORES)
-    c_q = send(x_q, "ctx", CORES)
     y_kv = send(x_kv, "groups", GROUPS)
+    c_kv = lax.ppermute(x_kv, "ctx", CORES)
     x_kv_b = send(kv_b, "ctx", CHIPS)
-    z_a = {k: send(out_a, PLANE, along(k)) for k in (2, 1, 3)}
+    shard_a = [out_a] + [send(out_a, PLANE, ALONG[k]) for k in (1, 2, 3)]
 
     send.turn()
-    cy_kv = send(y_kv, "ctx", CORES)
-    rest_a = jnp.stack([z_a[1], z_a[2], z_a[3]])
-    sent_a = send(jnp.concatenate([near_half(first), rest_a]), PLANE, FROM_SAME)
-    rest_y = send(rest_a, EVERY, SWAP_SAME)
-    z_b = {k: send(out_b, PLANE, along(k)) for k in (2, 1, 3)}
-    rest_b = jnp.stack([z_b[1], z_b[2], z_b[3]])
+    shard_a = jnp.stack(shard_a)
+    cross_a = send(shard_a, PLANE, TO_OTHER_KEEPER)
+    same_y = send(shard_a, EVERY, TO_KEEPER_OVER)
+    both = send(jnp.concatenate([x_q, y_kv]), "ctx", CORES)
+    same_a = send(shard_a, PLANE, TO_KEEPER)
+    shard_b = [out_b] + [send(after(out_b, both, same_a), PLANE, ALONG[k]) for k in (1, 2, 3)]
 
     send.turn()
-    sent_y = send(sent_a, EVERY, SWAP_CROSS)
-    x_q_b = send(q_b, "ctx", CHIPS)
-    weights_in = [[x_kv, y_kv, c_kv, cy_kv, x_q, c_q]]
-    weights_out = [[rest_a, rest_y, sent_a, sent_y]]
+    shard_b = jnp.stack(shard_b)
+    cross_y = send(cross_a, EVERY, OTHER_KEEPERS_OVER)
+    weights_in = [[x_kv, y_kv, x_q, both, c_kv]]
+    weights_out = [[shard_a, same_a, same_y, cross_a, cross_y]]
 
     own_hidden = lax.dynamic_slice_in_dim(whole, (2 * c + h) * width, width, 1)
     to_core = lax.dynamic_slice_in_dim(whole, (2 * (1 - c) + h) * width, width, 1)
     core_hidden = lax.ppermute(to_core, "ctx", CORES)
-    pieces, slices = [whole], []
+    inputs = in_weights, core_in
 
     for step in range(STEPS):
         count = 1 if step == 0 else 2
         section = plan[step]
         second = (section != first).astype(jnp.int32)
         section = section.reshape(1)
-        scalars = [second, g, (x == c).astype(jnp.int32), i, i ^ 1, i ^ 2, i ^ 3] + slices
+        scalars = [second, g, (x == c).astype(jnp.int32), (c == h).astype(jnp.int32)]
+        scalars += [i, i ^ 1, i ^ 2, i ^ 3]
         meta = jnp.stack([jnp.asarray(s, jnp.int32) for s in scalars])
-        query, mixed = project_in(meta, section, pieces, in_weights, core_in, weights_in[:count])
+        if step == 0:
+            query, mixed = project_in("whole", meta, section, [whole], [], *inputs, weights_in)
+        else:
+            part_sums = project_in("first", meta, section, near_pieces, [], *inputs, weights_in)
+            query, mixed = project_in("last", meta, section, far_pieces, part_sums, *inputs, weights_in)
         halo = lax.ppermute(mixed[-reach:], "ctx", HALO)
+        if step == 0:
+            c_kv_b = lax.ppermute(after(x_kv_b, halo), "ctx", CORES)
         gated = filter_and_gate(section, halo, mixed, query, bands, short_taps)
+        if step == 0:
+            cross_b = send(after(shard_b, halo), PLANE, TO_OTHER_KEEPER)
         g_2, g_3, g_1 = (send.join(gated, "chan", around(k)) for k in (2, 3, 1))
         if step == 0:
             send.turn()
             y_kv_b = send(x_kv_b, "groups", GROUPS)
-            sent_b = send(jnp.concatenate([near_half(1 - first), rest_b]), PLANE, FROM_SAME)
+            x_q_b = send(q_b, "ctx", CHIPS)
         own_gated = jnp.stack([gated, g_1, g_2, g_3])
         core_gated = lax.ppermute(own_gated, "ctx", CORES)
         own_hidden, core_hidden = project_out(
-            meta,
-            section,
-            own_gated,
-            core_gated,
-            own_hidden,
-            core_hidden,
-            near_out,
-            weights_out[:count],
+            meta, own_gated, core_gated, own_hidden, core_hidden, weights_out[:count]
         )
         swapped = lax.ppermute(core_hidden, "ctx", CORES)
         if step == STEPS - 1:
-            return jnp.where(near, own_hidden, swapped)
-        beside = send.join(own_hidden, "chan", BESIDE)
-        beside_core = send.join(swapped, "chan", BESIDE)
-        pieces = [own_hidden, swapped, beside, beside_core]
-        slices = [2 * c + h, 2 * (1 - c) + h, 2 * c + 1 - h, 2 * (1 - c) + 1 - h]
+            return jnp.where((j // 2) == c, own_hidden, swapped)
+        near_pieces = [own_hidden, swapped]
+        far_pieces = [send.join(piece, "chan", BESIDE) for piece in near_pieces]
         if step == 0:
             send.turn()
-            c_q_b = send(x_q_b, "ctx", CORES)
-            cy_kv_b = send(y_kv_b, "ctx", CORES)
-            c_kv_b = send(x_kv_b, "ctx", CORES)
-            rest_b_y = send(rest_b, EVERY, SWAP_SAME)
-            sent_b_y = send(sent_b, EVERY, SWAP_CROSS)
-            weights_in.append([x_kv_b, y_kv_b, c_kv_b, cy_kv_b, x_q_b, c_q_b])
-            weights_out.append([rest_b, rest_b_y, sent_b, sent_b_y])
+            both_b = send(jnp.concatenate([x_q_b, y_kv_b]), "ctx", CORES)
+            same_b_y = send(shard_b, EVERY, TO_KEEPER_OVER)
+            same_b = send(shard_b, PLANE, TO_KEEPER)
+            cross_b_y = send(cross_b, EVERY, OTHER_KEEPERS_OVER)
+            weights_in.append([x_kv_b, y_kv_b, x_q_b, both_b, c_kv_b])
+            weights_out.append([shard_b, same_b, same_b_y, cross_b, cross_b_y])
 
 
 def solution(mesh):

time: 411 us -> 384 us (0.934)
  waiting for transfers between devices: 189 us -> 163 us
  Pallas kernels: 56.9 us -> 70.9 us
  starting transfers between devices: 95.6 us -> 82.9 us
    ppermute x44 -> x41, waiting for transfers between devices: 176 us -> 150 us  [join(): self.now.append(lax.ppermute(value, axes, pairs))]
    pallas_call x4 -> x7, Pallas kernels: 27.7 us -> 40.6 us  [project_in(): pl.pallas_call(partial(in_kernel, mode, sections), out_shape=out, in_spec...]
    ppermute x44 -> x41, starting transfers between devices: 83.4 us -> 71.7 us  [join(): self.now.append(lax.ppermute(value, axes, pairs))]
    unnamed x99 -> x105, local copies, waits for them, and re-layouts: 28 us -> 29.2 us
  transfers between devices with their start and end apart: 58 -> 57, of which waited for: 33 -> 28; matrix products, arithmetic and copies ran while one was open for 4% -> 4% of each run, Pallas kernels for 6% -> 11%
where the time goes in v1:
time: 384 us; the launch traced here: 382 us
  waiting for transfers between devices  163 us (42%)
  starting transfers between devices  82.9 us (22%)
  Pallas kernels  70.9 us (18%)
  local copies, waits for them, and re-layouts  37.4 us (10%)
  between operations  18.5 us (5%)
  other arithmetic  9.63 us (3%)
    ppermute x41, waiting for transfers between devices, join(): self.now.append(lax.ppermute(value, axes, pairs))  150 us
    ppermute x41, starting transfers between devices, join(): self.now.append(lax.ppermute(value, axes, pairs))  71.7 us
    pallas_call x7, Pallas kernels, project_in(): pl.pallas_call(partial(in_kernel, mode, sections), out_shape=out, in_spec...  40.6 us
    unnamed x105, local copies, waits for them, and re-layouts  29.2 us
    pallas_call x4, Pallas kernels, project_out(): pl.pallas_call(partial(out_kernel, sections), out_shape=(out, out), in_sp...  18.6 us
  transfers between devices with their start and end apart: 57, of which 28 were waited for; matrix products, arithmetic and copies ran while one was open for 4% of the time, Pallas kernels for 11%

profile of v1, /device:TPU:0, one launch (start us, length us, event | category | flops | bytes accessed | tf_op | source)
XLA Modules:
  0.0 382.4 jit_solution(3534265154669006374)
XLA Ops:
  8.7 1.6 copy-done.32
  10.3 3.1 taken.2
  14.8 2.6 collective-permute-start.1
  18.4 1.6 copy.7
  20.0 5.1 %reshape.22 = bf16[32,64,255]{2,1,0:T(8,128)(2,1)} reshape(bf16[32,16320]{1,0:T(8,128)(2,1)} %bitcast.51) | data formatting | bytes 2088960 | tf_op jit(solution)/shard_map/reshape | solution.py:284
  25.2 1.7 copy-done.33
  26.8 2.9 taken.3
  29.8 11.8 %collective-permute-done.1.refs_3_.refs_4_.refs_6_ = bf16[2,512,512]{2,1,0:T(8,128)(2,1)S(1)} collective-permute-done((bf16[2,512,512]{2,1,0:T(8,128)(2,1)}, bf16[2,512,512]{2,1,0:T(8,128)(2,1)S(1)}, u32[]{:S(2)}, u32[]{:S(2)}) %collective-permute-start.1) | collective-permute-done | bytes 1048608 | tf_op jit(solution)/shard_map/ppermute | solution.py:405
  41.6 22.3 %collective-permute-done.2.refs_5_.refs_6_.refs_8_ = bf16[2,512,512]{2,1,0:T(8,128)(2,1)S(1)} collective-permute-done((bf16[2,512,512]{2,1,0:T(8,128)(2,1)}, bf16[2,512,512]{2,1,0:T(8,128)(2,1)S(1)}, u32[]{:S(2)}, u32[]{:S(2)}) %collective-permute-start.2) | collective-permute-done | bytes 1048608 | tf_op jit(solution)/shard_map/ppermute | solution.py:405
  63.9 1.8 collective-permute-start.3
  65.7 1.5 collective-permute-start.4
  68.4 4.5 %collective-permute-start.6 = (bf16[512,512]{1,0:T(8,128)(2,1)S(1)}, bf16[512,512]{1,0:T(8,128)(2,1)S(1)}, u32[]{:S(2)}, u32[]{:S(2)}) collective-permute-start(bf16[512,512]{1,0:T(8,128)(2,1)S(1)} %get-tuple-element.60), channel_id=1, source_target_pairs={{2,0},{7,5},{0,2},{5,7},{10,8},{15,13},{8,10},{13,15},{18,16},{23,... | collective-permute-start | bytes 1572872 | tf_op jit(solution)/shard_map/ppermute | solution.py:405
  74.2 5.1 %collective-permute-done.7 = bf16[512,512]{1,0:T(8,128)(2,1)S(1)} collective-permute-done((bf16[512,512]{1,0:T(8,128)(2,1)S(1)}, bf16[512,512]{1,0:T(8,128)(2,1)S(1)}, u32[]{:S(2)}, u32[]{:S(2)}) %collective-permute-start.7) | collective-permute-done | bytes 524320 | tf_op jit(solution)/shard_map/ppermute | solution.py:405
  79.3 15.0 %collective-permute-done.6 = bf16[512,512]{1,0:T(8,128)(2,1)S(1)} collective-permute-done((bf16[512,512]{1,0:T(8,128)(2,1)S(1)}, bf16[512,512]{1,0:T(8,128)(2,1)S(1)}, u32[]{:S(2)}, u32[]{:S(2)}) %collective-permute-start.6) | collective-permute-done | bytes 524320 | tf_op jit(solution)/shard_map/ppermute | solution.py:405
  94.3 1.7 pad_maximum_fusion.1.refs_4_
  97.7 5.5 %collective-permute-start.18 = (bf16[4,512,512]{2,1,0:T(8,128)(2,1)}, bf16[4,512,512]{2,1,0:T(8,128)(2,1)}, u32[]{:S(2)}, u32[]{:S(2)}) collective-permute-start(bf16[4,512,512]{2,1,0:T(8,128)(2,1)} %pad_maximum_fusion.1.refs_4_), channel_id=1, source_target_pairs={{0,8},{5,9},{2,10},{7,11},{8,4},{13,5},{10,6},{15,7},{16,24},{21,2... | collective-permute-start | bytes 6291464 | tf_op jit(solution)/shard_map/ppermute | solution.py:405
  103.3 2.4 collective-permute-start.17
  108.4 5.4 %collective-permute-start.20 = (bf16[512,512]{1,0:T(8,128)(2,1)}, bf16[512,512]{1,0:T(8,128)(2,1)}, u32[]{:S(2)}, u32[]{:S(2)}) collective-permute-start(bf16[512,512]{1,0:T(8,128)(2,1)} %get-tuple-element.66), channel_id=1, source_target_pairs={{2,0},{7,5},{0,2},{5,7},{10,8},{15,13},{8,10},{13,15},{18,16},{23,... | collective-permute-start | bytes 1572872 | tf_op jit(solution)/shard_map/ppermute | solution.py:405
  121.3 6.2 %project_in_whole.1 = (bf16[192,512]{1,0:T(8,128)(2,1)S(1)}, bf16[192,512]{1,0:T(8,128)(2,1)S(1)}) custom-call(s32[8]{0:T(128)S(1)} %stack.177.meta, s32[1]{0:T(128)} %get-tuple-element.100.section_ref.meta, bf16[192,4096]{1,0:T(8,128)(2,1)S(1)} %copy-done.34, bf16[2,3,1024,512]{3,2,1,0:T(8,128)(2,1)} %bitcast.7.in_ref.refs_1_.refs_2_.refs_4_, ...), custom_call_target="tpu_custom_call" | custom-call | flops 2415919104 | bytes 12582912 | tf_op jit(solution)/shard_map/project_in_whole/pallas_call | solution.py:198
  127.6 2.3 collective-permute-start.10
  129.9 1.6 collective-permute-done.17.refs_6_
  131.5 4.5 %collective-permute-done.20 = bf16[512,512]{1,0:T(8,128)(2,1)} collective-permute-done((bf16[512,512]{1,0:T(8,128)(2,1)}, bf16[512,512]{1,0:T(8,128)(2,1)}, u32[]{:S(2)}, u32[]{:S(2)}) %collective-permute-start.20) | collective-permute-done | bytes 524320 | tf_op jit(solution)/shard_map/ppermute | solution.py:405
  136.0 3.2 pad_maximum_fusion.2.refs_9_
  139.2 3.6 collective-permute-start.26
  142.8 2.0 collective-permute-start.22
  144.8 1.8 filter_and_gate.4
  146.6 3.6 collective-permute-start.12
  150.2 1.9 collective-permute-start.11
  153.2 13.8 %collective-permute-done.12 = bf16[192,512]{1,0:T(8,128)(2,1)S(1)} collective-permute-done((bf16[192,512]{1,0:T(8,128)(2,1)S(1)}, bf16[192,512]{1,0:T(8,128)(2,1)S(1)}, u32[]{:S(2)}, u32[]{:S(2)}) %collective-permute-start.12) | collective-permute-done | bytes 196640 | tf_op jit(solution)/shard_map/ppermute | solution.py:405
  171.2 5.0 %project_out.4 = (bf16[192,1024]{1,0:T(8,128)(2,1)S(1)}, bf16[192,1024]{1,0:T(8,128)(2,1)S(1)}) custom-call(s32[8]{0:T(128)S(1)} %stack.177.meta, bf16[4,192,512]{2,1,0:T(8,128)(2,1)} %pad_maximum_fusion.4.refs_0_, bf16[4,192,512]{2,1,0:T(8,128)(2,1)} %collective-permute-done.14.refs_1_, bf16[192,1024]{1,0:T(8,128)(2,1)S(1)} %get-tuple-element.98.refs_2_, ...), custom_call_target="tpu_custom_call" | custom-call | flops 1610612736 | bytes 4194304 | tf_op jit(solution)/shard_map/project_out/pallas_call | solution.py:336
  178.7 16.4 %collective-permute-done.27.refs_10_.refs_12_ = bf16[2,512,512]{2,1,0:T(8,128)(2,1)S(1)} collective-permute-done((bf16[2,512,512]{2,1,0:T(8,128)(2,1)}, bf16[2,512,512]{2,1,0:T(8,128)(2,1)S(1)}, u32[]{:S(2)}, u32[]{:S(2)}) %collective-permute-start.27) | collective-permute-done | bytes 1048608 | tf_op jit(solution)/shard_map/ppermute | solution.py:405
  195.4 1.7 pad_maximum_fusion.3
  199.1 3.3 collective-permute-start.37
  202.5 2.1 collective-permute-start.36
  204.5 2.0 collective-permute-start.38
  212.6 5.7 %project_in_first.3 = (f32[3,192,512]{2,1,0:T(8,128)}, f32[192,128]{1,0:T(8,128)S(1)}) custom-call(s32[8]{0:T(128)S(1)} %stack.176.meta, s32[1]{0:T(128)} %get-tuple-element.99.section_ref.meta, bf16[192,1024]{1,0:T(8,128)(2,1)S(1)} %get-tuple-element.68.refs_0_.refs_2_, bf16[192,1024]{1,0:T(8,128)(2,1)S(1)} %copy-done.42, ...), custom_call_target="tpu_custom_call" | custom-call | flops 1207959552 | bytes 6291456 | tf_op jit(solution)/shard_map/project_in_first/pallas_call | solution.py:198
  218.3 5.4 %project_in_last.3 = (bf16[192,512]{1,0:T(8,128)(2,1)S(1)}, bf16[192,512]{1,0:T(8,128)(2,1)S(1)}) custom-call(s32[8]{0:T(128)S(1)} %stack.176.meta, s32[1]{0:T(128)} %get-tuple-element.99.section_ref.meta, bf16[192,1024]{1,0:T(8,128)(2,1)S(1)} %copy-done.44, bf16[192,1024]{1,0:T(8,128)(2,1)S(1)} %copy-done.46, f32[3,192,512]{2,1,0:T(8,128)} %get-tuple-element.77.refs_2_, ...), custom_call_target="tpu_custom_call" | custom-call | flops 1207959552 | bytes 6291456 | tf_op jit(solution)/shard_map/project_in_last/pallas_call | solution.py:198
  223.7 1.6 collective-permute-start.31
  226.4 1.6 filter_and_gate.5
  228.0 4.3 %collective-permute-start.34 = (bf16[192,512]{1,0:T(8,128)(2,1)S(1)}, bf16[192,512]{1,0:T(8,128)(2,1)S(1)}, u32[]{:S(2)}, u32[]{:S(2)}) collective-permute-start(bf16[192,512]{1,0:T(8,128)(2,1)S(1)} %filter_and_gate.5), channel_id=1, source_target_pairs={{0,3},{1,0},{2,1},{3,2},{4,7},{5,4},{6,5},{7,6},{8,11},{9,8},{10,9... | collective-permute-start | bytes 589832 | tf_op jit(solution)/shard_map/ppermute | solution.py:405
  232.8 4.8 %collective-permute-done.34 = bf16[192,512]{1,0:T(8,128)(2,1)S(1)} collective-permute-done((bf16[192,512]{1,0:T(8,128)(2,1)S(1)}, bf16[192,512]{1,0:T(8,128)(2,1)S(1)}, u32[]{:S(2)}, u32[]{:S(2)}) %collective-permute-start.34) | collective-permute-done | bytes 196640 | tf_op jit(solution)/shard_map/ppermute | solution.py:405
  237.6 5.7 %collective-permute-start.32 = (bf16[192,512]{1,0:T(8,128)(2,1)S(1)}, bf16[192,512]{1,0:T(8,128)(2,1)S(1)}, u32[]{:S(2)}, u32[]{:S(2)}) collective-permute-start(bf16[192,512]{1,0:T(8,128)(2,1)S(1)} %filter_and_gate.5), channel_id=1, source_target_pairs={{0,1},{1,2},{2,3},{3,0},{4,5},{5,6},{6,7},{7,4},{8,9},{9,10},{10,1... | collective-permute-start | bytes 589832 | tf_op jit(solution)/shard_map/ppermute | solution.py:405
  243.3 7.9 %collective-permute-done.33 = bf16[192,512]{1,0:T(8,128)(2,1)S(1)} collective-permute-done((bf16[192,512]{1,0:T(8,128)(2,1)S(1)}, bf16[192,512]{1,0:T(8,128)(2,1)S(1)}, u32[]{:S(2)}, u32[]{:S(2)}) %collective-permute-start.33) | collective-permute-done | bytes 196640 | tf_op jit(solution)/shard_map/ppermute | solution.py:405
  251.5 2.2 collective-permute-done.35.refs_1_
  253.7 4.8 %project_out.5 = (bf16[192,1024]{1,0:T(8,128)(2,1)}, bf16[192,1024]{1,0:T(8,128)(2,1)S(1)}) custom-call(s32[8]{0:T(128)S(1)} %stack.176.meta, bf16[4,192,512]{2,1,0:T(8,128)(2,1)S(1)} %pad_maximum_fusion.5.refs_0_, bf16[4,192,512]{2,1,0:T(8,128)(2,1)S(1)} %collective-permute-done.35.refs_1_, bf16[192,1024]{1,0:T(8,128)(2,1)S(1)} %get-tuple-element.68.refs_0_.refs_2_, ...), custom_call_target="tpu_custom_call" | custom-call | flops 1610612736 | bytes 4194304 | tf_op jit(solution)/shard_map/project_out/pallas_call | solution.py:336
  266.5 6.1 %project_in_first.4 = (f32[3,192,512]{2,1,0:T(8,128)}, f32[192,128]{1,0:T(8,128)S(1)}) custom-call(s32[8]{0:T(128)S(1)} %stack.175.meta, s32[1]{0:T(128)} %get-tuple-element.102.section_ref.meta, bf16[192,1024]{1,0:T(8,128)(2,1)} %get-tuple-element.83.refs_0_.refs_2_, bf16[192,1024]{1,0:T(8,128)(2,1)} %collective-permute-done.40.refs_1_, ...), custom_call_target="tpu_custom_call" | custom-call | flops 1207959552 | bytes 6291456 | tf_op jit(solution)/shard_map/project_in_first/pallas_call | solution.py:198
  272.7 7.0 %collective-permute-done.41.refs_1_ = bf16[192,1024]{1,0:T(8,128)(2,1)} collective-permute-done((bf16[192,1024]{1,0:T(8,128)(2,1)}, bf16[192,1024]{1,0:T(8,128)(2,1)}, u32[]{:S(2)}, u32[]{:S(2)}) %collective-permute-start.41) | collective-permute-done | bytes 393248 | tf_op jit(solution)/shard_map/ppermute | solution.py:405
  279.6 5.8 %project_in_last.4 = (bf16[192,512]{1,0:T(8,128)(2,1)S(1)}, bf16[192,512]{1,0:T(8,128)(2,1)S(1)}) custom-call(s32[8]{0:T(128)S(1)} %stack.175.meta, s32[1]{0:T(128)} %get-tuple-element.102.section_ref.meta, bf16[192,1024]{1,0:T(8,128)(2,1)S(1)} %collective-permute-done.39.refs_0_, bf16[192,1024]{1,0:T(8,128)(2,1)} %collective-permute-done.41.refs_1_, ...), custom_call_target="tpu_custom_call" | custom-call | flops 1207959552 | bytes 6291456 | tf_op jit(solution)/shard_map/project_in_last/pallas_call | solution.py:198
  285.4 1.4 collective-permute-start.42
  289.8 1.5 collective-permute-start.44
  292.2 4.9 %collective-permute-done.45 = bf16[192,512]{1,0:T(8,128)(2,1)S(1)} collective-permute-done((bf16[192,512]{1,0:T(8,128)(2,1)S(1)}, bf16[192,512]{1,0:T(8,128)(2,1)S(1)}, u32[]{:S(2)}, u32[]{:S(2)}) %collective-permute-start.45) | collective-permute-done | bytes 196640 | tf_op jit(solution)/shard_map/ppermute | solution.py:405
  297.1 11.6 %collective-permute-done.44 = bf16[192,512]{1,0:T(8,128)(2,1)S(1)} collective-permute-done((bf16[192,512]{1,0:T(8,128)(2,1)S(1)}, bf16[192,512]{1,0:T(8,128)(2,1)S(1)}, u32[]{:S(2)}, u32[]{:S(2)}) %collective-permute-start.44) | collective-permute-done | bytes 196640 | tf_op jit(solution)/shard_map/ppermute | solution.py:405
  309.7 1.9 collective-permute-done.46.refs_1_
  311.6 4.6 %project_out.6 = (bf16[192,1024]{1,0:T(8,128)(2,1)S(1)}, bf16[192,1024]{1,0:T(8,128)(2,1)S(1)}) custom-call(s32[8]{0:T(128)S(1)} %stack.175.meta, bf16[4,192,512]{2,1,0:T(8,128)(2,1)S(1)} %pad_maximum_fusion.6.refs_0_, bf16[4,192,512]{2,1,0:T(8,128)(2,1)S(1)} %collective-permute-done.46.refs_1_, bf16[192,1024]{1,0:T(8,128)(2,1)} %get-tuple-element.83.refs_0_.refs_2_, ...), custom_call_target="tpu_custom_call" | custom-call | flops 1610612736 | bytes 4194304 | tf_op jit(solution)/shard_map/project_out/pallas_call | solution.py:336
  324.4 5.9 %project_in_first.5 = (f32[3,192,512]{2,1,0:T(8,128)}, f32[192,128]{1,0:T(8,128)S(1)}) custom-call(s32[8]{0:T(128)S(1)} %stack.174.meta, s32[1]{0:T(128)} %get-tuple-element.101.section_ref.meta, bf16[192,1024]{1,0:T(8,128)(2,1)S(1)} %get-tuple-element.89.refs_0_.refs_2_, bf16[192,1024]{1,0:T(8,128)(2,1)} %collective-permute-done.48.refs_1_, ...), custom_call_target="tpu_custom_call" | custom-call | flops 1207959552 | bytes 6291456 | tf_op jit(solution)/shard_map/project_in_first/pallas_call | solution.py:198
  330.3 6.8 %collective-permute-done.49.refs_1_ = bf16[192,1024]{1,0:T(8,128)(2,1)} collective-permute-done((bf16[192,1024]{1,0:T(8,128)(2,1)}, bf16[192,1024]{1,0:T(8,128)(2,1)}, u32[]{:S(2)}, u32[]{:S(2)}) %collective-permute-start.49) | collective-permute-done | bytes 393248 | tf_op jit(solution)/shard_map/ppermute | solution.py:405
  337.1 5.6 %project_in_last.5 = (bf16[192,512]{1,0:T(8,128)(2,1)S(1)}, bf16[192,512]{1,0:T(8,128)(2,1)S(1)}) custom-call(s32[8]{0:T(128)S(1)} %stack.174.meta, s32[1]{0:T(128)} %get-tuple-element.101.section_ref.meta, bf16[192,1024]{1,0:T(8,128)(2,1)} %collective-permute-done.47.refs_0_, bf16[192,1024]{1,0:T(8,128)(2,1)} %collective-permute-done.49.refs_1_, ...), custom_call_target="tpu_custom_call" | custom-call | flops 1207959552 | bytes 6291456 | tf_op jit(solution)/shard_map/project_in_last/pallas_call | solution.py:198
  342.7 1.4 collective-permute-start.50
  346.3 2.2 collective-permute-start.53
  348.5 1.9 collective-permute-start.51
  350.5 3.4 collective-permute-done.53
  353.9 11.9 %collective-permute-done.52 = bf16[192,512]{1,0:T(8,128)(2,1)S(1)} collective-permute-done((bf16[192,512]{1,0:T(8,128)(2,1)S(1)}, bf16[192,512]{1,0:T(8,128)(2,1)S(1)}, u32[]{:S(2)}, u32[]{:S(2)}) %collective-permute-start.52) | collective-permute-done | bytes 196640 | tf_op jit(solution)/shard_map/ppermute | solution.py:405
  366.9 1.9 collective-permute-done.54.refs_1_
  368.8 4.2 %project_out.7 = (bf16[192,1024]{1,0:T(8,128)(2,1)S(1)}, bf16[192,1024]{1,0:T(8,128)(2,1)S(1)}) custom-call(s32[8]{0:T(128)S(1)} %stack.174.meta, bf16[4,192,512]{2,1,0:T(8,128)(2,1)S(1)} %pad_maximum_fusion.7.refs_0_, bf16[4,192,512]{2,1,0:T(8,128)(2,1)S(1)} %collective-permute-done.54.refs_1_, bf16[192,1024]{1,0:T(8,128)(2,1)S(1)} %get-tuple-element.89.refs_0_.refs_2_, ...), custom_call_target="tpu_custom_call" | custom-call | flops 1610612736 | bytes 4194304 | tf_op jit(solution)/shard_map/project_out/pallas_call | solution.py:336
  (201 shorter events, 59.7 us)
Async XLA Ops:
  6.5 57.4 %all-gather.2.cloned.1.call-start = ((), (), s32[]{:S(2)}) async-start(), calls=%async_computation | async-start | bytes 1966080 | tf_op jit(solution)/shard_map/all_gather | solution.py:468
  14.3 49.5 %collective-permute-start = (bf16[2,3,1024,512]{3,2,1,0:T(8,128)(2,1)}, bf16[2,3,1024,512]{3,2,1,0:T(8,128)(2,1)}, u32[]{:S(2)}, u32[]{:S(2)}) collective-permute-start(bf16[2,3,1024,512]{3,2,1,0:T(8,128)(2,1)} %bitcast.7.in_ref.refs_1_.refs_2_.refs_4_), channel_id=1, source_target_pairs={{0,4},{4,0},{8,12},{12,8},{1,5},{5,1},{9,13},{13,9},{2,6},{6,2},{1... | collective-permute-start | bytes 18874376 | tf_op jit(solution)/shard_map/ppermute | solution.py:405
  14.8 26.8 %collective-permute-start.1 = (bf16[2,512,512]{2,1,0:T(8,128)(2,1)}, bf16[2,512,512]{2,1,0:T(8,128)(2,1)S(1)}, u32[]{:S(2)}, u32[]{:S(2)}) collective-permute-start(bf16[2,512,512]{2,1,0:T(8,128)(2,1)} %get-tuple-element.53), channel_id=1, source_target_pairs={{0,8},{4,12},{8,0},{12,4},{1,9},{5,13},{9,1},{13,5},{2,10},{6,14},... | collective-permute-start | bytes 3145736 | tf_op jit(solution)/shard_map/ppermute | solution.py:405
  17.4 46.5 %collective-permute-start.2 = (bf16[2,512,512]{2,1,0:T(8,128)(2,1)}, bf16[2,512,512]{2,1,0:T(8,128)(2,1)S(1)}, u32[]{:S(2)}, u32[]{:S(2)}) collective-permute-start(bf16[2,512,512]{2,1,0:T(8,128)(2,1)} %copy-done.50), channel_id=1, source_target_pairs={{0,8},{4,12},{8,0},{12,4},{1,9},{5,13},{9,1},{13,5},{2,10},{6,14},... | collective-permute-start | bytes 3145736 | tf_op jit(solution)/shard_map/ppermute | solution.py:405
  41.6 54.3 %copy-start.4 = (bf16[2,512,512]{2,1,0:T(8,128)(2,1)}, bf16[2,512,512]{2,1,0:T(8,128)(2,1)S(1)}, u32[]{:S(2)}) copy-start(bf16[2,512,512]{2,1,0:T(8,128)(2,1)S(1)} %collective-permute-done.1.refs_3_.refs_4_.refs_6_) | copy-start | bytes 3145732
  63.9 32.1 %collective-permute-start.3 = (bf16[2,512,512]{2,1,0:T(8,128)(2,1)S(1)}, bf16[2,512,512]{2,1,0:T(8,128)(2,1)S(1)}, u32[]{:S(2)}, u32[]{:S(2)}) collective-permute-start(bf16[2,512,512]{2,1,0:T(8,128)(2,1)S(1)} %collective-permute-done.1.refs_3_.refs_4_.refs_6_), channel_id=1, source_target_pairs={{0,16},{16,0},{1,17},{17,1},{2,18},{18,2},{3,19},{19,3},{4,20},{20... | collective-permute-start | bytes 3145736 | tf_op jit(solution)/shard_map/ppermute | solution.py:405
  65.7 30.3 %collective-permute-start.4 = (bf16[2,512,512]{2,1,0:T(8,128)(2,1)}, bf16[2,512,512]{2,1,0:T(8,128)(2,1)}, u32[]{:S(2)}, u32[]{:S(2)}) collective-permute-start(bf16[2,512,512]{2,1,0:T(8,128)(2,1)} %copy-done.49), channel_id=1, source_target_pairs={{0,8},{4,12},{8,0},{12,4},{1,9},{5,13},{9,1},{13,5},{2,10},{6,14},... | collective-permute-start | bytes 3145736 | tf_op jit(solution)/shard_map/ppermute | solution.py:405
  67.2 12.2 %collective-permute-start.7 = (bf16[512,512]{1,0:T(8,128)(2,1)S(1)}, bf16[512,512]{1,0:T(8,128)(2,1)S(1)}, u32[]{:S(2)}, u32[]{:S(2)}) collective-permute-start(bf16[512,512]{1,0:T(8,128)(2,1)S(1)} %get-tuple-element.60), channel_id=1, source_target_pairs={{1,0},{6,5},{3,2},{4,7},{9,8},{14,13},{11,10},{12,15},{17,16},{22,... | collective-permute-start | bytes 1572872 | tf_op jit(solution)/shard_map/ppermute | solution.py:405
  68.4 25.8 %collective-permute-start.6 = (bf16[512,512]{1,0:T(8,128)(2,1)S(1)}, bf16[512,512]{1,0:T(8,128)(2,1)S(1)}, u32[]{:S(2)}, u32[]{:S(2)}) collective-permute-start(bf16[512,512]{1,0:T(8,128)(2,1)S(1)} %get-tuple-element.60), channel_id=1, source_target_pairs={{2,0},{7,5},{0,2},{5,7},{10,8},{15,13},{8,10},{13,15},{18,16},{23,... | collective-permute-start | bytes 1572872 | tf_op jit(solution)/shard_map/ppermute | solution.py:405
  72.9 21.3 %collective-permute-start.5 = (bf16[512,512]{1,0:T(8,128)(2,1)S(1)}, bf16[512,512]{1,0:T(8,128)(2,1)S(1)}, u32[]{:S(2)}, u32[]{:S(2)}) collective-permute-start(bf16[512,512]{1,0:T(8,128)(2,1)S(1)} %get-tuple-element.60), channel_id=1, source_target_pairs={{3,0},{4,5},{1,2},{6,7},{11,8},{12,13},{9,10},{14,15},{19,16},{20,... | collective-permute-start | bytes 1572872 | tf_op jit(solution)/shard_map/ppermute | solution.py:405
  96.9 8.8 %collective-permute-start.8 = (bf16[4,512,512]{2,1,0:T(8,128)(2,1)S(1)}, bf16[4,512,512]{2,1,0:T(8,128)(2,1)S(1)}, u32[]{:S(2)}, u32[]{:S(2)}) collective-permute-start(bf16[4,512,512]{2,1,0:T(8,128)(2,1)S(1)} %pad_maximum_fusion), channel_id=1, source_target_pairs={{0,4},{4,0},{8,12},{12,8},{1,5},{5,1},{9,13},{13,9},{2,6},{6,2},{1... | collective-permute-start | bytes 6291464 | tf_op jit(solution)/shard_map/ppermute | solution.py:405
  96.9 8.9 %collective-permute-start.16 = (bf16[4,512,512]{2,1,0:T(8,128)(2,1)}, bf16[4,512,512]{2,1,0:T(8,128)(2,1)S(1)}, u32[]{:S(2)}, u32[]{:S(2)}) collective-permute-start(bf16[4,512,512]{2,1,0:T(8,128)(2,1)} %pad_maximum_fusion.1.refs_4_), channel_id=1, source_target_pairs={{5,1},{7,3},{8,12},{10,14},{21,17},{23,19},{24,28},{26,30}} | collective-permute-start | bytes 6291464 | tf_op jit(solution)/shard_map/ppermute | solution.py:405
  97.7 29.9 %collective-permute-start.18 = (bf16[4,512,512]{2,1,0:T(8,128)(2,1)}, bf16[4,512,512]{2,1,0:T(8,128)(2,1)}, u32[]{:S(2)}, u32[]{:S(2)}) collective-permute-start(bf16[4,512,512]{2,1,0:T(8,128)(2,1)} %pad_maximum_fusion.1.refs_4_), channel_id=1, source_target_pairs={{0,8},{5,9},{2,10},{7,11},{8,4},{13,5},{10,6},{15,7},{16,24},{21,2... | collective-permute-start | bytes 6291464 | tf_op jit(solution)/shard_map/ppermute | solution.py:405
  103.3 28.2 %collective-permute-start.17 = (bf16[4,512,512]{2,1,0:T(8,128)(2,1)}, bf16[4,512,512]{2,1,0:T(8,128)(2,1)}, u32[]{:S(2)}, u32[]{:S(2)}) collective-permute-start(bf16[4,512,512]{2,1,0:T(8,128)(2,1)} %pad_maximum_fusion.1.refs_4_), channel_id=1, source_target_pairs={{0,16},{16,0},{5,17},{21,1},{2,18},{18,2},{7,19},{23,3},{8,28},{24... | collective-permute-start | bytes 6291464 | tf_op jit(solution)/shard_map/ppermute | solution.py:405
  105.7 8.2 %collective-permute-start.9 = (bf16[2,512,512]{2,1,0:T(8,128)(2,1)S(1)}, bf16[2,512,512]{2,1,0:T(8,128)(2,1)S(1)}, u32[]{:S(2)}, u32[]{:S(2)}) collective-permute-start(bf16[2,512,512]{2,1,0:T(8,128)(2,1)S(1)} %copy-done.5), channel_id=1, source_target_pairs={{0,4},{4,0},{8,12},{12,8},{1,5},{5,1},{9,13},{13,9},{2,6},{6,2},{1... | collective-permute-start | bytes 3145736 | tf_op jit(solution)/shard_map/ppermute | solution.py:479
  107.2 24.3 %collective-permute-start.21 = (bf16[512,512]{1,0:T(8,128)(2,1)}, bf16[512,512]{1,0:T(8,128)(2,1)}, u32[]{:S(2)}, u32[]{:S(2)}) collective-permute-start(bf16[512,512]{1,0:T(8,128)(2,1)} %get-tuple-element.66), channel_id=1, source_target_pairs={{1,0},{6,5},{3,2},{4,7},{9,8},{14,13},{11,10},{12,15},{17,16},{22,... | collective-permute-start | bytes 1572872 | tf_op jit(solution)/shard_map/ppermute | solution.py:405
  108.4 27.6 %collective-permute-start.20 = (bf16[512,512]{1,0:T(8,128)(2,1)}, bf16[512,512]{1,0:T(8,128)(2,1)}, u32[]{:S(2)}, u32[]{:S(2)}) collective-permute-start(bf16[512,512]{1,0:T(8,128)(2,1)} %get-tuple-element.66), channel_id=1, source_target_pairs={{2,0},{7,5},{0,2},{5,7},{10,8},{15,13},{8,10},{13,15},{18,16},{23,... | collective-permute-start | bytes 1572872 | tf_op jit(solution)/shard_map/ppermute | solution.py:405
  114.8 21.2 %collective-permute-start.19 = (bf16[512,512]{1,0:T(8,128)(2,1)}, bf16[512,512]{1,0:T(8,128)(2,1)}, u32[]{:S(2)}, u32[]{:S(2)}) collective-permute-start(bf16[512,512]{1,0:T(8,128)(2,1)} %get-tuple-element.66), channel_id=1, source_target_pairs={{3,0},{4,5},{1,2},{6,7},{11,8},{12,13},{9,10},{14,15},{19,16},{20,... | collective-permute-start | bytes 1572872 | tf_op jit(solution)/shard_map/ppermute | solution.py:405
  127.6 11.6 %collective-permute-start.10 = (bf16[128,512]{1,0:T(8,128)(2,1)S(1)}, bf16[128,512]{1,0:T(8,128)(2,1)S(1)}, u32[]{:S(2)}, u32[]{:S(2)}) collective-permute-start(bf16[128,512]{1,0:T(8,128)(2,1)S(1)} %slice.37), channel_id=1, source_target_pairs={{0,4},{4,8},{8,12},{1,5},{5,9},{9,13},{2,6},{6,10},{10,14},{3,7},{... | collective-permute-start | bytes 393224 | tf_op jit(solution)/shard_map/ppermute | solution.py:515
  139.2 30.6 %collective-permute-start.26 = (bf16[4,512,512]{2,1,0:T(8,128)(2,1)}, bf16[4,512,512]{2,1,0:T(8,128)(2,1)}, u32[]{:S(2)}, u32[]{:S(2)}) collective-permute-start(bf16[4,512,512]{2,1,0:T(8,128)(2,1)} %pad_maximum_fusion.2.refs_9_), channel_id=1, source_target_pairs={{0,8},{5,9},{2,10},{7,11},{8,4},{13,5},{10,6},{15,7},{16,24},{21,2... | collective-permute-start | bytes 6291464 | tf_op jit(solution)/shard_map/ppermute | solution.py:405
  142.8 27.0 %collective-permute-start.22 = (bf16[4,512,512]{2,1,0:T(8,128)(2,1)}, bf16[4,512,512]{2,1,0:T(8,128)(2,1)}, u32[]{:S(2)}, u32[]{:S(2)}) collective-permute-start(bf16[4,512,512]{2,1,0:T(8,128)(2,1)} %collective-permute-done.18.refs_7_), channel_id=1, source_target_pairs={{8,24},{24,8},{9,25},{25,9},{10,26},{26,10},{11,27},{27,11},{4,20}... | collective-permute-start | bytes 6291464 | tf_op jit(solution)/shard_map/ppermute | solution.py:405
  144.8 26.5 %copy-start.24 = (bf16[4,512,512]{2,1,0:T(8,128)(2,1)S(1)}, bf16[4,512,512]{2,1,0:T(8,128)(2,1)}, u32[]{:S(2)}) copy-start(bf16[4,512,512]{2,1,0:T(8,128)(2,1)} %copy-done.23) | copy-start | bytes 6291460
  146.6 6.7 %collective-permute-start.13 = (bf16[192,512]{1,0:T(8,128)(2,1)S(1)}, bf16[192,512]{1,0:T(8,128)(2,1)S(1)}, u32[]{:S(2)}, u32[]{:S(2)}) collective-permute-start(bf16[192,512]{1,0:T(8,128)(2,1)S(1)} %filter_and_gate.4), channel_id=1, source_target_pairs={{0,3},{1,0},{2,1},{3,2},{4,7},{5,4},{6,5},{7,6},{8,11},{9,8},{10,9... | collective-permute-start | bytes 589832 | tf_op jit(solution)/shard_map/ppermute | solution.py:405
  146.6 20.4 %collective-permute-start.12 = (bf16[192,512]{1,0:T(8,128)(2,1)S(1)}, bf16[192,512]{1,0:T(8,128)(2,1)S(1)}, u32[]{:S(2)}, u32[]{:S(2)}) collective-permute-start(bf16[192,512]{1,0:T(8,128)(2,1)S(1)} %filter_and_gate.4), channel_id=1, source_target_pairs={{0,2},{1,3},{2,0},{3,1},{4,6},{5,7},{6,4},{7,5},{8,10},{9,11},{10,... | collective-permute-start | bytes 589832 | tf_op jit(solution)/shard_map/ppermute | solution.py:405
  150.2 16.9 %collective-permute-start.11 = (bf16[192,512]{1,0:T(8,128)(2,1)S(1)}, bf16[192,512]{1,0:T(8,128)(2,1)S(1)}, u32[]{:S(2)}, u32[]{:S(2)}) collective-permute-start(bf16[192,512]{1,0:T(8,128)(2,1)S(1)} %filter_and_gate.4), channel_id=1, source_target_pairs={{0,1},{1,2},{2,3},{3,0},{4,5},{5,6},{6,7},{7,4},{8,9},{9,10},{10,1... | collective-permute-start | bytes 589832 | tf_op jit(solution)/shard_map/ppermute | solution.py:405
  168.0 3.2 collective-permute-start.14
  169.2 2.0 collective-permute-start.15
  169.8 25.4 %collective-permute-start.27 = (bf16[2,512,512]{2,1,0:T(8,128)(2,1)}, bf16[2,512,512]{2,1,0:T(8,128)(2,1)S(1)}, u32[]{:S(2)}, u32[]{:S(2)}) collective-permute-start(bf16[2,512,512]{2,1,0:T(8,128)(2,1)} %collective-permute-done.4.refs_9_.refs_11_), channel_id=1, source_target_pairs={{0,16},{16,0},{1,17},{17,1},{2,18},{18,2},{3,19},{19,3},{4,20},{20... | collective-permute-start | bytes 3145736 | tf_op jit(solution)/shard_map/ppermute | solution.py:405
  170.3 25.1 %collective-permute-start.28 = (bf16[2,512,512]{2,1,0:T(8,128)(2,1)}, bf16[2,512,512]{2,1,0:T(8,128)(2,1)S(1)}, u32[]{:S(2)}, u32[]{:S(2)}) collective-permute-start(bf16[2,512,512]{2,1,0:T(8,128)(2,1)} %copy-done.48), channel_id=1, source_target_pairs={{0,8},{4,12},{8,0},{12,4},{1,9},{5,13},{9,1},{13,5},{2,10},{6,14},... | collective-permute-start | bytes 3145736 | tf_op jit(solution)/shard_map/ppermute | solution.py:405
  176.2 1.8 collective-permute-start.24
  176.6 31.4 %copy-start.3 = (bf16[2,512,512]{2,1,0:T(8,128)(2,1)S(1)}, bf16[2,512,512]{2,1,0:T(8,128)(2,1)}, u32[]{:S(2)}) copy-start(bf16[2,512,512]{2,1,0:T(8,128)(2,1)} %copy-done.1) | copy-start | bytes 3145732
  176.6 31.4 %copy-start.7 = (bf16[2,512,512]{2,1,0:T(8,128)(2,1)S(1)}, bf16[2,512,512]{2,1,0:T(8,128)(2,1)}, u32[]{:S(2)}) copy-start(bf16[2,512,512]{2,1,0:T(8,128)(2,1)} %copy-done.4) | copy-start | bytes 3145732
  176.6 20.5 %collective-permute-start.23 = (bf16[192,1024]{1,0:T(8,128)(2,1)S(1)}, bf16[192,1024]{1,0:T(8,128)(2,1)S(1)}, u32[]{:S(2)}, u32[]{:S(2)}) collective-permute-start(bf16[192,1024]{1,0:T(8,128)(2,1)S(1)} %get-tuple-element.68.refs_0_.refs_2_), channel_id=1, source_target_pairs={{0,1},{1,0},{2,3},{3,2},{4,5},{5,4},{6,7},{7,6},{8,9},{9,8},{10,11... | collective-permute-start | bytes 1179656 | tf_op jit(solution)/shard_map/ppermute | solution.py:405
  178.0 19.8 %collective-permute-start.25 = (bf16[192,1024]{1,0:T(8,128)(2,1)S(1)}, bf16[192,1024]{1,0:T(8,128)(2,1)S(1)}, u32[]{:S(2)}, u32[]{:S(2)}) collective-permute-start(bf16[192,1024]{1,0:T(8,128)(2,1)S(1)} %collective-permute-done.24.refs_1_), channel_id=1, source_target_pairs={{0,1},{1,0},{2,3},{3,2},{4,5},{5,4},{6,7},{7,6},{8,9},{9,8},{10,11... | collective-permute-start | bytes 1179656 | tf_op jit(solution)/shard_map/ppermute | solution.py:405
  198.6 9.3 %collective-permute-start.29 = (bf16[4,512,512]{2,1,0:T(8,128)(2,1)}, bf16[4,512,512]{2,1,0:T(8,128)(2,1)}, u32[]{:S(2)}, u32[]{:S(2)}) collective-permute-start(bf16[4,512,512]{2,1,0:T(8,128)(2,1)} %pad_maximum_fusion.3), channel_id=1, source_target_pairs={{0,4},{4,0},{8,12},{12,8},{1,5},{5,1},{9,13},{13,9},{2,6},{6,2},{1... | collective-permute-start | bytes 6291464 | tf_op jit(solution)/shard_map/ppermute | solution.py:405
  198.6 9.3 %collective-permute-start.30 = (bf16[2,512,512]{2,1,0:T(8,128)(2,1)}, bf16[2,512,512]{2,1,0:T(8,128)(2,1)}, u32[]{:S(2)}, u32[]{:S(2)}) collective-permute-start(bf16[2,512,512]{2,1,0:T(8,128)(2,1)} %collective-permute-done.4.refs_9_.refs_11_), channel_id=1, source_target_pairs={{0,4},{4,0},{8,12},{12,8},{1,5},{5,1},{9,13},{13,9},{2,6},{6,2},{1... | collective-permute-start | bytes 3145736 | tf_op jit(solution)/shard_map/ppermute | solution.py:517
  199.1 52.4 %collective-permute-start.37 = (bf16[4,512,512]{2,1,0:T(8,128)(2,1)}, bf16[4,512,512]{2,1,0:T(8,128)(2,1)}, u32[]{:S(2)}, u32[]{:S(2)}) collective-permute-start(bf16[4,512,512]{2,1,0:T(8,128)(2,1)} %pad_maximum_fusion.2.refs_9_), channel_id=1, source_target_pairs={{0,16},{16,0},{5,17},{21,1},{2,18},{18,2},{7,19},{23,3},{8,28},{24... | collective-permute-start | bytes 6291464 | tf_op jit(solution)/shard_map/ppermute | solution.py:405
  202.5 49.0 %collective-permute-start.36 = (bf16[4,512,512]{2,1,0:T(8,128)(2,1)}, bf16[4,512,512]{2,1,0:T(8,128)(2,1)}, u32[]{:S(2)}, u32[]{:S(2)}) collective-permute-start(bf16[4,512,512]{2,1,0:T(8,128)(2,1)} %pad_maximum_fusion.2.refs_9_), channel_id=1, source_target_pairs={{5,1},{7,3},{8,12},{10,14},{21,17},{23,19},{24,28},{26,30}} | collective-permute-start | bytes 6291464 | tf_op jit(solution)/shard_map/ppermute | solution.py:405
  204.5 47.0 %collective-permute-start.38 = (bf16[4,512,512]{2,1,0:T(8,128)(2,1)}, bf16[4,512,512]{2,1,0:T(8,128)(2,1)}, u32[]{:S(2)}, u32[]{:S(2)}) collective-permute-start(bf16[4,512,512]{2,1,0:T(8,128)(2,1)} %collective-permute-done.26.refs_12_), channel_id=1, source_target_pairs={{8,24},{24,8},{9,25},{25,9},{10,26},{26,10},{11,27},{27,11},{4,20}... | collective-permute-start | bytes 6291464 | tf_op jit(solution)/shard_map/ppermute | solution.py:405
  223.7 30.0 %copy-start.25 = (bf16[4,512,512]{2,1,0:T(8,128)(2,1)S(1)}, bf16[4,512,512]{2,1,0:T(8,128)(2,1)}, u32[]{:S(2)}) copy-start(bf16[4,512,512]{2,1,0:T(8,128)(2,1)} %copy-done.23) | copy-start | bytes 6291460
  223.7 30.0 %copy-start.36 = (bf16[192,1024]{1,0:T(8,128)(2,1)S(1)}, bf16[192,1024]{1,0:T(8,128)(2,1)}, u32[]{:S(2)}) copy-start(bf16[192,1024]{1,0:T(8,128)(2,1)} %copy-done.35) | copy-start | bytes 1179652
  223.7 2.6 collective-permute-start.31
  228.0 9.7 %collective-permute-start.34 = (bf16[192,512]{1,0:T(8,128)(2,1)S(1)}, bf16[192,512]{1,0:T(8,128)(2,1)S(1)}, u32[]{:S(2)}, u32[]{:S(2)}) collective-permute-start(bf16[192,512]{1,0:T(8,128)(2,1)S(1)} %filter_and_gate.5), channel_id=1, source_target_pairs={{0,3},{1,0},{2,1},{3,2},{4,7},{5,4},{6,5},{7,6},{8,11},{9,8},{10,9... | collective-permute-start | bytes 589832 | tf_op jit(solution)/shard_map/ppermute | solution.py:405
  232.3 18.9 %collective-permute-start.33 = (bf16[192,512]{1,0:T(8,128)(2,1)S(1)}, bf16[192,512]{1,0:T(8,128)(2,1)S(1)}, u32[]{:S(2)}, u32[]{:S(2)}) collective-permute-start(bf16[192,512]{1,0:T(8,128)(2,1)S(1)} %filter_and_gate.5), channel_id=1, source_target_pairs={{0,2},{1,3},{2,0},{3,1},{4,6},{5,7},{6,4},{7,5},{8,10},{9,11},{10,... | collective-permute-start | bytes 589832 | tf_op jit(solution)/shard_map/ppermute | solution.py:405
  237.6 13.6 %collective-permute-start.32 = (bf16[192,512]{1,0:T(8,128)(2,1)S(1)}, bf16[192,512]{1,0:T(8,128)(2,1)S(1)}, u32[]{:S(2)}, u32[]{:S(2)}) collective-permute-start(bf16[192,512]{1,0:T(8,128)(2,1)S(1)} %filter_and_gate.5), channel_id=1, source_target_pairs={{0,1},{1,2},{2,3},{3,0},{4,5},{5,6},{6,7},{7,4},{8,9},{9,10},{10,1... | collective-permute-start | bytes 589832 | tf_op jit(solution)/shard_map/ppermute | solution.py:405
  251.3 2.4 collective-permute-start.35
  258.5 1.9 collective-permute-start.40
  259.5 13.2 %collective-permute-start.39 = (bf16[192,1024]{1,0:T(8,128)(2,1)}, bf16[192,1024]{1,0:T(8,128)(2,1)S(1)}, u32[]{:S(2)}, u32[]{:S(2)}) collective-permute-start(bf16[192,1024]{1,0:T(8,128)(2,1)} %get-tuple-element.83.refs_0_.refs_2_), channel_id=1, source_target_pairs={{0,1},{1,0},{2,3},{3,2},{4,5},{5,4},{6,7},{7,6},{8,9},{9,8},{10,11... | collective-permute-start | bytes 1179656 | tf_op jit(solution)/shard_map/ppermute | solution.py:405
  260.4 19.2 %collective-permute-start.41 = (bf16[192,1024]{1,0:T(8,128)(2,1)}, bf16[192,1024]{1,0:T(8,128)(2,1)}, u32[]{:S(2)}, u32[]{:S(2)}) collective-permute-start(bf16[192,1024]{1,0:T(8,128)(2,1)} %collective-permute-done.40.refs_1_), channel_id=1, source_target_pairs={{0,1},{1,0},{2,3},{3,2},{4,5},{5,4},{6,7},{7,6},{8,9},{9,8},{10,11... | collective-permute-start | bytes 1179656 | tf_op jit(solution)/shard_map/ppermute | solution.py:405
  285.4 26.2 %copy-start.26 = (bf16[4,512,512]{2,1,0:T(8,128)(2,1)S(1)}, bf16[4,512,512]{2,1,0:T(8,128)(2,1)}, u32[]{:S(2)}) copy-start(bf16[4,512,512]{2,1,0:T(8,128)(2,1)} %copy-done.23) | copy-start | bytes 6291460
  285.4 2.4 collective-permute-start.42
  289.1 8.0 %collective-permute-start.45 = (bf16[192,512]{1,0:T(8,128)(2,1)S(1)}, bf16[192,512]{1,0:T(8,128)(2,1)S(1)}, u32[]{:S(2)}, u32[]{:S(2)}) collective-permute-start(bf16[192,512]{1,0:T(8,128)(2,1)S(1)} %filter_and_gate.6), channel_id=1, source_target_pairs={{0,3},{1,0},{2,1},{3,2},{4,7},{5,4},{6,5},{7,6},{8,11},{9,8},{10,9... | collective-permute-start | bytes 589832 | tf_op jit(solution)/shard_map/ppermute | solution.py:405
  289.8 18.9 %collective-permute-start.44 = (bf16[192,512]{1,0:T(8,128)(2,1)S(1)}, bf16[192,512]{1,0:T(8,128)(2,1)S(1)}, u32[]{:S(2)}, u32[]{:S(2)}) collective-permute-start(bf16[192,512]{1,0:T(8,128)(2,1)S(1)} %filter_and_gate.6), channel_id=1, source_target_pairs={{0,2},{1,3},{2,0},{3,1},{4,6},{5,7},{6,4},{7,5},{8,10},{9,11},{10,... | collective-permute-start | bytes 589832 | tf_op jit(solution)/shard_map/ppermute | solution.py:405
  291.3 17.4 %collective-permute-start.43 = (bf16[192,512]{1,0:T(8,128)(2,1)S(1)}, bf16[192,512]{1,0:T(8,128)(2,1)S(1)}, u32[]{:S(2)}, u32[]{:S(2)}) collective-permute-start(bf16[192,512]{1,0:T(8,128)(2,1)S(1)} %filter_and_gate.6), channel_id=1, source_target_pairs={{0,1},{1,2},{2,3},{3,0},{4,5},{5,6},{6,7},{7,4},{8,9},{9,10},{10,1... | collective-permute-start | bytes 589832 | tf_op jit(solution)/shard_map/ppermute | solution.py:405
  308.8 2.8 collective-permute-start.46
  316.2 1.9 collective-permute-start.48
  317.4 12.9 %collective-permute-start.47 = (bf16[192,1024]{1,0:T(8,128)(2,1)S(1)}, bf16[192,1024]{1,0:T(8,128)(2,1)}, u32[]{:S(2)}, u32[]{:S(2)}) collective-permute-start(bf16[192,1024]{1,0:T(8,128)(2,1)S(1)} %get-tuple-element.89.refs_0_.refs_2_), channel_id=1, source_target_pairs={{0,1},{1,0},{2,3},{3,2},{4,5},{5,4},{6,7},{7,6},{8,9},{9,8},{10,11... | collective-permute-start | bytes 1179656 | tf_op jit(solution)/shard_map/ppermute | solution.py:405
  318.1 19.0 %collective-permute-start.49 = (bf16[192,1024]{1,0:T(8,128)(2,1)}, bf16[192,1024]{1,0:T(8,128)(2,1)}, u32[]{:S(2)}, u32[]{:S(2)}) collective-permute-start(bf16[192,1024]{1,0:T(8,128)(2,1)} %collective-permute-done.48.refs_1_), channel_id=1, source_target_pairs={{0,1},{1,0},{2,3},{3,2},{4,5},{5,4},{6,7},{7,6},{8,9},{9,8},{10,11... | collective-permute-start | bytes 1179656 | tf_op jit(solution)/shard_map/ppermute | solution.py:405
  342.7 2.4 collective-permute-start.50
  346.3 7.6 %collective-permute-start.53 = (bf16[192,512]{1,0:T(8,128)(2,1)S(1)}, bf16[192,512]{1,0:T(8,128)(2,1)S(1)}, u32[]{:S(2)}, u32[]{:S(2)}) collective-permute-start(bf16[192,512]{1,0:T(8,128)(2,1)S(1)} %filter_and_gate.7), channel_id=1, source_target_pairs={{0,3},{1,0},{2,1},{3,2},{4,7},{5,4},{6,5},{7,6},{8,11},{9,8},{10,9... | collective-permute-start | bytes 589832 | tf_op jit(solution)/shard_map/ppermute | solution.py:405
  348.5 17.3 %collective-permute-start.52 = (bf16[192,512]{1,0:T(8,128)(2,1)S(1)}, bf16[192,512]{1,0:T(8,128)(2,1)S(1)}, u32[]{:S(2)}, u32[]{:S(2)}) collective-permute-start(bf16[192,512]{1,0:T(8,128)(2,1)S(1)} %filter_and_gate.7), channel_id=1, source_target_pairs={{0,2},{1,3},{2,0},{3,1},{4,6},{5,7},{6,4},{7,5},{8,10},{9,11},{10,... | collective-permute-start | bytes 589832 | tf_op jit(solution)/shard_map/ppermute | solution.py:405
  348.5 17.3 %collective-permute-start.51 = (bf16[192,512]{1,0:T(8,128)(2,1)S(1)}, bf16[192,512]{1,0:T(8,128)(2,1)S(1)}, u32[]{:S(2)}, u32[]{:S(2)}) collective-permute-start(bf16[192,512]{1,0:T(8,128)(2,1)S(1)} %filter_and_gate.7), channel_id=1, source_target_pairs={{0,1},{1,2},{2,3},{3,0},{4,5},{5,6},{6,7},{7,4},{8,9},{9,10},{10,1... | collective-permute-start | bytes 589832 | tf_op jit(solution)/shard_map/ppermute | solution.py:405
  365.9 2.9 collective-permute-start.54
  372.9 1.8 collective-permute-start.55
  (45 other events, 277.4 us)
Sparse Core Ops, SparseCore 0:
  14.9 39.4 all-gather.1

commit v2 on v1

--- a/solution.py
+++ b/solution.py
@@ -81,6 +81,14 @@
 SECOND, GROUP, SAME, MATCH, ROW = range(5)
 
 
+def scalars(plan, step):
+    g, i, j = lax.axis_index("groups"), lax.axis_index("ctx"), lax.axis_index("chan")
+    x, c, h = i >> 1, i & 1, j & 1
+    second = (plan[step] != plan[0]).astype(jnp.int32)
+    same, match = (x == c).astype(jnp.int32), (c == h).astype(jnp.int32)
+    return [second, g, same, match, i, i ^ 1, i ^ 2, i ^ 3]
+
+
 def ctx_pairs(change):
     return [(i, i ^ change) for i in range(4)]
 
@@ -92,35 +100,37 @@
 OWN, CORE, CHIP, BOTH = range(4)
 
 
-def in_kernel(mode, sections, meta, section_ref, *refs):
+def in_kernel(mode, step, sections, plan, *refs):
+    meta = scalars(plan, step)
+    section = plan[step]
     count = 1 if mode == "whole" else 2
     pieces, refs = refs[:count], refs[count:]
     if mode == "last":
         earlier, earlier_square, refs = refs[0], refs[1], refs[2:]
     own_in, core_in = refs[:2]
-    weights = [refs[2 + 5 * s : 7 + 5 * s] for s in range(sections)]
-    out_ref, out_ref2, hidden, held, total, held_sem = refs[2 + 5 * sections :]
+    weights, refs = [refs[2:6], refs[6:11]], refs[6 if sections == 1 else 11 :]
+    out_ref, out_ref2, hidden, held, total, held_sem = refs
     tokens, width = hidden.shape[1:]
     part = width // 2
     group = meta[GROUP]
-    section = section_ref[0]
     slots = held.shape[1]
 
     def span(q):
         return pl.ds(pl.multiple_of(q * part, part), part)
 
     def start(kind, p, slot, sources):
-        chip, chip_y, chip_q, both = sources[:4]
         if kind in (OWN, CORE):
             source = own_in if kind == OWN else core_in
             halves = [(source.at[section, p, span(q)], span(q)) for q in range(2)]
+        elif len(sources) == 4:
+            mine, other = sources[:2] if kind == CHIP else sources[2:]
+            halves = [(mine.at[p], span(group)), (other.at[p], span(1 - group))]
         elif p == 0:
-            sources = chip_q if kind == CHIP else both
-            halves = [(sources.at[q], span(q)) for q in range(2)]
-        elif kind == CHIP:
-            halves = [(chip.at[p - 1], span(group)), (chip_y.at[p - 1], span(1 - group))]
+            source = sources[2 if kind == CHIP else 3]
+            halves = [(source.at[q], span(q)) for q in range(2)]
         else:
-            halves = [(sources[4].at[p - 1], span(group)), (both.at[p + 1], span(1 - group))]
+            mine, other, at = (sources[0], sources[1], p - 1) if kind == CHIP else (sources[4], sources[3], p + 1)
+            halves = [(mine.at[p - 1], span(group)), (other.at[at], span(1 - group))]
         for q in range(2):
             pltpu.make_async_copy(
                 halves[q][0], held.at[p, slot, halves[q][1]], held_sem.at[p, slot, q]
@@ -180,7 +190,7 @@
         out_ref2[...] = ((total[1] * scale) * (total[2] * scale)).astype(out_ref2.dtype)
 
 
-def project_in(mode, meta, section, pieces, earlier, own_in, core_in, weights):
+def project_in(mode, step, plan, pieces, earlier, own_in, core_in, weights):
     width, channels = own_in.shape[2:]
     tokens = pieces[0].shape[0]
     sections = len(weights)
@@ -196,9 +206,9 @@
     else:
         out = (jax.ShapeDtypeStruct((tokens, channels), jnp.bfloat16),) * 2
     return pl.pallas_call(
-        partial(in_kernel, mode, sections),
+        partial(in_kernel, mode, step, sections),
         out_shape=out,
-        in_specs=[smem] * 2
+        in_specs=[smem]
         + [vmem] * (len(pieces) + len(earlier))
         + [anywhere] * (2 + sum(len(w) for w in weights)),
         out_specs=(vmem, vmem),
@@ -215,18 +225,18 @@
             transcendentals=0,
         ),
         name="project_in_" + mode,
-    )(meta, section, *pieces, *earlier, own_in, core_in, *[w for ws in weights for w in ws])
+    )(plan, *pieces, *earlier, own_in, core_in, *[w for ws in weights for w in ws])
 
 
 BLOCK = 64
 
 
-def filter_kernel(meta, halo, mixed, query, bands, short, gated, extended):
+def filter_kernel(step, plan, halo, mixed, query, bands, short, gated, extended):
     reach, tokens = halo.shape[0], mixed.shape[0]
     channels = mixed.shape[1]
     group_size = channels // (bands.shape[0] // BLOCK)
 
-    @pl.when(meta[0] == 0)
+    @pl.when(plan[step] == 0)
     def _():
         extended[:reach] = halo[...].astype(jnp.float32)
         extended[reach:] = mixed[...].astype(jnp.float32)
@@ -236,7 +246,7 @@
             total = total + taps[t : t + 1] * extended[reach - t : reach - t + tokens]
         gated[...] = (query[...].astype(jnp.float32) * total).astype(gated.dtype)
 
-    @pl.when(meta[0] != 0)
+    @pl.when(plan[step] != 0)
     def _():
         lanes = 128
         per_tile = lanes // group_size
@@ -257,11 +267,11 @@
                 gated[rows, at] = (query[rows, at].astype(jnp.float32) * total).astype(gated.dtype)
 
 
-def filter_and_gate(section, halo, mixed, query, bands, short):
+def filter_and_gate(step, plan, halo, mixed, query, bands, short):
     tokens, channels = mixed.shape
     vmem = pl.BlockSpec(memory_space=pltpu.VMEM)
     return pl.pallas_call(
-        filter_kernel,
+        partial(filter_kernel, step),
         out_shape=jax.ShapeDtypeStruct(mixed.shape, jnp.bfloat16),
         in_specs=[pl.BlockSpec(memory_space=pltpu.SMEM)] + [vmem] * 5,
         out_specs=vmem,
@@ -271,7 +281,7 @@
             flops=2 * tokens * channels * 1024, bytes_accessed=8 * tokens * channels, transcendentals=0
         ),
         name="filter_and_gate",
-    )(section, halo, mixed, query, bands, short)
+    )(plan, halo, mixed, query, bands, short)
 
 
 def tap_bands(medium_taps):
@@ -285,7 +295,8 @@
     return skewed[:, :, : reach + BLOCK].reshape(groups * BLOCK, reach + BLOCK)
 
 
-def out_kernel(sections, meta, *refs):
+def out_kernel(step, sections, plan, *refs):
+    meta = scalars(plan, step)
     own_gated, core_gated, own_hidden, core_hidden = refs[:4]
     weights = [refs[4 + 5 * s : 9 + 5 * s] for s in range(sections)]
     own_out, core_out, held, held_sem = refs[4 + 5 * sections :]
@@ -325,7 +336,7 @@
     core_out[...] = (core_hidden[...].astype(jnp.float32) + total[tokens:]).astype(core_out.dtype)
 
 
-def project_out(meta, own_gated, core_gated, own_hidden, core_hidden, weights):
+def project_out(step, plan, own_gated, core_gated, own_hidden, core_hidden, weights):
     tokens, width = own_hidden.shape
     channels = own_gated.shape[2]
     sections = len(weights)
@@ -334,7 +345,7 @@
     smem = pl.BlockSpec(memory_space=pltpu.SMEM)
     out = jax.ShapeDtypeStruct((tokens, width), jnp.bfloat16)
     return pl.pallas_call(
-        partial(out_kernel, sections),
+        partial(out_kernel, step, sections),
         out_shape=(out, out),
         in_specs=[smem] + [vmem] * 4 + [anywhere] * (5 * sections),
         out_specs=(vmem, vmem),
@@ -349,41 +360,40 @@
             transcendentals=0,
         ),
         name="project_out",
-    )(meta, own_gated, core_gated, own_hidden, core_hidden, *[w for ws in weights for w in ws])
-
-
-def taken_kernel(at, in_ref, out_ref, out_half, kv_half, query, sem):
-    section = at[0]
-    part = out_half.shape[0]
-    mine = pl.ds(pl.multiple_of(at[1] * part, part), part)
-    copies = [
-        pltpu.make_async_copy(in_ref.at[section, 1, mine], kv_half.at[0], sem.at[0]),
-        pltpu.make_async_copy(in_ref.at[section, 2, mine], kv_half.at[1], sem.at[1]),
-        pltpu.make_async_copy(out_ref.at[section, mine], out_half, sem.at[2]),
-        pltpu.make_async_copy(in_ref.at[section, 0, pl.ds(0, part)], query.at[0], sem.at[3]),
-        pltpu.make_async_copy(in_ref.at[section, 0, pl.ds(part, part)], query.at[1], sem.at[4]),
-    ]
-    for copy in copies:
+    )(plan, own_gated, core_gated, own_hidden, core_hidden, *[w for ws in weights for w in ws])
+
+
+def taken_kernel(second, runs, plan, in_ref, out_ref, *refs):
+    outs, sem = refs[:-1], refs[-1]
+    section = 1 - plan[0] if second else plan[0]
+    group = lax.axis_index("groups")
+    part = outs[0].shape[0]
+    mine = pl.ds(pl.multiple_of(group * part, part), part)
+    pairs = [(out_ref.at[section, mine], outs[0])]
+    for run, out in zip(runs, outs[1:]):
+        for n, (p, q) in enumerate(run):
+            pairs.append((in_ref.at[section, p, mine if q is None else pl.ds(q * part, part)], out.at[n]))
+    copies = [pltpu.make_async_copy(*pair, sem.at[n]) for n, pair in enumerate(pairs)]
+    for copy in copies[1:] + copies[:1]:
         copy.start()
     for copy in copies:
         copy.wait()
 
 
-def taken(section, g, in_weights, out_weights):
-    width, channels = out_weights.shape[1:]
-    part = width // 2
-    far = pl.BlockSpec(memory_space=pl.ANY)
+def taken(second, runs, plan, in_weights, out_weights):
+    part, channels = out_weights.shape[1] // 2, out_weights.shape[2]
+    far = pl.BlockSpec(memory_space=pltpu.HBM)
     near = pl.BlockSpec(memory_space=pltpu.VMEM)
-    shapes = [(part, channels), (2, part, channels), (2, part, channels)]
+    shapes = [(part, channels)] + [(len(run), part, channels) for run in runs]
     return pl.pallas_call(
-        taken_kernel,
+        partial(taken_kernel, second, runs),
         out_shape=tuple(jax.ShapeDtypeStruct(shape, jnp.bfloat16) for shape in shapes),
         in_specs=[pl.BlockSpec(memory_space=pltpu.SMEM), far, far],
         out_specs=(near,) * len(shapes),
         scratch_shapes=[pltpu.SemaphoreType.DMA((5,))],
         compiler_params=pltpu.CompilerParams(vmem_limit_bytes=8 * MIB),
         name="taken",
-    )(jnp.stack([section, g]).astype(jnp.int32), in_weights, out_weights)
+    )(plan, in_weights, out_weights)
 
 
 def after(value, *others):
@@ -456,42 +466,41 @@
 def shards(stream, in_weights, out_weights, short_taps, medium_taps, plan):
     g, i, j = lax.axis_index("groups"), lax.axis_index("ctx"), lax.axis_index("chan")
     x, c, h = i // 2, i % 2, j % 2
-    first = plan[0]
     reach = medium_taps.shape[0]
     width = stream.shape[1]
     part = width // 2
     in_weights = in_weights.transpose(0, 2, 1, 3)
     near = (j // 2) == c
     send = Rounds()
-    bands = tap_bands(medium_taps)
 
     whole = lax.all_gather(stream, "chan", axis=1, tiled=True)
     send.now.append(whole)
-    out_a, kv_a, q_a = taken(first, g, in_weights, out_weights)
-    x_kv = send(kv_a, "ctx", CHIPS)
-    x_q = send(q_a, "ctx", CHIPS)
-    core_in = send(after(in_weights, q_a), "ctx", CORES)
-    out_b, kv_b, q_b = taken(after(1 - first, q_a), g, in_weights, out_weights)
+    out_a, all_a = taken(False, (((0, None), (1, None), (2, None)),), plan, in_weights, out_weights)
+    x_a = send(all_a, "ctx", CHIPS)
+    core_in = send(after(in_weights, all_a), "ctx", CORES)
+    runs = (((1, None), (2, None)), ((0, 0), (0, 1)))
+    out_b, kv_b, q_b = taken(True, runs, after(plan, all_a), in_weights, out_weights)
+    bands = tap_bands(after(medium_taps, all_a))
     send.now += [out_b, bands]
 
     send.turn()
-    y_kv = send(x_kv, "groups", GROUPS)
-    c_kv = lax.ppermute(x_kv, "ctx", CORES)
+    y_a = send(x_a, "groups", GROUPS)
     x_kv_b = send(kv_b, "ctx", CHIPS)
     shard_a = [out_a] + [send(out_a, PLANE, ALONG[k]) for k in (1, 2, 3)]
+    c_x = lax.ppermute(x_a, "ctx", CORES)
 
     send.turn()
     shard_a = jnp.stack(shard_a)
     cross_a = send(shard_a, PLANE, TO_OTHER_KEEPER)
     same_y = send(shard_a, EVERY, TO_KEEPER_OVER)
-    both = send(jnp.concatenate([x_q, y_kv]), "ctx", CORES)
+    c_y = send(y_a, "ctx", CORES)
     same_a = send(shard_a, PLANE, TO_KEEPER)
-    shard_b = [out_b] + [send(after(out_b, both, same_a), PLANE, ALONG[k]) for k in (1, 2, 3)]
+    shard_b = [out_b] + [send(after(out_b, c_y, same_a), PLANE, ALONG[k]) for k in (1, 2, 3)]
 
     send.turn()
     shard_b = jnp.stack(shard_b)
     cross_y = send(cross_a, EVERY, OTHER_KEEPERS_OVER)
-    weights_in = [[x_kv, y_kv, x_q, both, c_kv]]
+    weights_in = [[x_a, y_a, c_x, c_y]]
     weights_out = [[shard_a, same_a, same_y, cross_a, cross_y]]
 
     own_hidden = lax.dynamic_slice_in_dim(whole, (2 * c + h) * width, width, 1)
@@ -501,21 +510,15 @@
 
     for step in range(STEPS):
         count = 1 if step == 0 else 2
-        section = plan[step]
-        second = (section != first).astype(jnp.int32)
-        section = section.reshape(1)
-        scalars = [second, g, (x == c).astype(jnp.int32), (c == h).astype(jnp.int32)]
-        scalars += [i, i ^ 1, i ^ 2, i ^ 3]
-        meta = jnp.stack([jnp.asarray(s, jnp.int32) for s in scalars])
         if step == 0:
-            query, mixed = project_in("whole", meta, section, [whole], [], *inputs, weights_in)
+            query, mixed = project_in("whole", step, plan, [whole], [], *inputs, weights_in)
         else:
-            part_sums = project_in("first", meta, section, near_pieces, [], *inputs, weights_in)
-            query, mixed = project_in("last", meta, section, far_pieces, part_sums, *inputs, weights_in)
+            part_sums = project_in("first", step, plan, near_pieces, [], *inputs, weights_in)
+            query, mixed = project_in("last", step, plan, far_pieces, part_sums, *inputs, weights_in)
         halo = lax.ppermute(mixed[-reach:], "ctx", HALO)
         if step == 0:
             c_kv_b = lax.ppermute(after(x_kv_b, halo), "ctx", CORES)
-        gated = filter_and_gate(section, halo, mixed, query, bands, short_taps)
+        gated = filter_and_gate(step, plan, halo, mixed, query, bands, short_taps)
         if step == 0:
             cross_b = send(after(shard_b, halo), PLANE, TO_OTHER_KEEPER)
         g_2, g_3, g_1 = (send.join(gated, "chan", around(k)) for k in (2, 3, 1))
@@ -526,7 +529,7 @@
         own_gated = jnp.stack([gated, g_1, g_2, g_3])
         core_gated = lax.ppermute(own_gated, "ctx", CORES)
         own_hidden, core_hidden = project_out(
-            meta, own_gated, core_gated, own_hidden, core_hidden, weights_out[:count]
+            step, plan, own_gated, core_gated, own_hidden, core_hidden, weights_out[:count]
         )
         swapped = lax.ppermute(core_hidden, "ctx", CORES)
         if step == STEPS - 1:

time: 384 us -> 364 us (0.948)
  waiting for transfers between devices: 163 us -> 183 us
  Pallas kernels: 70.9 us -> 53.6 us
  local copies, waits for them, and re-layouts: 37.4 us -> 23.5 us
  between operations: 18.5 us -> 14 us
  other arithmetic: 9.63 us -> 5.43 us
    ppermute x41 -> x40, waiting for transfers between devices: 150 us -> 171 us  [join(): self.now.append(lax.ppermute(value, axes, pairs))]
    pallas_call x17, Pallas kernels: 70.9 us -> 53.6 us  [the longest x7 29.3 us: project_in(): pl.pallas_call(partial(in_kernel, mode, step, sections), out_shape=out, i...]
    unnamed x105 -> x63, local copies, waits for them, and re-layouts: 29.2 us -> 17 us
    ppermute x41 -> x40, starting transfers between devices: 71.7 us -> 66.6 us  [join(): self.now.append(lax.ppermute(value, axes, pairs))]
  transfers between devices with their start and end apart: 57 -> 56, of which waited for: 28 -> 33; matrix products, arithmetic and copies ran while one was open for 4% -> 3% of each run, Pallas kernels for 11% -> 8%
where the time goes in v2:
time: 364 us; the launch traced here: 363 us
  waiting for transfers between devices  183 us (50%)
  starting transfers between devices  83.6 us (23%)
  Pallas kernels  53.6 us (15%)
  local copies, waits for them, and re-layouts  23.5 us (6%)
  between operations  14 us (4%)
  other arithmetic  5.43 us (1%)
    ppermute x40, waiting for transfers between devices, join(): self.now.append(lax.ppermute(value, axes, pairs))  171 us
    ppermute x40, starting transfers between devices, join(): self.now.append(lax.ppermute(value, axes, pairs))  66.6 us
    pallas_call x7, Pallas kernels, project_in(): pl.pallas_call(partial(in_kernel, mode, step, sections), out_shape=out, i...  29.3 us
    unnamed x63, local copies, waits for them, and re-layouts  17 us
    pallas_call x4, Pallas kernels, project_out(): pl.pallas_call(partial(out_kernel, step, sections), out_shape=(out, out),...  14.9 us
  transfers between devices with their start and end apart: 56, of which 33 were waited for; matrix products, arithmetic and copies ran while one was open for 3% of the time, Pallas kernels for 8%

profile of v2, /device:TPU:0, one launch (start us, length us, event | category | flops | bytes accessed | tf_op | source)
XLA Modules:
  0.0 363.3 jit_solution(10952480558414681036)
XLA Ops:
  6.5 1.6 copy-done.17
  8.8 2.0 taken.2
  12.5 2.6 collective-permute-start.1
  15.4 1.6 copy.7
  17.0 5.1 %reshape.11 = bf16[32,64,255]{2,1,0:T(8,128)(2,1)} reshape(bf16[32,16320]{1,0:T(8,128)(2,1)} %bitcast.43) | data formatting | bytes 2088960 | tf_op jit(solution)/shard_map/reshape | solution.py:294
  22.0 1.6 copy-done.18
  23.7 2.1 taken.3
  28.6 21.7 %collective-permute-done.1.refs_3_.refs_4_.refs_6_ = bf16[3,512,512]{2,1,0:T(8,128)(2,1)S(1)} collective-permute-done((bf16[3,512,512]{2,1,0:T(8,128)(2,1)}, bf16[3,512,512]{2,1,0:T(8,128)(2,1)S(1)}, u32[]{:S(2)}, u32[]{:S(2)}) %collective-permute-start.1) | collective-permute-done | bytes 1572896 | tf_op jit(solution)/shard_map/ppermute | solution.py:415
  50.3 1.8 all-gather.2.cloned.1.call-done.refs_0_
  56.3 3.2 collective-permute-start.6
  60.8 6.6 %collective-permute-done.7 = bf16[512,512]{1,0:T(8,128)(2,1)S(1)} collective-permute-done((bf16[512,512]{1,0:T(8,128)(2,1)}, bf16[512,512]{1,0:T(8,128)(2,1)S(1)}, u32[]{:S(2)}, u32[]{:S(2)}) %collective-permute-start.7) | collective-permute-done | bytes 524320 | tf_op jit(solution)/shard_map/ppermute | solution.py:415
  67.4 13.7 %collective-permute-done.6 = bf16[512,512]{1,0:T(8,128)(2,1)S(1)} collective-permute-done((bf16[512,512]{1,0:T(8,128)(2,1)}, bf16[512,512]{1,0:T(8,128)(2,1)S(1)}, u32[]{:S(2)}, u32[]{:S(2)}) %collective-permute-start.6) | collective-permute-done | bytes 524320 | tf_op jit(solution)/shard_map/ppermute | solution.py:415
  82.7 5.4 %collective-permute-done.2.refs_4_.refs_5_.refs_7_ = bf16[3,512,512]{2,1,0:T(8,128)(2,1)S(1)} collective-permute-done((bf16[3,512,512]{2,1,0:T(8,128)(2,1)S(1)}, bf16[3,512,512]{2,1,0:T(8,128)(2,1)S(1)}, u32[]{:S(2)}, u32[]{:S(2)}) %collective-permute-start.2) | collective-permute-done | bytes 1572896 | tf_op jit(solution)/shard_map/ppermute | solution.py:415
  89.0 5.4 %collective-permute-start.17 = (bf16[4,512,512]{2,1,0:T(8,128)(2,1)S(1)}, bf16[4,512,512]{2,1,0:T(8,128)(2,1)}, u32[]{:S(2)}, u32[]{:S(2)}) collective-permute-start(bf16[4,512,512]{2,1,0:T(8,128)(2,1)S(1)} %pad_maximum_fusion.refs_4_), channel_id=1, source_target_pairs={{0,8},{5,9},{2,10},{7,11},{8,4},{13,5},{10,6},{15,7},{16,24},{21,2... | collective-permute-start | bytes 6291464 | tf_op jit(solution)/shard_map/ppermute | solution.py:415
  94.4 3.4 collective-permute-start.16
  100.5 3.3 collective-permute-start.19
  105.2 5.6 %project_in_whole.1 = (bf16[192,512]{1,0:T(8,128)(2,1)S(1)}, bf16[192,512]{1,0:T(8,128)(2,1)S(1)}) custom-call(s32[4]{0:T(128)S(1)} %copy-done.24, bf16[192,4096]{1,0:T(8,128)(2,1)S(1)} %copy-done.19, bf16[2,3,1024,512]{3,2,1,0:T(8,128)(2,1)} %bitcast.in_ref.refs_1_.refs_2_.refs_4_, bf16[2,3,1024,512]{3,2,1,0:T(8,128)(2,1)} %collective-permute-done.refs_2_.refs_3_.refs_5_, ...), custom_call_target="tpu_custom_call" | custom-call | flops 2415919104 | bytes 12582912 | tf_op jit(solution)/shard_map/project_in_whole/pallas_call | solution.py:208
  110.9 5.6 %collective-permute-done.17.refs_7_ = bf16[4,512,512]{2,1,0:T(8,128)(2,1)} collective-permute-done((bf16[4,512,512]{2,1,0:T(8,128)(2,1)S(1)}, bf16[4,512,512]{2,1,0:T(8,128)(2,1)}, u32[]{:S(2)}, u32[]{:S(2)}) %collective-permute-start.17) | collective-permute-done | bytes 2097184 | tf_op jit(solution)/shard_map/ppermute | solution.py:415
  116.5 2.5 collective-permute-start.9
  119.0 3.3 collective-permute-done.16.refs_6_
  122.3 3.4 collective-permute-done.19
  125.7 1.6 pad_maximum_fusion.1.refs_9_
  127.3 4.6 %collective-permute-start.25 = (bf16[4,512,512]{2,1,0:T(8,128)(2,1)}, bf16[4,512,512]{2,1,0:T(8,128)(2,1)}, u32[]{:S(2)}, u32[]{:S(2)}) collective-permute-start(bf16[4,512,512]{2,1,0:T(8,128)(2,1)} %pad_maximum_fusion.1.refs_9_), channel_id=1, source_target_pairs={{0,8},{5,9},{2,10},{7,11},{8,4},{13,5},{10,6},{15,7},{16,24},{21,2... | collective-permute-start | bytes 6291464 | tf_op jit(solution)/shard_map/ppermute | solution.py:415
  131.9 2.1 collective-permute-start.21
  135.6 2.7 collective-permute-start.11
  138.3 1.9 collective-permute-start.10
  141.2 13.4 %collective-permute-done.11 = bf16[192,512]{1,0:T(8,128)(2,1)S(1)} collective-permute-done((bf16[192,512]{1,0:T(8,128)(2,1)S(1)}, bf16[192,512]{1,0:T(8,128)(2,1)S(1)}, u32[]{:S(2)}, u32[]{:S(2)}) %collective-permute-start.11) | collective-permute-done | bytes 196640 | tf_op jit(solution)/shard_map/ppermute | solution.py:415
  159.4 1.6 copy-done.3
  161.0 1.6 copy-done.8
  162.6 1.6 copy-done.11
  164.2 4.0 %project_out.4 = (bf16[192,1024]{1,0:T(8,128)(2,1)S(1)}, bf16[192,1024]{1,0:T(8,128)(2,1)S(1)}) custom-call(s32[4]{0:T(128)S(1)} %copy-done.24, bf16[4,192,512]{2,1,0:T(8,128)(2,1)} %pad_maximum_fusion.3.refs_0_, bf16[4,192,512]{2,1,0:T(8,128)(2,1)} %collective-permute-done.13.refs_1_, bf16[192,1024]{1,0:T(8,128)(2,1)S(1)} %get-tuple-element.98.refs_2_, ...), custom_call_target="tpu_custom_call" | custom-call | flops 1610612736 | bytes 4194304 | tf_op jit(solution)/shard_map/project_out/pallas_call | solution.py:347
  171.0 11.8 %collective-permute-done.26.refs_9_.refs_11_ = bf16[2,512,512]{2,1,0:T(8,128)(2,1)S(1)} collective-permute-done((bf16[2,512,512]{2,1,0:T(8,128)(2,1)}, bf16[2,512,512]{2,1,0:T(8,128)(2,1)S(1)}, u32[]{:S(2)}, u32[]{:S(2)}) %collective-permute-start.26) | collective-permute-done | bytes 1048608 | tf_op jit(solution)/shard_map/ppermute | solution.py:415
  183.7 4.8 %collective-permute-done.24.refs_1_ = bf16[192,1024]{1,0:T(8,128)(2,1)S(1)} collective-permute-done((bf16[192,1024]{1,0:T(8,128)(2,1)S(1)}, bf16[192,1024]{1,0:T(8,128)(2,1)S(1)}, u32[]{:S(2)}, u32[]{:S(2)}) %collective-permute-start.24) | collective-permute-done | bytes 393248 | tf_op jit(solution)/shard_map/ppermute | solution.py:415
  189.0 3.1 collective-permute-start.36
  192.2 2.0 collective-permute-start.35
  194.2 2.1 collective-permute-start.37
  197.5 3.9 %project_in_first.3 = (f32[3,192,512]{2,1,0:T(8,128)S(1)}, f32[192,128]{1,0:T(8,128)S(1)}) custom-call(s32[4]{0:T(128)S(1)} %copy-done.24, bf16[192,1024]{1,0:T(8,128)(2,1)S(1)} %get-tuple-element.68.refs_0_.refs_2_, bf16[192,1024]{1,0:T(8,128)(2,1)S(1)} %collective-permute-done.23.refs_1_, bf16[2,3,1024,512]{3,2,1,0:T(8,128)(2,1)} %bitcast.in_ref.refs_1_.refs_2_.refs_4_, ...), custom_call_target="tpu_custom_call" | custom-call | flops 1207959552 | bytes 6291456 | tf_op jit(solution)/shard_map/project_in_first/pallas_call | solution.py:208
  201.4 4.2 %project_in_last.3 = (bf16[192,512]{1,0:T(8,128)(2,1)S(1)}, bf16[192,512]{1,0:T(8,128)(2,1)S(1)}) custom-call(s32[4]{0:T(128)S(1)} %copy-done.24, bf16[192,1024]{1,0:T(8,128)(2,1)S(1)} %collective-permute-done.22.refs_0_, bf16[192,1024]{1,0:T(8,128)(2,1)S(1)} %collective-permute-done.24.refs_1_, f32[3,192,512]{2,1,0:T(8,128)S(1)} %get-tuple-element.77.refs_2_, ...), custom_call_target="tpu_custom_call" | custom-call | flops 1207959552 | bytes 6291456 | tf_op jit(solution)/shard_map/project_in_last/pallas_call | solution.py:208
  209.3 4.5 %collective-permute-start.33 = (bf16[192,512]{1,0:T(8,128)(2,1)S(1)}, bf16[192,512]{1,0:T(8,128)(2,1)S(1)}, u32[]{:S(2)}, u32[]{:S(2)}) collective-permute-start(bf16[192,512]{1,0:T(8,128)(2,1)S(1)} %filter_and_gate.5), channel_id=1, source_target_pairs={{0,3},{1,0},{2,1},{3,2},{4,7},{5,4},{6,5},{7,6},{8,11},{9,8},{10,9... | collective-permute-start | bytes 589832 | tf_op jit(solution)/shard_map/ppermute | solution.py:415
  213.8 5.3 %collective-permute-done.33 = bf16[192,512]{1,0:T(8,128)(2,1)S(1)} collective-permute-done((bf16[192,512]{1,0:T(8,128)(2,1)S(1)}, bf16[192,512]{1,0:T(8,128)(2,1)S(1)}, u32[]{:S(2)}, u32[]{:S(2)}) %collective-permute-start.33) | collective-permute-done | bytes 196640 | tf_op jit(solution)/shard_map/ppermute | solution.py:415
  219.1 11.2 %collective-permute-done.32 = bf16[192,512]{1,0:T(8,128)(2,1)S(1)} collective-permute-done((bf16[192,512]{1,0:T(8,128)(2,1)S(1)}, bf16[192,512]{1,0:T(8,128)(2,1)S(1)}, u32[]{:S(2)}, u32[]{:S(2)}) %collective-permute-start.32) | collective-permute-done | bytes 196640 | tf_op jit(solution)/shard_map/ppermute | solution.py:415
  231.5 6.3 %collective-permute-done.36.refs_11_ = bf16[4,512,512]{2,1,0:T(8,128)(2,1)S(1)} collective-permute-done((bf16[4,512,512]{2,1,0:T(8,128)(2,1)}, bf16[4,512,512]{2,1,0:T(8,128)(2,1)S(1)}, u32[]{:S(2)}, u32[]{:S(2)}) %collective-permute-start.36) | collective-permute-done | bytes 2097184 | tf_op jit(solution)/shard_map/ppermute | solution.py:415
  237.8 3.9 %project_out.5 = (bf16[192,1024]{1,0:T(8,128)(2,1)S(1)}, bf16[192,1024]{1,0:T(8,128)(2,1)S(1)}) custom-call(s32[4]{0:T(128)S(1)} %copy-done.24, bf16[4,192,512]{2,1,0:T(8,128)(2,1)S(1)} %pad_maximum_fusion.4.refs_0_, bf16[4,192,512]{2,1,0:T(8,128)(2,1)S(1)} %collective-permute-done.34.refs_1_, bf16[192,1024]{1,0:T(8,128)(2,1)S(1)} %get-tuple-element.68.refs_0_.refs_2_, ...), custom_call_target="tpu_custom_call" | custom-call | flops 1610612736 | bytes 4194304 | tf_op jit(solution)/shard_map/project_out/pallas_call | solution.py:347
  241.8 2.1 collective-permute-start.39
  245.9 3.9 %project_in_first.4 = (f32[3,192,512]{2,1,0:T(8,128)S(1)}, f32[192,128]{1,0:T(8,128)S(1)}) custom-call(s32[4]{0:T(128)S(1)} %copy-done.24, bf16[192,1024]{1,0:T(8,128)(2,1)S(1)} %get-tuple-element.83.refs_0_.refs_2_, bf16[192,1024]{1,0:T(8,128)(2,1)S(1)} %collective-permute-done.39.refs_1_, bf16[2,3,1024,512]{3,2,1,0:T(8,128)(2,1)} %bitcast.in_ref.refs_1_.refs_2_.refs_4_, ...), custom_call_target="tpu_custom_call" | custom-call | flops 1207959552 | bytes 6291456 | tf_op jit(solution)/shard_map/project_in_first/pallas_call | solution.py:208
  249.7 6.1 %collective-permute-done.38.refs_0_ = bf16[192,1024]{1,0:T(8,128)(2,1)S(1)} collective-permute-done((bf16[192,1024]{1,0:T(8,128)(2,1)S(1)}, bf16[192,1024]{1,0:T(8,128)(2,1)S(1)}, u32[]{:S(2)}, u32[]{:S(2)}) %collective-permute-start.38) | collective-permute-done | bytes 393248 | tf_op jit(solution)/shard_map/ppermute | solution.py:415
  255.8 7.6 %collective-permute-done.40.refs_1_ = bf16[192,1024]{1,0:T(8,128)(2,1)S(1)} collective-permute-done((bf16[192,1024]{1,0:T(8,128)(2,1)S(1)}, bf16[192,1024]{1,0:T(8,128)(2,1)S(1)}, u32[]{:S(2)}, u32[]{:S(2)}) %collective-permute-start.40) | collective-permute-done | bytes 393248 | tf_op jit(solution)/shard_map/ppermute | solution.py:415
  263.4 3.9 %project_in_last.4 = (bf16[192,512]{1,0:T(8,128)(2,1)S(1)}, bf16[192,512]{1,0:T(8,128)(2,1)S(1)}) custom-call(s32[4]{0:T(128)S(1)} %copy-done.24, bf16[192,1024]{1,0:T(8,128)(2,1)S(1)} %collective-permute-done.38.refs_0_, bf16[192,1024]{1,0:T(8,128)(2,1)S(1)} %collective-permute-done.40.refs_1_, f32[3,192,512]{2,1,0:T(8,128)S(1)} %get-tuple-element.85.refs_2_, ...), custom_call_target="tpu_custom_call" | custom-call | flops 1207959552 | bytes 6291456 | tf_op jit(solution)/shard_map/project_in_last/pallas_call | solution.py:208
  271.2 2.9 collective-permute-start.44
  274.3 1.9 collective-permute-start.42
  277.7 13.4 %collective-permute-done.43 = bf16[192,512]{1,0:T(8,128)(2,1)S(1)} collective-permute-done((bf16[192,512]{1,0:T(8,128)(2,1)S(1)}, bf16[192,512]{1,0:T(8,128)(2,1)S(1)}, u32[]{:S(2)}, u32[]{:S(2)}) %collective-permute-start.43) | collective-permute-done | bytes 196640 | tf_op jit(solution)/shard_map/ppermute | solution.py:415
  292.7 1.9 collective-permute-done.45.refs_1_
  294.6 3.0 project_out.6
  297.6 1.5 collective-permute-start.47
  301.8 3.9 %project_in_first.5 = (f32[3,192,512]{2,1,0:T(8,128)S(1)}, f32[192,128]{1,0:T(8,128)S(1)}) custom-call(s32[4]{0:T(128)S(1)} %copy-done.24, bf16[192,1024]{1,0:T(8,128)(2,1)S(1)} %get-tuple-element.89.refs_0_.refs_2_, bf16[192,1024]{1,0:T(8,128)(2,1)S(1)} %collective-permute-done.47.refs_1_, bf16[2,3,1024,512]{3,2,1,0:T(8,128)(2,1)} %bitcast.in_ref.refs_1_.refs_2_.refs_4_, ...), custom_call_target="tpu_custom_call" | custom-call | flops 1207959552 | bytes 6291456 | tf_op jit(solution)/shard_map/project_in_first/pallas_call | solution.py:208
  305.7 5.5 %collective-permute-done.46.refs_0_ = bf16[192,1024]{1,0:T(8,128)(2,1)S(1)} collective-permute-done((bf16[192,1024]{1,0:T(8,128)(2,1)S(1)}, bf16[192,1024]{1,0:T(8,128)(2,1)S(1)}, u32[]{:S(2)}, u32[]{:S(2)}) %collective-permute-start.46) | collective-permute-done | bytes 393248 | tf_op jit(solution)/shard_map/ppermute | solution.py:415
  311.1 7.6 %collective-permute-done.48.refs_1_ = bf16[192,1024]{1,0:T(8,128)(2,1)S(1)} collective-permute-done((bf16[192,1024]{1,0:T(8,128)(2,1)S(1)}, bf16[192,1024]{1,0:T(8,128)(2,1)S(1)}, u32[]{:S(2)}, u32[]{:S(2)}) %collective-permute-start.48) | collective-permute-done | bytes 393248 | tf_op jit(solution)/shard_map/ppermute | solution.py:415
  318.7 3.9 %project_in_last.5 = (bf16[192,512]{1,0:T(8,128)(2,1)S(1)}, bf16[192,512]{1,0:T(8,128)(2,1)S(1)}) custom-call(s32[4]{0:T(128)S(1)} %copy-done.24, bf16[192,1024]{1,0:T(8,128)(2,1)S(1)} %collective-permute-done.46.refs_0_, bf16[192,1024]{1,0:T(8,128)(2,1)S(1)} %collective-permute-done.48.refs_1_, f32[3,192,512]{2,1,0:T(8,128)S(1)} %get-tuple-element.91.refs_2_, ...), custom_call_target="tpu_custom_call" | custom-call | flops 1207959552 | bytes 6291456 | tf_op jit(solution)/shard_map/project_in_last/pallas_call | solution.py:208
  326.1 3.0 collective-permute-start.52
  329.2 1.9 collective-permute-start.50
  332.3 13.7 %collective-permute-done.51 = bf16[192,512]{1,0:T(8,128)(2,1)S(1)} collective-permute-done((bf16[192,512]{1,0:T(8,128)(2,1)S(1)}, bf16[192,512]{1,0:T(8,128)(2,1)S(1)}, u32[]{:S(2)}, u32[]{:S(2)}) %collective-permute-start.51) | collective-permute-done | bytes 196640 | tf_op jit(solution)/shard_map/ppermute | solution.py:415
  346.1 1.7 collective-permute-start.53
  347.8 1.9 collective-permute-done.53.refs_1_
  349.7 3.9 %project_out.7 = (bf16[192,1024]{1,0:T(8,128)(2,1)S(1)}, bf16[192,1024]{1,0:T(8,128)(2,1)S(1)}) custom-call(s32[4]{0:T(128)S(1)} %copy-done.24, bf16[4,192,512]{2,1,0:T(8,128)(2,1)S(1)} %pad_maximum_fusion.6.refs_0_, bf16[4,192,512]{2,1,0:T(8,128)(2,1)S(1)} %collective-permute-done.53.refs_1_, bf16[192,1024]{1,0:T(8,128)(2,1)S(1)} %get-tuple-element.89.refs_0_.refs_2_, ...), custom_call_target="tpu_custom_call" | custom-call | flops 1610612736 | bytes 4194304 | tf_op jit(solution)/shard_map/project_out/pallas_call | solution.py:347
  (149 shorter events, 54.4 us)
Async XLA Ops:
  6.5 45.6 %all-gather.2.cloned.1.call-start = ((), (), s32[]{:S(2)}) async-start(), calls=%async_computation | async-start | bytes 1966080 | tf_op jit(solution)/shard_map/all_gather | solution.py:476
  12.0 40.1 %collective-permute-start = (bf16[2,3,1024,512]{3,2,1,0:T(8,128)(2,1)}, bf16[2,3,1024,512]{3,2,1,0:T(8,128)(2,1)}, u32[]{:S(2)}, u32[]{:S(2)}) collective-permute-start(bf16[2,3,1024,512]{3,2,1,0:T(8,128)(2,1)} %bitcast.in_ref.refs_1_.refs_2_.refs_4_), channel_id=1, source_target_pairs={{0,4},{4,0},{8,12},{12,8},{1,5},{5,1},{9,13},{13,9},{2,6},{6,2},{1... | collective-permute-start | bytes 18874376 | tf_op jit(solution)/shard_map/ppermute | solution.py:415
  12.5 37.8 %collective-permute-start.1 = (bf16[3,512,512]{2,1,0:T(8,128)(2,1)}, bf16[3,512,512]{2,1,0:T(8,128)(2,1)S(1)}, u32[]{:S(2)}, u32[]{:S(2)}) collective-permute-start(bf16[3,512,512]{2,1,0:T(8,128)(2,1)} %copy-done.26), channel_id=1, source_target_pairs={{0,8},{4,12},{8,0},{12,4},{1,9},{5,13},{9,1},{13,5},{2,10},{6,14},... | collective-permute-start | bytes 4718600 | tf_op jit(solution)/shard_map/ppermute | solution.py:415
  52.1 36.0 %collective-permute-start.2 = (bf16[3,512,512]{2,1,0:T(8,128)(2,1)S(1)}, bf16[3,512,512]{2,1,0:T(8,128)(2,1)S(1)}, u32[]{:S(2)}, u32[]{:S(2)}) collective-permute-start(bf16[3,512,512]{2,1,0:T(8,128)(2,1)S(1)} %collective-permute-done.1.refs_3_.refs_4_.refs_6_), channel_id=1, source_target_pairs={{0,16},{16,0},{1,17},{17,1},{2,18},{18,2},{3,19},{19,3},{4,20},{20... | collective-permute-start | bytes 4718600 | tf_op jit(solution)/shard_map/ppermute | solution.py:415
  53.6 29.1 %collective-permute-start.4 = (bf16[2,512,512]{2,1,0:T(8,128)(2,1)}, bf16[2,512,512]{2,1,0:T(8,128)(2,1)S(1)}, u32[]{:S(2)}, u32[]{:S(2)}) collective-permute-start(bf16[2,512,512]{2,1,0:T(8,128)(2,1)} %copy-done.28), channel_id=1, source_target_pairs={{0,8},{4,12},{8,0},{12,4},{1,9},{5,13},{9,1},{13,5},{2,10},{6,14},... | collective-permute-start | bytes 3145736 | tf_op jit(solution)/shard_map/ppermute | solution.py:415
  55.1 12.4 %collective-permute-start.7 = (bf16[512,512]{1,0:T(8,128)(2,1)}, bf16[512,512]{1,0:T(8,128)(2,1)S(1)}, u32[]{:S(2)}, u32[]{:S(2)}) collective-permute-start(bf16[512,512]{1,0:T(8,128)(2,1)} %copy-done.22), channel_id=1, source_target_pairs={{1,0},{6,5},{3,2},{4,7},{9,8},{14,13},{11,10},{12,15},{17,16},{22,... | collective-permute-start | bytes 1572872 | tf_op jit(solution)/shard_map/ppermute | solution.py:415
  56.3 24.8 %collective-permute-start.6 = (bf16[512,512]{1,0:T(8,128)(2,1)}, bf16[512,512]{1,0:T(8,128)(2,1)S(1)}, u32[]{:S(2)}, u32[]{:S(2)}) collective-permute-start(bf16[512,512]{1,0:T(8,128)(2,1)} %copy-done.22), channel_id=1, source_target_pairs={{2,0},{7,5},{0,2},{5,7},{10,8},{15,13},{8,10},{13,15},{18,16},{23,... | collective-permute-start | bytes 1572872 | tf_op jit(solution)/shard_map/ppermute | solution.py:415
  59.5 21.6 %collective-permute-start.5 = (bf16[512,512]{1,0:T(8,128)(2,1)}, bf16[512,512]{1,0:T(8,128)(2,1)S(1)}, u32[]{:S(2)}, u32[]{:S(2)}) collective-permute-start(bf16[512,512]{1,0:T(8,128)(2,1)} %copy-done.22), channel_id=1, source_target_pairs={{3,0},{4,5},{1,2},{6,7},{11,8},{12,13},{9,10},{14,15},{19,16},{20,... | collective-permute-start | bytes 1572872 | tf_op jit(solution)/shard_map/ppermute | solution.py:415
  81.2 24.0 %copy-start.19 = (bf16[192,4096]{1,0:T(8,128)(2,1)S(1)}, bf16[192,4096]{1,0:T(8,128)(2,1)}, u32[]{:S(2)}) copy-start(bf16[192,4096]{1,0:T(8,128)(2,1)} %all-gather.2.cloned.1.call-done.refs_0_) | copy-start | bytes 4718596
  82.6 28.2 %copy-start.2 = (bf16[4,512,512]{2,1,0:T(8,128)(2,1)}, bf16[4,512,512]{2,1,0:T(8,128)(2,1)S(1)}, u32[]{:S(2)}) copy-start(bf16[4,512,512]{2,1,0:T(8,128)(2,1)S(1)} %pad_maximum_fusion.refs_4_) | copy-start | bytes 6291460
  82.7 21.2 %copy-start.5 = (bf16[2,512,512]{2,1,0:T(8,128)(2,1)}, bf16[2,512,512]{2,1,0:T(8,128)(2,1)S(1)}, u32[]{:S(2)}) copy-start(bf16[2,512,512]{2,1,0:T(8,128)(2,1)S(1)} %collective-permute-done.4.refs_8_.refs_10_) | copy-start | bytes 3145732
  88.1 9.8 %collective-permute-start.15 = (bf16[4,512,512]{2,1,0:T(8,128)(2,1)S(1)}, bf16[4,512,512]{2,1,0:T(8,128)(2,1)S(1)}, u32[]{:S(2)}, u32[]{:S(2)}) collective-permute-start(bf16[4,512,512]{2,1,0:T(8,128)(2,1)S(1)} %pad_maximum_fusion.refs_4_), channel_id=1, source_target_pairs={{5,1},{7,3},{8,12},{10,14},{21,17},{23,19},{24,28},{26,30}} | collective-permute-start | bytes 6291464 | tf_op jit(solution)/shard_map/ppermute | solution.py:415
  88.9 8.9 %collective-permute-start.8 = (bf16[3,512,512]{2,1,0:T(8,128)(2,1)S(1)}, bf16[3,512,512]{2,1,0:T(8,128)(2,1)S(1)}, u32[]{:S(2)}, u32[]{:S(2)}) collective-permute-start(bf16[3,512,512]{2,1,0:T(8,128)(2,1)S(1)} %collective-permute-done.2.refs_4_.refs_5_.refs_7_), channel_id=1, source_target_pairs={{0,4},{4,0},{8,12},{12,8},{1,5},{5,1},{9,13},{13,9},{2,6},{6,2},{1... | collective-permute-start | bytes 4718600 | tf_op jit(solution)/shard_map/ppermute | solution.py:415
  89.0 27.5 %collective-permute-start.17 = (bf16[4,512,512]{2,1,0:T(8,128)(2,1)S(1)}, bf16[4,512,512]{2,1,0:T(8,128)(2,1)}, u32[]{:S(2)}, u32[]{:S(2)}) collective-permute-start(bf16[4,512,512]{2,1,0:T(8,128)(2,1)S(1)} %pad_maximum_fusion.refs_4_), channel_id=1, source_target_pairs={{0,8},{5,9},{2,10},{7,11},{8,4},{13,5},{10,6},{15,7},{16,24},{21,2... | collective-permute-start | bytes 6291464 | tf_op jit(solution)/shard_map/ppermute | solution.py:415
  94.4 27.9 %collective-permute-start.16 = (bf16[4,512,512]{2,1,0:T(8,128)(2,1)S(1)}, bf16[4,512,512]{2,1,0:T(8,128)(2,1)S(1)}, u32[]{:S(2)}, u32[]{:S(2)}) collective-permute-start(bf16[4,512,512]{2,1,0:T(8,128)(2,1)S(1)} %pad_maximum_fusion.refs_4_), channel_id=1, source_target_pairs={{0,16},{16,0},{5,17},{21,1},{2,18},{18,2},{7,19},{23,3},{8,28},{24... | collective-permute-start | bytes 6291464 | tf_op jit(solution)/shard_map/ppermute | solution.py:415
  97.8 6.1 %collective-permute-start.3 = (bf16[3,512,512]{2,1,0:T(8,128)(2,1)S(1)}, bf16[3,512,512]{2,1,0:T(8,128)(2,1)S(1)}, u32[]{:S(2)}, u32[]{:S(2)}) collective-permute-start(bf16[3,512,512]{2,1,0:T(8,128)(2,1)S(1)} %collective-permute-done.1.refs_3_.refs_4_.refs_6_), channel_id=1, source_target_pairs={{0,4},{4,0},{8,12},{12,8},{1,5},{5,1},{9,13},{13,9},{2,6},{6,2},{1... | collective-permute-start | bytes 4718600 | tf_op jit(solution)/shard_map/ppermute | solution.py:490
  99.2 23.1 %collective-permute-start.20 = (bf16[512,512]{1,0:T(8,128)(2,1)S(1)}, bf16[512,512]{1,0:T(8,128)(2,1)S(1)}, u32[]{:S(2)}, u32[]{:S(2)}) collective-permute-start(bf16[512,512]{1,0:T(8,128)(2,1)S(1)} %copy-done.21), channel_id=1, source_target_pairs={{1,0},{6,5},{3,2},{4,7},{9,8},{14,13},{11,10},{12,15},{17,16},{22,... | collective-permute-start | bytes 1572872 | tf_op jit(solution)/shard_map/ppermute | solution.py:415
  100.5 25.2 %collective-permute-start.19 = (bf16[512,512]{1,0:T(8,128)(2,1)S(1)}, bf16[512,512]{1,0:T(8,128)(2,1)S(1)}, u32[]{:S(2)}, u32[]{:S(2)}) collective-permute-start(bf16[512,512]{1,0:T(8,128)(2,1)S(1)} %copy-done.21), channel_id=1, source_target_pairs={{2,0},{7,5},{0,2},{5,7},{10,8},{15,13},{8,10},{13,15},{18,16},{23,... | collective-permute-start | bytes 1572872 | tf_op jit(solution)/shard_map/ppermute | solution.py:415
  103.9 21.8 %collective-permute-start.18 = (bf16[512,512]{1,0:T(8,128)(2,1)S(1)}, bf16[512,512]{1,0:T(8,128)(2,1)S(1)}, u32[]{:S(2)}, u32[]{:S(2)}) collective-permute-start(bf16[512,512]{1,0:T(8,128)(2,1)S(1)} %copy-done.21), channel_id=1, source_target_pairs={{3,0},{4,5},{1,2},{6,7},{11,8},{12,13},{9,10},{14,15},{19,16},{20,... | collective-permute-start | bytes 1572872 | tf_op jit(solution)/shard_map/ppermute | solution.py:415
  116.5 10.8 %collective-permute-start.9 = (bf16[128,512]{1,0:T(8,128)(2,1)S(1)}, bf16[128,512]{1,0:T(8,128)(2,1)S(1)}, u32[]{:S(2)}, u32[]{:S(2)}) collective-permute-start(bf16[128,512]{1,0:T(8,128)(2,1)S(1)} %slice.20), channel_id=1, source_target_pairs={{0,4},{4,8},{8,12},{1,5},{5,9},{9,13},{2,6},{6,10},{10,14},{3,7},{... | collective-permute-start | bytes 393224 | tf_op jit(solution)/shard_map/ppermute | solution.py:518
  127.3 30.1 %collective-permute-start.25 = (bf16[4,512,512]{2,1,0:T(8,128)(2,1)}, bf16[4,512,512]{2,1,0:T(8,128)(2,1)}, u32[]{:S(2)}, u32[]{:S(2)}) collective-permute-start(bf16[4,512,512]{2,1,0:T(8,128)(2,1)} %pad_maximum_fusion.1.refs_9_), channel_id=1, source_target_pairs={{0,8},{5,9},{2,10},{7,11},{8,4},{13,5},{10,6},{15,7},{16,24},{21,2... | collective-permute-start | bytes 6291464 | tf_op jit(solution)/shard_map/ppermute | solution.py:415
  131.9 25.5 %collective-permute-start.21 = (bf16[4,512,512]{2,1,0:T(8,128)(2,1)}, bf16[4,512,512]{2,1,0:T(8,128)(2,1)}, u32[]{:S(2)}, u32[]{:S(2)}) collective-permute-start(bf16[4,512,512]{2,1,0:T(8,128)(2,1)} %collective-permute-done.17.refs_7_), channel_id=1, source_target_pairs={{8,24},{24,8},{9,25},{25,9},{10,26},{26,10},{11,27},{27,11},{4,20}... | collective-permute-start | bytes 6291464 | tf_op jit(solution)/shard_map/ppermute | solution.py:415
  135.5 5.7 %collective-permute-start.12 = (bf16[192,512]{1,0:T(8,128)(2,1)S(1)}, bf16[192,512]{1,0:T(8,128)(2,1)S(1)}, u32[]{:S(2)}, u32[]{:S(2)}) collective-permute-start(bf16[192,512]{1,0:T(8,128)(2,1)S(1)} %filter_and_gate.4), channel_id=1, source_target_pairs={{0,3},{1,0},{2,1},{3,2},{4,7},{5,4},{6,5},{7,6},{8,11},{9,8},{10,9... | collective-permute-start | bytes 589832 | tf_op jit(solution)/shard_map/ppermute | solution.py:415
  135.6 19.1 %collective-permute-start.11 = (bf16[192,512]{1,0:T(8,128)(2,1)S(1)}, bf16[192,512]{1,0:T(8,128)(2,1)S(1)}, u32[]{:S(2)}, u32[]{:S(2)}) collective-permute-start(bf16[192,512]{1,0:T(8,128)(2,1)S(1)} %filter_and_gate.4), channel_id=1, source_target_pairs={{0,2},{1,3},{2,0},{3,1},{4,6},{5,7},{6,4},{7,5},{8,10},{9,11},{10,... | collective-permute-start | bytes 589832 | tf_op jit(solution)/shard_map/ppermute | solution.py:415
  138.3 16.3 %collective-permute-start.10 = (bf16[192,512]{1,0:T(8,128)(2,1)S(1)}, bf16[192,512]{1,0:T(8,128)(2,1)S(1)}, u32[]{:S(2)}, u32[]{:S(2)}) collective-permute-start(bf16[192,512]{1,0:T(8,128)(2,1)S(1)} %filter_and_gate.4), channel_id=1, source_target_pairs={{0,1},{1,2},{2,3},{3,0},{4,5},{5,6},{6,7},{7,4},{8,9},{9,10},{10,1... | collective-permute-start | bytes 589832 | tf_op jit(solution)/shard_map/ppermute | solution.py:415
  155.7 3.8 %collective-permute-start.13 = (bf16[4,192,512]{2,1,0:T(8,128)(2,1)}, bf16[4,192,512]{2,1,0:T(8,128)(2,1)}, u32[]{:S(2)}, u32[]{:S(2)}) collective-permute-start(bf16[4,192,512]{2,1,0:T(8,128)(2,1)} %pad_maximum_fusion.3.refs_0_), channel_id=1, source_target_pairs={{0,4},{4,0},{8,12},{12,8},{1,5},{5,1},{9,13},{13,9},{2,6},{6,2},{1... | collective-permute-start | bytes 2359304 | tf_op jit(solution)/shard_map/ppermute | solution.py:530
  156.9 2.6 collective-permute-start.14
  157.4 25.4 %collective-permute-start.26 = (bf16[2,512,512]{2,1,0:T(8,128)(2,1)}, bf16[2,512,512]{2,1,0:T(8,128)(2,1)S(1)}, u32[]{:S(2)}, u32[]{:S(2)}) collective-permute-start(bf16[2,512,512]{2,1,0:T(8,128)(2,1)} %copy-done.5), channel_id=1, source_target_pairs={{0,16},{16,0},{1,17},{17,1},{2,18},{18,2},{3,19},{19,3},{4,20},{20... | collective-permute-start | bytes 3145736 | tf_op jit(solution)/shard_map/ppermute | solution.py:415
  158.4 25.1 %collective-permute-start.27 = (bf16[2,512,512]{2,1,0:T(8,128)(2,1)}, bf16[2,512,512]{2,1,0:T(8,128)(2,1)S(1)}, u32[]{:S(2)}, u32[]{:S(2)}) collective-permute-start(bf16[2,512,512]{2,1,0:T(8,128)(2,1)} %copy-done.27), channel_id=1, source_target_pairs={{0,8},{4,12},{8,0},{12,4},{1,9},{5,13},{9,1},{13,5},{2,10},{6,14},... | collective-permute-start | bytes 3145736 | tf_op jit(solution)/shard_map/ppermute | solution.py:415
  168.3 2.1 collective-permute-start.23
  169.0 19.5 %copy-start.6 = (bf16[2,512,512]{2,1,0:T(8,128)(2,1)S(1)}, bf16[2,512,512]{2,1,0:T(8,128)(2,1)}, u32[]{:S(2)}) copy-start(bf16[2,512,512]{2,1,0:T(8,128)(2,1)} %copy-done.5) | copy-start | bytes 3145732
  169.0 14.7 %collective-permute-start.22 = (bf16[192,1024]{1,0:T(8,128)(2,1)S(1)}, bf16[192,1024]{1,0:T(8,128)(2,1)S(1)}, u32[]{:S(2)}, u32[]{:S(2)}) collective-permute-start(bf16[192,1024]{1,0:T(8,128)(2,1)S(1)} %get-tuple-element.68.refs_0_.refs_2_), channel_id=1, source_target_pairs={{0,1},{1,0},{2,3},{3,2},{4,5},{5,4},{6,7},{7,6},{8,9},{9,8},{10,11... | collective-permute-start | bytes 1179656 | tf_op jit(solution)/shard_map/ppermute | solution.py:415
  170.3 18.2 %collective-permute-start.24 = (bf16[192,1024]{1,0:T(8,128)(2,1)S(1)}, bf16[192,1024]{1,0:T(8,128)(2,1)S(1)}, u32[]{:S(2)}, u32[]{:S(2)}) collective-permute-start(bf16[192,1024]{1,0:T(8,128)(2,1)S(1)} %collective-permute-done.23.refs_1_), channel_id=1, source_target_pairs={{0,1},{1,0},{2,3},{3,2},{4,5},{5,4},{6,7},{7,6},{8,9},{9,8},{10,11... | collective-permute-start | bytes 1179656 | tf_op jit(solution)/shard_map/ppermute | solution.py:415
  188.5 7.7 %collective-permute-start.28 = (bf16[4,512,512]{2,1,0:T(8,128)(2,1)S(1)}, bf16[4,512,512]{2,1,0:T(8,128)(2,1)S(1)}, u32[]{:S(2)}, u32[]{:S(2)}) collective-permute-start(bf16[4,512,512]{2,1,0:T(8,128)(2,1)S(1)} %pad_maximum_fusion.2), channel_id=1, source_target_pairs={{0,4},{4,0},{8,12},{12,8},{1,5},{5,1},{9,13},{13,9},{2,6},{6,2},{1... | collective-permute-start | bytes 6291464 | tf_op jit(solution)/shard_map/ppermute | solution.py:415
  188.5 7.7 %collective-permute-start.29 = (bf16[2,512,512]{2,1,0:T(8,128)(2,1)S(1)}, bf16[2,512,512]{2,1,0:T(8,128)(2,1)S(1)}, u32[]{:S(2)}, u32[]{:S(2)}) collective-permute-start(bf16[2,512,512]{2,1,0:T(8,128)(2,1)S(1)} %copy-done.6), channel_id=1, source_target_pairs={{0,4},{4,0},{8,12},{12,8},{1,5},{5,1},{9,13},{13,9},{2,6},{6,2},{1... | collective-permute-start | bytes 3145736 | tf_op jit(solution)/shard_map/ppermute | solution.py:520
  189.0 48.7 %collective-permute-start.36 = (bf16[4,512,512]{2,1,0:T(8,128)(2,1)}, bf16[4,512,512]{2,1,0:T(8,128)(2,1)S(1)}, u32[]{:S(2)}, u32[]{:S(2)}) collective-permute-start(bf16[4,512,512]{2,1,0:T(8,128)(2,1)} %pad_maximum_fusion.1.refs_9_), channel_id=1, source_target_pairs={{0,16},{16,0},{5,17},{21,1},{2,18},{18,2},{7,19},{23,3},{8,28},{24... | collective-permute-start | bytes 6291464 | tf_op jit(solution)/shard_map/ppermute | solution.py:415
  192.2 45.6 %collective-permute-start.35 = (bf16[4,512,512]{2,1,0:T(8,128)(2,1)}, bf16[4,512,512]{2,1,0:T(8,128)(2,1)}, u32[]{:S(2)}, u32[]{:S(2)}) collective-permute-start(bf16[4,512,512]{2,1,0:T(8,128)(2,1)} %pad_maximum_fusion.1.refs_9_), channel_id=1, source_target_pairs={{5,1},{7,3},{8,12},{10,14},{21,17},{23,19},{24,28},{26,30}} | collective-permute-start | bytes 6291464 | tf_op jit(solution)/shard_map/ppermute | solution.py:415
  194.2 43.6 %collective-permute-start.37 = (bf16[4,512,512]{2,1,0:T(8,128)(2,1)}, bf16[4,512,512]{2,1,0:T(8,128)(2,1)}, u32[]{:S(2)}, u32[]{:S(2)}) collective-permute-start(bf16[4,512,512]{2,1,0:T(8,128)(2,1)} %collective-permute-done.25.refs_12_), channel_id=1, source_target_pairs={{8,24},{24,8},{9,25},{25,9},{10,26},{26,10},{11,27},{27,11},{4,20}... | collective-permute-start | bytes 6291464 | tf_op jit(solution)/shard_map/ppermute | solution.py:415
  201.4 36.4 %copy-start.9 = (bf16[4,512,512]{2,1,0:T(8,128)(2,1)S(1)}, bf16[4,512,512]{2,1,0:T(8,128)(2,1)}, u32[]{:S(2)}) copy-start(bf16[4,512,512]{2,1,0:T(8,128)(2,1)} %copy-done.7) | copy-start | bytes 6291460
  201.4 36.4 %copy-start.12 = (bf16[4,512,512]{2,1,0:T(8,128)(2,1)S(1)}, bf16[4,512,512]{2,1,0:T(8,128)(2,1)}, u32[]{:S(2)}) copy-start(bf16[4,512,512]{2,1,0:T(8,128)(2,1)} %copy-done.10) | copy-start | bytes 6291460
  205.7 32.1 %copy-start.4 = (bf16[4,512,512]{2,1,0:T(8,128)(2,1)S(1)}, bf16[4,512,512]{2,1,0:T(8,128)(2,1)}, u32[]{:S(2)}) copy-start(bf16[4,512,512]{2,1,0:T(8,128)(2,1)} %copy-done.2) | copy-start | bytes 6291460
  205.7 2.4 collective-permute-start.30
  209.3 9.9 %collective-permute-start.33 = (bf16[192,512]{1,0:T(8,128)(2,1)S(1)}, bf16[192,512]{1,0:T(8,128)(2,1)S(1)}, u32[]{:S(2)}, u32[]{:S(2)}) collective-permute-start(bf16[192,512]{1,0:T(8,128)(2,1)S(1)} %filter_and_gate.5), channel_id=1, source_target_pairs={{0,3},{1,0},{2,1},{3,2},{4,7},{5,4},{6,5},{7,6},{8,11},{9,8},{10,9... | collective-permute-start | bytes 589832 | tf_op jit(solution)/shard_map/ppermute | solution.py:415
  213.8 16.5 %collective-permute-start.32 = (bf16[192,512]{1,0:T(8,128)(2,1)S(1)}, bf16[192,512]{1,0:T(8,128)(2,1)S(1)}, u32[]{:S(2)}, u32[]{:S(2)}) collective-permute-start(bf16[192,512]{1,0:T(8,128)(2,1)S(1)} %filter_and_gate.5), channel_id=1, source_target_pairs={{0,2},{1,3},{2,0},{3,1},{4,6},{5,7},{6,4},{7,5},{8,10},{9,11},{10,... | collective-permute-start | bytes 589832 | tf_op jit(solution)/shard_map/ppermute | solution.py:415
  219.1 11.2 %collective-permute-start.31 = (bf16[192,512]{1,0:T(8,128)(2,1)S(1)}, bf16[192,512]{1,0:T(8,128)(2,1)S(1)}, u32[]{:S(2)}, u32[]{:S(2)}) collective-permute-start(bf16[192,512]{1,0:T(8,128)(2,1)S(1)} %filter_and_gate.5), channel_id=1, source_target_pairs={{0,1},{1,2},{2,3},{3,0},{4,5},{5,6},{6,7},{7,4},{8,9},{9,10},{10,1... | collective-permute-start | bytes 589832 | tf_op jit(solution)/shard_map/ppermute | solution.py:415
  230.4 7.4 %collective-permute-start.34 = (bf16[4,192,512]{2,1,0:T(8,128)(2,1)S(1)}, bf16[4,192,512]{2,1,0:T(8,128)(2,1)S(1)}, u32[]{:S(2)}, u32[]{:S(2)}) collective-permute-start(bf16[4,192,512]{2,1,0:T(8,128)(2,1)S(1)} %pad_maximum_fusion.4.refs_0_), channel_id=1, source_target_pairs={{0,4},{4,0},{8,12},{12,8},{1,5},{5,1},{9,13},{13,9},{2,6},{6,2},{1... | collective-permute-start | bytes 2359304 | tf_op jit(solution)/shard_map/ppermute | solution.py:530
  241.8 3.4 collective-permute-start.39
  243.8 12.0 %collective-permute-start.38 = (bf16[192,1024]{1,0:T(8,128)(2,1)S(1)}, bf16[192,1024]{1,0:T(8,128)(2,1)S(1)}, u32[]{:S(2)}, u32[]{:S(2)}) collective-permute-start(bf16[192,1024]{1,0:T(8,128)(2,1)S(1)} %get-tuple-element.83.refs_0_.refs_2_), channel_id=1, source_target_pairs={{0,1},{1,0},{2,3},{3,2},{4,5},{5,4},{6,7},{7,6},{8,9},{9,8},{10,11... | collective-permute-start | bytes 1179656 | tf_op jit(solution)/shard_map/ppermute | solution.py:415
  245.2 18.2 %collective-permute-start.40 = (bf16[192,1024]{1,0:T(8,128)(2,1)S(1)}, bf16[192,1024]{1,0:T(8,128)(2,1)S(1)}, u32[]{:S(2)}, u32[]{:S(2)}) collective-permute-start(bf16[192,1024]{1,0:T(8,128)(2,1)S(1)} %collective-permute-done.39.refs_1_), channel_id=1, source_target_pairs={{0,1},{1,0},{2,3},{3,2},{4,5},{5,4},{6,7},{7,6},{8,9},{9,8},{10,11... | collective-permute-start | bytes 1179656 | tf_op jit(solution)/shard_map/ppermute | solution.py:415
  267.3 27.3 %copy-start.16 = (bf16[4,512,512]{2,1,0:T(8,128)(2,1)S(1)}, bf16[4,512,512]{2,1,0:T(8,128)(2,1)}, u32[]{:S(2)}) copy-start(bf16[4,512,512]{2,1,0:T(8,128)(2,1)} %copy-done.15) | copy-start | bytes 6291460
  267.3 2.4 collective-permute-start.41
  271.2 6.5 %collective-permute-start.44 = (bf16[192,512]{1,0:T(8,128)(2,1)S(1)}, bf16[192,512]{1,0:T(8,128)(2,1)S(1)}, u32[]{:S(2)}, u32[]{:S(2)}) collective-permute-start(bf16[192,512]{1,0:T(8,128)(2,1)S(1)} %filter_and_gate.6), channel_id=1, source_target_pairs={{0,3},{1,0},{2,1},{3,2},{4,7},{5,4},{6,5},{7,6},{8,11},{9,8},{10,9... | collective-permute-start | bytes 589832 | tf_op jit(solution)/shard_map/ppermute | solution.py:415
  274.1 17.0 %collective-permute-start.43 = (bf16[192,512]{1,0:T(8,128)(2,1)S(1)}, bf16[192,512]{1,0:T(8,128)(2,1)S(1)}, u32[]{:S(2)}, u32[]{:S(2)}) collective-permute-start(bf16[192,512]{1,0:T(8,128)(2,1)S(1)} %filter_and_gate.6), channel_id=1, source_target_pairs={{0,2},{1,3},{2,0},{3,1},{4,6},{5,7},{6,4},{7,5},{8,10},{9,11},{10,... | collective-permute-start | bytes 589832 | tf_op jit(solution)/shard_map/ppermute | solution.py:415
  274.3 16.9 %collective-permute-start.42 = (bf16[192,512]{1,0:T(8,128)(2,1)S(1)}, bf16[192,512]{1,0:T(8,128)(2,1)S(1)}, u32[]{:S(2)}, u32[]{:S(2)}) collective-permute-start(bf16[192,512]{1,0:T(8,128)(2,1)S(1)} %filter_and_gate.6), channel_id=1, source_target_pairs={{0,1},{1,2},{2,3},{3,0},{4,5},{5,6},{6,7},{7,4},{8,9},{9,10},{10,1... | collective-permute-start | bytes 589832 | tf_op jit(solution)/shard_map/ppermute | solution.py:415
  291.3 3.3 collective-permute-start.45
  297.6 2.9 collective-permute-start.47
  299.2 12.0 %collective-permute-start.46 = (bf16[192,1024]{1,0:T(8,128)(2,1)S(1)}, bf16[192,1024]{1,0:T(8,128)(2,1)S(1)}, u32[]{:S(2)}, u32[]{:S(2)}) collective-permute-start(bf16[192,1024]{1,0:T(8,128)(2,1)S(1)} %get-tuple-element.89.refs_0_.refs_2_), channel_id=1, source_target_pairs={{0,1},{1,0},{2,3},{3,2},{4,5},{5,4},{6,7},{7,6},{8,9},{9,8},{10,11... | collective-permute-start | bytes 1179656 | tf_op jit(solution)/shard_map/ppermute | solution.py:415
  300.5 18.2 %collective-permute-start.48 = (bf16[192,1024]{1,0:T(8,128)(2,1)S(1)}, bf16[192,1024]{1,0:T(8,128)(2,1)S(1)}, u32[]{:S(2)}, u32[]{:S(2)}) collective-permute-start(bf16[192,1024]{1,0:T(8,128)(2,1)S(1)} %collective-permute-done.47.refs_1_), channel_id=1, source_target_pairs={{0,1},{1,0},{2,3},{3,2},{4,5},{5,4},{6,7},{7,6},{8,9},{9,8},{10,11... | collective-permute-start | bytes 1179656 | tf_op jit(solution)/shard_map/ppermute | solution.py:415
  322.6 2.3 collective-permute-start.49
  326.1 6.3 %collective-permute-start.52 = (bf16[192,512]{1,0:T(8,128)(2,1)S(1)}, bf16[192,512]{1,0:T(8,128)(2,1)S(1)}, u32[]{:S(2)}, u32[]{:S(2)}) collective-permute-start(bf16[192,512]{1,0:T(8,128)(2,1)S(1)} %filter_and_gate.7), channel_id=1, source_target_pairs={{0,3},{1,0},{2,1},{3,2},{4,7},{5,4},{6,5},{7,6},{8,11},{9,8},{10,9... | collective-permute-start | bytes 589832 | tf_op jit(solution)/shard_map/ppermute | solution.py:415
  329.0 17.0 %collective-permute-start.51 = (bf16[192,512]{1,0:T(8,128)(2,1)S(1)}, bf16[192,512]{1,0:T(8,128)(2,1)S(1)}, u32[]{:S(2)}, u32[]{:S(2)}) collective-permute-start(bf16[192,512]{1,0:T(8,128)(2,1)S(1)} %filter_and_gate.7), channel_id=1, source_target_pairs={{0,2},{1,3},{2,0},{3,1},{4,6},{5,7},{6,4},{7,5},{8,10},{9,11},{10,... | collective-permute-start | bytes 589832 | tf_op jit(solution)/shard_map/ppermute | solution.py:415
  329.2 16.8 %collective-permute-start.50 = (bf16[192,512]{1,0:T(8,128)(2,1)S(1)}, bf16[192,512]{1,0:T(8,128)(2,1)S(1)}, u32[]{:S(2)}, u32[]{:S(2)}) collective-permute-start(bf16[192,512]{1,0:T(8,128)(2,1)S(1)} %filter_and_gate.7), channel_id=1, source_target_pairs={{0,1},{1,2},{2,3},{3,0},{4,5},{5,6},{6,7},{7,4},{8,9},{9,10},{10,1... | collective-permute-start | bytes 589832 | tf_op jit(solution)/shard_map/ppermute | solution.py:415
  346.1 3.6 collective-permute-start.53
  353.6 2.1 collective-permute-start.54
  (23 other events, 103.6 us)
Sparse Core Ops, SparseCore 0:
  12.6 39.4 all-gather.1

commit v3 on v2

--- a/solution.py
+++ b/solution.py
@@ -391,7 +391,7 @@
         in_specs=[pl.BlockSpec(memory_space=pltpu.SMEM), far, far],
         out_specs=(near,) * len(shapes),
         scratch_shapes=[pltpu.SemaphoreType.DMA((5,))],
-        compiler_params=pltpu.CompilerParams(vmem_limit_bytes=8 * MIB),
+        compiler_params=pltpu.CompilerParams(vmem_limit_bytes=(8 if second else 56) * MIB),
         name="taken",
     )(plan, in_weights, out_weights)
 
@@ -499,7 +499,7 @@
 
     send.turn()
     shard_b = jnp.stack(shard_b)
-    cross_y = send(cross_a, EVERY, OTHER_KEEPERS_OVER)
+    cross_y = send.join(cross_a, EVERY, OTHER_KEEPERS_OVER)
     weights_in = [[x_a, y_a, c_x, c_y]]
     weights_out = [[shard_a, same_a, same_y, cross_a, cross_y]]
 
@@ -524,8 +524,9 @@
         g_2, g_3, g_1 = (send.join(gated, "chan", around(k)) for k in (2, 3, 1))
         if step == 0:
             send.turn()
-            y_kv_b = send(x_kv_b, "groups", GROUPS)
+            y_kv_b = send.join(after(x_kv_b, cross_y), "groups", GROUPS)
             x_q_b = send(q_b, "ctx", CHIPS)
+            same_b_y = lax.ppermute(after(shard_b, *send.before), EVERY, TO_KEEPER_OVER)
         own_gated = jnp.stack([gated, g_1, g_2, g_3])
         core_gated = lax.ppermute(own_gated, "ctx", CORES)
         own_hidden, core_hidden = project_out(
@@ -535,11 +536,11 @@
         if step == STEPS - 1:
             return jnp.where((j // 2) == c, own_hidden, swapped)
         near_pieces = [own_hidden, swapped]
-        far_pieces = [send.join(piece, "chan", BESIDE) for piece in near_pieces]
+        beside_core = send.join(core_hidden, "chan", BESIDE)
+        far_pieces = [send.join(own_hidden, "chan", BESIDE), lax.ppermute(beside_core, "ctx", CORES)]
         if step == 0:
             send.turn()
             both_b = send(jnp.concatenate([x_q_b, y_kv_b]), "ctx", CORES)
-            same_b_y = send(shard_b, EVERY, TO_KEEPER_OVER)
             same_b = send(shard_b, PLANE, TO_KEEPER)
             cross_b_y = send(cross_b, EVERY, OTHER_KEEPERS_OVER)
             weights_in.append([x_kv_b, y_kv_b, x_q_b, both_b, c_kv_b])

time: 364 us -> 362 us (level)
  waiting for transfers between devices: 183 us -> 163 us
  starting transfers between devices: 83.6 us -> 95 us
    ppermute x40 -> x39, waiting for transfers between devices: 171 us -> 149 us  [join(): self.now.append(lax.ppermute(value, axes, pairs))]
    ppermute x0 -> x4, starting transfers between devices: none -> 11 us  [the longest x3 7.95 us: shards(): lax.ppermute(beside_core, 'ctx', CORES)]
    ppermute x40 -> x39, starting transfers between devices: 66.6 us -> 63.7 us  [join(): self.now.append(lax.ppermute(value, axes, pairs))]
    unnamed x63 -> x61, local copies, waits for them, and re-layouts: 17 us -> 18.6 us
  transfers between devices with their start and end apart: 56 -> 59, of which waited for: 33 -> 33; matrix products, arithmetic and copies ran while one was open for 3% -> 4% of each run, Pallas kernels for 8% -> 9%
where the time goes in v3:
time: 362 us; the launch traced here: 361 us
  waiting for transfers between devices  163 us (45%)
  starting transfers between devices  95 us (26%)
  Pallas kernels  56.3 us (16%)
  local copies, waits for them, and re-layouts  25.1 us (7%)
  between operations  14 us (4%)
  other arithmetic  7.03 us (2%)
    ppermute x39, waiting for transfers between devices, join(): self.now.append(lax.ppermute(value, axes, pairs))  149 us
    ppermute x39, starting transfers between devices, join(): self.now.append(lax.ppermute(value, axes, pairs))  63.7 us
    pallas_call x7, Pallas kernels, project_in(): pl.pallas_call(partial(in_kernel, mode, step, sections), out_shape=out, i...  29.4 us
    unnamed x61, local copies, waits for them, and re-layouts  18.6 us
    pallas_call x4, Pallas kernels, project_out(): pl.pallas_call(partial(out_kernel, step, sections), out_shape=(out, out),...  14.3 us
    ppermute x4, starting transfers between devices, shards(): halo = lax.ppermute(mixed[-reach:], 'ctx', HALO)  8.87 us
    ppermute x3, starting transfers between devices, shards(): lax.ppermute(beside_core, 'ctx', CORES)  7.95 us
    ppermute x4, starting transfers between devices, shards(): core_gated = lax.ppermute(own_gated, 'ctx', CORES)  7.37 us
  transfers between devices with their start and end apart: 59, of which 33 were waited for; matrix products, arithmetic and copies ran while one was open for 4% of the time, Pallas kernels for 9%

profile of v3, /device:TPU:0, one launch (start us, length us, event | category | flops | bytes accessed | tf_op | source)
XLA Modules:
  0.0 360.6 jit_solution(13474495815852275886)
XLA Ops:
  6.5 3.8 %taken.2 = (bf16[512,512]{1,0:T(8,128)(2,1)}, bf16[3,512,512]{2,1,0:T(8,128)(2,1)}) custom-call(s32[4]{0:T(128)} %plan.32, bf16[2,3,1024,512]{3,2,1,0:T(8,128)(2,1)} %bitcast.in_ref.refs_1_.refs_2_.refs_4_, bf16[2,1024,512]{2,1,0:T(8,128)(2,1)} %out_ref.3), custom_call_target="tpu_custom_call" | custom-call | tf_op jit(solution)/shard_map/taken/pallas_call | solution.py:388
  10.9 2.6 collective-permute-start.1
  15.4 5.1 %reshape.11 = bf16[32,64,255]{2,1,0:T(8,128)(2,1)} reshape(bf16[32,16320]{1,0:T(8,128)(2,1)} %bitcast.42) | data formatting | bytes 2088960 | tf_op jit(solution)/shard_map/reshape | solution.py:294
  20.4 1.6 copy-done.21
  22.1 3.1 taken.3
  27.0 21.7 %collective-permute-done.1.refs_3_.refs_4_.refs_6_ = bf16[3,512,512]{2,1,0:T(8,128)(2,1)S(1)} collective-permute-done((bf16[3,512,512]{2,1,0:T(8,128)(2,1)}, bf16[3,512,512]{2,1,0:T(8,128)(2,1)S(1)}, u32[]{:S(2)}, u32[]{:S(2)}) %collective-permute-start.1) | collective-permute-done | bytes 1572896 | tf_op jit(solution)/shard_map/ppermute | solution.py:415
  48.7 1.8 all-gather.2.cloned.1.call-done.refs_0_
  54.7 3.2 collective-permute-start.6
  59.2 6.6 %collective-permute-done.7 = bf16[512,512]{1,0:T(8,128)(2,1)S(1)} collective-permute-done((bf16[512,512]{1,0:T(8,128)(2,1)}, bf16[512,512]{1,0:T(8,128)(2,1)S(1)}, u32[]{:S(2)}, u32[]{:S(2)}) %collective-permute-start.7) | collective-permute-done | bytes 524320 | tf_op jit(solution)/shard_map/ppermute | solution.py:415
  65.8 13.7 %collective-permute-done.6 = bf16[512,512]{1,0:T(8,128)(2,1)S(1)} collective-permute-done((bf16[512,512]{1,0:T(8,128)(2,1)}, bf16[512,512]{1,0:T(8,128)(2,1)S(1)}, u32[]{:S(2)}, u32[]{:S(2)}) %collective-permute-start.6) | collective-permute-done | bytes 524320 | tf_op jit(solution)/shard_map/ppermute | solution.py:415
  81.1 5.4 %collective-permute-done.2.refs_4_.refs_5_.refs_7_ = bf16[3,512,512]{2,1,0:T(8,128)(2,1)S(1)} collective-permute-done((bf16[3,512,512]{2,1,0:T(8,128)(2,1)S(1)}, bf16[3,512,512]{2,1,0:T(8,128)(2,1)S(1)}, u32[]{:S(2)}, u32[]{:S(2)}) %collective-permute-start.2) | collective-permute-done | bytes 1572896 | tf_op jit(solution)/shard_map/ppermute | solution.py:415
  87.4 4.1 %collective-permute-start.17 = (bf16[4,512,512]{2,1,0:T(8,128)(2,1)S(1)}, bf16[4,512,512]{2,1,0:T(8,128)(2,1)S(1)}, u32[]{:S(2)}, u32[]{:S(2)}) collective-permute-start(bf16[4,512,512]{2,1,0:T(8,128)(2,1)S(1)} %pad_maximum_fusion.refs_4_), channel_id=1, source_target_pairs={{0,8},{5,9},{2,10},{7,11},{8,4},{13,5},{10,6},{15,7},{16,24},{21,2... | collective-permute-start | bytes 6291464 | tf_op jit(solution)/shard_map/ppermute | solution.py:415
  91.6 3.4 collective-permute-start.16
  97.7 3.3 collective-permute-start.25
  102.3 5.6 %project_in_whole.1 = (bf16[192,512]{1,0:T(8,128)(2,1)S(1)}, bf16[192,512]{1,0:T(8,128)(2,1)S(1)}) custom-call(s32[4]{0:T(128)S(1)} %copy-done.25, bf16[192,4096]{1,0:T(8,128)(2,1)S(1)} %copy-done.22, bf16[2,3,1024,512]{3,2,1,0:T(8,128)(2,1)} %bitcast.in_ref.refs_1_.refs_2_.refs_4_, bf16[2,3,1024,512]{3,2,1,0:T(8,128)(2,1)} %collective-permute-done.refs_2_.refs_3_.refs_5_, ...), custom_call_target="tpu_custom_call" | custom-call | flops 2415919104 | bytes 12582912 | tf_op jit(solution)/shard_map/project_in_whole/pallas_call | solution.py:208
  108.0 6.9 %collective-permute-done.17.refs_7_ = bf16[4,512,512]{2,1,0:T(8,128)(2,1)S(1)} collective-permute-done((bf16[4,512,512]{2,1,0:T(8,128)(2,1)S(1)}, bf16[4,512,512]{2,1,0:T(8,128)(2,1)S(1)}, u32[]{:S(2)}, u32[]{:S(2)}) %collective-permute-start.17) | collective-permute-done | bytes 2097184 | tf_op jit(solution)/shard_map/ppermute | solution.py:415
  114.9 2.5 collective-permute-start.9
  118.2 4.8 %collective-permute-done.25 = bf16[512,512]{1,0:T(8,128)(2,1)S(1)} collective-permute-done((bf16[512,512]{1,0:T(8,128)(2,1)S(1)}, bf16[512,512]{1,0:T(8,128)(2,1)S(1)}, u32[]{:S(2)}, u32[]{:S(2)}) %collective-permute-start.25) | collective-permute-done | bytes 524320 | tf_op jit(solution)/shard_map/ppermute | solution.py:415
  123.1 1.6 pad_maximum_fusion.1.refs_9_
  124.8 4.4 %collective-permute-start.27 = (bf16[4,512,512]{2,1,0:T(8,128)(2,1)}, bf16[4,512,512]{2,1,0:T(8,128)(2,1)}, u32[]{:S(2)}, u32[]{:S(2)}) collective-permute-start(bf16[4,512,512]{2,1,0:T(8,128)(2,1)} %pad_maximum_fusion.1.refs_9_), channel_id=1, source_target_pairs={{0,8},{5,9},{2,10},{7,11},{8,4},{13,5},{10,6},{15,7},{16,24},{21,2... | collective-permute-start | bytes 6291464 | tf_op jit(solution)/shard_map/ppermute | solution.py:415
  130.8 3.2 collective-permute-start.11
  134.0 1.9 collective-permute-start.10
  136.5 13.2 %collective-permute-done.11 = bf16[192,512]{1,0:T(8,128)(2,1)S(1)} collective-permute-done((bf16[192,512]{1,0:T(8,128)(2,1)S(1)}, bf16[192,512]{1,0:T(8,128)(2,1)S(1)}, u32[]{:S(2)}, u32[]{:S(2)}) %collective-permute-start.11) | collective-permute-done | bytes 196640 | tf_op jit(solution)/shard_map/ppermute | solution.py:415
  155.4 1.7 collective-permute-done.14.refs_3_
  157.2 1.6 copy-done.3
  160.3 1.6 copy-done.9
  165.1 4.0 %project_out.4 = (bf16[192,1024]{1,0:T(8,128)(2,1)S(1)}, bf16[192,1024]{1,0:T(8,128)(2,1)S(1)}) custom-call(s32[4]{0:T(128)S(1)} %copy-done.25, bf16[4,192,512]{2,1,0:T(8,128)(2,1)} %pad_maximum_fusion.3.refs_0_, bf16[4,192,512]{2,1,0:T(8,128)(2,1)} %collective-permute-done.13.refs_1_, bf16[192,1024]{1,0:T(8,128)(2,1)S(1)} %get-tuple-element.98.refs_2_, ...), custom_call_target="tpu_custom_call" | custom-call | flops 1610612736 | bytes 4194304 | tf_op jit(solution)/shard_map/project_out/pallas_call | solution.py:347
  171.2 6.8 %collective-permute-done.23.refs_9_.refs_11_ = bf16[2,512,512]{2,1,0:T(8,128)(2,1)} collective-permute-done((bf16[2,512,512]{2,1,0:T(8,128)(2,1)}, bf16[2,512,512]{2,1,0:T(8,128)(2,1)}, u32[]{:S(2)}, u32[]{:S(2)}) %collective-permute-start.23) | collective-permute-done | bytes 1048608 | tf_op jit(solution)/shard_map/ppermute | solution.py:415
  178.7 1.7 pad_maximum_fusion.2
  181.2 7.6 %collective-permute-done.20 = bf16[192,1024]{1,0:T(8,128)(2,1)S(1)} collective-permute-done((bf16[192,1024]{1,0:T(8,128)(2,1)S(1)}, bf16[192,1024]{1,0:T(8,128)(2,1)S(1)}, u32[]{:S(2)}, u32[]{:S(2)}) %collective-permute-start.20) | collective-permute-done | bytes 393248 | tf_op jit(solution)/shard_map/ppermute | solution.py:415
  189.3 3.0 collective-permute-start.37
  192.3 2.0 collective-permute-start.36
  194.9 2.0 collective-permute-start.38
  199.4 3.9 %project_in_first.3 = (f32[3,192,512]{2,1,0:T(8,128)S(1)}, f32[192,128]{1,0:T(8,128)S(1)}) custom-call(s32[4]{0:T(128)S(1)} %copy-done.25, bf16[192,1024]{1,0:T(8,128)(2,1)S(1)} %get-tuple-element.65.refs_0_.refs_2_, bf16[192,1024]{1,0:T(8,128)(2,1)S(1)} %collective-permute-done.22.refs_1_, bf16[2,3,1024,512]{3,2,1,0:T(8,128)(2,1)} %bitcast.in_ref.refs_1_.refs_2_.refs_4_, ...), custom_call_target="tpu_custom_call" | custom-call | flops 1207959552 | bytes 6291456 | tf_op jit(solution)/shard_map/project_in_first/pallas_call | solution.py:208
  203.4 4.3 %project_in_last.3 = (bf16[192,512]{1,0:T(8,128)(2,1)S(1)}, bf16[192,512]{1,0:T(8,128)(2,1)S(1)}) custom-call(s32[4]{0:T(128)S(1)} %copy-done.25, bf16[192,1024]{1,0:T(8,128)(2,1)S(1)} %collective-permute-done.19.refs_0_, bf16[192,1024]{1,0:T(8,128)(2,1)S(1)} %collective-permute-done.21.refs_1_, f32[3,192,512]{2,1,0:T(8,128)S(1)} %get-tuple-element.76.refs_2_, ...), custom_call_target="tpu_custom_call" | custom-call | flops 1207959552 | bytes 6291456 | tf_op jit(solution)/shard_map/project_in_last/pallas_call | solution.py:208
  207.6 2.0 collective-permute-start.31
  212.2 3.9 %collective-permute-start.34 = (bf16[192,512]{1,0:T(8,128)(2,1)S(1)}, bf16[192,512]{1,0:T(8,128)(2,1)S(1)}, u32[]{:S(2)}, u32[]{:S(2)}) collective-permute-start(bf16[192,512]{1,0:T(8,128)(2,1)S(1)} %filter_and_gate.5), channel_id=1, source_target_pairs={{0,3},{1,0},{2,1},{3,2},{4,7},{5,4},{6,5},{7,6},{8,11},{9,8},{10,9... | collective-permute-start | bytes 589832 | tf_op jit(solution)/shard_map/ppermute | solution.py:415
  216.1 5.3 %collective-permute-done.34 = bf16[192,512]{1,0:T(8,128)(2,1)S(1)} collective-permute-done((bf16[192,512]{1,0:T(8,128)(2,1)S(1)}, bf16[192,512]{1,0:T(8,128)(2,1)S(1)}, u32[]{:S(2)}, u32[]{:S(2)}) %collective-permute-start.34) | collective-permute-done | bytes 196640 | tf_op jit(solution)/shard_map/ppermute | solution.py:415
  221.4 11.5 %collective-permute-done.33 = bf16[192,512]{1,0:T(8,128)(2,1)S(1)} collective-permute-done((bf16[192,512]{1,0:T(8,128)(2,1)S(1)}, bf16[192,512]{1,0:T(8,128)(2,1)S(1)}, u32[]{:S(2)}, u32[]{:S(2)}) %collective-permute-start.33) | collective-permute-done | bytes 196640 | tf_op jit(solution)/shard_map/ppermute | solution.py:415
  237.2 3.0 project_out.5
  241.7 3.0 collective-permute-start.42
  244.7 1.7 collective-permute-start.39
  246.3 2.6 collective-permute-done.40
  249.0 6.8 %collective-permute-start.41 = (bf16[192,1024]{1,0:T(8,128)(2,1)S(1)}, bf16[192,1024]{1,0:T(8,128)(2,1)S(1)}, u32[]{:S(2)}, u32[]{:S(2)}) collective-permute-start(bf16[192,1024]{1,0:T(8,128)(2,1)S(1)} %collective-permute-done.40), channel_id=1, source_target_pairs={{0,4},{4,0},{8,12},{12,8},{1,5},{5,1},{9,13},{13,9},{2,6},{6,2},{1... | collective-permute-start | bytes 1179656 | tf_op jit(solution)/shard_map/ppermute | solution.py:540
  255.8 4.0 %project_in_first.4 = (f32[3,192,512]{2,1,0:T(8,128)S(1)}, f32[192,128]{1,0:T(8,128)S(1)}) custom-call(s32[4]{0:T(128)S(1)} %copy-done.25, bf16[192,1024]{1,0:T(8,128)(2,1)S(1)} %get-tuple-element.83.refs_0_.refs_2_, bf16[192,1024]{1,0:T(8,128)(2,1)S(1)} %collective-permute-done.42.refs_1_, bf16[2,3,1024,512]{3,2,1,0:T(8,128)(2,1)} %bitcast.in_ref.refs_1_.refs_2_.refs_4_, ...), custom_call_target="tpu_custom_call" | custom-call | flops 1207959552 | bytes 6291456 | tf_op jit(solution)/shard_map/project_in_first/pallas_call | solution.py:208
  259.8 3.9 %project_in_last.4 = (bf16[192,512]{1,0:T(8,128)(2,1)S(1)}, bf16[192,512]{1,0:T(8,128)(2,1)S(1)}) custom-call(s32[4]{0:T(128)S(1)} %copy-done.25, bf16[192,1024]{1,0:T(8,128)(2,1)S(1)} %collective-permute-done.39.refs_0_, bf16[192,1024]{1,0:T(8,128)(2,1)S(1)} %collective-permute-done.41.refs_1_, f32[3,192,512]{2,1,0:T(8,128)S(1)} %get-tuple-element.85.refs_2_, ...), custom_call_target="tpu_custom_call" | custom-call | flops 1207959552 | bytes 6291456 | tf_op jit(solution)/shard_map/project_in_last/pallas_call | solution.py:208
  263.7 2.8 collective-permute-start.43
  268.7 2.9 collective-permute-start.46
  272.2 1.9 collective-permute-start.44
  274.9 5.4 %collective-permute-done.45 = bf16[192,512]{1,0:T(8,128)(2,1)S(1)} collective-permute-done((bf16[192,512]{1,0:T(8,128)(2,1)S(1)}, bf16[192,512]{1,0:T(8,128)(2,1)S(1)}, u32[]{:S(2)}, u32[]{:S(2)}) %collective-permute-start.45) | collective-permute-done | bytes 196640 | tf_op jit(solution)/shard_map/ppermute | solution.py:415
  280.3 5.9 %collective-permute-done.44 = bf16[192,512]{1,0:T(8,128)(2,1)S(1)} collective-permute-done((bf16[192,512]{1,0:T(8,128)(2,1)S(1)}, bf16[192,512]{1,0:T(8,128)(2,1)S(1)}, u32[]{:S(2)}, u32[]{:S(2)}) %collective-permute-start.44) | collective-permute-done | bytes 196640 | tf_op jit(solution)/shard_map/ppermute | solution.py:415
  286.3 4.5 %collective-permute-start.47 = (bf16[4,192,512]{2,1,0:T(8,128)(2,1)S(1)}, bf16[4,192,512]{2,1,0:T(8,128)(2,1)S(1)}, u32[]{:S(2)}, u32[]{:S(2)}) collective-permute-start(bf16[4,192,512]{2,1,0:T(8,128)(2,1)S(1)} %pad_maximum_fusion.5.refs_0_), channel_id=1, source_target_pairs={{0,4},{4,0},{8,12},{12,8},{1,5},{5,1},{9,13},{13,9},{2,6},{6,2},{1... | collective-permute-start | bytes 2359304 | tf_op jit(solution)/shard_map/ppermute | solution.py:531
  290.8 1.9 collective-permute-done.47.refs_1_
  292.7 4.2 %project_out.6 = (bf16[192,1024]{1,0:T(8,128)(2,1)S(1)}, bf16[192,1024]{1,0:T(8,128)(2,1)S(1)}) custom-call(s32[4]{0:T(128)S(1)} %copy-done.25, bf16[4,192,512]{2,1,0:T(8,128)(2,1)S(1)} %pad_maximum_fusion.5.refs_0_, bf16[4,192,512]{2,1,0:T(8,128)(2,1)S(1)} %collective-permute-done.47.refs_1_, bf16[192,1024]{1,0:T(8,128)(2,1)S(1)} %get-tuple-element.83.refs_0_.refs_2_, ...), custom_call_target="tpu_custom_call" | custom-call | flops 1610612736 | bytes 4194304 | tf_op jit(solution)/shard_map/project_out/pallas_call | solution.py:347
  299.1 9.8 %collective-permute-done.49 = bf16[192,1024]{1,0:T(8,128)(2,1)S(1)} collective-permute-done((bf16[192,1024]{1,0:T(8,128)(2,1)S(1)}, bf16[192,1024]{1,0:T(8,128)(2,1)S(1)}, u32[]{:S(2)}, u32[]{:S(2)}) %collective-permute-start.49) | collective-permute-done | bytes 393248 | tf_op jit(solution)/shard_map/ppermute | solution.py:415
  308.9 3.9 %project_in_first.5 = (f32[3,192,512]{2,1,0:T(8,128)S(1)}, f32[192,128]{1,0:T(8,128)S(1)}) custom-call(s32[4]{0:T(128)S(1)} %copy-done.25, bf16[192,1024]{1,0:T(8,128)(2,1)S(1)} %get-tuple-element.89.refs_0_.refs_2_, bf16[192,1024]{1,0:T(8,128)(2,1)S(1)} %collective-permute-done.51.refs_1_, bf16[2,3,1024,512]{3,2,1,0:T(8,128)(2,1)} %bitcast.in_ref.refs_1_.refs_2_.refs_4_, ...), custom_call_target="tpu_custom_call" | custom-call | flops 1207959552 | bytes 6291456 | tf_op jit(solution)/shard_map/project_in_first/pallas_call | solution.py:208
  312.8 4.0 %collective-permute-done.48.refs_0_ = bf16[192,1024]{1,0:T(8,128)(2,1)S(1)} collective-permute-done((bf16[192,1024]{1,0:T(8,128)(2,1)S(1)}, bf16[192,1024]{1,0:T(8,128)(2,1)S(1)}, u32[]{:S(2)}, u32[]{:S(2)}) %collective-permute-start.48) | collective-permute-done | bytes 393248 | tf_op jit(solution)/shard_map/ppermute | solution.py:415
  316.8 3.9 %project_in_last.5 = (bf16[192,512]{1,0:T(8,128)(2,1)S(1)}, bf16[192,512]{1,0:T(8,128)(2,1)S(1)}) custom-call(s32[4]{0:T(128)S(1)} %copy-done.25, bf16[192,1024]{1,0:T(8,128)(2,1)S(1)} %collective-permute-done.48.refs_0_, bf16[192,1024]{1,0:T(8,128)(2,1)S(1)} %collective-permute-done.50.refs_1_, f32[3,192,512]{2,1,0:T(8,128)S(1)} %get-tuple-element.91.refs_2_, ...), custom_call_target="tpu_custom_call" | custom-call | flops 1207959552 | bytes 6291456 | tf_op jit(solution)/shard_map/project_in_last/pallas_call | solution.py:208
  324.8 2.2 collective-permute-start.55
  327.1 1.9 collective-permute-start.53
  330.5 13.4 %collective-permute-done.54 = bf16[192,512]{1,0:T(8,128)(2,1)S(1)} collective-permute-done((bf16[192,512]{1,0:T(8,128)(2,1)S(1)}, bf16[192,512]{1,0:T(8,128)(2,1)S(1)}, u32[]{:S(2)}, u32[]{:S(2)}) %collective-permute-start.54) | collective-permute-done | bytes 196640 | tf_op jit(solution)/shard_map/ppermute | solution.py:415
  344.0 2.2 collective-permute-start.56
  346.2 1.9 collective-permute-done.56.refs_1_
  348.1 3.0 project_out.7
  (153 shorter events, 58.8 us)
Async XLA Ops:
  6.5 44.0 %all-gather.2.cloned.1.call-start = ((), (), s32[]{:S(2)}) async-start(), calls=%async_computation | async-start | bytes 1966080 | tf_op jit(solution)/shard_map/all_gather | solution.py:476
  10.3 40.2 %collective-permute-start = (bf16[2,3,1024,512]{3,2,1,0:T(8,128)(2,1)}, bf16[2,3,1024,512]{3,2,1,0:T(8,128)(2,1)}, u32[]{:S(2)}, u32[]{:S(2)}) collective-permute-start(bf16[2,3,1024,512]{3,2,1,0:T(8,128)(2,1)} %bitcast.in_ref.refs_1_.refs_2_.refs_4_), channel_id=1, source_target_pairs={{0,4},{4,0},{8,12},{12,8},{1,5},{5,1},{9,13},{13,9},{2,6},{6,2},{1... | collective-permute-start | bytes 18874376 | tf_op jit(solution)/shard_map/ppermute | solution.py:415
  10.9 37.8 %collective-permute-start.1 = (bf16[3,512,512]{2,1,0:T(8,128)(2,1)}, bf16[3,512,512]{2,1,0:T(8,128)(2,1)S(1)}, u32[]{:S(2)}, u32[]{:S(2)}) collective-permute-start(bf16[3,512,512]{2,1,0:T(8,128)(2,1)} %get-tuple-element.51), channel_id=1, source_target_pairs={{0,8},{4,12},{8,0},{12,4},{1,9},{5,13},{9,1},{13,5},{2,10},{6,14},... | collective-permute-start | bytes 4718600 | tf_op jit(solution)/shard_map/ppermute | solution.py:415
  50.5 36.0 %collective-permute-start.2 = (bf16[3,512,512]{2,1,0:T(8,128)(2,1)S(1)}, bf16[3,512,512]{2,1,0:T(8,128)(2,1)S(1)}, u32[]{:S(2)}, u32[]{:S(2)}) collective-permute-start(bf16[3,512,512]{2,1,0:T(8,128)(2,1)S(1)} %collective-permute-done.1.refs_3_.refs_4_.refs_6_), channel_id=1, source_target_pairs={{0,16},{16,0},{1,17},{17,1},{2,18},{18,2},{3,19},{19,3},{4,20},{20... | collective-permute-start | bytes 4718600 | tf_op jit(solution)/shard_map/ppermute | solution.py:415
  52.0 29.1 %collective-permute-start.4 = (bf16[2,512,512]{2,1,0:T(8,128)(2,1)}, bf16[2,512,512]{2,1,0:T(8,128)(2,1)}, u32[]{:S(2)}, u32[]{:S(2)}) collective-permute-start(bf16[2,512,512]{2,1,0:T(8,128)(2,1)} %copy-done.27), channel_id=1, source_target_pairs={{0,8},{4,12},{8,0},{12,4},{1,9},{5,13},{9,1},{13,5},{2,10},{6,14},... | collective-permute-start | bytes 3145736 | tf_op jit(solution)/shard_map/ppermute | solution.py:415
  53.5 12.4 %collective-permute-start.7 = (bf16[512,512]{1,0:T(8,128)(2,1)}, bf16[512,512]{1,0:T(8,128)(2,1)S(1)}, u32[]{:S(2)}, u32[]{:S(2)}) collective-permute-start(bf16[512,512]{1,0:T(8,128)(2,1)} %get-tuple-element.60), channel_id=1, source_target_pairs={{1,0},{6,5},{3,2},{4,7},{9,8},{14,13},{11,10},{12,15},{17,16},{22,... | collective-permute-start | bytes 1572872 | tf_op jit(solution)/shard_map/ppermute | solution.py:415
  54.7 24.8 %collective-permute-start.6 = (bf16[512,512]{1,0:T(8,128)(2,1)}, bf16[512,512]{1,0:T(8,128)(2,1)S(1)}, u32[]{:S(2)}, u32[]{:S(2)}) collective-permute-start(bf16[512,512]{1,0:T(8,128)(2,1)} %get-tuple-element.60), channel_id=1, source_target_pairs={{2,0},{7,5},{0,2},{5,7},{10,8},{15,13},{8,10},{13,15},{18,16},{23,... | collective-permute-start | bytes 1572872 | tf_op jit(solution)/shard_map/ppermute | solution.py:415
  57.9 21.6 %collective-permute-start.5 = (bf16[512,512]{1,0:T(8,128)(2,1)}, bf16[512,512]{1,0:T(8,128)(2,1)S(1)}, u32[]{:S(2)}, u32[]{:S(2)}) collective-permute-start(bf16[512,512]{1,0:T(8,128)(2,1)} %get-tuple-element.60), channel_id=1, source_target_pairs={{3,0},{4,5},{1,2},{6,7},{11,8},{12,13},{9,10},{14,15},{19,16},{20,... | collective-permute-start | bytes 1572872 | tf_op jit(solution)/shard_map/ppermute | solution.py:415
  86.5 8.5 %collective-permute-start.15 = (bf16[4,512,512]{2,1,0:T(8,128)(2,1)S(1)}, bf16[4,512,512]{2,1,0:T(8,128)(2,1)S(1)}, u32[]{:S(2)}, u32[]{:S(2)}) collective-permute-start(bf16[4,512,512]{2,1,0:T(8,128)(2,1)S(1)} %pad_maximum_fusion.refs_4_), channel_id=1, source_target_pairs={{5,1},{7,3},{8,12},{10,14},{21,17},{23,19},{24,28},{26,30}} | collective-permute-start | bytes 6291464 | tf_op jit(solution)/shard_map/ppermute | solution.py:415
  87.3 7.7 %collective-permute-start.8 = (bf16[3,512,512]{2,1,0:T(8,128)(2,1)S(1)}, bf16[3,512,512]{2,1,0:T(8,128)(2,1)S(1)}, u32[]{:S(2)}, u32[]{:S(2)}) collective-permute-start(bf16[3,512,512]{2,1,0:T(8,128)(2,1)S(1)} %collective-permute-done.2.refs_4_.refs_5_.refs_7_), channel_id=1, source_target_pairs={{0,4},{4,0},{8,12},{12,8},{1,5},{5,1},{9,13},{13,9},{2,6},{6,2},{1... | collective-permute-start | bytes 4718600 | tf_op jit(solution)/shard_map/ppermute | solution.py:415
  87.4 27.5 %collective-permute-start.17 = (bf16[4,512,512]{2,1,0:T(8,128)(2,1)S(1)}, bf16[4,512,512]{2,1,0:T(8,128)(2,1)S(1)}, u32[]{:S(2)}, u32[]{:S(2)}) collective-permute-start(bf16[4,512,512]{2,1,0:T(8,128)(2,1)S(1)} %pad_maximum_fusion.refs_4_), channel_id=1, source_target_pairs={{0,8},{5,9},{2,10},{7,11},{8,4},{13,5},{10,6},{15,7},{16,24},{21,2... | collective-permute-start | bytes 6291464 | tf_op jit(solution)/shard_map/ppermute | solution.py:415
  91.5 9.5 %collective-permute-start.3 = (bf16[3,512,512]{2,1,0:T(8,128)(2,1)S(1)}, bf16[3,512,512]{2,1,0:T(8,128)(2,1)S(1)}, u32[]{:S(2)}, u32[]{:S(2)}) collective-permute-start(bf16[3,512,512]{2,1,0:T(8,128)(2,1)S(1)} %collective-permute-done.1.refs_3_.refs_4_.refs_6_), channel_id=1, source_target_pairs={{0,4},{4,0},{8,12},{12,8},{1,5},{5,1},{9,13},{13,9},{2,6},{6,2},{1... | collective-permute-start | bytes 4718600 | tf_op jit(solution)/shard_map/ppermute | solution.py:490
  91.6 33.1 %collective-permute-start.16 = (bf16[4,512,512]{2,1,0:T(8,128)(2,1)S(1)}, bf16[4,512,512]{2,1,0:T(8,128)(2,1)S(1)}, u32[]{:S(2)}, u32[]{:S(2)}) collective-permute-start(bf16[4,512,512]{2,1,0:T(8,128)(2,1)S(1)} %pad_maximum_fusion.refs_4_), channel_id=1, source_target_pairs={{0,16},{16,0},{5,17},{21,1},{2,18},{18,2},{7,19},{23,3},{8,28},{24... | collective-permute-start | bytes 6291464 | tf_op jit(solution)/shard_map/ppermute | solution.py:415
  96.4 21.0 %collective-permute-start.26 = (bf16[512,512]{1,0:T(8,128)(2,1)S(1)}, bf16[512,512]{1,0:T(8,128)(2,1)S(1)}, u32[]{:S(2)}, u32[]{:S(2)}) collective-permute-start(bf16[512,512]{1,0:T(8,128)(2,1)S(1)} %copy-done.24), channel_id=1, source_target_pairs={{1,0},{6,5},{3,2},{4,7},{9,8},{14,13},{11,10},{12,15},{17,16},{22,... | collective-permute-start | bytes 1572872 | tf_op jit(solution)/shard_map/ppermute | solution.py:415
  97.7 25.4 %collective-permute-start.25 = (bf16[512,512]{1,0:T(8,128)(2,1)S(1)}, bf16[512,512]{1,0:T(8,128)(2,1)S(1)}, u32[]{:S(2)}, u32[]{:S(2)}) collective-permute-start(bf16[512,512]{1,0:T(8,128)(2,1)S(1)} %copy-done.24), channel_id=1, source_target_pairs={{2,0},{7,5},{0,2},{5,7},{10,8},{15,13},{8,10},{13,15},{18,16},{23,... | collective-permute-start | bytes 1572872 | tf_op jit(solution)/shard_map/ppermute | solution.py:415
  101.0 22.1 %collective-permute-start.24 = (bf16[512,512]{1,0:T(8,128)(2,1)S(1)}, bf16[512,512]{1,0:T(8,128)(2,1)S(1)}, u32[]{:S(2)}, u32[]{:S(2)}) collective-permute-start(bf16[512,512]{1,0:T(8,128)(2,1)S(1)} %copy-done.24), channel_id=1, source_target_pairs={{3,0},{4,5},{1,2},{6,7},{11,8},{12,13},{9,10},{14,15},{19,16},{20,... | collective-permute-start | bytes 1572872 | tf_op jit(solution)/shard_map/ppermute | solution.py:415
  114.9 9.8 %collective-permute-start.9 = (bf16[128,512]{1,0:T(8,128)(2,1)S(1)}, bf16[128,512]{1,0:T(8,128)(2,1)S(1)}, u32[]{:S(2)}, u32[]{:S(2)}) collective-permute-start(bf16[128,512]{1,0:T(8,128)(2,1)S(1)} %slice.20), channel_id=1, source_target_pairs={{0,4},{4,8},{8,12},{1,5},{5,9},{9,13},{2,6},{6,10},{10,14},{3,7},{... | collective-permute-start | bytes 393224 | tf_op jit(solution)/shard_map/ppermute | solution.py:518
  117.4 33.4 %collective-permute-start.18 = (bf16[4,512,512]{2,1,0:T(8,128)(2,1)S(1)}, bf16[4,512,512]{2,1,0:T(8,128)(2,1)S(1)}, u32[]{:S(2)}, u32[]{:S(2)}) collective-permute-start(bf16[4,512,512]{2,1,0:T(8,128)(2,1)S(1)} %collective-permute-done.17.refs_7_), channel_id=1, source_target_pairs={{8,24},{24,8},{9,25},{25,9},{10,26},{26,10},{11,27},{27,11},{4,20}... | collective-permute-start | bytes 6291464 | tf_op jit(solution)/shard_map/ppermute | solution.py:415
  124.8 28.4 %collective-permute-start.27 = (bf16[4,512,512]{2,1,0:T(8,128)(2,1)}, bf16[4,512,512]{2,1,0:T(8,128)(2,1)}, u32[]{:S(2)}, u32[]{:S(2)}) collective-permute-start(bf16[4,512,512]{2,1,0:T(8,128)(2,1)} %pad_maximum_fusion.1.refs_9_), channel_id=1, source_target_pairs={{0,8},{5,9},{2,10},{7,11},{8,4},{13,5},{10,6},{15,7},{16,24},{21,2... | collective-permute-start | bytes 6291464 | tf_op jit(solution)/shard_map/ppermute | solution.py:415
  130.7 5.8 %collective-permute-start.12 = (bf16[192,512]{1,0:T(8,128)(2,1)S(1)}, bf16[192,512]{1,0:T(8,128)(2,1)S(1)}, u32[]{:S(2)}, u32[]{:S(2)}) collective-permute-start(bf16[192,512]{1,0:T(8,128)(2,1)S(1)} %filter_and_gate.4), channel_id=1, source_target_pairs={{0,3},{1,0},{2,1},{3,2},{4,7},{5,4},{6,5},{7,6},{8,11},{9,8},{10,9... | collective-permute-start | bytes 589832 | tf_op jit(solution)/shard_map/ppermute | solution.py:415
  130.8 19.0 %collective-permute-start.11 = (bf16[192,512]{1,0:T(8,128)(2,1)S(1)}, bf16[192,512]{1,0:T(8,128)(2,1)S(1)}, u32[]{:S(2)}, u32[]{:S(2)}) collective-permute-start(bf16[192,512]{1,0:T(8,128)(2,1)S(1)} %filter_and_gate.4), channel_id=1, source_target_pairs={{0,2},{1,3},{2,0},{3,1},{4,6},{5,7},{6,4},{7,5},{8,10},{9,11},{10,... | collective-permute-start | bytes 589832 | tf_op jit(solution)/shard_map/ppermute | solution.py:415
  134.0 15.7 %collective-permute-start.10 = (bf16[192,512]{1,0:T(8,128)(2,1)S(1)}, bf16[192,512]{1,0:T(8,128)(2,1)S(1)}, u32[]{:S(2)}, u32[]{:S(2)}) collective-permute-start(bf16[192,512]{1,0:T(8,128)(2,1)S(1)} %filter_and_gate.4), channel_id=1, source_target_pairs={{0,1},{1,2},{2,3},{3,0},{4,5},{5,6},{6,7},{7,4},{8,9},{9,10},{10,1... | collective-permute-start | bytes 589832 | tf_op jit(solution)/shard_map/ppermute | solution.py:415
  150.8 6.4 %collective-permute-start.13 = (bf16[4,192,512]{2,1,0:T(8,128)(2,1)}, bf16[4,192,512]{2,1,0:T(8,128)(2,1)}, u32[]{:S(2)}, u32[]{:S(2)}) collective-permute-start(bf16[4,192,512]{2,1,0:T(8,128)(2,1)} %pad_maximum_fusion.3.refs_0_), channel_id=1, source_target_pairs={{0,4},{4,0},{8,12},{12,8},{1,5},{5,1},{9,13},{13,9},{2,6},{6,2},{1... | collective-permute-start | bytes 2359304 | tf_op jit(solution)/shard_map/ppermute | solution.py:531
  152.1 25.9 %collective-permute-start.23 = (bf16[2,512,512]{2,1,0:T(8,128)(2,1)}, bf16[2,512,512]{2,1,0:T(8,128)(2,1)}, u32[]{:S(2)}, u32[]{:S(2)}) collective-permute-start(bf16[2,512,512]{2,1,0:T(8,128)(2,1)} %collective-permute-done.4.refs_8_.refs_10_), channel_id=1, source_target_pairs={{0,16},{16,0},{1,17},{17,1},{2,18},{18,2},{3,19},{19,3},{4,20},{20... | collective-permute-start | bytes 3145736 | tf_op jit(solution)/shard_map/ppermute | solution.py:415
  153.1 25.6 %collective-permute-start.28 = (bf16[2,512,512]{2,1,0:T(8,128)(2,1)}, bf16[2,512,512]{2,1,0:T(8,128)(2,1)}, u32[]{:S(2)}, u32[]{:S(2)}) collective-permute-start(bf16[2,512,512]{2,1,0:T(8,128)(2,1)} %get-tuple-element.73), channel_id=1, source_target_pairs={{0,8},{4,12},{8,0},{12,4},{1,9},{5,13},{9,1},{13,5},{2,10},{6,14},... | collective-permute-start | bytes 3145736 | tf_op jit(solution)/shard_map/ppermute | solution.py:415
  155.4 1.8 collective-permute-start.14
  169.2 12.0 %collective-permute-start.19 = (bf16[192,1024]{1,0:T(8,128)(2,1)S(1)}, bf16[192,1024]{1,0:T(8,128)(2,1)S(1)}, u32[]{:S(2)}, u32[]{:S(2)}) collective-permute-start(bf16[192,1024]{1,0:T(8,128)(2,1)S(1)} %get-tuple-element.65.refs_0_.refs_2_), channel_id=1, source_target_pairs={{0,1},{1,0},{2,3},{3,2},{4,5},{5,4},{6,7},{7,6},{8,9},{9,8},{10,11... | collective-permute-start | bytes 1179656 | tf_op jit(solution)/shard_map/ppermute | solution.py:415
  169.9 18.9 %collective-permute-start.20 = (bf16[192,1024]{1,0:T(8,128)(2,1)S(1)}, bf16[192,1024]{1,0:T(8,128)(2,1)S(1)}, u32[]{:S(2)}, u32[]{:S(2)}) collective-permute-start(bf16[192,1024]{1,0:T(8,128)(2,1)S(1)} %get-tuple-element.66.refs_3_), channel_id=1, source_target_pairs={{0,1},{1,0},{2,3},{3,2},{4,5},{5,4},{6,7},{7,6},{8,9},{9,8},{10,11... | collective-permute-start | bytes 1179656 | tf_op jit(solution)/shard_map/ppermute | solution.py:415
  188.8 9.3 %collective-permute-start.29 = (bf16[4,512,512]{2,1,0:T(8,128)(2,1)S(1)}, bf16[4,512,512]{2,1,0:T(8,128)(2,1)S(1)}, u32[]{:S(2)}, u32[]{:S(2)}) collective-permute-start(bf16[4,512,512]{2,1,0:T(8,128)(2,1)S(1)} %pad_maximum_fusion.2), channel_id=1, source_target_pairs={{0,4},{4,0},{8,12},{12,8},{1,5},{5,1},{9,13},{13,9},{2,6},{6,2},{1... | collective-permute-start | bytes 6291464 | tf_op jit(solution)/shard_map/ppermute | solution.py:415
  188.8 6.1 %collective-permute-start.30 = (bf16[2,512,512]{2,1,0:T(8,128)(2,1)}, bf16[2,512,512]{2,1,0:T(8,128)(2,1)S(1)}, u32[]{:S(2)}, u32[]{:S(2)}) collective-permute-start(bf16[2,512,512]{2,1,0:T(8,128)(2,1)} %collective-permute-done.4.refs_8_.refs_10_), channel_id=1, source_target_pairs={{0,4},{4,0},{8,12},{12,8},{1,5},{5,1},{9,13},{13,9},{2,6},{6,2},{1... | collective-permute-start | bytes 3145736 | tf_op jit(solution)/shard_map/ppermute | solution.py:520
  189.3 7.6 %collective-permute-start.22 = (bf16[192,1024]{1,0:T(8,128)(2,1)S(1)}, bf16[192,1024]{1,0:T(8,128)(2,1)S(1)}, u32[]{:S(2)}, u32[]{:S(2)}) collective-permute-start(bf16[192,1024]{1,0:T(8,128)(2,1)S(1)} %get-tuple-element.66.refs_3_), channel_id=1, source_target_pairs={{0,4},{4,0},{8,12},{12,8},{1,5},{5,1},{9,13},{13,9},{2,6},{6,2},{1... | collective-permute-start | bytes 1179656 | tf_op jit(solution)/shard_map/ppermute | solution.py:535
  189.3 45.7 %collective-permute-start.37 = (bf16[4,512,512]{2,1,0:T(8,128)(2,1)}, bf16[4,512,512]{2,1,0:T(8,128)(2,1)}, u32[]{:S(2)}, u32[]{:S(2)}) collective-permute-start(bf16[4,512,512]{2,1,0:T(8,128)(2,1)} %pad_maximum_fusion.1.refs_9_), channel_id=1, source_target_pairs={{0,16},{16,0},{5,17},{21,1},{2,18},{18,2},{7,19},{23,3},{8,28},{24... | collective-permute-start | bytes 6291464 | tf_op jit(solution)/shard_map/ppermute | solution.py:529
  192.3 42.7 %collective-permute-start.36 = (bf16[4,512,512]{2,1,0:T(8,128)(2,1)}, bf16[4,512,512]{2,1,0:T(8,128)(2,1)}, u32[]{:S(2)}, u32[]{:S(2)}) collective-permute-start(bf16[4,512,512]{2,1,0:T(8,128)(2,1)} %pad_maximum_fusion.1.refs_9_), channel_id=1, source_target_pairs={{5,1},{7,3},{8,12},{10,14},{21,17},{23,19},{24,28},{26,30}} | collective-permute-start | bytes 6291464 | tf_op jit(solution)/shard_map/ppermute | solution.py:415
  194.9 40.1 %collective-permute-start.38 = (bf16[4,512,512]{2,1,0:T(8,128)(2,1)}, bf16[4,512,512]{2,1,0:T(8,128)(2,1)}, u32[]{:S(2)}, u32[]{:S(2)}) collective-permute-start(bf16[4,512,512]{2,1,0:T(8,128)(2,1)} %collective-permute-done.27.refs_12_), channel_id=1, source_target_pairs={{8,24},{24,8},{9,25},{25,9},{10,26},{26,10},{11,27},{27,11},{4,20}... | collective-permute-start | bytes 6291464 | tf_op jit(solution)/shard_map/ppermute | solution.py:415
  196.9 6.4 %collective-permute-start.21 = (bf16[192,1024]{1,0:T(8,128)(2,1)S(1)}, bf16[192,1024]{1,0:T(8,128)(2,1)S(1)}, u32[]{:S(2)}, u32[]{:S(2)}) collective-permute-start(bf16[192,1024]{1,0:T(8,128)(2,1)S(1)} %collective-permute-done.20), channel_id=1, source_target_pairs={{0,4},{4,0},{8,12},{12,8},{1,5},{5,1},{9,13},{13,9},{2,6},{6,2},{1... | collective-permute-start | bytes 1179656 | tf_op jit(solution)/shard_map/ppermute | solution.py:540
  203.3 32.3 %copy-start.7 = (bf16[4,512,512]{2,1,0:T(8,128)(2,1)S(1)}, bf16[4,512,512]{2,1,0:T(8,128)(2,1)}, u32[]{:S(2)}) copy-start(bf16[4,512,512]{2,1,0:T(8,128)(2,1)} %copy-done.5) | copy-start | bytes 6291460
  203.3 32.3 %copy-start.10 = (bf16[4,512,512]{2,1,0:T(8,128)(2,1)S(1)}, bf16[4,512,512]{2,1,0:T(8,128)(2,1)}, u32[]{:S(2)}) copy-start(bf16[4,512,512]{2,1,0:T(8,128)(2,1)} %copy-done.8) | copy-start | bytes 6291460
  203.3 32.3 %copy-start.13 = (bf16[4,512,512]{2,1,0:T(8,128)(2,1)S(1)}, bf16[4,512,512]{2,1,0:T(8,128)(2,1)}, u32[]{:S(2)}) copy-start(bf16[4,512,512]{2,1,0:T(8,128)(2,1)} %copy-done.11) | copy-start | bytes 6291460
  207.6 28.0 %copy-start.4 = (bf16[4,512,512]{2,1,0:T(8,128)(2,1)S(1)}, bf16[4,512,512]{2,1,0:T(8,128)(2,1)}, u32[]{:S(2)}) copy-start(bf16[4,512,512]{2,1,0:T(8,128)(2,1)} %copy-done.2) | copy-start | bytes 6291460
  207.6 3.0 collective-permute-start.31
  212.2 9.3 %collective-permute-start.34 = (bf16[192,512]{1,0:T(8,128)(2,1)S(1)}, bf16[192,512]{1,0:T(8,128)(2,1)S(1)}, u32[]{:S(2)}, u32[]{:S(2)}) collective-permute-start(bf16[192,512]{1,0:T(8,128)(2,1)S(1)} %filter_and_gate.5), channel_id=1, source_target_pairs={{0,3},{1,0},{2,1},{3,2},{4,7},{5,4},{6,5},{7,6},{8,11},{9,8},{10,9... | collective-permute-start | bytes 589832 | tf_op jit(solution)/shard_map/ppermute | solution.py:415
  216.1 16.9 %collective-permute-start.33 = (bf16[192,512]{1,0:T(8,128)(2,1)S(1)}, bf16[192,512]{1,0:T(8,128)(2,1)S(1)}, u32[]{:S(2)}, u32[]{:S(2)}) collective-permute-start(bf16[192,512]{1,0:T(8,128)(2,1)S(1)} %filter_and_gate.5), channel_id=1, source_target_pairs={{0,2},{1,3},{2,0},{3,1},{4,6},{5,7},{6,4},{7,5},{8,10},{9,11},{10,... | collective-permute-start | bytes 589832 | tf_op jit(solution)/shard_map/ppermute | solution.py:415
  221.4 11.5 %collective-permute-start.32 = (bf16[192,512]{1,0:T(8,128)(2,1)S(1)}, bf16[192,512]{1,0:T(8,128)(2,1)S(1)}, u32[]{:S(2)}, u32[]{:S(2)}) collective-permute-start(bf16[192,512]{1,0:T(8,128)(2,1)S(1)} %filter_and_gate.5), channel_id=1, source_target_pairs={{0,1},{1,2},{2,3},{3,0},{4,5},{5,6},{6,7},{7,4},{8,9},{9,10},{10,1... | collective-permute-start | bytes 589832 | tf_op jit(solution)/shard_map/ppermute | solution.py:415
  233.1 2.6 collective-permute-start.35
  240.3 8.7 %collective-permute-start.40 = (bf16[192,1024]{1,0:T(8,128)(2,1)S(1)}, bf16[192,1024]{1,0:T(8,128)(2,1)S(1)}, u32[]{:S(2)}, u32[]{:S(2)}) collective-permute-start(bf16[192,1024]{1,0:T(8,128)(2,1)S(1)} %get-tuple-element.84.refs_3_), channel_id=1, source_target_pairs={{0,1},{1,0},{2,3},{3,2},{4,5},{5,4},{6,7},{7,6},{8,9},{9,8},{10,11... | collective-permute-start | bytes 1179656 | tf_op jit(solution)/shard_map/ppermute | solution.py:415
  241.7 14.1 %collective-permute-start.42 = (bf16[192,1024]{1,0:T(8,128)(2,1)S(1)}, bf16[192,1024]{1,0:T(8,128)(2,1)S(1)}, u32[]{:S(2)}, u32[]{:S(2)}) collective-permute-start(bf16[192,1024]{1,0:T(8,128)(2,1)S(1)} %get-tuple-element.84.refs_3_), channel_id=1, source_target_pairs={{0,4},{4,0},{8,12},{12,8},{1,5},{5,1},{9,13},{13,9},{2,6},{6,2},{1... | collective-permute-start | bytes 1179656 | tf_op jit(solution)/shard_map/ppermute | solution.py:535
  244.7 15.1 %collective-permute-start.39 = (bf16[192,1024]{1,0:T(8,128)(2,1)S(1)}, bf16[192,1024]{1,0:T(8,128)(2,1)S(1)}, u32[]{:S(2)}, u32[]{:S(2)}) collective-permute-start(bf16[192,1024]{1,0:T(8,128)(2,1)S(1)} %get-tuple-element.83.refs_0_.refs_2_), channel_id=1, source_target_pairs={{0,1},{1,0},{2,3},{3,2},{4,5},{5,4},{6,7},{7,6},{8,9},{9,8},{10,11... | collective-permute-start | bytes 1179656 | tf_op jit(solution)/shard_map/ppermute | solution.py:415
  249.0 10.8 %collective-permute-start.41 = (bf16[192,1024]{1,0:T(8,128)(2,1)S(1)}, bf16[192,1024]{1,0:T(8,128)(2,1)S(1)}, u32[]{:S(2)}, u32[]{:S(2)}) collective-permute-start(bf16[192,1024]{1,0:T(8,128)(2,1)S(1)} %collective-permute-done.40), channel_id=1, source_target_pairs={{0,4},{4,0},{8,12},{12,8},{1,5},{5,1},{9,13},{13,9},{2,6},{6,2},{1... | collective-permute-start | bytes 1179656 | tf_op jit(solution)/shard_map/ppermute | solution.py:540
  263.7 29.0 %copy-start.17 = (bf16[4,512,512]{2,1,0:T(8,128)(2,1)S(1)}, bf16[4,512,512]{2,1,0:T(8,128)(2,1)}, u32[]{:S(2)}) copy-start(bf16[4,512,512]{2,1,0:T(8,128)(2,1)} %copy-done.14) | copy-start | bytes 6291460
  263.7 3.8 %collective-permute-start.43 = (bf16[128,512]{1,0:T(8,128)(2,1)S(1)}, bf16[128,512]{1,0:T(8,128)(2,1)S(1)}, u32[]{:S(2)}, u32[]{:S(2)}) collective-permute-start(bf16[128,512]{1,0:T(8,128)(2,1)S(1)} %slice.22), channel_id=1, source_target_pairs={{0,4},{4,8},{8,12},{1,5},{5,9},{9,13},{2,6},{6,10},{10,14},{3,7},{... | collective-permute-start | bytes 393224 | tf_op jit(solution)/shard_map/ppermute | solution.py:518
  268.7 6.2 %collective-permute-start.46 = (bf16[192,512]{1,0:T(8,128)(2,1)S(1)}, bf16[192,512]{1,0:T(8,128)(2,1)S(1)}, u32[]{:S(2)}, u32[]{:S(2)}) collective-permute-start(bf16[192,512]{1,0:T(8,128)(2,1)S(1)} %filter_and_gate.6), channel_id=1, source_target_pairs={{0,3},{1,0},{2,1},{3,2},{4,7},{5,4},{6,5},{7,6},{8,11},{9,8},{10,9... | collective-permute-start | bytes 589832 | tf_op jit(solution)/shard_map/ppermute | solution.py:415
  271.6 8.7 %collective-permute-start.45 = (bf16[192,512]{1,0:T(8,128)(2,1)S(1)}, bf16[192,512]{1,0:T(8,128)(2,1)S(1)}, u32[]{:S(2)}, u32[]{:S(2)}) collective-permute-start(bf16[192,512]{1,0:T(8,128)(2,1)S(1)} %filter_and_gate.6), channel_id=1, source_target_pairs={{0,2},{1,3},{2,0},{3,1},{4,6},{5,7},{6,4},{7,5},{8,10},{9,11},{10,... | collective-permute-start | bytes 589832 | tf_op jit(solution)/shard_map/ppermute | solution.py:415
  272.2 14.0 %collective-permute-start.44 = (bf16[192,512]{1,0:T(8,128)(2,1)S(1)}, bf16[192,512]{1,0:T(8,128)(2,1)S(1)}, u32[]{:S(2)}, u32[]{:S(2)}) collective-permute-start(bf16[192,512]{1,0:T(8,128)(2,1)S(1)} %filter_and_gate.6), channel_id=1, source_target_pairs={{0,1},{1,2},{2,3},{3,0},{4,5},{5,6},{6,7},{7,4},{8,9},{9,10},{10,1... | collective-permute-start | bytes 589832 | tf_op jit(solution)/shard_map/ppermute | solution.py:415
  286.3 6.4 %collective-permute-start.47 = (bf16[4,192,512]{2,1,0:T(8,128)(2,1)S(1)}, bf16[4,192,512]{2,1,0:T(8,128)(2,1)S(1)}, u32[]{:S(2)}, u32[]{:S(2)}) collective-permute-start(bf16[4,192,512]{2,1,0:T(8,128)(2,1)S(1)} %pad_maximum_fusion.5.refs_0_), channel_id=1, source_target_pairs={{0,4},{4,0},{8,12},{12,8},{1,5},{5,1},{9,13},{13,9},{2,6},{6,2},{1... | collective-permute-start | bytes 2359304 | tf_op jit(solution)/shard_map/ppermute | solution.py:531
  296.9 12.0 %collective-permute-start.49 = (bf16[192,1024]{1,0:T(8,128)(2,1)S(1)}, bf16[192,1024]{1,0:T(8,128)(2,1)S(1)}, u32[]{:S(2)}, u32[]{:S(2)}) collective-permute-start(bf16[192,1024]{1,0:T(8,128)(2,1)S(1)} %get-tuple-element.90.refs_3_), channel_id=1, source_target_pairs={{0,1},{1,0},{2,3},{3,2},{4,5},{5,4},{6,7},{7,6},{8,9},{9,8},{10,11... | collective-permute-start | bytes 1179656 | tf_op jit(solution)/shard_map/ppermute | solution.py:415
  297.6 11.3 %collective-permute-start.51 = (bf16[192,1024]{1,0:T(8,128)(2,1)S(1)}, bf16[192,1024]{1,0:T(8,128)(2,1)S(1)}, u32[]{:S(2)}, u32[]{:S(2)}) collective-permute-start(bf16[192,1024]{1,0:T(8,128)(2,1)S(1)} %get-tuple-element.90.refs_3_), channel_id=1, source_target_pairs={{0,4},{4,0},{8,12},{12,8},{1,5},{5,1},{9,13},{13,9},{2,6},{6,2},{1... | collective-permute-start | bytes 1179656 | tf_op jit(solution)/shard_map/ppermute | solution.py:535
  297.6 19.1 %collective-permute-start.48 = (bf16[192,1024]{1,0:T(8,128)(2,1)S(1)}, bf16[192,1024]{1,0:T(8,128)(2,1)S(1)}, u32[]{:S(2)}, u32[]{:S(2)}) collective-permute-start(bf16[192,1024]{1,0:T(8,128)(2,1)S(1)} %get-tuple-element.89.refs_0_.refs_2_), channel_id=1, source_target_pairs={{0,1},{1,0},{2,3},{3,2},{4,5},{5,4},{6,7},{7,6},{8,9},{9,8},{10,11... | collective-permute-start | bytes 1179656 | tf_op jit(solution)/shard_map/ppermute | solution.py:415
  308.9 7.9 %collective-permute-start.50 = (bf16[192,1024]{1,0:T(8,128)(2,1)S(1)}, bf16[192,1024]{1,0:T(8,128)(2,1)S(1)}, u32[]{:S(2)}, u32[]{:S(2)}) collective-permute-start(bf16[192,1024]{1,0:T(8,128)(2,1)S(1)} %collective-permute-done.49), channel_id=1, source_target_pairs={{0,4},{4,0},{8,12},{12,8},{1,5},{5,1},{9,13},{13,9},{2,6},{6,2},{1... | collective-permute-start | bytes 1179656 | tf_op jit(solution)/shard_map/ppermute | solution.py:540
  320.7 2.5 collective-permute-start.52
  324.8 5.7 %collective-permute-start.55 = (bf16[192,512]{1,0:T(8,128)(2,1)S(1)}, bf16[192,512]{1,0:T(8,128)(2,1)S(1)}, u32[]{:S(2)}, u32[]{:S(2)}) collective-permute-start(bf16[192,512]{1,0:T(8,128)(2,1)S(1)} %filter_and_gate.7), channel_id=1, source_target_pairs={{0,3},{1,0},{2,1},{3,2},{4,7},{5,4},{6,5},{7,6},{8,11},{9,8},{10,9... | collective-permute-start | bytes 589832 | tf_op jit(solution)/shard_map/ppermute | solution.py:415
  327.0 16.9 %collective-permute-start.54 = (bf16[192,512]{1,0:T(8,128)(2,1)S(1)}, bf16[192,512]{1,0:T(8,128)(2,1)S(1)}, u32[]{:S(2)}, u32[]{:S(2)}) collective-permute-start(bf16[192,512]{1,0:T(8,128)(2,1)S(1)} %filter_and_gate.7), channel_id=1, source_target_pairs={{0,2},{1,3},{2,0},{3,1},{4,6},{5,7},{6,4},{7,5},{8,10},{9,11},{10,... | collective-permute-start | bytes 589832 | tf_op jit(solution)/shard_map/ppermute | solution.py:415
  327.1 16.8 %collective-permute-start.53 = (bf16[192,512]{1,0:T(8,128)(2,1)S(1)}, bf16[192,512]{1,0:T(8,128)(2,1)S(1)}, u32[]{:S(2)}, u32[]{:S(2)}) collective-permute-start(bf16[192,512]{1,0:T(8,128)(2,1)S(1)} %filter_and_gate.7), channel_id=1, source_target_pairs={{0,1},{1,2},{2,3},{3,0},{4,5},{5,6},{6,7},{7,4},{8,9},{9,10},{10,1... | collective-permute-start | bytes 589832 | tf_op jit(solution)/shard_map/ppermute | solution.py:415
  344.0 4.1 %collective-permute-start.56 = (bf16[4,192,512]{2,1,0:T(8,128)(2,1)S(1)}, bf16[4,192,512]{2,1,0:T(8,128)(2,1)S(1)}, u32[]{:S(2)}, u32[]{:S(2)}) collective-permute-start(bf16[4,192,512]{2,1,0:T(8,128)(2,1)S(1)} %pad_maximum_fusion.6.refs_0_), channel_id=1, source_target_pairs={{0,4},{4,0},{8,12},{12,8},{1,5},{5,1},{9,13},{13,9},{2,6},{6,2},{1... | collective-permute-start | bytes 2359304 | tf_op jit(solution)/shard_map/ppermute | solution.py:531
  351.2 1.8 collective-permute-start.57
  (25 other events, 199.9 us)
Sparse Core Ops, SparseCore 0:
  11.0 39.4 all-gather.1

commit v4 on v3

--- a/solution.py
+++ b/solution.py
@@ -108,7 +108,7 @@
     if mode == "last":
         earlier, earlier_square, refs = refs[0], refs[1], refs[2:]
     own_in, core_in = refs[:2]
-    weights, refs = [refs[2:6], refs[6:11]], refs[6 if sections == 1 else 11 :]
+    weights, refs = [refs[2:8], refs[8:13]], refs[8 if sections == 1 else 13 :]
     out_ref, out_ref2, hidden, held, total, held_sem = refs
     tokens, width = hidden.shape[1:]
     part = width // 2
@@ -122,9 +122,12 @@
         if kind in (OWN, CORE):
             source = own_in if kind == OWN else core_in
             halves = [(source.at[section, p, span(q)], span(q)) for q in range(2)]
-        elif len(sources) == 4:
-            mine, other = sources[:2] if kind == CHIP else sources[2:]
-            halves = [(mine.at[p], span(group)), (other.at[p], span(1 - group))]
+        elif len(sources) == 6:
+            if kind == BOTH:
+                mine, other, at = sources[4], sources[5], p
+            else:
+                mine, other, at = (sources[2], sources[3], 0) if p == 0 else (sources[0], sources[1], p - 1)
+            halves = [(mine.at[at], span(group)), (other.at[at], span(1 - group))]
         elif p == 0:
             source = sources[2 if kind == CHIP else 3]
             halves = [(source.at[q], span(q)) for q in range(2)]
@@ -474,33 +477,36 @@
     send = Rounds()
 
     whole = lax.all_gather(stream, "chan", axis=1, tiled=True)
-    send.now.append(whole)
-    out_a, all_a = taken(False, (((0, None), (1, None), (2, None)),), plan, in_weights, out_weights)
-    x_a = send(all_a, "ctx", CHIPS)
-    core_in = send(after(in_weights, all_a), "ctx", CORES)
+    runs = (((1, None), (2, None)), ((0, None),))
+    out_a, kv_a, q_a = taken(False, runs, plan, in_weights, out_weights)
+    x_kv = send(kv_a, "ctx", CHIPS)
+    x_q = lax.ppermute(q_a, "ctx", CHIPS)
+    core_in = send(after(in_weights, kv_a), "ctx", CORES)
     runs = (((1, None), (2, None)), ((0, 0), (0, 1)))
-    out_b, kv_b, q_b = taken(True, runs, after(plan, all_a), in_weights, out_weights)
-    bands = tap_bands(after(medium_taps, all_a))
+    out_b, kv_b, q_b = taken(True, runs, after(plan, kv_a), in_weights, out_weights)
+    bands = tap_bands(after(medium_taps, kv_a))
     send.now += [out_b, bands]
 
     send.turn()
-    y_a = send(x_a, "groups", GROUPS)
+    y_kv = send(x_kv, "groups", GROUPS)
     x_kv_b = send(kv_b, "ctx", CHIPS)
     shard_a = [out_a] + [send(out_a, PLANE, ALONG[k]) for k in (1, 2, 3)]
-    c_x = lax.ppermute(x_a, "ctx", CORES)
+    y_q = send(x_q, "groups", GROUPS)
+    send.now.append(whole)
+    c_x = lax.ppermute(jnp.concatenate([x_q, x_kv]), "ctx", CORES)
 
     send.turn()
     shard_a = jnp.stack(shard_a)
     cross_a = send(shard_a, PLANE, TO_OTHER_KEEPER)
     same_y = send(shard_a, EVERY, TO_KEEPER_OVER)
-    c_y = send(y_a, "ctx", CORES)
+    c_y = send(jnp.concatenate([y_q, y_kv]), "ctx", CORES)
     same_a = send(shard_a, PLANE, TO_KEEPER)
     shard_b = [out_b] + [send(after(out_b, c_y, same_a), PLANE, ALONG[k]) for k in (1, 2, 3)]
 
     send.turn()
     shard_b = jnp.stack(shard_b)
     cross_y = send.join(cross_a, EVERY, OTHER_KEEPERS_OVER)
-    weights_in = [[x_a, y_a, c_x, c_y]]
+    weights_in = [[x_kv, y_kv, x_q, y_q, c_x, c_y]]
     weights_out = [[shard_a, same_a, same_y, cross_a, cross_y]]
 
     own_hidden = lax.dynamic_slice_in_dim(whole, (2 * c + h) * width, width, 1)

time: 362 us -> 354 us (0.978)
  waiting for transfers between devices: 163 us -> 146 us
  starting transfers between devices: 95 us -> 102 us
    ppermute x39 -> x40, waiting for transfers between devices: 149 us -> 132 us  [join(): self.now.append(lax.ppermute(value, axes, pairs))]
    ppermute x39 -> x40, starting transfers between devices: 63.7 us -> 71.4 us  [join(): self.now.append(lax.ppermute(value, axes, pairs))]
    unnamed x61 -> x81, local copies, waits for them, and re-layouts: 18.6 us -> 21 us
  transfers between devices with their start and end apart: 59 -> 61, of which waited for: 33 -> 31; matrix products, arithmetic and copies ran while one was open for 4% -> 4% of each run, Pallas kernels for 9% -> 9%
where the time goes in v4:
time: 354 us; the launch traced here: 353 us
  waiting for transfers between devices  146 us (41%)
  starting transfers between devices  102 us (29%)
  Pallas kernels  56.4 us (16%)
  local copies, waits for them, and re-layouts  27.5 us (8%)
  between operations  14.1 us (4%)
  other arithmetic  7.16 us (2%)
    ppermute x40, waiting for transfers between devices, join(): self.now.append(lax.ppermute(value, axes, pairs))  132 us
    ppermute x40, starting transfers between devices, join(): self.now.append(lax.ppermute(value, axes, pairs))  71.4 us
    pallas_call x7, Pallas kernels, project_in(): pl.pallas_call(partial(in_kernel, mode, step, sections), out_shape=out, i...  29.3 us
    unnamed x81, local copies, waits for them, and re-layouts  21 us
    pallas_call x4, Pallas kernels, project_out(): pl.pallas_call(partial(out_kernel, step, sections), out_shape=(out, out),...  14.3 us
    ppermute x3, starting transfers between devices, shards(): lax.ppermute(beside_core, 'ctx', CORES)  8.56 us
    ppermute x4, starting transfers between devices, shards(): halo = lax.ppermute(mixed[-reach:], 'ctx', HALO)  8.31 us
    pallas_call x2, Pallas kernels, taken(): pl.pallas_call(partial(taken_kernel, second, runs), out_shape=tuple((jax....  7.15 us
  transfers between devices with their start and end apart: 61, of which 31 were waited for; matrix products, arithmetic and copies ran while one was open for 4% of the time, Pallas kernels for 9%

profile of v4, /device:TPU:0, one launch (start us, length us, event | category | flops | bytes accessed | tf_op | source)
XLA Modules:
  0.0 352.7 jit_solution(3520616826147520219)
XLA Ops:
  6.5 3.7 %taken.2 = (bf16[512,512]{1,0:T(8,128)(2,1)}, bf16[2,512,512]{2,1,0:T(8,128)(2,1)}, bf16[1,512,512]{2,1,0:T(8,128)(2,1)}) custom-call(s32[4]{0:T(128)} %plan.32, bf16[2,3,1024,512]{3,2,1,0:T(8,128)(2,1)} %bitcast.in_ref.refs_1_.refs_2_.refs_4_, bf16[2,1024,512]{2,1,0:T(8,128)(2,1)} %out_ref.3), custom_call_target="tpu_custom_call" | custom-call | tf_op jit(solution)/shard_map/taken/pallas_call | solution.py:391
  10.8 2.6 collective-permute-start.1
  15.4 5.1 %reshape.11 = bf16[32,64,255]{2,1,0:T(8,128)(2,1)} reshape(bf16[32,16320]{1,0:T(8,128)(2,1)} %bitcast.42) | data formatting | bytes 2088960 | tf_op jit(solution)/shard_map/reshape | solution.py:297
  22.1 3.5 taken.3
  26.4 11.2 %collective-permute-done.1.refs_3_.refs_4_.refs_6_ = bf16[2,512,512]{2,1,0:T(8,128)(2,1)S(1)} collective-permute-done((bf16[2,512,512]{2,1,0:T(8,128)(2,1)}, bf16[2,512,512]{2,1,0:T(8,128)(2,1)S(1)}, u32[]{:S(2)}, u32[]{:S(2)}) %collective-permute-start.1) | collective-permute-done | bytes 1048608 | tf_op jit(solution)/shard_map/ppermute | solution.py:418
  38.9 2.0 collective-permute-start.2
  42.4 4.5 %collective-permute-start.8 = (bf16[512,512]{1,0:T(8,128)(2,1)S(1)}, bf16[512,512]{1,0:T(8,128)(2,1)S(1)}, u32[]{:S(2)}, u32[]{:S(2)}) collective-permute-start(bf16[512,512]{1,0:T(8,128)(2,1)S(1)} %copy-done.38), channel_id=1, source_target_pairs={{2,0},{7,5},{0,2},{5,7},{10,8},{15,13},{8,10},{13,15},{18,16},{23,... | collective-permute-start | bytes 1572872 | tf_op jit(solution)/shard_map/ppermute | solution.py:418
  46.9 1.9 collective-permute-done.3.refs_5_.refs_6_.refs_8_
  50.1 5.7 %collective-permute-done.9 = bf16[512,512]{1,0:T(8,128)(2,1)S(1)} collective-permute-done((bf16[512,512]{1,0:T(8,128)(2,1)S(1)}, bf16[512,512]{1,0:T(8,128)(2,1)S(1)}, u32[]{:S(2)}, u32[]{:S(2)}) %collective-permute-start.9) | collective-permute-done | bytes 524320 | tf_op jit(solution)/shard_map/ppermute | solution.py:418
  57.3 15.2 %collective-permute-done.8 = bf16[512,512]{1,0:T(8,128)(2,1)S(1)} collective-permute-done((bf16[512,512]{1,0:T(8,128)(2,1)S(1)}, bf16[512,512]{1,0:T(8,128)(2,1)S(1)}, u32[]{:S(2)}, u32[]{:S(2)}) %collective-permute-start.8) | collective-permute-done | bytes 524320 | tf_op jit(solution)/shard_map/ppermute | solution.py:418
  72.5 1.7 pad_maximum_fusion.refs_4_
  75.2 6.9 %collective-permute-start.19 = (bf16[4,512,512]{2,1,0:T(8,128)(2,1)}, bf16[4,512,512]{2,1,0:T(8,128)(2,1)S(1)}, u32[]{:S(2)}, u32[]{:S(2)}) collective-permute-start(bf16[4,512,512]{2,1,0:T(8,128)(2,1)} %pad_maximum_fusion.refs_4_), channel_id=1, source_target_pairs={{0,8},{5,9},{2,10},{7,11},{8,4},{13,5},{10,6},{15,7},{16,24},{21,2... | collective-permute-start | bytes 6291464 | tf_op jit(solution)/shard_map/ppermute | solution.py:418
  85.6 3.4 collective-permute-start.18
  91.8 5.0 %collective-permute-start.27 = (bf16[512,512]{1,0:T(8,128)(2,1)S(1)}, bf16[512,512]{1,0:T(8,128)(2,1)S(1)}, u32[]{:S(2)}, u32[]{:S(2)}) collective-permute-start(bf16[512,512]{1,0:T(8,128)(2,1)S(1)} %copy-done.34), channel_id=1, source_target_pairs={{2,0},{7,5},{0,2},{5,7},{10,8},{15,13},{8,10},{13,15},{18,16},{23,... | collective-permute-start | bytes 1572872 | tf_op jit(solution)/shard_map/ppermute | solution.py:418
  100.4 5.6 %project_in_whole.1 = (bf16[192,512]{1,0:T(8,128)(2,1)S(1)}, bf16[192,512]{1,0:T(8,128)(2,1)S(1)}) custom-call(s32[4]{0:T(128)S(1)} %copy-done.35, bf16[192,4096]{1,0:T(8,128)(2,1)S(1)} %copy-done.32, bf16[2,3,1024,512]{3,2,1,0:T(8,128)(2,1)} %bitcast.in_ref.refs_1_.refs_2_.refs_4_, bf16[2,3,1024,512]{3,2,1,0:T(8,128)(2,1)} %collective-permute-done.refs_2_.refs_3_.refs_5_, ...), custom_call_target="tpu_custom_call" | custom-call | flops 2415919104 | bytes 12582912 | tf_op jit(solution)/shard_map/project_in_whole/pallas_call | solution.py:211
  106.0 2.1 collective-permute-start.11
  109.0 8.6 %collective-permute-done.27 = bf16[512,512]{1,0:T(8,128)(2,1)S(1)} collective-permute-done((bf16[512,512]{1,0:T(8,128)(2,1)S(1)}, bf16[512,512]{1,0:T(8,128)(2,1)S(1)}, u32[]{:S(2)}, u32[]{:S(2)}) %collective-permute-start.27) | collective-permute-done | bytes 524320 | tf_op jit(solution)/shard_map/ppermute | solution.py:418
  117.6 1.7 pad_maximum_fusion.1.refs_9_
  119.3 4.9 %collective-permute-start.29 = (bf16[4,512,512]{2,1,0:T(8,128)(2,1)}, bf16[4,512,512]{2,1,0:T(8,128)(2,1)}, u32[]{:S(2)}, u32[]{:S(2)}) collective-permute-start(bf16[4,512,512]{2,1,0:T(8,128)(2,1)} %pad_maximum_fusion.1.refs_9_), channel_id=1, source_target_pairs={{0,8},{5,9},{2,10},{7,11},{8,4},{13,5},{10,6},{15,7},{16,24},{21,2... | collective-permute-start | bytes 6291464 | tf_op jit(solution)/shard_map/ppermute | solution.py:418
  125.8 1.8 collective-permute-start.13
  127.6 1.9 collective-permute-start.12
  129.5 4.0 %collective-permute-done.14 = bf16[192,512]{1,0:T(8,128)(2,1)S(1)} collective-permute-done((bf16[192,512]{1,0:T(8,128)(2,1)S(1)}, bf16[192,512]{1,0:T(8,128)(2,1)S(1)}, u32[]{:S(2)}, u32[]{:S(2)}) %collective-permute-start.14) | collective-permute-done | bytes 196640 | tf_op jit(solution)/shard_map/ppermute | solution.py:418
  133.5 9.8 %collective-permute-done.13 = bf16[192,512]{1,0:T(8,128)(2,1)S(1)} collective-permute-done((bf16[192,512]{1,0:T(8,128)(2,1)S(1)}, bf16[192,512]{1,0:T(8,128)(2,1)S(1)}, u32[]{:S(2)}, u32[]{:S(2)}) %collective-permute-start.13) | collective-permute-done | bytes 196640 | tf_op jit(solution)/shard_map/ppermute | solution.py:418
  146.7 2.5 collective-permute-start.30
  150.5 1.7 collective-permute-done.16.refs_3_
  158.5 4.0 %project_out.4 = (bf16[192,1024]{1,0:T(8,128)(2,1)S(1)}, bf16[192,1024]{1,0:T(8,128)(2,1)S(1)}) custom-call(s32[4]{0:T(128)S(1)} %copy-done.35, bf16[4,192,512]{2,1,0:T(8,128)(2,1)} %pad_maximum_fusion.5.refs_0_, bf16[4,192,512]{2,1,0:T(8,128)(2,1)} %collective-permute-done.15.refs_1_, bf16[192,1024]{1,0:T(8,128)(2,1)S(1)} %get-tuple-element.102.refs_2_, ...), custom_call_target="tpu_custom_call" | custom-call | flops 1610612736 | bytes 4194304 | tf_op jit(solution)/shard_map/project_out/pallas_call | solution.py:350
  162.7 2.0 collective-permute-start.22
  164.7 6.7 %collective-permute-done.25.refs_11_.refs_13_ = bf16[2,512,512]{2,1,0:T(8,128)(2,1)S(1)} collective-permute-done((bf16[2,512,512]{2,1,0:T(8,128)(2,1)}, bf16[2,512,512]{2,1,0:T(8,128)(2,1)S(1)}, u32[]{:S(2)}, u32[]{:S(2)}) %collective-permute-start.25) | collective-permute-done | bytes 1048608 | tf_op jit(solution)/shard_map/ppermute | solution.py:418
  174.6 7.6 %collective-permute-done.22 = bf16[192,1024]{1,0:T(8,128)(2,1)S(1)} collective-permute-done((bf16[192,1024]{1,0:T(8,128)(2,1)S(1)}, bf16[192,1024]{1,0:T(8,128)(2,1)S(1)}, u32[]{:S(2)}, u32[]{:S(2)}) %collective-permute-start.22) | collective-permute-done | bytes 393248 | tf_op jit(solution)/shard_map/ppermute | solution.py:418
  182.7 3.1 collective-permute-start.39
  185.8 2.0 collective-permute-start.38
  188.3 2.0 collective-permute-start.40
  192.8 3.9 %project_in_first.3 = (f32[3,192,512]{2,1,0:T(8,128)S(1)}, f32[192,128]{1,0:T(8,128)S(1)}) custom-call(s32[4]{0:T(128)S(1)} %copy-done.35, bf16[192,1024]{1,0:T(8,128)(2,1)S(1)} %get-tuple-element.69.refs_0_.refs_2_, bf16[192,1024]{1,0:T(8,128)(2,1)S(1)} %collective-permute-done.24.refs_1_, bf16[2,3,1024,512]{3,2,1,0:T(8,128)(2,1)} %bitcast.in_ref.refs_1_.refs_2_.refs_4_, ...), custom_call_target="tpu_custom_call" | custom-call | flops 1207959552 | bytes 6291456 | tf_op jit(solution)/shard_map/project_in_first/pallas_call | solution.py:211
  196.8 4.2 %project_in_last.3 = (bf16[192,512]{1,0:T(8,128)(2,1)S(1)}, bf16[192,512]{1,0:T(8,128)(2,1)S(1)}) custom-call(s32[4]{0:T(128)S(1)} %copy-done.35, bf16[192,1024]{1,0:T(8,128)(2,1)S(1)} %collective-permute-done.21.refs_0_, bf16[192,1024]{1,0:T(8,128)(2,1)S(1)} %collective-permute-done.23.refs_1_, f32[3,192,512]{2,1,0:T(8,128)S(1)} %get-tuple-element.80.refs_2_, ...), custom_call_target="tpu_custom_call" | custom-call | flops 1207959552 | bytes 6291456 | tf_op jit(solution)/shard_map/project_in_last/pallas_call | solution.py:211
  201.0 2.0 collective-permute-start.33
  205.6 2.5 collective-permute-start.36
  208.3 5.1 %collective-permute-done.36 = bf16[192,512]{1,0:T(8,128)(2,1)S(1)} collective-permute-done((bf16[192,512]{1,0:T(8,128)(2,1)S(1)}, bf16[192,512]{1,0:T(8,128)(2,1)S(1)}, u32[]{:S(2)}, u32[]{:S(2)}) %collective-permute-start.36) | collective-permute-done | bytes 196640 | tf_op jit(solution)/shard_map/ppermute | solution.py:418
  213.4 2.0 collective-permute-start.34
  215.4 10.6 %collective-permute-done.35 = bf16[192,512]{1,0:T(8,128)(2,1)S(1)} collective-permute-done((bf16[192,512]{1,0:T(8,128)(2,1)S(1)}, bf16[192,512]{1,0:T(8,128)(2,1)S(1)}, u32[]{:S(2)}, u32[]{:S(2)}) %collective-permute-start.35) | collective-permute-done | bytes 196640 | tf_op jit(solution)/shard_map/ppermute | solution.py:418
  226.7 1.7 collective-permute-done.39.refs_11_
  230.2 3.0 project_out.5
  234.8 3.2 collective-permute-start.44
  238.1 1.7 collective-permute-start.41
  239.7 2.1 collective-permute-done.42
  241.8 7.3 %collective-permute-start.43 = (bf16[192,1024]{1,0:T(8,128)(2,1)S(1)}, bf16[192,1024]{1,0:T(8,128)(2,1)S(1)}, u32[]{:S(2)}, u32[]{:S(2)}) collective-permute-start(bf16[192,1024]{1,0:T(8,128)(2,1)S(1)} %collective-permute-done.42), channel_id=1, source_target_pairs={{0,4},{4,0},{8,12},{12,8},{1,5},{5,1},{9,13},{13,9},{2,6},{6,2},{1... | collective-permute-start | bytes 1179656 | tf_op jit(solution)/shard_map/ppermute | solution.py:546
  249.1 3.9 %project_in_first.4 = (f32[3,192,512]{2,1,0:T(8,128)S(1)}, f32[192,128]{1,0:T(8,128)S(1)}) custom-call(s32[4]{0:T(128)S(1)} %copy-done.35, bf16[192,1024]{1,0:T(8,128)(2,1)S(1)} %get-tuple-element.87.refs_0_.refs_2_, bf16[192,1024]{1,0:T(8,128)(2,1)S(1)} %collective-permute-done.44.refs_1_, bf16[2,3,1024,512]{3,2,1,0:T(8,128)(2,1)} %bitcast.in_ref.refs_1_.refs_2_.refs_4_, ...), custom_call_target="tpu_custom_call" | custom-call | flops 1207959552 | bytes 6291456 | tf_op jit(solution)/shard_map/project_in_first/pallas_call | solution.py:211
  253.0 3.9 %project_in_last.4 = (bf16[192,512]{1,0:T(8,128)(2,1)S(1)}, bf16[192,512]{1,0:T(8,128)(2,1)S(1)}) custom-call(s32[4]{0:T(128)S(1)} %copy-done.35, bf16[192,1024]{1,0:T(8,128)(2,1)S(1)} %collective-permute-done.41.refs_0_, bf16[192,1024]{1,0:T(8,128)(2,1)S(1)} %collective-permute-done.43.refs_1_, f32[3,192,512]{2,1,0:T(8,128)S(1)} %get-tuple-element.89.refs_2_, ...), custom_call_target="tpu_custom_call" | custom-call | flops 1207959552 | bytes 6291456 | tf_op jit(solution)/shard_map/project_in_last/pallas_call | solution.py:211
  256.9 2.6 collective-permute-start.45
  261.6 2.3 collective-permute-start.48
  267.6 12.5 %collective-permute-done.47 = bf16[192,512]{1,0:T(8,128)(2,1)S(1)} collective-permute-done((bf16[192,512]{1,0:T(8,128)(2,1)S(1)}, bf16[192,512]{1,0:T(8,128)(2,1)S(1)}, u32[]{:S(2)}, u32[]{:S(2)}) %collective-permute-start.47) | collective-permute-done | bytes 196640 | tf_op jit(solution)/shard_map/ppermute | solution.py:418
  280.2 2.9 collective-permute-start.49
  283.1 1.9 collective-permute-done.49.refs_1_
  285.0 4.2 %project_out.6 = (bf16[192,1024]{1,0:T(8,128)(2,1)S(1)}, bf16[192,1024]{1,0:T(8,128)(2,1)S(1)}) custom-call(s32[4]{0:T(128)S(1)} %copy-done.35, bf16[4,192,512]{2,1,0:T(8,128)(2,1)S(1)} %pad_maximum_fusion.7.refs_0_, bf16[4,192,512]{2,1,0:T(8,128)(2,1)S(1)} %collective-permute-done.49.refs_1_, bf16[192,1024]{1,0:T(8,128)(2,1)S(1)} %get-tuple-element.87.refs_0_.refs_2_, ...), custom_call_target="tpu_custom_call" | custom-call | flops 1610612736 | bytes 4194304 | tf_op jit(solution)/shard_map/project_out/pallas_call | solution.py:350
  291.4 9.8 %collective-permute-done.51 = bf16[192,1024]{1,0:T(8,128)(2,1)S(1)} collective-permute-done((bf16[192,1024]{1,0:T(8,128)(2,1)S(1)}, bf16[192,1024]{1,0:T(8,128)(2,1)S(1)}, u32[]{:S(2)}, u32[]{:S(2)}) %collective-permute-start.51) | collective-permute-done | bytes 393248 | tf_op jit(solution)/shard_map/ppermute | solution.py:418
  301.2 3.9 %project_in_first.5 = (f32[3,192,512]{2,1,0:T(8,128)S(1)}, f32[192,128]{1,0:T(8,128)S(1)}) custom-call(s32[4]{0:T(128)S(1)} %copy-done.35, bf16[192,1024]{1,0:T(8,128)(2,1)S(1)} %get-tuple-element.93.refs_0_.refs_2_, bf16[192,1024]{1,0:T(8,128)(2,1)S(1)} %collective-permute-done.53.refs_1_, bf16[2,3,1024,512]{3,2,1,0:T(8,128)(2,1)} %bitcast.in_ref.refs_1_.refs_2_.refs_4_, ...), custom_call_target="tpu_custom_call" | custom-call | flops 1207959552 | bytes 6291456 | tf_op jit(solution)/shard_map/project_in_first/pallas_call | solution.py:211
  305.1 4.0 %collective-permute-done.50.refs_0_ = bf16[192,1024]{1,0:T(8,128)(2,1)S(1)} collective-permute-done((bf16[192,1024]{1,0:T(8,128)(2,1)S(1)}, bf16[192,1024]{1,0:T(8,128)(2,1)S(1)}, u32[]{:S(2)}, u32[]{:S(2)}) %collective-permute-start.50) | collective-permute-done | bytes 393248 | tf_op jit(solution)/shard_map/ppermute | solution.py:418
  309.1 3.9 %project_in_last.5 = (bf16[192,512]{1,0:T(8,128)(2,1)S(1)}, bf16[192,512]{1,0:T(8,128)(2,1)S(1)}) custom-call(s32[4]{0:T(128)S(1)} %copy-done.35, bf16[192,1024]{1,0:T(8,128)(2,1)S(1)} %collective-permute-done.50.refs_0_, bf16[192,1024]{1,0:T(8,128)(2,1)S(1)} %collective-permute-done.52.refs_1_, f32[3,192,512]{2,1,0:T(8,128)S(1)} %get-tuple-element.95.refs_2_, ...), custom_call_target="tpu_custom_call" | custom-call | flops 1207959552 | bytes 6291456 | tf_op jit(solution)/shard_map/project_in_last/pallas_call | solution.py:211
  317.1 2.2 collective-permute-start.57
  319.4 1.9 collective-permute-start.55
  321.4 1.8 collective-permute-done.57
  323.2 13.2 %collective-permute-done.56 = bf16[192,512]{1,0:T(8,128)(2,1)S(1)} collective-permute-done((bf16[192,512]{1,0:T(8,128)(2,1)S(1)}, bf16[192,512]{1,0:T(8,128)(2,1)S(1)}, u32[]{:S(2)}, u32[]{:S(2)}) %collective-permute-start.56) | collective-permute-done | bytes 196640 | tf_op jit(solution)/shard_map/ppermute | solution.py:418
  336.5 1.8 collective-permute-start.58
  338.3 1.9 collective-permute-done.58.refs_1_
  340.3 3.0 project_out.7
  (179 shorter events, 63.2 us)
Async XLA Ops:
  6.5 67.7 %all-gather.2.cloned.1.call-start = ((), (), s32[]{:S(2)}) async-start(), calls=%async_computation | async-start | bytes 1966080 | tf_op jit(solution)/shard_map/all_gather | solution.py:479
  10.2 27.3 %collective-permute-start = (bf16[2,3,1024,512]{3,2,1,0:T(8,128)(2,1)}, bf16[2,3,1024,512]{3,2,1,0:T(8,128)(2,1)}, u32[]{:S(2)}, u32[]{:S(2)}) collective-permute-start(bf16[2,3,1024,512]{3,2,1,0:T(8,128)(2,1)} %bitcast.in_ref.refs_1_.refs_2_.refs_4_), channel_id=1, source_target_pairs={{0,4},{4,0},{8,12},{12,8},{1,5},{5,1},{9,13},{13,9},{2,6},{6,2},{1... | collective-permute-start | bytes 18874376 | tf_op jit(solution)/shard_map/ppermute | solution.py:418
  10.8 26.8 %collective-permute-start.1 = (bf16[2,512,512]{2,1,0:T(8,128)(2,1)}, bf16[2,512,512]{2,1,0:T(8,128)(2,1)S(1)}, u32[]{:S(2)}, u32[]{:S(2)}) collective-permute-start(bf16[2,512,512]{2,1,0:T(8,128)(2,1)} %get-tuple-element.53), channel_id=1, source_target_pairs={{0,8},{4,12},{8,0},{12,4},{1,9},{5,13},{9,1},{13,5},{2,10},{6,14},... | collective-permute-start | bytes 3145736 | tf_op jit(solution)/shard_map/ppermute | solution.py:418
  13.4 35.5 %collective-permute-start.3 = (bf16[1,512,512]{2,1,0:T(8,128)(2,1)}, bf16[1,512,512]{2,1,0:T(8,128)(2,1)S(1)}, u32[]{:S(2)}, u32[]{:S(2)}) collective-permute-start(bf16[1,512,512]{2,1,0:T(8,128)(2,1)} %get-tuple-element.59), channel_id=1, source_target_pairs={{0,8},{4,12},{8,0},{12,4},{1,9},{5,13},{9,1},{13,5},{2,10},{6,14},... | collective-permute-start | bytes 1572872 | tf_op jit(solution)/shard_map/ppermute | solution.py:483
  37.6 46.4 %copy-start.2 = (bf16[2,512,512]{2,1,0:T(8,128)(2,1)}, bf16[2,512,512]{2,1,0:T(8,128)(2,1)S(1)}, u32[]{:S(2)}) copy-start(bf16[2,512,512]{2,1,0:T(8,128)(2,1)S(1)} %collective-permute-done.1.refs_3_.refs_4_.refs_6_) | copy-start | bytes 3145732
  37.6 18.3 %collective-permute-start.9 = (bf16[512,512]{1,0:T(8,128)(2,1)S(1)}, bf16[512,512]{1,0:T(8,128)(2,1)S(1)}, u32[]{:S(2)}, u32[]{:S(2)}) collective-permute-start(bf16[512,512]{1,0:T(8,128)(2,1)S(1)} %copy-done.38), channel_id=1, source_target_pairs={{1,0},{6,5},{3,2},{4,7},{9,8},{14,13},{11,10},{12,15},{17,16},{22,... | collective-permute-start | bytes 1572872 | tf_op jit(solution)/shard_map/ppermute | solution.py:418
  38.9 35.3 %collective-permute-start.2 = (bf16[2,512,512]{2,1,0:T(8,128)(2,1)S(1)}, bf16[2,512,512]{2,1,0:T(8,128)(2,1)S(1)}, u32[]{:S(2)}, u32[]{:S(2)}) collective-permute-start(bf16[2,512,512]{2,1,0:T(8,128)(2,1)S(1)} %collective-permute-done.1.refs_3_.refs_4_.refs_6_), channel_id=1, source_target_pairs={{0,16},{16,0},{1,17},{17,1},{2,18},{18,2},{3,19},{19,3},{4,20},{20... | collective-permute-start | bytes 3145736 | tf_op jit(solution)/shard_map/ppermute | solution.py:418
  40.9 33.3 %collective-permute-start.6 = (bf16[2,512,512]{2,1,0:T(8,128)(2,1)}, bf16[2,512,512]{2,1,0:T(8,128)(2,1)}, u32[]{:S(2)}, u32[]{:S(2)}) collective-permute-start(bf16[2,512,512]{2,1,0:T(8,128)(2,1)} %get-tuple-element.62), channel_id=1, source_target_pairs={{0,8},{4,12},{8,0},{12,4},{1,9},{5,13},{9,1},{13,5},{2,10},{6,14},... | collective-permute-start | bytes 3145736 | tf_op jit(solution)/shard_map/ppermute | solution.py:418
  42.4 30.1 %collective-permute-start.8 = (bf16[512,512]{1,0:T(8,128)(2,1)S(1)}, bf16[512,512]{1,0:T(8,128)(2,1)S(1)}, u32[]{:S(2)}, u32[]{:S(2)}) collective-permute-start(bf16[512,512]{1,0:T(8,128)(2,1)S(1)} %copy-done.38), channel_id=1, source_target_pairs={{2,0},{7,5},{0,2},{5,7},{10,8},{15,13},{8,10},{13,15},{18,16},{23,... | collective-permute-start | bytes 1572872 | tf_op jit(solution)/shard_map/ppermute | solution.py:418
  48.8 23.7 %collective-permute-start.7 = (bf16[512,512]{1,0:T(8,128)(2,1)S(1)}, bf16[512,512]{1,0:T(8,128)(2,1)S(1)}, u32[]{:S(2)}, u32[]{:S(2)}) collective-permute-start(bf16[512,512]{1,0:T(8,128)(2,1)S(1)} %copy-done.38), channel_id=1, source_target_pairs={{3,0},{4,5},{1,2},{6,7},{11,8},{12,13},{9,10},{14,15},{19,16},{20,... | collective-permute-start | bytes 1572872 | tf_op jit(solution)/shard_map/ppermute | solution.py:418
  55.8 18.4 %collective-permute-start.4 = (bf16[1,512,512]{2,1,0:T(8,128)(2,1)S(1)}, bf16[1,512,512]{2,1,0:T(8,128)(2,1)S(1)}, u32[]{:S(2)}, u32[]{:S(2)}) collective-permute-start(bf16[1,512,512]{2,1,0:T(8,128)(2,1)S(1)} %collective-permute-done.3.refs_5_.refs_6_.refs_8_), channel_id=1, source_target_pairs={{0,16},{16,0},{1,17},{17,1},{2,18},{18,2},{3,19},{19,3},{4,20},{20... | collective-permute-start | bytes 1572872 | tf_op jit(solution)/shard_map/ppermute | solution.py:418
  74.2 14.8 %collective-permute-start.17 = (bf16[4,512,512]{2,1,0:T(8,128)(2,1)}, bf16[4,512,512]{2,1,0:T(8,128)(2,1)S(1)}, u32[]{:S(2)}, u32[]{:S(2)}) collective-permute-start(bf16[4,512,512]{2,1,0:T(8,128)(2,1)} %pad_maximum_fusion.refs_4_), channel_id=1, source_target_pairs={{5,1},{7,3},{8,12},{10,14},{21,17},{23,19},{24,28},{26,30}} | collective-permute-start | bytes 6291464 | tf_op jit(solution)/shard_map/ppermute | solution.py:418
  75.2 30.9 %collective-permute-start.19 = (bf16[4,512,512]{2,1,0:T(8,128)(2,1)}, bf16[4,512,512]{2,1,0:T(8,128)(2,1)S(1)}, u32[]{:S(2)}, u32[]{:S(2)}) collective-permute-start(bf16[4,512,512]{2,1,0:T(8,128)(2,1)} %pad_maximum_fusion.refs_4_), channel_id=1, source_target_pairs={{0,8},{5,9},{2,10},{7,11},{8,4},{13,5},{10,6},{15,7},{16,24},{21,2... | collective-permute-start | bytes 6291464 | tf_op jit(solution)/shard_map/ppermute | solution.py:418
  84.0 5.0 %collective-permute-start.10 = (bf16[3,512,512]{2,1,0:T(8,128)(2,1)S(1)}, bf16[3,512,512]{2,1,0:T(8,128)(2,1)S(1)}, u32[]{:S(2)}, u32[]{:S(2)}) collective-permute-start(bf16[3,512,512]{2,1,0:T(8,128)(2,1)S(1)} %pad_maximum_fusion.4), channel_id=1, source_target_pairs={{0,4},{4,0},{8,12},{12,8},{1,5},{5,1},{9,13},{13,9},{2,6},{6,2},{1... | collective-permute-start | bytes 4718600 | tf_op jit(solution)/shard_map/ppermute | solution.py:418
  84.2 12.6 %collective-permute-start.5 = (bf16[3,512,512]{2,1,0:T(8,128)(2,1)S(1)}, bf16[3,512,512]{2,1,0:T(8,128)(2,1)S(1)}, u32[]{:S(2)}, u32[]{:S(2)}) collective-permute-start(bf16[3,512,512]{2,1,0:T(8,128)(2,1)S(1)} %pad_maximum_fusion.3), channel_id=1, source_target_pairs={{0,4},{4,0},{8,12},{12,8},{1,5},{5,1},{9,13},{13,9},{2,6},{6,2},{1... | collective-permute-start | bytes 4718600 | tf_op jit(solution)/shard_map/ppermute | solution.py:496
  85.6 33.7 %collective-permute-start.18 = (bf16[4,512,512]{2,1,0:T(8,128)(2,1)S(1)}, bf16[4,512,512]{2,1,0:T(8,128)(2,1)S(1)}, u32[]{:S(2)}, u32[]{:S(2)}) collective-permute-start(bf16[4,512,512]{2,1,0:T(8,128)(2,1)S(1)} %copy-done.8), channel_id=1, source_target_pairs={{0,16},{16,0},{5,17},{21,1},{2,18},{18,2},{7,19},{23,3},{8,28},{24... | collective-permute-start | bytes 6291464 | tf_op jit(solution)/shard_map/ppermute | solution.py:418
  90.5 17.7 %collective-permute-start.28 = (bf16[512,512]{1,0:T(8,128)(2,1)S(1)}, bf16[512,512]{1,0:T(8,128)(2,1)S(1)}, u32[]{:S(2)}, u32[]{:S(2)}) collective-permute-start(bf16[512,512]{1,0:T(8,128)(2,1)S(1)} %copy-done.34), channel_id=1, source_target_pairs={{1,0},{6,5},{3,2},{4,7},{9,8},{14,13},{11,10},{12,15},{17,16},{22,... | collective-permute-start | bytes 1572872 | tf_op jit(solution)/shard_map/ppermute | solution.py:418
  91.8 25.8 %collective-permute-start.27 = (bf16[512,512]{1,0:T(8,128)(2,1)S(1)}, bf16[512,512]{1,0:T(8,128)(2,1)S(1)}, u32[]{:S(2)}, u32[]{:S(2)}) collective-permute-start(bf16[512,512]{1,0:T(8,128)(2,1)S(1)} %copy-done.34), channel_id=1, source_target_pairs={{2,0},{7,5},{0,2},{5,7},{10,8},{15,13},{8,10},{13,15},{18,16},{23,... | collective-permute-start | bytes 1572872 | tf_op jit(solution)/shard_map/ppermute | solution.py:418
  96.8 20.8 %collective-permute-start.26 = (bf16[512,512]{1,0:T(8,128)(2,1)S(1)}, bf16[512,512]{1,0:T(8,128)(2,1)S(1)}, u32[]{:S(2)}, u32[]{:S(2)}) collective-permute-start(bf16[512,512]{1,0:T(8,128)(2,1)S(1)} %copy-done.34), channel_id=1, source_target_pairs={{3,0},{4,5},{1,2},{6,7},{11,8},{12,13},{9,10},{14,15},{19,16},{20,... | collective-permute-start | bytes 1572872 | tf_op jit(solution)/shard_map/ppermute | solution.py:418
  106.0 13.2 %collective-permute-start.11 = (bf16[128,512]{1,0:T(8,128)(2,1)S(1)}, bf16[128,512]{1,0:T(8,128)(2,1)S(1)}, u32[]{:S(2)}, u32[]{:S(2)}) collective-permute-start(bf16[128,512]{1,0:T(8,128)(2,1)S(1)} %slice.20), channel_id=1, source_target_pairs={{0,4},{4,8},{8,12},{1,5},{5,9},{9,13},{2,6},{6,10},{10,14},{3,7},{... | collective-permute-start | bytes 393224 | tf_op jit(solution)/shard_map/ppermute | solution.py:524
  108.2 36.1 %collective-permute-start.20 = (bf16[4,512,512]{2,1,0:T(8,128)(2,1)S(1)}, bf16[4,512,512]{2,1,0:T(8,128)(2,1)S(1)}, u32[]{:S(2)}, u32[]{:S(2)}) collective-permute-start(bf16[4,512,512]{2,1,0:T(8,128)(2,1)S(1)} %collective-permute-done.19.refs_7_), channel_id=1, source_target_pairs={{8,24},{24,8},{9,25},{25,9},{10,26},{26,10},{11,27},{27,11},{4,20}... | collective-permute-start | bytes 6291464 | tf_op jit(solution)/shard_map/ppermute | solution.py:418
  119.3 27.4 %collective-permute-start.29 = (bf16[4,512,512]{2,1,0:T(8,128)(2,1)}, bf16[4,512,512]{2,1,0:T(8,128)(2,1)}, u32[]{:S(2)}, u32[]{:S(2)}) collective-permute-start(bf16[4,512,512]{2,1,0:T(8,128)(2,1)} %pad_maximum_fusion.1.refs_9_), channel_id=1, source_target_pairs={{0,8},{5,9},{2,10},{7,11},{8,4},{13,5},{10,6},{15,7},{16,24},{21,2... | collective-permute-start | bytes 6291464 | tf_op jit(solution)/shard_map/ppermute | solution.py:418
  125.7 7.8 %collective-permute-start.14 = (bf16[192,512]{1,0:T(8,128)(2,1)S(1)}, bf16[192,512]{1,0:T(8,128)(2,1)S(1)}, u32[]{:S(2)}, u32[]{:S(2)}) collective-permute-start(bf16[192,512]{1,0:T(8,128)(2,1)S(1)} %filter_and_gate.4), channel_id=1, source_target_pairs={{0,3},{1,0},{2,1},{3,2},{4,7},{5,4},{6,5},{7,6},{8,11},{9,8},{10,9... | collective-permute-start | bytes 589832 | tf_op jit(solution)/shard_map/ppermute | solution.py:418
  125.8 17.6 %collective-permute-start.13 = (bf16[192,512]{1,0:T(8,128)(2,1)S(1)}, bf16[192,512]{1,0:T(8,128)(2,1)S(1)}, u32[]{:S(2)}, u32[]{:S(2)}) collective-permute-start(bf16[192,512]{1,0:T(8,128)(2,1)S(1)} %filter_and_gate.4), channel_id=1, source_target_pairs={{0,2},{1,3},{2,0},{3,1},{4,6},{5,7},{6,4},{7,5},{8,10},{9,11},{10,... | collective-permute-start | bytes 589832 | tf_op jit(solution)/shard_map/ppermute | solution.py:418
  127.6 15.7 %collective-permute-start.12 = (bf16[192,512]{1,0:T(8,128)(2,1)S(1)}, bf16[192,512]{1,0:T(8,128)(2,1)S(1)}, u32[]{:S(2)}, u32[]{:S(2)}) collective-permute-start(bf16[192,512]{1,0:T(8,128)(2,1)S(1)} %filter_and_gate.4), channel_id=1, source_target_pairs={{0,1},{1,2},{2,3},{3,0},{4,5},{5,6},{6,7},{7,4},{8,9},{9,10},{10,1... | collective-permute-start | bytes 589832 | tf_op jit(solution)/shard_map/ppermute | solution.py:418
  144.3 7.9 %collective-permute-start.15 = (bf16[4,192,512]{2,1,0:T(8,128)(2,1)}, bf16[4,192,512]{2,1,0:T(8,128)(2,1)}, u32[]{:S(2)}, u32[]{:S(2)}) collective-permute-start(bf16[4,192,512]{2,1,0:T(8,128)(2,1)} %pad_maximum_fusion.5.refs_0_), channel_id=1, source_target_pairs={{0,4},{4,0},{8,12},{12,8},{1,5},{5,1},{9,13},{13,9},{2,6},{6,2},{1... | collective-permute-start | bytes 2359304 | tf_op jit(solution)/shard_map/ppermute | solution.py:537
  145.6 25.8 %collective-permute-start.25 = (bf16[2,512,512]{2,1,0:T(8,128)(2,1)}, bf16[2,512,512]{2,1,0:T(8,128)(2,1)S(1)}, u32[]{:S(2)}, u32[]{:S(2)}) collective-permute-start(bf16[2,512,512]{2,1,0:T(8,128)(2,1)} %collective-permute-done.6.refs_10_.refs_12_), channel_id=1, source_target_pairs={{0,16},{16,0},{1,17},{17,1},{2,18},{18,2},{3,19},{19,3},{4,20},{20... | collective-permute-start | bytes 3145736 | tf_op jit(solution)/shard_map/ppermute | solution.py:418
  146.7 25.7 %collective-permute-start.30 = (bf16[2,512,512]{2,1,0:T(8,128)(2,1)}, bf16[2,512,512]{2,1,0:T(8,128)(2,1)}, u32[]{:S(2)}, u32[]{:S(2)}) collective-permute-start(bf16[2,512,512]{2,1,0:T(8,128)(2,1)} %get-tuple-element.77), channel_id=1, source_target_pairs={{0,8},{4,12},{8,0},{12,4},{1,9},{5,13},{9,1},{13,5},{2,10},{6,14},... | collective-permute-start | bytes 3145736 | tf_op jit(solution)/shard_map/ppermute | solution.py:418
  150.4 1.8 collective-permute-start.16
  162.6 12.0 %collective-permute-start.21 = (bf16[192,1024]{1,0:T(8,128)(2,1)S(1)}, bf16[192,1024]{1,0:T(8,128)(2,1)S(1)}, u32[]{:S(2)}, u32[]{:S(2)}) collective-permute-start(bf16[192,1024]{1,0:T(8,128)(2,1)S(1)} %get-tuple-element.69.refs_0_.refs_2_), channel_id=1, source_target_pairs={{0,1},{1,0},{2,3},{3,2},{4,5},{5,4},{6,7},{7,6},{8,9},{9,8},{10,11... | collective-permute-start | bytes 1179656 | tf_op jit(solution)/shard_map/ppermute | solution.py:418
  162.7 19.5 %collective-permute-start.22 = (bf16[192,1024]{1,0:T(8,128)(2,1)S(1)}, bf16[192,1024]{1,0:T(8,128)(2,1)S(1)}, u32[]{:S(2)}, u32[]{:S(2)}) collective-permute-start(bf16[192,1024]{1,0:T(8,128)(2,1)S(1)} %get-tuple-element.70.refs_3_), channel_id=1, source_target_pairs={{0,1},{1,0},{2,3},{3,2},{4,5},{5,4},{6,7},{7,6},{8,9},{9,8},{10,11... | collective-permute-start | bytes 1179656 | tf_op jit(solution)/shard_map/ppermute | solution.py:418
  182.2 9.3 %collective-permute-start.31 = (bf16[4,512,512]{2,1,0:T(8,128)(2,1)S(1)}, bf16[4,512,512]{2,1,0:T(8,128)(2,1)S(1)}, u32[]{:S(2)}, u32[]{:S(2)}) collective-permute-start(bf16[4,512,512]{2,1,0:T(8,128)(2,1)S(1)} %pad_maximum_fusion.2), channel_id=1, source_target_pairs={{0,4},{4,0},{8,12},{12,8},{1,5},{5,1},{9,13},{13,9},{2,6},{6,2},{1... | collective-permute-start | bytes 6291464 | tf_op jit(solution)/shard_map/ppermute | solution.py:418
  182.2 6.1 %collective-permute-start.32 = (bf16[2,512,512]{2,1,0:T(8,128)(2,1)}, bf16[2,512,512]{2,1,0:T(8,128)(2,1)S(1)}, u32[]{:S(2)}, u32[]{:S(2)}) collective-permute-start(bf16[2,512,512]{2,1,0:T(8,128)(2,1)} %collective-permute-done.6.refs_10_.refs_12_), channel_id=1, source_target_pairs={{0,4},{4,0},{8,12},{12,8},{1,5},{5,1},{9,13},{13,9},{2,6},{6,2},{1... | collective-permute-start | bytes 3145736 | tf_op jit(solution)/shard_map/ppermute | solution.py:526
  182.7 7.5 %collective-permute-start.24 = (bf16[192,1024]{1,0:T(8,128)(2,1)S(1)}, bf16[192,1024]{1,0:T(8,128)(2,1)S(1)}, u32[]{:S(2)}, u32[]{:S(2)}) collective-permute-start(bf16[192,1024]{1,0:T(8,128)(2,1)S(1)} %get-tuple-element.70.refs_3_), channel_id=1, source_target_pairs={{0,4},{4,0},{8,12},{12,8},{1,5},{5,1},{9,13},{13,9},{2,6},{6,2},{1... | collective-permute-start | bytes 1179656 | tf_op jit(solution)/shard_map/ppermute | solution.py:541
  182.7 45.7 %collective-permute-start.39 = (bf16[4,512,512]{2,1,0:T(8,128)(2,1)}, bf16[4,512,512]{2,1,0:T(8,128)(2,1)}, u32[]{:S(2)}, u32[]{:S(2)}) collective-permute-start(bf16[4,512,512]{2,1,0:T(8,128)(2,1)} %pad_maximum_fusion.1.refs_9_), channel_id=1, source_target_pairs={{0,16},{16,0},{5,17},{21,1},{2,18},{18,2},{7,19},{23,3},{8,28},{24... | collective-permute-start | bytes 6291464 | tf_op jit(solution)/shard_map/ppermute | solution.py:535
  185.8 42.6 %collective-permute-start.38 = (bf16[4,512,512]{2,1,0:T(8,128)(2,1)}, bf16[4,512,512]{2,1,0:T(8,128)(2,1)}, u32[]{:S(2)}, u32[]{:S(2)}) collective-permute-start(bf16[4,512,512]{2,1,0:T(8,128)(2,1)} %pad_maximum_fusion.1.refs_9_), channel_id=1, source_target_pairs={{5,1},{7,3},{8,12},{10,14},{21,17},{23,19},{24,28},{26,30}} | collective-permute-start | bytes 6291464 | tf_op jit(solution)/shard_map/ppermute | solution.py:418
  188.3 40.1 %collective-permute-start.40 = (bf16[4,512,512]{2,1,0:T(8,128)(2,1)}, bf16[4,512,512]{2,1,0:T(8,128)(2,1)}, u32[]{:S(2)}, u32[]{:S(2)}) collective-permute-start(bf16[4,512,512]{2,1,0:T(8,128)(2,1)} %collective-permute-done.29.refs_12_), channel_id=1, source_target_pairs={{8,24},{24,8},{9,25},{25,9},{10,26},{26,10},{11,27},{27,11},{4,20}... | collective-permute-start | bytes 6291464 | tf_op jit(solution)/shard_map/ppermute | solution.py:418
  190.2 6.5 %collective-permute-start.23 = (bf16[192,1024]{1,0:T(8,128)(2,1)S(1)}, bf16[192,1024]{1,0:T(8,128)(2,1)S(1)}, u32[]{:S(2)}, u32[]{:S(2)}) collective-permute-start(bf16[192,1024]{1,0:T(8,128)(2,1)S(1)} %collective-permute-done.22), channel_id=1, source_target_pairs={{0,4},{4,0},{8,12},{12,8},{1,5},{5,1},{9,13},{13,9},{2,6},{6,2},{1... | collective-permute-start | bytes 1179656 | tf_op jit(solution)/shard_map/ppermute | solution.py:546
  196.7 31.9 %copy-start.14 = (bf16[4,512,512]{2,1,0:T(8,128)(2,1)S(1)}, bf16[4,512,512]{2,1,0:T(8,128)(2,1)}, u32[]{:S(2)}) copy-start(bf16[4,512,512]{2,1,0:T(8,128)(2,1)} %copy-done.12) | copy-start | bytes 6291460
  196.7 31.8 %copy-start.17 = (bf16[4,512,512]{2,1,0:T(8,128)(2,1)S(1)}, bf16[4,512,512]{2,1,0:T(8,128)(2,1)}, u32[]{:S(2)}) copy-start(bf16[4,512,512]{2,1,0:T(8,128)(2,1)} %copy-done.15) | copy-start | bytes 6291460
  201.0 3.0 collective-permute-start.33
  205.6 7.8 %collective-permute-start.36 = (bf16[192,512]{1,0:T(8,128)(2,1)S(1)}, bf16[192,512]{1,0:T(8,128)(2,1)S(1)}, u32[]{:S(2)}, u32[]{:S(2)}) collective-permute-start(bf16[192,512]{1,0:T(8,128)(2,1)S(1)} %filter_and_gate.5), channel_id=1, source_target_pairs={{0,3},{1,0},{2,1},{3,2},{4,7},{5,4},{6,5},{7,6},{8,11},{9,8},{10,9... | collective-permute-start | bytes 589832 | tf_op jit(solution)/shard_map/ppermute | solution.py:418
  208.0 18.0 %collective-permute-start.35 = (bf16[192,512]{1,0:T(8,128)(2,1)S(1)}, bf16[192,512]{1,0:T(8,128)(2,1)S(1)}, u32[]{:S(2)}, u32[]{:S(2)}) collective-permute-start(bf16[192,512]{1,0:T(8,128)(2,1)S(1)} %filter_and_gate.5), channel_id=1, source_target_pairs={{0,2},{1,3},{2,0},{3,1},{4,6},{5,7},{6,4},{7,5},{8,10},{9,11},{10,... | collective-permute-start | bytes 589832 | tf_op jit(solution)/shard_map/ppermute | solution.py:418
  213.4 12.7 %collective-permute-start.34 = (bf16[192,512]{1,0:T(8,128)(2,1)S(1)}, bf16[192,512]{1,0:T(8,128)(2,1)S(1)}, u32[]{:S(2)}, u32[]{:S(2)}) collective-permute-start(bf16[192,512]{1,0:T(8,128)(2,1)S(1)} %filter_and_gate.5), channel_id=1, source_target_pairs={{0,1},{1,2},{2,3},{3,0},{4,5},{5,6},{6,7},{7,4},{8,9},{9,10},{10,1... | collective-permute-start | bytes 589832 | tf_op jit(solution)/shard_map/ppermute | solution.py:418
  226.1 2.5 collective-permute-start.37
  233.2 8.5 %collective-permute-start.42 = (bf16[192,1024]{1,0:T(8,128)(2,1)S(1)}, bf16[192,1024]{1,0:T(8,128)(2,1)S(1)}, u32[]{:S(2)}, u32[]{:S(2)}) collective-permute-start(bf16[192,1024]{1,0:T(8,128)(2,1)S(1)} %get-tuple-element.88.refs_3_), channel_id=1, source_target_pairs={{0,1},{1,0},{2,3},{3,2},{4,5},{5,4},{6,7},{7,6},{8,9},{9,8},{10,11... | collective-permute-start | bytes 1179656 | tf_op jit(solution)/shard_map/ppermute | solution.py:418
  234.8 14.3 %collective-permute-start.44 = (bf16[192,1024]{1,0:T(8,128)(2,1)S(1)}, bf16[192,1024]{1,0:T(8,128)(2,1)S(1)}, u32[]{:S(2)}, u32[]{:S(2)}) collective-permute-start(bf16[192,1024]{1,0:T(8,128)(2,1)S(1)} %get-tuple-element.88.refs_3_), channel_id=1, source_target_pairs={{0,4},{4,0},{8,12},{12,8},{1,5},{5,1},{9,13},{13,9},{2,6},{6,2},{1... | collective-permute-start | bytes 1179656 | tf_op jit(solution)/shard_map/ppermute | solution.py:541
  238.1 14.9 %collective-permute-start.41 = (bf16[192,1024]{1,0:T(8,128)(2,1)S(1)}, bf16[192,1024]{1,0:T(8,128)(2,1)S(1)}, u32[]{:S(2)}, u32[]{:S(2)}) collective-permute-start(bf16[192,1024]{1,0:T(8,128)(2,1)S(1)} %get-tuple-element.87.refs_0_.refs_2_), channel_id=1, source_target_pairs={{0,1},{1,0},{2,3},{3,2},{4,5},{5,4},{6,7},{7,6},{8,9},{9,8},{10,11... | collective-permute-start | bytes 1179656 | tf_op jit(solution)/shard_map/ppermute | solution.py:418
  241.8 11.2 %collective-permute-start.43 = (bf16[192,1024]{1,0:T(8,128)(2,1)S(1)}, bf16[192,1024]{1,0:T(8,128)(2,1)S(1)}, u32[]{:S(2)}, u32[]{:S(2)}) collective-permute-start(bf16[192,1024]{1,0:T(8,128)(2,1)S(1)} %collective-permute-done.42), channel_id=1, source_target_pairs={{0,4},{4,0},{8,12},{12,8},{1,5},{5,1},{9,13},{13,9},{2,6},{6,2},{1... | collective-permute-start | bytes 1179656 | tf_op jit(solution)/shard_map/ppermute | solution.py:546
  256.9 3.5 %collective-permute-start.45 = (bf16[128,512]{1,0:T(8,128)(2,1)S(1)}, bf16[128,512]{1,0:T(8,128)(2,1)S(1)}, u32[]{:S(2)}, u32[]{:S(2)}) collective-permute-start(bf16[128,512]{1,0:T(8,128)(2,1)S(1)} %slice.22), channel_id=1, source_target_pairs={{0,4},{4,8},{8,12},{1,5},{5,9},{9,13},{2,6},{6,10},{10,14},{3,7},{... | collective-permute-start | bytes 393224 | tf_op jit(solution)/shard_map/ppermute | solution.py:524
  261.6 6.0 %collective-permute-start.48 = (bf16[192,512]{1,0:T(8,128)(2,1)S(1)}, bf16[192,512]{1,0:T(8,128)(2,1)S(1)}, u32[]{:S(2)}, u32[]{:S(2)}) collective-permute-start(bf16[192,512]{1,0:T(8,128)(2,1)S(1)} %filter_and_gate.6), channel_id=1, source_target_pairs={{0,3},{1,0},{2,1},{3,2},{4,7},{5,4},{6,5},{7,6},{8,11},{9,8},{10,9... | collective-permute-start | bytes 589832 | tf_op jit(solution)/shard_map/ppermute | solution.py:418
  263.9 16.2 %collective-permute-start.47 = (bf16[192,512]{1,0:T(8,128)(2,1)S(1)}, bf16[192,512]{1,0:T(8,128)(2,1)S(1)}, u32[]{:S(2)}, u32[]{:S(2)}) collective-permute-start(bf16[192,512]{1,0:T(8,128)(2,1)S(1)} %filter_and_gate.6), channel_id=1, source_target_pairs={{0,2},{1,3},{2,0},{3,1},{4,6},{5,7},{6,4},{7,5},{8,10},{9,11},{10,... | collective-permute-start | bytes 589832 | tf_op jit(solution)/shard_map/ppermute | solution.py:418
  264.7 15.4 %collective-permute-start.46 = (bf16[192,512]{1,0:T(8,128)(2,1)S(1)}, bf16[192,512]{1,0:T(8,128)(2,1)S(1)}, u32[]{:S(2)}, u32[]{:S(2)}) collective-permute-start(bf16[192,512]{1,0:T(8,128)(2,1)S(1)} %filter_and_gate.6), channel_id=1, source_target_pairs={{0,1},{1,2},{2,3},{3,0},{4,5},{5,6},{6,7},{7,4},{8,9},{9,10},{10,1... | collective-permute-start | bytes 589832 | tf_op jit(solution)/shard_map/ppermute | solution.py:418
  280.2 4.8 %collective-permute-start.49 = (bf16[4,192,512]{2,1,0:T(8,128)(2,1)S(1)}, bf16[4,192,512]{2,1,0:T(8,128)(2,1)S(1)}, u32[]{:S(2)}, u32[]{:S(2)}) collective-permute-start(bf16[4,192,512]{2,1,0:T(8,128)(2,1)S(1)} %pad_maximum_fusion.7.refs_0_), channel_id=1, source_target_pairs={{0,4},{4,0},{8,12},{12,8},{1,5},{5,1},{9,13},{13,9},{2,6},{6,2},{1... | collective-permute-start | bytes 2359304 | tf_op jit(solution)/shard_map/ppermute | solution.py:537
  289.2 12.0 %collective-permute-start.51 = (bf16[192,1024]{1,0:T(8,128)(2,1)S(1)}, bf16[192,1024]{1,0:T(8,128)(2,1)S(1)}, u32[]{:S(2)}, u32[]{:S(2)}) collective-permute-start(bf16[192,1024]{1,0:T(8,128)(2,1)S(1)} %get-tuple-element.94.refs_3_), channel_id=1, source_target_pairs={{0,1},{1,0},{2,3},{3,2},{4,5},{5,4},{6,7},{7,6},{8,9},{9,8},{10,11... | collective-permute-start | bytes 1179656 | tf_op jit(solution)/shard_map/ppermute | solution.py:418
  289.9 11.3 %collective-permute-start.53 = (bf16[192,1024]{1,0:T(8,128)(2,1)S(1)}, bf16[192,1024]{1,0:T(8,128)(2,1)S(1)}, u32[]{:S(2)}, u32[]{:S(2)}) collective-permute-start(bf16[192,1024]{1,0:T(8,128)(2,1)S(1)} %get-tuple-element.94.refs_3_), channel_id=1, source_target_pairs={{0,4},{4,0},{8,12},{12,8},{1,5},{5,1},{9,13},{13,9},{2,6},{6,2},{1... | collective-permute-start | bytes 1179656 | tf_op jit(solution)/shard_map/ppermute | solution.py:541
  290.0 19.1 %collective-permute-start.50 = (bf16[192,1024]{1,0:T(8,128)(2,1)S(1)}, bf16[192,1024]{1,0:T(8,128)(2,1)S(1)}, u32[]{:S(2)}, u32[]{:S(2)}) collective-permute-start(bf16[192,1024]{1,0:T(8,128)(2,1)S(1)} %get-tuple-element.93.refs_0_.refs_2_), channel_id=1, source_target_pairs={{0,1},{1,0},{2,3},{3,2},{4,5},{5,4},{6,7},{7,6},{8,9},{9,8},{10,11... | collective-permute-start | bytes 1179656 | tf_op jit(solution)/shard_map/ppermute | solution.py:418
  301.2 7.9 %collective-permute-start.52 = (bf16[192,1024]{1,0:T(8,128)(2,1)S(1)}, bf16[192,1024]{1,0:T(8,128)(2,1)S(1)}, u32[]{:S(2)}, u32[]{:S(2)}) collective-permute-start(bf16[192,1024]{1,0:T(8,128)(2,1)S(1)} %collective-permute-done.51), channel_id=1, source_target_pairs={{0,4},{4,0},{8,12},{12,8},{1,5},{5,1},{9,13},{13,9},{2,6},{6,2},{1... | collective-permute-start | bytes 1179656 | tf_op jit(solution)/shard_map/ppermute | solution.py:546
  313.0 2.5 collective-permute-start.54
  317.1 6.1 %collective-permute-start.57 = (bf16[192,512]{1,0:T(8,128)(2,1)S(1)}, bf16[192,512]{1,0:T(8,128)(2,1)S(1)}, u32[]{:S(2)}, u32[]{:S(2)}) collective-permute-start(bf16[192,512]{1,0:T(8,128)(2,1)S(1)} %filter_and_gate.7), channel_id=1, source_target_pairs={{0,3},{1,0},{2,1},{3,2},{4,7},{5,4},{6,5},{7,6},{8,11},{9,8},{10,9... | collective-permute-start | bytes 589832 | tf_op jit(solution)/shard_map/ppermute | solution.py:418
  319.3 17.1 %collective-permute-start.56 = (bf16[192,512]{1,0:T(8,128)(2,1)S(1)}, bf16[192,512]{1,0:T(8,128)(2,1)S(1)}, u32[]{:S(2)}, u32[]{:S(2)}) collective-permute-start(bf16[192,512]{1,0:T(8,128)(2,1)S(1)} %filter_and_gate.7), channel_id=1, source_target_pairs={{0,2},{1,3},{2,0},{3,1},{4,6},{5,7},{6,4},{7,5},{8,10},{9,11},{10,... | collective-permute-start | bytes 589832 | tf_op jit(solution)/shard_map/ppermute | solution.py:418
  319.4 17.0 %collective-permute-start.55 = (bf16[192,512]{1,0:T(8,128)(2,1)S(1)}, bf16[192,512]{1,0:T(8,128)(2,1)S(1)}, u32[]{:S(2)}, u32[]{:S(2)}) collective-permute-start(bf16[192,512]{1,0:T(8,128)(2,1)S(1)} %filter_and_gate.7), channel_id=1, source_target_pairs={{0,1},{1,2},{2,3},{3,0},{4,5},{5,6},{6,7},{7,4},{8,9},{9,10},{10,1... | collective-permute-start | bytes 589832 | tf_op jit(solution)/shard_map/ppermute | solution.py:418
  336.5 3.7 %collective-permute-start.58 = (bf16[4,192,512]{2,1,0:T(8,128)(2,1)S(1)}, bf16[4,192,512]{2,1,0:T(8,128)(2,1)S(1)}, u32[]{:S(2)}, u32[]{:S(2)}) collective-permute-start(bf16[4,192,512]{2,1,0:T(8,128)(2,1)S(1)} %pad_maximum_fusion.8.refs_0_), channel_id=1, source_target_pairs={{0,4},{4,0},{8,12},{12,8},{1,5},{5,1},{9,13},{13,9},{2,6},{6,2},{1... | collective-permute-start | bytes 2359304 | tf_op jit(solution)/shard_map/ppermute | solution.py:537
  343.3 1.8 collective-permute-start.59
  (37 other events, 411.4 us)
Sparse Core Ops, SparseCore 0:
  10.9 43.8 all-gather.1

commit v5 on v4

--- a/solution.py
+++ b/solution.py
@@ -356,7 +356,7 @@
             pltpu.VMEM((4, width, channels), jnp.bfloat16),
             pltpu.SemaphoreType.DMA((4, 2)),
         ],
-        compiler_params=pltpu.CompilerParams(vmem_limit_bytes=16 * MIB),
+        compiler_params=pltpu.CompilerParams(vmem_limit_bytes=(44 if sections == 1 else 16) * MIB),
         cost_estimate=pl.CostEstimate(
             flops=16 * tokens * width * channels,
             bytes_accessed=8 * width * channels,

time: 354 us -> 351 us (level)
  local copies, waits for them, and re-layouts: 27.5 us -> 23.8 us
    unnamed x81 -> x77, local copies, waits for them, and re-layouts: 21 us -> 17.3 us
  transfers between devices with their start and end apart: 61 -> 61, of which waited for: 31 -> 29; matrix products, arithmetic and copies ran while one was open for 4% -> 4% of each run, Pallas kernels for 9% -> 9%
where the time goes in v5:
time: 351 us; the launch traced here: 350 us
  waiting for transfers between devices  148 us (42%)
  starting transfers between devices  99.8 us (28%)
  Pallas kernels  57.2 us (16%)
  local copies, waits for them, and re-layouts  23.8 us (7%)
  between operations  14.2 us (4%)
  other arithmetic  7.16 us (2%)
    ppermute x40, waiting for transfers between devices, join(): self.now.append(lax.ppermute(value, axes, pairs))  134 us
    ppermute x40, starting transfers between devices, join(): self.now.append(lax.ppermute(value, axes, pairs))  69.3 us
    pallas_call x7, Pallas kernels, project_in(): pl.pallas_call(partial(in_kernel, mode, step, sections), out_shape=out, i...  29.3 us
    unnamed x77, local copies, waits for them, and re-layouts  17.3 us
    pallas_call x4, Pallas kernels, project_out(): pl.pallas_call(partial(out_kernel, step, sections), out_shape=(out, out),...  15.4 us
    ppermute x3, starting transfers between devices, shards(): lax.ppermute(beside_core, 'ctx', CORES)  8.85 us
    ppermute x4, starting transfers between devices, shards(): halo = lax.ppermute(mixed[-reach:], 'ctx', HALO)  8.46 us
    pallas_call x2, Pallas kernels, taken(): pl.pallas_call(partial(taken_kernel, second, runs), out_shape=tuple((jax....  7.18 us
  transfers between devices with their start and end apart: 61, of which 29 were waited for; matrix products, arithmetic and copies ran while one was open for 4% of the time, Pallas kernels for 9%

profile of v5, /device:TPU:0, one launch (start us, length us, event | category | flops | bytes accessed | tf_op | source)
XLA Modules:
  0.0 350.3 jit_solution(10593468726485642432)
XLA Ops:
  6.5 3.7 %taken.2 = (bf16[512,512]{1,0:T(8,128)(2,1)}, bf16[2,512,512]{2,1,0:T(8,128)(2,1)}, bf16[1,512,512]{2,1,0:T(8,128)(2,1)}) custom-call(s32[4]{0:T(128)} %plan.32, bf16[2,3,1024,512]{3,2,1,0:T(8,128)(2,1)} %bitcast.in_ref.refs_1_.refs_2_.refs_4_, bf16[2,1024,512]{2,1,0:T(8,128)(2,1)} %out_ref.3), custom_call_target="tpu_custom_call" | custom-call | tf_op jit(solution)/shard_map/taken/pallas_call | solution.py:391
  10.8 2.6 collective-permute-start.1
  15.4 5.1 %reshape.11 = bf16[32,64,255]{2,1,0:T(8,128)(2,1)} reshape(bf16[32,16320]{1,0:T(8,128)(2,1)} %bitcast.42) | data formatting | bytes 2088960 | tf_op jit(solution)/shard_map/reshape | solution.py:297
  20.5 1.7 copy-done.29
  22.2 3.5 taken.3
  26.5 11.1 %collective-permute-done.1.refs_3_.refs_4_.refs_6_ = bf16[2,512,512]{2,1,0:T(8,128)(2,1)S(1)} collective-permute-done((bf16[2,512,512]{2,1,0:T(8,128)(2,1)}, bf16[2,512,512]{2,1,0:T(8,128)(2,1)S(1)}, u32[]{:S(2)}, u32[]{:S(2)}) %collective-permute-start.1) | collective-permute-done | bytes 1048608 | tf_op jit(solution)/shard_map/ppermute | solution.py:418
  38.9 2.0 collective-permute-start.2
  42.4 4.5 %collective-permute-start.8 = (bf16[512,512]{1,0:T(8,128)(2,1)S(1)}, bf16[512,512]{1,0:T(8,128)(2,1)S(1)}, u32[]{:S(2)}, u32[]{:S(2)}) collective-permute-start(bf16[512,512]{1,0:T(8,128)(2,1)S(1)} %copy-done.36), channel_id=1, source_target_pairs={{2,0},{7,5},{0,2},{5,7},{10,8},{15,13},{8,10},{13,15},{18,16},{23,... | collective-permute-start | bytes 1572872 | tf_op jit(solution)/shard_map/ppermute | solution.py:418
  46.9 1.9 collective-permute-done.3.refs_5_.refs_6_.refs_8_
  50.1 5.7 %collective-permute-done.9 = bf16[512,512]{1,0:T(8,128)(2,1)S(1)} collective-permute-done((bf16[512,512]{1,0:T(8,128)(2,1)S(1)}, bf16[512,512]{1,0:T(8,128)(2,1)S(1)}, u32[]{:S(2)}, u32[]{:S(2)}) %collective-permute-start.9) | collective-permute-done | bytes 524320 | tf_op jit(solution)/shard_map/ppermute | solution.py:418
  57.3 15.2 %collective-permute-done.8 = bf16[512,512]{1,0:T(8,128)(2,1)S(1)} collective-permute-done((bf16[512,512]{1,0:T(8,128)(2,1)S(1)}, bf16[512,512]{1,0:T(8,128)(2,1)S(1)}, u32[]{:S(2)}, u32[]{:S(2)}) %collective-permute-start.8) | collective-permute-done | bytes 524320 | tf_op jit(solution)/shard_map/ppermute | solution.py:418
  72.5 1.7 pad_maximum_fusion.refs_4_
  75.2 6.9 %collective-permute-start.19 = (bf16[4,512,512]{2,1,0:T(8,128)(2,1)}, bf16[4,512,512]{2,1,0:T(8,128)(2,1)S(1)}, u32[]{:S(2)}, u32[]{:S(2)}) collective-permute-start(bf16[4,512,512]{2,1,0:T(8,128)(2,1)} %pad_maximum_fusion.refs_4_), channel_id=1, source_target_pairs={{0,8},{5,9},{2,10},{7,11},{8,4},{13,5},{10,6},{15,7},{16,24},{21,2... | collective-permute-start | bytes 6291464 | tf_op jit(solution)/shard_map/ppermute | solution.py:418
  85.6 3.4 collective-permute-start.18
  91.8 5.0 %collective-permute-start.27 = (bf16[512,512]{1,0:T(8,128)(2,1)S(1)}, bf16[512,512]{1,0:T(8,128)(2,1)S(1)}, u32[]{:S(2)}, u32[]{:S(2)}) collective-permute-start(bf16[512,512]{1,0:T(8,128)(2,1)S(1)} %copy-done.32), channel_id=1, source_target_pairs={{2,0},{7,5},{0,2},{5,7},{10,8},{15,13},{8,10},{13,15},{18,16},{23,... | collective-permute-start | bytes 1572872 | tf_op jit(solution)/shard_map/ppermute | solution.py:418
  100.4 5.6 %project_in_whole.1 = (bf16[192,512]{1,0:T(8,128)(2,1)S(1)}, bf16[192,512]{1,0:T(8,128)(2,1)S(1)}) custom-call(s32[4]{0:T(128)S(1)} %copy-done.33, bf16[192,4096]{1,0:T(8,128)(2,1)S(1)} %copy-done.30, bf16[2,3,1024,512]{3,2,1,0:T(8,128)(2,1)} %bitcast.in_ref.refs_1_.refs_2_.refs_4_, bf16[2,3,1024,512]{3,2,1,0:T(8,128)(2,1)} %collective-permute-done.refs_2_.refs_3_.refs_5_, ...), custom_call_target="tpu_custom_call" | custom-call | flops 2415919104 | bytes 12582912 | tf_op jit(solution)/shard_map/project_in_whole/pallas_call | solution.py:211
  106.0 2.1 collective-permute-start.11
  109.0 8.6 %collective-permute-done.27 = bf16[512,512]{1,0:T(8,128)(2,1)S(1)} collective-permute-done((bf16[512,512]{1,0:T(8,128)(2,1)S(1)}, bf16[512,512]{1,0:T(8,128)(2,1)S(1)}, u32[]{:S(2)}, u32[]{:S(2)}) %collective-permute-start.27) | collective-permute-done | bytes 524320 | tf_op jit(solution)/shard_map/ppermute | solution.py:418
  119.3 4.9 %collective-permute-start.29 = (bf16[4,512,512]{2,1,0:T(8,128)(2,1)}, bf16[4,512,512]{2,1,0:T(8,128)(2,1)}, u32[]{:S(2)}, u32[]{:S(2)}) collective-permute-start(bf16[4,512,512]{2,1,0:T(8,128)(2,1)} %pad_maximum_fusion.1.refs_9_), channel_id=1, source_target_pairs={{0,8},{5,9},{2,10},{7,11},{8,4},{13,5},{10,6},{15,7},{16,24},{21,2... | collective-permute-start | bytes 6291464 | tf_op jit(solution)/shard_map/ppermute | solution.py:418
  125.8 1.8 collective-permute-start.13
  127.6 1.9 collective-permute-start.12
  129.6 4.0 %collective-permute-done.14 = bf16[192,512]{1,0:T(8,128)(2,1)S(1)} collective-permute-done((bf16[192,512]{1,0:T(8,128)(2,1)S(1)}, bf16[192,512]{1,0:T(8,128)(2,1)S(1)}, u32[]{:S(2)}, u32[]{:S(2)}) %collective-permute-start.14) | collective-permute-done | bytes 196640 | tf_op jit(solution)/shard_map/ppermute | solution.py:418
  133.5 9.8 %collective-permute-done.13 = bf16[192,512]{1,0:T(8,128)(2,1)S(1)} collective-permute-done((bf16[192,512]{1,0:T(8,128)(2,1)S(1)}, bf16[192,512]{1,0:T(8,128)(2,1)S(1)}, u32[]{:S(2)}, u32[]{:S(2)}) %collective-permute-start.13) | collective-permute-done | bytes 196640 | tf_op jit(solution)/shard_map/ppermute | solution.py:418
  146.7 2.5 collective-permute-start.30
  150.5 1.7 collective-permute-done.16.refs_3_
  155.4 4.0 %project_out.4 = (bf16[192,1024]{1,0:T(8,128)(2,1)S(1)}, bf16[192,1024]{1,0:T(8,128)(2,1)S(1)}) custom-call(s32[4]{0:T(128)S(1)} %copy-done.33, bf16[4,192,512]{2,1,0:T(8,128)(2,1)} %pad_maximum_fusion.5.refs_0_, bf16[4,192,512]{2,1,0:T(8,128)(2,1)} %collective-permute-done.15.refs_1_, bf16[192,1024]{1,0:T(8,128)(2,1)S(1)} %get-tuple-element.102.refs_2_, ...), custom_call_target="tpu_custom_call" | custom-call | flops 1610612736 | bytes 4194304 | tf_op jit(solution)/shard_map/project_out/pallas_call | solution.py:350
  159.5 2.0 collective-permute-start.22
  161.6 8.6 %collective-permute-done.25.refs_11_.refs_13_ = bf16[2,512,512]{2,1,0:T(8,128)(2,1)S(1)} collective-permute-done((bf16[2,512,512]{2,1,0:T(8,128)(2,1)}, bf16[2,512,512]{2,1,0:T(8,128)(2,1)S(1)}, u32[]{:S(2)}, u32[]{:S(2)}) %collective-permute-start.25) | collective-permute-done | bytes 1048608 | tf_op jit(solution)/shard_map/ppermute | solution.py:418
  170.2 2.2 collective-permute-done.30.refs_12_.refs_14_
  173.8 6.0 %collective-permute-done.22 = bf16[192,1024]{1,0:T(8,128)(2,1)S(1)} collective-permute-done((bf16[192,1024]{1,0:T(8,128)(2,1)S(1)}, bf16[192,1024]{1,0:T(8,128)(2,1)S(1)}, u32[]{:S(2)}, u32[]{:S(2)}) %collective-permute-start.22) | collective-permute-done | bytes 393248 | tf_op jit(solution)/shard_map/ppermute | solution.py:418
  180.4 3.1 collective-permute-start.39
  183.5 2.0 collective-permute-start.38
  186.0 2.0 collective-permute-start.40
  190.5 3.9 %project_in_first.3 = (f32[3,192,512]{2,1,0:T(8,128)S(1)}, f32[192,128]{1,0:T(8,128)S(1)}) custom-call(s32[4]{0:T(128)S(1)} %copy-done.33, bf16[192,1024]{1,0:T(8,128)(2,1)S(1)} %get-tuple-element.69.refs_0_.refs_2_, bf16[192,1024]{1,0:T(8,128)(2,1)S(1)} %collective-permute-done.24.refs_1_, bf16[2,3,1024,512]{3,2,1,0:T(8,128)(2,1)} %bitcast.in_ref.refs_1_.refs_2_.refs_4_, ...), custom_call_target="tpu_custom_call" | custom-call | flops 1207959552 | bytes 6291456 | tf_op jit(solution)/shard_map/project_in_first/pallas_call | solution.py:211
  194.5 4.2 %project_in_last.3 = (bf16[192,512]{1,0:T(8,128)(2,1)S(1)}, bf16[192,512]{1,0:T(8,128)(2,1)S(1)}) custom-call(s32[4]{0:T(128)S(1)} %copy-done.33, bf16[192,1024]{1,0:T(8,128)(2,1)S(1)} %collective-permute-done.21.refs_0_, bf16[192,1024]{1,0:T(8,128)(2,1)S(1)} %collective-permute-done.23.refs_1_, f32[3,192,512]{2,1,0:T(8,128)S(1)} %get-tuple-element.80.refs_2_, ...), custom_call_target="tpu_custom_call" | custom-call | flops 1207959552 | bytes 6291456 | tf_op jit(solution)/shard_map/project_in_last/pallas_call | solution.py:211
  198.7 2.0 collective-permute-start.33
  203.3 2.0 collective-permute-start.36
  205.5 5.3 %collective-permute-done.36 = bf16[192,512]{1,0:T(8,128)(2,1)S(1)} collective-permute-done((bf16[192,512]{1,0:T(8,128)(2,1)S(1)}, bf16[192,512]{1,0:T(8,128)(2,1)S(1)}, u32[]{:S(2)}, u32[]{:S(2)}) %collective-permute-start.36) | collective-permute-done | bytes 196640 | tf_op jit(solution)/shard_map/ppermute | solution.py:418
  211.9 11.7 %collective-permute-done.35 = bf16[192,512]{1,0:T(8,128)(2,1)S(1)} collective-permute-done((bf16[192,512]{1,0:T(8,128)(2,1)S(1)}, bf16[192,512]{1,0:T(8,128)(2,1)S(1)}, u32[]{:S(2)}, u32[]{:S(2)}) %collective-permute-start.35) | collective-permute-done | bytes 196640 | tf_op jit(solution)/shard_map/ppermute | solution.py:418
  223.9 2.2 collective-permute-done.39.refs_11_
  227.7 3.0 project_out.5
  231.3 4.4 %collective-permute-start.44 = (bf16[192,1024]{1,0:T(8,128)(2,1)S(1)}, bf16[192,1024]{1,0:T(8,128)(2,1)S(1)}, u32[]{:S(2)}, u32[]{:S(2)}) collective-permute-start(bf16[192,1024]{1,0:T(8,128)(2,1)S(1)} %get-tuple-element.88.refs_3_), channel_id=1, source_target_pairs={{0,4},{4,0},{8,12},{12,8},{1,5},{5,1},{9,13},{13,9},{2,6},{6,2},{1... | collective-permute-start | bytes 1179656 | tf_op jit(solution)/shard_map/ppermute | solution.py:541
  235.7 1.7 collective-permute-start.41
  238.9 7.6 %collective-permute-start.43 = (bf16[192,1024]{1,0:T(8,128)(2,1)S(1)}, bf16[192,1024]{1,0:T(8,128)(2,1)S(1)}, u32[]{:S(2)}, u32[]{:S(2)}) collective-permute-start(bf16[192,1024]{1,0:T(8,128)(2,1)S(1)} %collective-permute-done.42), channel_id=1, source_target_pairs={{0,4},{4,0},{8,12},{12,8},{1,5},{5,1},{9,13},{13,9},{2,6},{6,2},{1... | collective-permute-start | bytes 1179656 | tf_op jit(solution)/shard_map/ppermute | solution.py:546
  246.5 3.9 %project_in_first.4 = (f32[3,192,512]{2,1,0:T(8,128)S(1)}, f32[192,128]{1,0:T(8,128)S(1)}) custom-call(s32[4]{0:T(128)S(1)} %copy-done.33, bf16[192,1024]{1,0:T(8,128)(2,1)S(1)} %get-tuple-element.87.refs_0_.refs_2_, bf16[192,1024]{1,0:T(8,128)(2,1)S(1)} %collective-permute-done.44.refs_1_, bf16[2,3,1024,512]{3,2,1,0:T(8,128)(2,1)} %bitcast.in_ref.refs_1_.refs_2_.refs_4_, ...), custom_call_target="tpu_custom_call" | custom-call | flops 1207959552 | bytes 6291456 | tf_op jit(solution)/shard_map/project_in_first/pallas_call | solution.py:211
  250.4 3.9 %project_in_last.4 = (bf16[192,512]{1,0:T(8,128)(2,1)S(1)}, bf16[192,512]{1,0:T(8,128)(2,1)S(1)}) custom-call(s32[4]{0:T(128)S(1)} %copy-done.33, bf16[192,1024]{1,0:T(8,128)(2,1)S(1)} %collective-permute-done.41.refs_0_, bf16[192,1024]{1,0:T(8,128)(2,1)S(1)} %collective-permute-done.43.refs_1_, f32[3,192,512]{2,1,0:T(8,128)S(1)} %get-tuple-element.89.refs_2_, ...), custom_call_target="tpu_custom_call" | custom-call | flops 1207959552 | bytes 6291456 | tf_op jit(solution)/shard_map/project_in_last/pallas_call | solution.py:211
  254.3 2.7 collective-permute-start.45
  259.2 2.0 collective-permute-start.48
  261.8 1.9 collective-permute-start.46
  263.7 1.7 collective-permute-done.48
  265.5 12.4 %collective-permute-done.47 = bf16[192,512]{1,0:T(8,128)(2,1)S(1)} collective-permute-done((bf16[192,512]{1,0:T(8,128)(2,1)S(1)}, bf16[192,512]{1,0:T(8,128)(2,1)S(1)}, u32[]{:S(2)}, u32[]{:S(2)}) %collective-permute-start.47) | collective-permute-done | bytes 196640 | tf_op jit(solution)/shard_map/ppermute | solution.py:418
  278.0 2.4 collective-permute-start.49
  280.4 1.9 collective-permute-done.49.refs_1_
  282.3 4.2 %project_out.6 = (bf16[192,1024]{1,0:T(8,128)(2,1)S(1)}, bf16[192,1024]{1,0:T(8,128)(2,1)S(1)}) custom-call(s32[4]{0:T(128)S(1)} %copy-done.33, bf16[4,192,512]{2,1,0:T(8,128)(2,1)S(1)} %pad_maximum_fusion.7.refs_0_, bf16[4,192,512]{2,1,0:T(8,128)(2,1)S(1)} %collective-permute-done.49.refs_1_, bf16[192,1024]{1,0:T(8,128)(2,1)S(1)} %get-tuple-element.87.refs_0_.refs_2_, ...), custom_call_target="tpu_custom_call" | custom-call | flops 1610612736 | bytes 4194304 | tf_op jit(solution)/shard_map/project_out/pallas_call | solution.py:350
  288.6 9.8 %collective-permute-done.51 = bf16[192,1024]{1,0:T(8,128)(2,1)S(1)} collective-permute-done((bf16[192,1024]{1,0:T(8,128)(2,1)S(1)}, bf16[192,1024]{1,0:T(8,128)(2,1)S(1)}, u32[]{:S(2)}, u32[]{:S(2)}) %collective-permute-start.51) | collective-permute-done | bytes 393248 | tf_op jit(solution)/shard_map/ppermute | solution.py:418
  298.5 3.9 %project_in_first.5 = (f32[3,192,512]{2,1,0:T(8,128)S(1)}, f32[192,128]{1,0:T(8,128)S(1)}) custom-call(s32[4]{0:T(128)S(1)} %copy-done.33, bf16[192,1024]{1,0:T(8,128)(2,1)S(1)} %get-tuple-element.93.refs_0_.refs_2_, bf16[192,1024]{1,0:T(8,128)(2,1)S(1)} %collective-permute-done.53.refs_1_, bf16[2,3,1024,512]{3,2,1,0:T(8,128)(2,1)} %bitcast.in_ref.refs_1_.refs_2_.refs_4_, ...), custom_call_target="tpu_custom_call" | custom-call | flops 1207959552 | bytes 6291456 | tf_op jit(solution)/shard_map/project_in_first/pallas_call | solution.py:211
  302.4 4.0 %collective-permute-done.50.refs_0_ = bf16[192,1024]{1,0:T(8,128)(2,1)S(1)} collective-permute-done((bf16[192,1024]{1,0:T(8,128)(2,1)S(1)}, bf16[192,1024]{1,0:T(8,128)(2,1)S(1)}, u32[]{:S(2)}, u32[]{:S(2)}) %collective-permute-start.50) | collective-permute-done | bytes 393248 | tf_op jit(solution)/shard_map/ppermute | solution.py:418
  306.4 3.9 %project_in_last.5 = (bf16[192,512]{1,0:T(8,128)(2,1)S(1)}, bf16[192,512]{1,0:T(8,128)(2,1)S(1)}) custom-call(s32[4]{0:T(128)S(1)} %copy-done.33, bf16[192,1024]{1,0:T(8,128)(2,1)S(1)} %collective-permute-done.50.refs_0_, bf16[192,1024]{1,0:T(8,128)(2,1)S(1)} %collective-permute-done.52.refs_1_, f32[3,192,512]{2,1,0:T(8,128)S(1)} %get-tuple-element.95.refs_2_, ...), custom_call_target="tpu_custom_call" | custom-call | flops 1207959552 | bytes 6291456 | tf_op jit(solution)/shard_map/project_in_last/pallas_call | solution.py:211
  314.0 2.3 collective-permute-start.57
  316.4 1.9 collective-permute-start.55
  318.3 2.4 collective-permute-done.57
  320.7 12.6 %collective-permute-done.56 = bf16[192,512]{1,0:T(8,128)(2,1)S(1)} collective-permute-done((bf16[192,512]{1,0:T(8,128)(2,1)S(1)}, bf16[192,512]{1,0:T(8,128)(2,1)S(1)}, u32[]{:S(2)}, u32[]{:S(2)}) %collective-permute-start.56) | collective-permute-done | bytes 196640 | tf_op jit(solution)/shard_map/ppermute | solution.py:418
  334.8 1.9 collective-permute-done.58.refs_1_
  336.7 4.2 %project_out.7 = (bf16[192,1024]{1,0:T(8,128)(2,1)S(1)}, bf16[192,1024]{1,0:T(8,128)(2,1)S(1)}) custom-call(s32[4]{0:T(128)S(1)} %copy-done.33, bf16[4,192,512]{2,1,0:T(8,128)(2,1)S(1)} %pad_maximum_fusion.8.refs_0_, bf16[4,192,512]{2,1,0:T(8,128)(2,1)S(1)} %collective-permute-done.58.refs_1_, bf16[192,1024]{1,0:T(8,128)(2,1)S(1)} %get-tuple-element.93.refs_0_.refs_2_, ...), custom_call_target="tpu_custom_call" | custom-call | flops 1610612736 | bytes 4194304 | tf_op jit(solution)/shard_map/project_out/pallas_call | solution.py:350
  (175 shorter events, 57.4 us)
Async XLA Ops:
  6.5 67.7 %all-gather.2.cloned.1.call-start = ((), (), s32[]{:S(2)}) async-start(), calls=%async_computation | async-start | bytes 1966080 | tf_op jit(solution)/shard_map/all_gather | solution.py:479
  10.2 27.3 %collective-permute-start = (bf16[2,3,1024,512]{3,2,1,0:T(8,128)(2,1)}, bf16[2,3,1024,512]{3,2,1,0:T(8,128)(2,1)}, u32[]{:S(2)}, u32[]{:S(2)}) collective-permute-start(bf16[2,3,1024,512]{3,2,1,0:T(8,128)(2,1)} %bitcast.in_ref.refs_1_.refs_2_.refs_4_), channel_id=1, source_target_pairs={{0,4},{4,0},{8,12},{12,8},{1,5},{5,1},{9,13},{13,9},{2,6},{6,2},{1... | collective-permute-start | bytes 18874376 | tf_op jit(solution)/shard_map/ppermute | solution.py:418
  10.8 26.8 %collective-permute-start.1 = (bf16[2,512,512]{2,1,0:T(8,128)(2,1)}, bf16[2,512,512]{2,1,0:T(8,128)(2,1)S(1)}, u32[]{:S(2)}, u32[]{:S(2)}) collective-permute-start(bf16[2,512,512]{2,1,0:T(8,128)(2,1)} %get-tuple-element.53), channel_id=1, source_target_pairs={{0,8},{4,12},{8,0},{12,4},{1,9},{5,13},{9,1},{13,5},{2,10},{6,14},... | collective-permute-start | bytes 3145736 | tf_op jit(solution)/shard_map/ppermute | solution.py:418
  13.4 35.5 %collective-permute-start.3 = (bf16[1,512,512]{2,1,0:T(8,128)(2,1)}, bf16[1,512,512]{2,1,0:T(8,128)(2,1)S(1)}, u32[]{:S(2)}, u32[]{:S(2)}) collective-permute-start(bf16[1,512,512]{2,1,0:T(8,128)(2,1)} %get-tuple-element.59), channel_id=1, source_target_pairs={{0,8},{4,12},{8,0},{12,4},{1,9},{5,13},{9,1},{13,5},{2,10},{6,14},... | collective-permute-start | bytes 1572872 | tf_op jit(solution)/shard_map/ppermute | solution.py:483
  37.6 46.4 %copy-start.2 = (bf16[2,512,512]{2,1,0:T(8,128)(2,1)}, bf16[2,512,512]{2,1,0:T(8,128)(2,1)S(1)}, u32[]{:S(2)}) copy-start(bf16[2,512,512]{2,1,0:T(8,128)(2,1)S(1)} %collective-permute-done.1.refs_3_.refs_4_.refs_6_) | copy-start | bytes 3145732
  37.6 18.3 %collective-permute-start.9 = (bf16[512,512]{1,0:T(8,128)(2,1)S(1)}, bf16[512,512]{1,0:T(8,128)(2,1)S(1)}, u32[]{:S(2)}, u32[]{:S(2)}) collective-permute-start(bf16[512,512]{1,0:T(8,128)(2,1)S(1)} %copy-done.36), channel_id=1, source_target_pairs={{1,0},{6,5},{3,2},{4,7},{9,8},{14,13},{11,10},{12,15},{17,16},{22,... | collective-permute-start | bytes 1572872 | tf_op jit(solution)/shard_map/ppermute | solution.py:418
  38.9 35.3 %collective-permute-start.2 = (bf16[2,512,512]{2,1,0:T(8,128)(2,1)S(1)}, bf16[2,512,512]{2,1,0:T(8,128)(2,1)S(1)}, u32[]{:S(2)}, u32[]{:S(2)}) collective-permute-start(bf16[2,512,512]{2,1,0:T(8,128)(2,1)S(1)} %collective-permute-done.1.refs_3_.refs_4_.refs_6_), channel_id=1, source_target_pairs={{0,16},{16,0},{1,17},{17,1},{2,18},{18,2},{3,19},{19,3},{4,20},{20... | collective-permute-start | bytes 3145736 | tf_op jit(solution)/shard_map/ppermute | solution.py:418
  40.9 33.3 %collective-permute-start.6 = (bf16[2,512,512]{2,1,0:T(8,128)(2,1)}, bf16[2,512,512]{2,1,0:T(8,128)(2,1)}, u32[]{:S(2)}, u32[]{:S(2)}) collective-permute-start(bf16[2,512,512]{2,1,0:T(8,128)(2,1)} %get-tuple-element.62), channel_id=1, source_target_pairs={{0,8},{4,12},{8,0},{12,4},{1,9},{5,13},{9,1},{13,5},{2,10},{6,14},... | collective-permute-start | bytes 3145736 | tf_op jit(solution)/shard_map/ppermute | solution.py:418
  42.4 30.1 %collective-permute-start.8 = (bf16[512,512]{1,0:T(8,128)(2,1)S(1)}, bf16[512,512]{1,0:T(8,128)(2,1)S(1)}, u32[]{:S(2)}, u32[]{:S(2)}) collective-permute-start(bf16[512,512]{1,0:T(8,128)(2,1)S(1)} %copy-done.36), channel_id=1, source_target_pairs={{2,0},{7,5},{0,2},{5,7},{10,8},{15,13},{8,10},{13,15},{18,16},{23,... | collective-permute-start | bytes 1572872 | tf_op jit(solution)/shard_map/ppermute | solution.py:418
  48.8 23.7 %collective-permute-start.7 = (bf16[512,512]{1,0:T(8,128)(2,1)S(1)}, bf16[512,512]{1,0:T(8,128)(2,1)S(1)}, u32[]{:S(2)}, u32[]{:S(2)}) collective-permute-start(bf16[512,512]{1,0:T(8,128)(2,1)S(1)} %copy-done.36), channel_id=1, source_target_pairs={{3,0},{4,5},{1,2},{6,7},{11,8},{12,13},{9,10},{14,15},{19,16},{20,... | collective-permute-start | bytes 1572872 | tf_op jit(solution)/shard_map/ppermute | solution.py:418
  55.8 18.4 %collective-permute-start.4 = (bf16[1,512,512]{2,1,0:T(8,128)(2,1)S(1)}, bf16[1,512,512]{2,1,0:T(8,128)(2,1)S(1)}, u32[]{:S(2)}, u32[]{:S(2)}) collective-permute-start(bf16[1,512,512]{2,1,0:T(8,128)(2,1)S(1)} %collective-permute-done.3.refs_5_.refs_6_.refs_8_), channel_id=1, source_target_pairs={{0,16},{16,0},{1,17},{17,1},{2,18},{18,2},{3,19},{19,3},{4,20},{20... | collective-permute-start | bytes 1572872 | tf_op jit(solution)/shard_map/ppermute | solution.py:418
  74.2 14.8 %collective-permute-start.17 = (bf16[4,512,512]{2,1,0:T(8,128)(2,1)}, bf16[4,512,512]{2,1,0:T(8,128)(2,1)S(1)}, u32[]{:S(2)}, u32[]{:S(2)}) collective-permute-start(bf16[4,512,512]{2,1,0:T(8,128)(2,1)} %pad_maximum_fusion.refs_4_), channel_id=1, source_target_pairs={{5,1},{7,3},{8,12},{10,14},{21,17},{23,19},{24,28},{26,30}} | collective-permute-start | bytes 6291464 | tf_op jit(solution)/shard_map/ppermute | solution.py:418
  75.2 30.8 %collective-permute-start.19 = (bf16[4,512,512]{2,1,0:T(8,128)(2,1)}, bf16[4,512,512]{2,1,0:T(8,128)(2,1)S(1)}, u32[]{:S(2)}, u32[]{:S(2)}) collective-permute-start(bf16[4,512,512]{2,1,0:T(8,128)(2,1)} %pad_maximum_fusion.refs_4_), channel_id=1, source_target_pairs={{0,8},{5,9},{2,10},{7,11},{8,4},{13,5},{10,6},{15,7},{16,24},{21,2... | collective-permute-start | bytes 6291464 | tf_op jit(solution)/shard_map/ppermute | solution.py:418
  84.0 5.0 %collective-permute-start.10 = (bf16[3,512,512]{2,1,0:T(8,128)(2,1)S(1)}, bf16[3,512,512]{2,1,0:T(8,128)(2,1)S(1)}, u32[]{:S(2)}, u32[]{:S(2)}) collective-permute-start(bf16[3,512,512]{2,1,0:T(8,128)(2,1)S(1)} %pad_maximum_fusion.4), channel_id=1, source_target_pairs={{0,4},{4,0},{8,12},{12,8},{1,5},{5,1},{9,13},{13,9},{2,6},{6,2},{1... | collective-permute-start | bytes 4718600 | tf_op jit(solution)/shard_map/ppermute | solution.py:418
  84.2 12.6 %collective-permute-start.5 = (bf16[3,512,512]{2,1,0:T(8,128)(2,1)S(1)}, bf16[3,512,512]{2,1,0:T(8,128)(2,1)S(1)}, u32[]{:S(2)}, u32[]{:S(2)}) collective-permute-start(bf16[3,512,512]{2,1,0:T(8,128)(2,1)S(1)} %pad_maximum_fusion.3), channel_id=1, source_target_pairs={{0,4},{4,0},{8,12},{12,8},{1,5},{5,1},{9,13},{13,9},{2,6},{6,2},{1... | collective-permute-start | bytes 4718600 | tf_op jit(solution)/shard_map/ppermute | solution.py:496
  85.6 33.7 %collective-permute-start.18 = (bf16[4,512,512]{2,1,0:T(8,128)(2,1)S(1)}, bf16[4,512,512]{2,1,0:T(8,128)(2,1)S(1)}, u32[]{:S(2)}, u32[]{:S(2)}) collective-permute-start(bf16[4,512,512]{2,1,0:T(8,128)(2,1)S(1)} %copy-done.8), channel_id=1, source_target_pairs={{0,16},{16,0},{5,17},{21,1},{2,18},{18,2},{7,19},{23,3},{8,28},{24... | collective-permute-start | bytes 6291464 | tf_op jit(solution)/shard_map/ppermute | solution.py:418
  90.5 17.7 %collective-permute-start.28 = (bf16[512,512]{1,0:T(8,128)(2,1)S(1)}, bf16[512,512]{1,0:T(8,128)(2,1)S(1)}, u32[]{:S(2)}, u32[]{:S(2)}) collective-permute-start(bf16[512,512]{1,0:T(8,128)(2,1)S(1)} %copy-done.32), channel_id=1, source_target_pairs={{1,0},{6,5},{3,2},{4,7},{9,8},{14,13},{11,10},{12,15},{17,16},{22,... | collective-permute-start | bytes 1572872 | tf_op jit(solution)/shard_map/ppermute | solution.py:418
  91.8 25.8 %collective-permute-start.27 = (bf16[512,512]{1,0:T(8,128)(2,1)S(1)}, bf16[512,512]{1,0:T(8,128)(2,1)S(1)}, u32[]{:S(2)}, u32[]{:S(2)}) collective-permute-start(bf16[512,512]{1,0:T(8,128)(2,1)S(1)} %copy-done.32), channel_id=1, source_target_pairs={{2,0},{7,5},{0,2},{5,7},{10,8},{15,13},{8,10},{13,15},{18,16},{23,... | collective-permute-start | bytes 1572872 | tf_op jit(solution)/shard_map/ppermute | solution.py:418
  96.8 20.8 %collective-permute-start.26 = (bf16[512,512]{1,0:T(8,128)(2,1)S(1)}, bf16[512,512]{1,0:T(8,128)(2,1)S(1)}, u32[]{:S(2)}, u32[]{:S(2)}) collective-permute-start(bf16[512,512]{1,0:T(8,128)(2,1)S(1)} %copy-done.32), channel_id=1, source_target_pairs={{3,0},{4,5},{1,2},{6,7},{11,8},{12,13},{9,10},{14,15},{19,16},{20,... | collective-permute-start | bytes 1572872 | tf_op jit(solution)/shard_map/ppermute | solution.py:418
  106.0 13.2 %collective-permute-start.11 = (bf16[128,512]{1,0:T(8,128)(2,1)S(1)}, bf16[128,512]{1,0:T(8,128)(2,1)S(1)}, u32[]{:S(2)}, u32[]{:S(2)}) collective-permute-start(bf16[128,512]{1,0:T(8,128)(2,1)S(1)} %slice.20), channel_id=1, source_target_pairs={{0,4},{4,8},{8,12},{1,5},{5,9},{9,13},{2,6},{6,10},{10,14},{3,7},{... | collective-permute-start | bytes 393224 | tf_op jit(solution)/shard_map/ppermute | solution.py:524
  108.2 36.1 %collective-permute-start.20 = (bf16[4,512,512]{2,1,0:T(8,128)(2,1)S(1)}, bf16[4,512,512]{2,1,0:T(8,128)(2,1)S(1)}, u32[]{:S(2)}, u32[]{:S(2)}) collective-permute-start(bf16[4,512,512]{2,1,0:T(8,128)(2,1)S(1)} %collective-permute-done.19.refs_7_), channel_id=1, source_target_pairs={{8,24},{24,8},{9,25},{25,9},{10,26},{26,10},{11,27},{27,11},{4,20}... | collective-permute-start | bytes 6291464 | tf_op jit(solution)/shard_map/ppermute | solution.py:418
  119.3 27.4 %collective-permute-start.29 = (bf16[4,512,512]{2,1,0:T(8,128)(2,1)}, bf16[4,512,512]{2,1,0:T(8,128)(2,1)}, u32[]{:S(2)}, u32[]{:S(2)}) collective-permute-start(bf16[4,512,512]{2,1,0:T(8,128)(2,1)} %pad_maximum_fusion.1.refs_9_), channel_id=1, source_target_pairs={{0,8},{5,9},{2,10},{7,11},{8,4},{13,5},{10,6},{15,7},{16,24},{21,2... | collective-permute-start | bytes 6291464 | tf_op jit(solution)/shard_map/ppermute | solution.py:418
  125.7 7.8 %collective-permute-start.14 = (bf16[192,512]{1,0:T(8,128)(2,1)S(1)}, bf16[192,512]{1,0:T(8,128)(2,1)S(1)}, u32[]{:S(2)}, u32[]{:S(2)}) collective-permute-start(bf16[192,512]{1,0:T(8,128)(2,1)S(1)} %filter_and_gate.4), channel_id=1, source_target_pairs={{0,3},{1,0},{2,1},{3,2},{4,7},{5,4},{6,5},{7,6},{8,11},{9,8},{10,9... | collective-permute-start | bytes 589832 | tf_op jit(solution)/shard_map/ppermute | solution.py:418
  125.8 17.6 %collective-permute-start.13 = (bf16[192,512]{1,0:T(8,128)(2,1)S(1)}, bf16[192,512]{1,0:T(8,128)(2,1)S(1)}, u32[]{:S(2)}, u32[]{:S(2)}) collective-permute-start(bf16[192,512]{1,0:T(8,128)(2,1)S(1)} %filter_and_gate.4), channel_id=1, source_target_pairs={{0,2},{1,3},{2,0},{3,1},{4,6},{5,7},{6,4},{7,5},{8,10},{9,11},{10,... | collective-permute-start | bytes 589832 | tf_op jit(solution)/shard_map/ppermute | solution.py:418
  127.6 15.7 %collective-permute-start.12 = (bf16[192,512]{1,0:T(8,128)(2,1)S(1)}, bf16[192,512]{1,0:T(8,128)(2,1)S(1)}, u32[]{:S(2)}, u32[]{:S(2)}) collective-permute-start(bf16[192,512]{1,0:T(8,128)(2,1)S(1)} %filter_and_gate.4), channel_id=1, source_target_pairs={{0,1},{1,2},{2,3},{3,0},{4,5},{5,6},{6,7},{7,4},{8,9},{9,10},{10,1... | collective-permute-start | bytes 589832 | tf_op jit(solution)/shard_map/ppermute | solution.py:418
  144.3 7.9 %collective-permute-start.15 = (bf16[4,192,512]{2,1,0:T(8,128)(2,1)}, bf16[4,192,512]{2,1,0:T(8,128)(2,1)}, u32[]{:S(2)}, u32[]{:S(2)}) collective-permute-start(bf16[4,192,512]{2,1,0:T(8,128)(2,1)} %pad_maximum_fusion.5.refs_0_), channel_id=1, source_target_pairs={{0,4},{4,0},{8,12},{12,8},{1,5},{5,1},{9,13},{13,9},{2,6},{6,2},{1... | collective-permute-start | bytes 2359304 | tf_op jit(solution)/shard_map/ppermute | solution.py:537
  144.3 25.8 %collective-permute-start.25 = (bf16[2,512,512]{2,1,0:T(8,128)(2,1)}, bf16[2,512,512]{2,1,0:T(8,128)(2,1)S(1)}, u32[]{:S(2)}, u32[]{:S(2)}) collective-permute-start(bf16[2,512,512]{2,1,0:T(8,128)(2,1)} %collective-permute-done.6.refs_10_.refs_12_), channel_id=1, source_target_pairs={{0,16},{16,0},{1,17},{17,1},{2,18},{18,2},{3,19},{19,3},{4,20},{20... | collective-permute-start | bytes 3145736 | tf_op jit(solution)/shard_map/ppermute | solution.py:418
  146.7 25.7 %collective-permute-start.30 = (bf16[2,512,512]{2,1,0:T(8,128)(2,1)}, bf16[2,512,512]{2,1,0:T(8,128)(2,1)}, u32[]{:S(2)}, u32[]{:S(2)}) collective-permute-start(bf16[2,512,512]{2,1,0:T(8,128)(2,1)} %get-tuple-element.77), channel_id=1, source_target_pairs={{0,8},{4,12},{8,0},{12,4},{1,9},{5,13},{9,1},{13,5},{2,10},{6,14},... | collective-permute-start | bytes 3145736 | tf_op jit(solution)/shard_map/ppermute | solution.py:418
  150.4 1.8 collective-permute-start.16
  159.4 14.4 %collective-permute-start.21 = (bf16[192,1024]{1,0:T(8,128)(2,1)S(1)}, bf16[192,1024]{1,0:T(8,128)(2,1)S(1)}, u32[]{:S(2)}, u32[]{:S(2)}) collective-permute-start(bf16[192,1024]{1,0:T(8,128)(2,1)S(1)} %get-tuple-element.69.refs_0_.refs_2_), channel_id=1, source_target_pairs={{0,1},{1,0},{2,3},{3,2},{4,5},{5,4},{6,7},{7,6},{8,9},{9,8},{10,11... | collective-permute-start | bytes 1179656 | tf_op jit(solution)/shard_map/ppermute | solution.py:418
  159.5 20.3 %collective-permute-start.22 = (bf16[192,1024]{1,0:T(8,128)(2,1)S(1)}, bf16[192,1024]{1,0:T(8,128)(2,1)S(1)}, u32[]{:S(2)}, u32[]{:S(2)}) collective-permute-start(bf16[192,1024]{1,0:T(8,128)(2,1)S(1)} %get-tuple-element.70.refs_3_), channel_id=1, source_target_pairs={{0,1},{1,0},{2,3},{3,2},{4,5},{5,4},{6,7},{7,6},{8,9},{9,8},{10,11... | collective-permute-start | bytes 1179656 | tf_op jit(solution)/shard_map/ppermute | solution.py:418
  179.8 9.5 %collective-permute-start.31 = (bf16[4,512,512]{2,1,0:T(8,128)(2,1)S(1)}, bf16[4,512,512]{2,1,0:T(8,128)(2,1)S(1)}, u32[]{:S(2)}, u32[]{:S(2)}) collective-permute-start(bf16[4,512,512]{2,1,0:T(8,128)(2,1)S(1)} %pad_maximum_fusion.2), channel_id=1, source_target_pairs={{0,4},{4,0},{8,12},{12,8},{1,5},{5,1},{9,13},{13,9},{2,6},{6,2},{1... | collective-permute-start | bytes 6291464 | tf_op jit(solution)/shard_map/ppermute | solution.py:418
  179.9 6.1 %collective-permute-start.32 = (bf16[2,512,512]{2,1,0:T(8,128)(2,1)}, bf16[2,512,512]{2,1,0:T(8,128)(2,1)S(1)}, u32[]{:S(2)}, u32[]{:S(2)}) collective-permute-start(bf16[2,512,512]{2,1,0:T(8,128)(2,1)} %collective-permute-done.6.refs_10_.refs_12_), channel_id=1, source_target_pairs={{0,4},{4,0},{8,12},{12,8},{1,5},{5,1},{9,13},{13,9},{2,6},{6,2},{1... | collective-permute-start | bytes 3145736 | tf_op jit(solution)/shard_map/ppermute | solution.py:526
  180.3 7.6 %collective-permute-start.24 = (bf16[192,1024]{1,0:T(8,128)(2,1)S(1)}, bf16[192,1024]{1,0:T(8,128)(2,1)S(1)}, u32[]{:S(2)}, u32[]{:S(2)}) collective-permute-start(bf16[192,1024]{1,0:T(8,128)(2,1)S(1)} %get-tuple-element.70.refs_3_), channel_id=1, source_target_pairs={{0,4},{4,0},{8,12},{12,8},{1,5},{5,1},{9,13},{13,9},{2,6},{6,2},{1... | collective-permute-start | bytes 1179656 | tf_op jit(solution)/shard_map/ppermute | solution.py:541
  180.4 45.7 %collective-permute-start.39 = (bf16[4,512,512]{2,1,0:T(8,128)(2,1)}, bf16[4,512,512]{2,1,0:T(8,128)(2,1)}, u32[]{:S(2)}, u32[]{:S(2)}) collective-permute-start(bf16[4,512,512]{2,1,0:T(8,128)(2,1)} %pad_maximum_fusion.1.refs_9_), channel_id=1, source_target_pairs={{0,16},{16,0},{5,17},{21,1},{2,18},{18,2},{7,19},{23,3},{8,28},{24... | collective-permute-start | bytes 6291464 | tf_op jit(solution)/shard_map/ppermute | solution.py:535
  183.5 42.6 %collective-permute-start.38 = (bf16[4,512,512]{2,1,0:T(8,128)(2,1)}, bf16[4,512,512]{2,1,0:T(8,128)(2,1)}, u32[]{:S(2)}, u32[]{:S(2)}) collective-permute-start(bf16[4,512,512]{2,1,0:T(8,128)(2,1)} %pad_maximum_fusion.1.refs_9_), channel_id=1, source_target_pairs={{5,1},{7,3},{8,12},{10,14},{21,17},{23,19},{24,28},{26,30}} | collective-permute-start | bytes 6291464 | tf_op jit(solution)/shard_map/ppermute | solution.py:418
  186.0 40.1 %collective-permute-start.40 = (bf16[4,512,512]{2,1,0:T(8,128)(2,1)}, bf16[4,512,512]{2,1,0:T(8,128)(2,1)}, u32[]{:S(2)}, u32[]{:S(2)}) collective-permute-start(bf16[4,512,512]{2,1,0:T(8,128)(2,1)} %collective-permute-done.29.refs_12_), channel_id=1, source_target_pairs={{8,24},{24,8},{9,25},{25,9},{10,26},{26,10},{11,27},{27,11},{4,20}... | collective-permute-start | bytes 6291464 | tf_op jit(solution)/shard_map/ppermute | solution.py:418
  187.9 6.5 %collective-permute-start.23 = (bf16[192,1024]{1,0:T(8,128)(2,1)S(1)}, bf16[192,1024]{1,0:T(8,128)(2,1)S(1)}, u32[]{:S(2)}, u32[]{:S(2)}) collective-permute-start(bf16[192,1024]{1,0:T(8,128)(2,1)S(1)} %collective-permute-done.22), channel_id=1, source_target_pairs={{0,4},{4,0},{8,12},{12,8},{1,5},{5,1},{9,13},{13,9},{2,6},{6,2},{1... | collective-permute-start | bytes 1179656 | tf_op jit(solution)/shard_map/ppermute | solution.py:546
  194.5 31.6 %copy-start.13 = (bf16[4,512,512]{2,1,0:T(8,128)(2,1)S(1)}, bf16[4,512,512]{2,1,0:T(8,128)(2,1)}, u32[]{:S(2)}) copy-start(bf16[4,512,512]{2,1,0:T(8,128)(2,1)} %copy-done.12) | copy-start | bytes 6291460
  194.5 31.6 %copy-start.16 = (bf16[4,512,512]{2,1,0:T(8,128)(2,1)S(1)}, bf16[4,512,512]{2,1,0:T(8,128)(2,1)}, u32[]{:S(2)}) copy-start(bf16[4,512,512]{2,1,0:T(8,128)(2,1)} %copy-done.14) | copy-start | bytes 6291460
  198.7 3.0 collective-permute-start.33
  203.3 7.5 %collective-permute-start.36 = (bf16[192,512]{1,0:T(8,128)(2,1)S(1)}, bf16[192,512]{1,0:T(8,128)(2,1)S(1)}, u32[]{:S(2)}, u32[]{:S(2)}) collective-permute-start(bf16[192,512]{1,0:T(8,128)(2,1)S(1)} %filter_and_gate.5), channel_id=1, source_target_pairs={{0,3},{1,0},{2,1},{3,2},{4,7},{5,4},{6,5},{7,6},{8,11},{9,8},{10,9... | collective-permute-start | bytes 589832 | tf_op jit(solution)/shard_map/ppermute | solution.py:418
  205.2 18.3 %collective-permute-start.35 = (bf16[192,512]{1,0:T(8,128)(2,1)S(1)}, bf16[192,512]{1,0:T(8,128)(2,1)S(1)}, u32[]{:S(2)}, u32[]{:S(2)}) collective-permute-start(bf16[192,512]{1,0:T(8,128)(2,1)S(1)} %filter_and_gate.5), channel_id=1, source_target_pairs={{0,2},{1,3},{2,0},{3,1},{4,6},{5,7},{6,4},{7,5},{8,10},{9,11},{10,... | collective-permute-start | bytes 589832 | tf_op jit(solution)/shard_map/ppermute | solution.py:418
  210.8 12.8 %collective-permute-start.34 = (bf16[192,512]{1,0:T(8,128)(2,1)S(1)}, bf16[192,512]{1,0:T(8,128)(2,1)S(1)}, u32[]{:S(2)}, u32[]{:S(2)}) collective-permute-start(bf16[192,512]{1,0:T(8,128)(2,1)S(1)} %filter_and_gate.5), channel_id=1, source_target_pairs={{0,1},{1,2},{2,3},{3,0},{4,5},{5,6},{6,7},{7,4},{8,9},{9,10},{10,1... | collective-permute-start | bytes 589832 | tf_op jit(solution)/shard_map/ppermute | solution.py:418
  223.6 2.4 collective-permute-start.37
  230.8 8.1 %collective-permute-start.42 = (bf16[192,1024]{1,0:T(8,128)(2,1)S(1)}, bf16[192,1024]{1,0:T(8,128)(2,1)S(1)}, u32[]{:S(2)}, u32[]{:S(2)}) collective-permute-start(bf16[192,1024]{1,0:T(8,128)(2,1)S(1)} %get-tuple-element.88.refs_3_), channel_id=1, source_target_pairs={{0,1},{1,0},{2,3},{3,2},{4,5},{5,4},{6,7},{7,6},{8,9},{9,8},{10,11... | collective-permute-start | bytes 1179656 | tf_op jit(solution)/shard_map/ppermute | solution.py:418
  231.3 15.1 %collective-permute-start.44 = (bf16[192,1024]{1,0:T(8,128)(2,1)S(1)}, bf16[192,1024]{1,0:T(8,128)(2,1)S(1)}, u32[]{:S(2)}, u32[]{:S(2)}) collective-permute-start(bf16[192,1024]{1,0:T(8,128)(2,1)S(1)} %get-tuple-element.88.refs_3_), channel_id=1, source_target_pairs={{0,4},{4,0},{8,12},{12,8},{1,5},{5,1},{9,13},{13,9},{2,6},{6,2},{1... | collective-permute-start | bytes 1179656 | tf_op jit(solution)/shard_map/ppermute | solution.py:541
  235.7 14.6 %collective-permute-start.41 = (bf16[192,1024]{1,0:T(8,128)(2,1)S(1)}, bf16[192,1024]{1,0:T(8,128)(2,1)S(1)}, u32[]{:S(2)}, u32[]{:S(2)}) collective-permute-start(bf16[192,1024]{1,0:T(8,128)(2,1)S(1)} %get-tuple-element.87.refs_0_.refs_2_), channel_id=1, source_target_pairs={{0,1},{1,0},{2,3},{3,2},{4,5},{5,4},{6,7},{7,6},{8,9},{9,8},{10,11... | collective-permute-start | bytes 1179656 | tf_op jit(solution)/shard_map/ppermute | solution.py:418
  238.9 11.5 %collective-permute-start.43 = (bf16[192,1024]{1,0:T(8,128)(2,1)S(1)}, bf16[192,1024]{1,0:T(8,128)(2,1)S(1)}, u32[]{:S(2)}, u32[]{:S(2)}) collective-permute-start(bf16[192,1024]{1,0:T(8,128)(2,1)S(1)} %collective-permute-done.42), channel_id=1, source_target_pairs={{0,4},{4,0},{8,12},{12,8},{1,5},{5,1},{9,13},{13,9},{2,6},{6,2},{1... | collective-permute-start | bytes 1179656 | tf_op jit(solution)/shard_map/ppermute | solution.py:546
  254.3 3.7 %collective-permute-start.45 = (bf16[128,512]{1,0:T(8,128)(2,1)S(1)}, bf16[128,512]{1,0:T(8,128)(2,1)S(1)}, u32[]{:S(2)}, u32[]{:S(2)}) collective-permute-start(bf16[128,512]{1,0:T(8,128)(2,1)S(1)} %slice.22), channel_id=1, source_target_pairs={{0,4},{4,8},{8,12},{1,5},{5,9},{9,13},{2,6},{6,10},{10,14},{3,7},{... | collective-permute-start | bytes 393224 | tf_op jit(solution)/shard_map/ppermute | solution.py:524
  259.2 6.3 %collective-permute-start.48 = (bf16[192,512]{1,0:T(8,128)(2,1)S(1)}, bf16[192,512]{1,0:T(8,128)(2,1)S(1)}, u32[]{:S(2)}, u32[]{:S(2)}) collective-permute-start(bf16[192,512]{1,0:T(8,128)(2,1)S(1)} %filter_and_gate.6), channel_id=1, source_target_pairs={{0,3},{1,0},{2,1},{3,2},{4,7},{5,4},{6,5},{7,6},{8,11},{9,8},{10,9... | collective-permute-start | bytes 589832 | tf_op jit(solution)/shard_map/ppermute | solution.py:418
  261.2 16.7 %collective-permute-start.47 = (bf16[192,512]{1,0:T(8,128)(2,1)S(1)}, bf16[192,512]{1,0:T(8,128)(2,1)S(1)}, u32[]{:S(2)}, u32[]{:S(2)}) collective-permute-start(bf16[192,512]{1,0:T(8,128)(2,1)S(1)} %filter_and_gate.6), channel_id=1, source_target_pairs={{0,2},{1,3},{2,0},{3,1},{4,6},{5,7},{6,4},{7,5},{8,10},{9,11},{10,... | collective-permute-start | bytes 589832 | tf_op jit(solution)/shard_map/ppermute | solution.py:418
  261.8 16.1 %collective-permute-start.46 = (bf16[192,512]{1,0:T(8,128)(2,1)S(1)}, bf16[192,512]{1,0:T(8,128)(2,1)S(1)}, u32[]{:S(2)}, u32[]{:S(2)}) collective-permute-start(bf16[192,512]{1,0:T(8,128)(2,1)S(1)} %filter_and_gate.6), channel_id=1, source_target_pairs={{0,1},{1,2},{2,3},{3,0},{4,5},{5,6},{6,7},{7,4},{8,9},{9,10},{10,1... | collective-permute-start | bytes 589832 | tf_op jit(solution)/shard_map/ppermute | solution.py:418
  278.0 4.3 %collective-permute-start.49 = (bf16[4,192,512]{2,1,0:T(8,128)(2,1)S(1)}, bf16[4,192,512]{2,1,0:T(8,128)(2,1)S(1)}, u32[]{:S(2)}, u32[]{:S(2)}) collective-permute-start(bf16[4,192,512]{2,1,0:T(8,128)(2,1)S(1)} %pad_maximum_fusion.7.refs_0_), channel_id=1, source_target_pairs={{0,4},{4,0},{8,12},{12,8},{1,5},{5,1},{9,13},{13,9},{2,6},{6,2},{1... | collective-permute-start | bytes 2359304 | tf_op jit(solution)/shard_map/ppermute | solution.py:537
  286.5 12.0 %collective-permute-start.51 = (bf16[192,1024]{1,0:T(8,128)(2,1)S(1)}, bf16[192,1024]{1,0:T(8,128)(2,1)S(1)}, u32[]{:S(2)}, u32[]{:S(2)}) collective-permute-start(bf16[192,1024]{1,0:T(8,128)(2,1)S(1)} %get-tuple-element.94.refs_3_), channel_id=1, source_target_pairs={{0,1},{1,0},{2,3},{3,2},{4,5},{5,4},{6,7},{7,6},{8,9},{9,8},{10,11... | collective-permute-start | bytes 1179656 | tf_op jit(solution)/shard_map/ppermute | solution.py:418
  287.3 11.2 %collective-permute-start.53 = (bf16[192,1024]{1,0:T(8,128)(2,1)S(1)}, bf16[192,1024]{1,0:T(8,128)(2,1)S(1)}, u32[]{:S(2)}, u32[]{:S(2)}) collective-permute-start(bf16[192,1024]{1,0:T(8,128)(2,1)S(1)} %get-tuple-element.94.refs_3_), channel_id=1, source_target_pairs={{0,4},{4,0},{8,12},{12,8},{1,5},{5,1},{9,13},{13,9},{2,6},{6,2},{1... | collective-permute-start | bytes 1179656 | tf_op jit(solution)/shard_map/ppermute | solution.py:541
  287.3 19.1 %collective-permute-start.50 = (bf16[192,1024]{1,0:T(8,128)(2,1)S(1)}, bf16[192,1024]{1,0:T(8,128)(2,1)S(1)}, u32[]{:S(2)}, u32[]{:S(2)}) collective-permute-start(bf16[192,1024]{1,0:T(8,128)(2,1)S(1)} %get-tuple-element.93.refs_0_.refs_2_), channel_id=1, source_target_pairs={{0,1},{1,0},{2,3},{3,2},{4,5},{5,4},{6,7},{7,6},{8,9},{9,8},{10,11... | collective-permute-start | bytes 1179656 | tf_op jit(solution)/shard_map/ppermute | solution.py:418
  298.5 7.9 %collective-permute-start.52 = (bf16[192,1024]{1,0:T(8,128)(2,1)S(1)}, bf16[192,1024]{1,0:T(8,128)(2,1)S(1)}, u32[]{:S(2)}, u32[]{:S(2)}) collective-permute-start(bf16[192,1024]{1,0:T(8,128)(2,1)S(1)} %collective-permute-done.51), channel_id=1, source_target_pairs={{0,4},{4,0},{8,12},{12,8},{1,5},{5,1},{9,13},{13,9},{2,6},{6,2},{1... | collective-permute-start | bytes 1179656 | tf_op jit(solution)/shard_map/ppermute | solution.py:546
  310.3 2.5 collective-permute-start.54
  314.0 6.7 %collective-permute-start.57 = (bf16[192,512]{1,0:T(8,128)(2,1)S(1)}, bf16[192,512]{1,0:T(8,128)(2,1)S(1)}, u32[]{:S(2)}, u32[]{:S(2)}) collective-permute-start(bf16[192,512]{1,0:T(8,128)(2,1)S(1)} %filter_and_gate.7), channel_id=1, source_target_pairs={{0,3},{1,0},{2,1},{3,2},{4,7},{5,4},{6,5},{7,6},{8,11},{9,8},{10,9... | collective-permute-start | bytes 589832 | tf_op jit(solution)/shard_map/ppermute | solution.py:418
  316.2 17.0 %collective-permute-start.56 = (bf16[192,512]{1,0:T(8,128)(2,1)S(1)}, bf16[192,512]{1,0:T(8,128)(2,1)S(1)}, u32[]{:S(2)}, u32[]{:S(2)}) collective-permute-start(bf16[192,512]{1,0:T(8,128)(2,1)S(1)} %filter_and_gate.7), channel_id=1, source_target_pairs={{0,2},{1,3},{2,0},{3,1},{4,6},{5,7},{6,4},{7,5},{8,10},{9,11},{10,... | collective-permute-start | bytes 589832 | tf_op jit(solution)/shard_map/ppermute | solution.py:418
  316.4 16.9 %collective-permute-start.55 = (bf16[192,512]{1,0:T(8,128)(2,1)S(1)}, bf16[192,512]{1,0:T(8,128)(2,1)S(1)}, u32[]{:S(2)}, u32[]{:S(2)}) collective-permute-start(bf16[192,512]{1,0:T(8,128)(2,1)S(1)} %filter_and_gate.7), channel_id=1, source_target_pairs={{0,1},{1,2},{2,3},{3,0},{4,5},{5,6},{6,7},{7,4},{8,9},{9,10},{10,1... | collective-permute-start | bytes 589832 | tf_op jit(solution)/shard_map/ppermute | solution.py:418
  333.4 3.3 collective-permute-start.58
  340.9 1.8 collective-permute-start.59
  (35 other events, 410.7 us)
Sparse Core Ops, SparseCore 0:
  10.9 43.8 all-gather.1
